TPU v7x, 32 devices: a whole 2x2x4 slice. The times are simulated.
32 devices in a mesh: expert: 8 (over y, x, core), shard: 4 (over z).
Axes of the slice: x: 2, y: 2, z: 4, core: 2. Of those that a mesh axis runs over, the one named last changes fastest.
Arguments:
- tokens: bfloat16 [4096, 2048], P(('expert', 'shard')), may hold values from -6 to 6
- segments: int32 [32, 128], P(('expert', 'shard')), may hold values from 0 to 15, never falling along the last dimension, each value on 1 to 64 neighbouring positions
- routes: int32 [4096, 8], P(('expert', 'shard')), may hold values from 0 to 63, all different within a row; in each aligned block of 128 rows (0 to 127, 128 to 255, ...) at most 24 rows name the same one
- attn_gain: bfloat16 [2048], P('shard'), may hold values from 0.25 to 1.75
- query_key_value_weight: bfloat16 [2048, 5120], P('shard'), may hold values from -0.125 to 0.125
- query_norm_gain: bfloat16 [128], P('shard'), may hold values from 0.25 to 1.75
- k_gain: bfloat16 [128], P('shard'), may hold values from 0.25 to 1.75
- w_out: bfloat16 [4096, 2048], P('shard'), may hold values from -0.5 to 0.5
- ffn_gain: bfloat16 [2048], P('shard'), may hold values from 0.25 to 1.75
- router: bfloat16 [2048, 64], P('shard'), may hold values from -0.0625 to 0.0625
- w_gate: bfloat16 [64, 768, 2048], P('expert', 'shard'), may hold values from -0.125 to 0.125
- w_up: bfloat16 [64, 768, 2048], P('expert', 'shard'), may hold values from -0.125 to 0.125
- w_down: bfloat16 [64, 2048, 768], P('expert', None, 'shard'), may hold values from -0.625 to 0.625
- d_out: bfloat16 [4096, 2048], P(('expert', 'shard')), may hold values from -6 to 6
Outputs:
- result: bfloat16 [4096, 2048], P(('expert', 'shard'))
- d_tokens: bfloat16 [4096, 2048], P(('expert', 'shard'))
- d_attn_gain: float32 [2048], P('shard')
- d_w_qkv: float32 [2048, 5120], P('shard')
- d_q_gain: float32 [128], P('shard')
- d_k_gain: float32 [128], P('shard')
- d_w_out: float32 [4096, 2048], P('shard')
- d_ffn_gain: float32 [2048], P('shard')
- d_router: float32 [2048, 64], P('shard')
- d_w_gate: float32 [64, 768, 2048], P('expert', 'shard')
- d_w_up: float32 [64, 768, 2048], P('expert', 'shard')
- d_w_down: float32 [64, 2048, 768], P('expert', None, 'shard')
Inputs may be any that keep to these rules, and one draw needn't show every extreme that they name: `segments`: in each device's row the numbers never fall, each document has 1 to 64 tokens and one has exactly 64. `routes`: each token names 8 different experts; among the tokens of one device no expert is named more than 24 times, a bound that some block reaches.
All inputs are finite; a program needn't handle non-finite values.
Results may differ from a plain program's by a relative error of at most 0.023.
Values may be sent and summed in bfloat16 or wider, within the bound.
A program may use at most 448 MiB of HBM per device.

v0:
```python
import jax
import jax.numpy as jnp
from jax import lax
from jax.sharding import PartitionSpec as P

MODEL_WIDTH = 2048
QUERY_HEADS = 32
KEY_VALUE_HEADS = 4
HEAD_SIZE = 128
TOPK = 8
EXP_DEV = 8


EPS = 1e-06
THETA = 1000000.0


def row_norm_values(values, gain):
    inverse = lax.rsqrt(jnp.mean(values * values, axis=-1, keepdims=True) + EPS)
    unit_rows = values * inverse
    return (unit_rows * gain, unit_rows, inverse)


def norm_back(incoming, unit_rows, inverse, gain):
    inner = incoming * gain
    return inverse * (inner - unit_rows * jnp.mean(inner * unit_rows, axis=-1, keepdims=True))


def rotary_tables(token_positions):
    half_width = HEAD_SIZE // 2
    frequency = THETA ** (-2.0 * jnp.arange(half_width, dtype=jnp.float32) / HEAD_SIZE)
    angles = token_positions.astype(jnp.float32)[:, None] * frequency[None, :]
    return (jnp.cos(angles)[:, None, :], jnp.sin(angles)[:, None, :])


def apply_rotary(values, cosine, sine_part):
    half_width = values.shape[-1] // 2
    first_half = values[..., :half_width]
    second_half = values[..., half_width:]
    return jnp.concatenate(
        [
            first_half * cosine - second_half * sine_part,
            second_half * cosine + first_half * sine_part,
        ],
        axis=-1,
    )


def rotate_back(incoming, cosine, sine_part):
    half_width = incoming.shape[-1] // 2
    first_half = incoming[..., :half_width]
    second_half = incoming[..., half_width:]
    return jnp.concatenate(
        [
            first_half * cosine + second_half * sine_part,
            second_half * cosine - first_half * sine_part,
        ],
        axis=-1,
    )


def per_device(
    tokens,
    segments,
    routes,
    attn_gain,
    query_key_value_weight,
    query_norm_gain,
    k_gain,
    w_out,
    ffn_gain,
    router,
    w_gate,
    w_up,
    w_down,
    d_out,
):
    gain_one, qkv_weight, gain_query, gain_key, out_weight, gain_two, router_weight = (
        lax.all_gather(attn_gain, "shard", axis=0, tiled=True),
        lax.all_gather(query_key_value_weight, "shard", axis=0, tiled=True),
        lax.all_gather(query_norm_gain, "shard", axis=0, tiled=True),
        lax.all_gather(k_gain, "shard", axis=0, tiled=True),
        lax.all_gather(w_out, "shard", axis=0, tiled=True),
        lax.all_gather(ffn_gain, "shard", axis=0, tiled=True),
        lax.all_gather(router, "shard", axis=0, tiled=True),
    )
    sequence_length = tokens.shape[0]
    experts_all = router.shape[1]
    owners = lax.axis_size("expert")
    capacity = 3 * sequence_length * TOPK // (2 * experts_all)
    query_group_width = QUERY_HEADS // KEY_VALUE_HEADS
    scaling = HEAD_SIZE ** (-0.5)
    resident = tokens.astype(jnp.float32)
    normed_one, unit_one, inverse_one = row_norm_values(resident, gain_one)
    normed_low = normed_one.astype(jnp.bfloat16)
    projected_rows = jnp.dot(normed_low, qkv_weight, preferred_element_type=jnp.float32)
    segment_row = segments[0]
    places = jnp.arange(sequence_length, dtype=jnp.int32)
    change = jnp.concatenate(
        [jnp.ones((1,), jnp.int32), (segment_row[1:] != segment_row[:-1]).astype(jnp.int32)]
    )
    token_positions = places - lax.cummax(places * change, axis=0)
    cosine, sine_part = rotary_tables(token_positions)
    query_raw = projected_rows[:, : QUERY_HEADS * HEAD_SIZE].reshape(
        sequence_length, QUERY_HEADS, HEAD_SIZE
    )
    unnormed_key = projected_rows[
        :, QUERY_HEADS * HEAD_SIZE : (QUERY_HEADS + KEY_VALUE_HEADS) * HEAD_SIZE
    ].reshape(sequence_length, KEY_VALUE_HEADS, HEAD_SIZE)
    unnormed_value = projected_rows[:, (QUERY_HEADS + KEY_VALUE_HEADS) * HEAD_SIZE :].reshape(
        sequence_length, KEY_VALUE_HEADS, HEAD_SIZE
    )
    query_normed, query_unit, query_inverse = row_norm_values(query_raw, gain_query)
    key_normed, key_unit, key_inverse = row_norm_values(unnormed_key, gain_key)
    query_matrix = (
        apply_rotary(query_normed, cosine, sine_part)
        .astype(jnp.bfloat16)
        .reshape(sequence_length, KEY_VALUE_HEADS, query_group_width, HEAD_SIZE)
    )
    keyset = apply_rotary(key_normed, cosine, sine_part).astype(jnp.bfloat16)
    valueset = unnormed_value.astype(jnp.bfloat16)
    allowed = (segment_row[:, None] == segment_row[None, :]) & (places[None, :] <= places[:, None])
    scores = (
        jnp.einsum("qhgd,khd->hgqk", query_matrix, keyset, preferred_element_type=jnp.float32)
        * scaling
    )
    scores = jnp.where(allowed, scores, -1e30)
    highest = jnp.max(scores, axis=-1, keepdims=True)
    exponent = jnp.exp(scores - highest)
    totals = jnp.sum(exponent, axis=-1, keepdims=True)
    log_total = highest + jnp.log(totals)
    probs_low = (exponent / totals).astype(jnp.bfloat16)
    mixed_heads = jnp.einsum(
        "hgqk,khd->qhgd", probs_low, valueset, preferred_element_type=jnp.float32
    ).reshape(sequence_length, QUERY_HEADS * HEAD_SIZE)
    mixed_low = mixed_heads.astype(jnp.bfloat16)
    branch = jnp.dot(mixed_low, out_weight, preferred_element_type=jnp.float32)
    middle = resident + branch
    normed_two, unit_two, inverse_two = row_norm_values(middle, gain_two)
    normed_low_two = normed_two.astype(jnp.bfloat16)
    logits = jnp.dot(normed_low_two, router_weight, preferred_element_type=jnp.float32)
    chance = jax.nn.softmax(logits, axis=-1)
    chosen = jnp.take_along_axis(chance, routes, axis=1)
    chosen_sum = jnp.sum(chosen, axis=1, keepdims=True)
    gates = chosen / chosen_sum
    flat_routes = routes.reshape(-1)
    onehot = (flat_routes[:, None] == jnp.arange(experts_all, dtype=jnp.int32)[None, :]).astype(
        jnp.int32
    )
    ranks = jnp.sum((jnp.cumsum(onehot, axis=0) - 1) * onehot, axis=1)
    slots = flat_routes * capacity + ranks
    pair_count = sequence_length * TOPK
    pair_of_slot = (
        jnp.full((experts_all * capacity,), pair_count, jnp.int32)
        .at[slots]
        .set(jnp.arange(pair_count, dtype=jnp.int32))
    )
    token_of_slot = pair_of_slot // TOPK
    padded_rows = jnp.concatenate(
        [normed_low_two, jnp.zeros((1, MODEL_WIDTH), jnp.bfloat16)], axis=0
    )
    outgoing = padded_rows[token_of_slot].reshape(owners, EXP_DEV, capacity, MODEL_WIDTH)
    arrived = lax.all_to_all(outgoing, "expert", split_axis=0, concat_axis=2, tiled=True)[0]
    saved = []
    returned = []
    for expert_slot in range(EXP_DEV):
        block_rows = arrived[expert_slot]
        gate_mat, up_mat, down_mat = (
            lax.all_gather(w_gate[expert_slot], "shard", axis=0, tiled=True),
            lax.all_gather(w_up[expert_slot], "shard", axis=0, tiled=True),
            lax.all_gather(w_down[expert_slot], "shard", axis=1, tiled=True),
        )
        input_rows = block_rows
        gate_proj = jnp.einsum(
            "rd,fd->rf", input_rows, gate_mat, preferred_element_type=jnp.float32
        )
        up_proj = jnp.einsum("rd,fd->rf", input_rows, up_mat, preferred_element_type=jnp.float32)
        activation = (jax.nn.silu(gate_proj) * up_proj).astype(jnp.bfloat16)
        partial_out = jnp.einsum(
            "rf,df->rd", activation, down_mat, preferred_element_type=jnp.float32
        )
        expert_out = partial_out.astype(jnp.bfloat16)
        saved.append((gate_mat, up_mat, down_mat, gate_proj, up_proj, activation))
        returned.append(expert_out)
    back_home = lax.all_to_all(
        jnp.stack(returned)[None], "expert", split_axis=2, concat_axis=0, tiled=True
    ).reshape(experts_all * capacity, MODEL_WIDTH)
    pair_rows = back_home[slots].reshape(sequence_length, TOPK, MODEL_WIDTH)
    mixture = jnp.sum(gates[:, :, None] * pair_rows.astype(jnp.float32), axis=1)
    result = (middle + mixture).astype(jnp.bfloat16)
    upstream = d_out.astype(jnp.float32)
    d_gates = jnp.einsum("nkd,nd->nk", pair_rows, d_out, preferred_element_type=jnp.float32)
    d_pairs = (
        (gates[:, :, None] * upstream[:, None, :])
        .astype(jnp.bfloat16)
        .reshape(pair_count, MODEL_WIDTH)
    )
    d_padded = jnp.concatenate([d_pairs, jnp.zeros((1, MODEL_WIDTH), jnp.bfloat16)], axis=0)
    d_outgoing = d_padded[pair_of_slot].reshape(owners, EXP_DEV, capacity, MODEL_WIDTH)
    d_arrived = lax.all_to_all(d_outgoing, "expert", split_axis=0, concat_axis=2, tiled=True)[0]
    d_returned = []
    gate_grads = []
    up_grads = []
    down_grads = []
    for expert_slot in range(EXP_DEV):
        gate_mat, up_mat, down_mat, gate_proj, up_proj, activation = saved[expert_slot]
        block_rows = arrived[expert_slot]
        d_block = d_arrived[expert_slot]
        input_rows = block_rows
        d_activation = jnp.einsum(
            "rd,df->rf", d_block, down_mat, preferred_element_type=jnp.float32
        )
        d_down = jnp.einsum("rd,rf->df", d_block, activation, preferred_element_type=jnp.float32)
        sigma = jax.nn.sigmoid(gate_proj)
        d_gate_proj = (d_activation * up_proj * sigma * (1.0 + gate_proj * (1.0 - sigma))).astype(
            jnp.bfloat16
        )
        d_up_proj = (d_activation * gate_proj * sigma).astype(jnp.bfloat16)
        d_gate_mat = jnp.einsum(
            "rf,rd->fd", d_gate_proj, input_rows, preferred_element_type=jnp.float32
        )
        d_up_mat = jnp.einsum(
            "rf,rd->fd", d_up_proj, input_rows, preferred_element_type=jnp.float32
        )
        d_input = jnp.einsum("rf,fd->rd", d_gate_proj, gate_mat, preferred_element_type=jnp.float32)
        d_input = d_input + jnp.einsum(
            "rf,fd->rd", d_up_proj, up_mat, preferred_element_type=jnp.float32
        )
        d_gate_mat, d_up_mat, d_down = (
            lax.psum_scatter(
                d_gate_mat.astype(jnp.bfloat16), "shard", scatter_dimension=0, tiled=True
            ).astype(jnp.float32),
            lax.psum_scatter(
                d_up_mat.astype(jnp.bfloat16), "shard", scatter_dimension=0, tiled=True
            ).astype(jnp.float32),
            lax.psum_scatter(
                d_down.astype(jnp.bfloat16), "shard", scatter_dimension=1, tiled=True
            ).astype(jnp.float32),
        )
        d_returned.append(d_input.astype(jnp.bfloat16))
        gate_grads.append(d_gate_mat)
        up_grads.append(d_up_mat)
        down_grads.append(d_down)
    d_back = lax.all_to_all(
        jnp.stack(d_returned)[None], "expert", split_axis=2, concat_axis=0, tiled=True
    ).reshape(experts_all * capacity, MODEL_WIDTH)
    d_from_experts = jnp.sum(
        d_back[slots].reshape(sequence_length, TOPK, MODEL_WIDTH).astype(jnp.float32), axis=1
    )
    d_chosen = (d_gates - jnp.sum(d_gates * gates, axis=1, keepdims=True)) / chosen_sum
    route_match = (
        routes[:, :, None] == jnp.arange(experts_all, dtype=jnp.int32)[None, None, :]
    ).astype(jnp.float32)
    d_chance = jnp.sum(route_match * d_chosen[:, :, None], axis=1)
    d_logits = chance * (d_chance - jnp.sum(d_chance * chance, axis=1, keepdims=True))
    d_logits_low = d_logits.astype(jnp.bfloat16)
    d_router_full = jnp.einsum(
        "nd,ne->de", normed_low_two, d_logits_low, preferred_element_type=jnp.float32
    )
    d_normed_two = d_from_experts + jnp.einsum(
        "ne,de->nd", d_logits_low, router_weight, preferred_element_type=jnp.float32
    )
    d_gain_two = jnp.sum(d_normed_two * unit_two, axis=0)
    d_middle = upstream + norm_back(d_normed_two, unit_two, inverse_two, gain_two)
    d_branch_low = d_middle.astype(jnp.bfloat16)
    d_out_weight = jnp.einsum(
        "nf,nd->fd", mixed_low, d_branch_low, preferred_element_type=jnp.float32
    )
    mixed_gradient = jnp.einsum(
        "nd,fd->nf", d_branch_low, out_weight, preferred_element_type=jnp.float32
    )
    mixed_gradient = mixed_gradient.astype(jnp.bfloat16).reshape(
        sequence_length, KEY_VALUE_HEADS, query_group_width, HEAD_SIZE
    )
    again = (
        jnp.einsum("qhgd,khd->hgqk", query_matrix, keyset, preferred_element_type=jnp.float32)
        * scaling
    )
    again = jnp.where(allowed, again, -1e30)
    probs_again = jnp.exp(again - log_total)
    probs_again_low = probs_again.astype(jnp.bfloat16)
    d_probs = jnp.einsum(
        "qhgd,khd->hgqk", mixed_gradient, valueset, preferred_element_type=jnp.float32
    )
    d_scores = (
        probs_again * (d_probs - jnp.sum(d_probs * probs_again, axis=-1, keepdims=True))
    ).astype(jnp.bfloat16)
    d_queries = (
        jnp.einsum("hgqk,khd->qhgd", d_scores, keyset, preferred_element_type=jnp.float32).reshape(
            sequence_length, QUERY_HEADS, HEAD_SIZE
        )
        * scaling
    )
    d_keys = (
        jnp.einsum("hgqk,qhgd->khd", d_scores, query_matrix, preferred_element_type=jnp.float32)
        * scaling
    )
    value_gradient = jnp.einsum(
        "hgqk,qhgd->khd", probs_again_low, mixed_gradient, preferred_element_type=jnp.float32
    )
    d_query_normed = rotate_back(d_queries, cosine, sine_part)
    d_key_normed = rotate_back(d_keys, cosine, sine_part)
    d_gain_query = jnp.sum(d_query_normed * query_unit, axis=(0, 1))
    d_gain_key = jnp.sum(d_key_normed * key_unit, axis=(0, 1))
    d_query_raw = norm_back(d_query_normed, query_unit, query_inverse, gain_query)
    key_raw_gradient = norm_back(d_key_normed, key_unit, key_inverse, gain_key)
    d_projected = jnp.concatenate(
        [
            d_query_raw.reshape(sequence_length, QUERY_HEADS * HEAD_SIZE),
            key_raw_gradient.reshape(sequence_length, KEY_VALUE_HEADS * HEAD_SIZE),
            value_gradient.reshape(sequence_length, KEY_VALUE_HEADS * HEAD_SIZE),
        ],
        axis=1,
    ).astype(jnp.bfloat16)
    d_qkv_weight = jnp.einsum(
        "nd,nf->df", normed_low, d_projected, preferred_element_type=jnp.float32
    )
    d_normed_one = jnp.einsum(
        "nf,df->nd", d_projected, qkv_weight, preferred_element_type=jnp.float32
    )
    d_gain_one = jnp.sum(d_normed_one * unit_one, axis=0)
    d_tokens = (d_middle + norm_back(d_normed_one, unit_one, inverse_one, gain_one)).astype(
        jnp.bfloat16
    )
    shared_sums = (
        lax.psum_scatter(
            d_gain_one.astype(jnp.bfloat16), "shard", scatter_dimension=0, tiled=True
        ).astype(jnp.float32),
        lax.psum_scatter(
            d_qkv_weight.astype(jnp.bfloat16), "shard", scatter_dimension=0, tiled=True
        ).astype(jnp.float32),
        lax.psum_scatter(
            d_gain_query.astype(jnp.bfloat16), "shard", scatter_dimension=0, tiled=True
        ).astype(jnp.float32),
        lax.psum_scatter(
            d_gain_key.astype(jnp.bfloat16), "shard", scatter_dimension=0, tiled=True
        ).astype(jnp.float32),
        lax.psum_scatter(
            d_out_weight.astype(jnp.bfloat16), "shard", scatter_dimension=0, tiled=True
        ).astype(jnp.float32),
        lax.psum_scatter(
            d_gain_two.astype(jnp.bfloat16), "shard", scatter_dimension=0, tiled=True
        ).astype(jnp.float32),
        lax.psum_scatter(
            d_router_full.astype(jnp.bfloat16), "shard", scatter_dimension=0, tiled=True
        ).astype(jnp.float32),
    )
    grand = (
        lax.psum(shared_sums[0].astype(jnp.bfloat16), "expert").astype(jnp.float32),
        lax.psum(shared_sums[1].astype(jnp.bfloat16), "expert").astype(jnp.float32),
        lax.psum(shared_sums[2].astype(jnp.bfloat16), "expert").astype(jnp.float32),
        lax.psum(shared_sums[3].astype(jnp.bfloat16), "expert").astype(jnp.float32),
        lax.psum(shared_sums[4].astype(jnp.bfloat16), "expert").astype(jnp.float32),
        lax.psum(shared_sums[5].astype(jnp.bfloat16), "expert").astype(jnp.float32),
        lax.psum(shared_sums[6].astype(jnp.bfloat16), "expert").astype(jnp.float32),
    )
    return (
        result,
        d_tokens,
        grand[0],
        grand[1],
        grand[2],
        grand[3],
        grand[4],
        grand[5],
        grand[6],
        jnp.stack(gate_grads),
        jnp.stack(up_grads),
        jnp.stack(down_grads),
    )


def solution(mesh):
    placed = (
        P(("expert", "shard"), None),
        P(("expert", "shard"), None),
        P(("expert", "shard"), None),
        P("shard"),
        P("shard", None),
        P("shard"),
        P("shard"),
        P("shard", None),
        P("shard"),
        P("shard", None),
        P("expert", "shard", None),
        P("expert", "shard", None),
        P("expert", None, "shard"),
        P(("expert", "shard"), None),
    )
    return jax.shard_map(
        per_device,
        mesh=mesh,
        in_specs=placed,
        out_specs=(
            P(("expert", "shard"), None),
            P(("expert", "shard"), None),
            P("shard"),
            P("shard", None),
            P("shard"),
            P("shard"),
            P("shard", None),
            P("shard"),
            P("shard", None),
            P("expert", "shard", None),
            P("expert", "shard", None),
            P("expert", None, "shard"),
        ),
        check_vma=False,
    )
```

profile of v0, /device:TPU:0, one launch (start us, length us, event | category | flops | bytes accessed | tf_op | source)
XLA Modules:
  0.0 4727.1 jit_solution(15491412198900777145)
XLA Ops:
  142.6 227.1 %all-gather.53.cloned.1.call-done = bf16[2048,5120]{1,0:T(8,128)(2,1)} async-done(((bf16[512,5120]{1,0:T(8,128)(2,1)}), bf16[2048,5120]{1,0:T(8,128)(2,1)}) %all-gather.53.cloned.1.call-update) | async-done | bytes 20971536 | tf_op jit(solution)/shard_map/all_gather | solution.py:80
  388.1 268.6 %all-gather.55.cloned.1.call-done = bf16[4096,2048]{1,0:T(8,128)(2,1)} async-done(((bf16[1024,2048]{1,0:T(8,128)(2,1)}), bf16[4096,2048]{1,0:T(8,128)(2,1)}) %all-gather.55.cloned.1.call-update) | async-done | bytes 16777232 | tf_op jit(solution)/shard_map/all_gather | solution.py:83
  679.2 70.3 %all-to-all-done = bf16[8,8,24,2048]{3,2,1,0:T(8,128)(2,1)} async-done(((bf16[8,8,24,2048]{3,2,1,0:T(8,128)(2,1)}), bf16[8,8,24,2048]{3,2,1,0:T(8,128)(2,1)}, u32[]{:S(2)}, u32[]{:S(2)}) %all-to-all-start) | async-done | bytes 6291488 | tf_op jit(solution)/shard_map/all_to_all | solution.py:163
  787.7 59.5 %all-gather.69.cloned.1.call-done = bf16[1,768,2048]{2,1,0:T(8,128)(2,1)} async-done(((bf16[1,192,2048]{2,1,0:T(8,128)(2,1)}), bf16[1,768,2048]{2,1,0:T(8,128)(2,1)}) %all-gather.69.cloned.1.call-update) | async-done | bytes 3145744 | tf_op jit(solution)/shard_map/all_gather | solution.py:169
  851.3 60.0 %all-gather.75.cloned.1.call-done = bf16[1,768,2048]{2,1,0:T(8,128)(2,1)} async-done(((bf16[1,192,2048]{2,1,0:T(8,128)(2,1)}), bf16[1,768,2048]{2,1,0:T(8,128)(2,1)}) %all-gather.75.cloned.1.call-update) | async-done | bytes 3145744 | tf_op jit(solution)/shard_map/all_gather | solution.py:169
  915.5 59.6 %all-gather.59.cloned.1.call-done = bf16[1,768,2048]{2,1,0:T(8,128)(2,1)} async-done(((bf16[1,192,2048]{2,1,0:T(8,128)(2,1)}), bf16[1,768,2048]{2,1,0:T(8,128)(2,1)}) %all-gather.59.cloned.1.call-update) | async-done | bytes 3145744 | tf_op jit(solution)/shard_map/all_gather | solution.py:170
  979.5 59.4 %all-gather.65.cloned.1.call-done = bf16[1,768,2048]{2,1,0:T(8,128)(2,1)} async-done(((bf16[1,192,2048]{2,1,0:T(8,128)(2,1)}), bf16[1,768,2048]{2,1,0:T(8,128)(2,1)}) %all-gather.65.cloned.1.call-update) | async-done | bytes 3145744 | tf_op jit(solution)/shard_map/all_gather | solution.py:170
  1043.3 59.4 %all-gather.71.cloned.1.call-done = bf16[1,768,2048]{2,1,0:T(8,128)(2,1)} async-done(((bf16[1,192,2048]{2,1,0:T(8,128)(2,1)}), bf16[1,768,2048]{2,1,0:T(8,128)(2,1)}) %all-gather.71.cloned.1.call-update) | async-done | bytes 3145744 | tf_op jit(solution)/shard_map/all_gather | solution.py:170
  1106.9 59.3 %all-gather.61.cloned.1.call-done = bf16[1,2048,768]{1,2,0:T(8,128)(2,1)} async-done(((bf16[1,2048,192]{1,2,0:T(8,128)(2,1)}), bf16[1,2048,768]{1,2,0:T(8,128)(2,1)}) %all-gather.61.cloned.1.call-update) | async-done | bytes 3145744 | tf_op jit(solution)/shard_map/all_gather | solution.py:171
  1169.9 60.1 %all-gather.67.cloned.1.call-done = bf16[1,2048,768]{1,2,0:T(8,128)(2,1)} async-done(((bf16[1,2048,192]{1,2,0:T(8,128)(2,1)}), bf16[1,2048,768]{1,2,0:T(8,128)(2,1)}) %all-gather.67.cloned.1.call-update) | async-done | bytes 3145744 | tf_op jit(solution)/shard_map/all_gather | solution.py:171
  1233.6 60.0 %all-gather.73.cloned.1.call-done = bf16[1,2048,768]{1,2,0:T(8,128)(2,1)} async-done(((bf16[1,2048,192]{1,2,0:T(8,128)(2,1)}), bf16[1,2048,768]{1,2,0:T(8,128)(2,1)}) %all-gather.73.cloned.1.call-update) | async-done | bytes 3145744 | tf_op jit(solution)/shard_map/all_gather | solution.py:171
  1297.1 60.2 %all-gather.77.cloned.1.call-done = bf16[1,768,2048]{2,1,0:T(8,128)(2,1)} async-done(((bf16[1,192,2048]{2,1,0:T(8,128)(2,1)}), bf16[1,768,2048]{2,1,0:T(8,128)(2,1)}) %all-gather.77.cloned.1.call-update) | async-done | bytes 3145744 | tf_op jit(solution)/shard_map/all_gather | solution.py:170
  1361.6 59.3 %all-gather.79.cloned.1.call-done = bf16[1,2048,768]{1,2,0:T(8,128)(2,1)} async-done(((bf16[1,2048,192]{1,2,0:T(8,128)(2,1)}), bf16[1,2048,768]{1,2,0:T(8,128)(2,1)}) %all-gather.79.cloned.1.call-update) | async-done | bytes 3145744 | tf_op jit(solution)/shard_map/all_gather | solution.py:171
  1424.5 60.6 %all-gather.81.cloned.1.call-done = bf16[1,768,2048]{2,1,0:T(8,128)(2,1)} async-done(((bf16[1,192,2048]{2,1,0:T(8,128)(2,1)}), bf16[1,768,2048]{2,1,0:T(8,128)(2,1)}) %all-gather.81.cloned.1.call-update) | async-done | bytes 3145744 | tf_op jit(solution)/shard_map/all_gather | solution.py:169
  1489.3 59.5 %all-gather.83.cloned.1.call-done = bf16[1,768,2048]{2,1,0:T(8,128)(2,1)} async-done(((bf16[1,192,2048]{2,1,0:T(8,128)(2,1)}), bf16[1,768,2048]{2,1,0:T(8,128)(2,1)}) %all-gather.83.cloned.1.call-update) | async-done | bytes 3145744 | tf_op jit(solution)/shard_map/all_gather | solution.py:170
  1553.2 59.1 %all-gather.85.cloned.1.call-done = bf16[1,2048,768]{1,2,0:T(8,128)(2,1)} async-done(((bf16[1,2048,192]{1,2,0:T(8,128)(2,1)}), bf16[1,2048,768]{1,2,0:T(8,128)(2,1)}) %all-gather.85.cloned.1.call-update) | async-done | bytes 3145744 | tf_op jit(solution)/shard_map/all_gather | solution.py:171
  1615.9 60.6 %all-gather.87.cloned.1.call-done = bf16[1,768,2048]{2,1,0:T(8,128)(2,1)} async-done(((bf16[1,192,2048]{2,1,0:T(8,128)(2,1)}), bf16[1,768,2048]{2,1,0:T(8,128)(2,1)}) %all-gather.87.cloned.1.call-update) | async-done | bytes 3145744 | tf_op jit(solution)/shard_map/all_gather | solution.py:169
  1680.5 59.8 %all-gather.89.cloned.1.call-done = bf16[1,768,2048]{2,1,0:T(8,128)(2,1)} async-done(((bf16[1,192,2048]{2,1,0:T(8,128)(2,1)}), bf16[1,768,2048]{2,1,0:T(8,128)(2,1)}) %all-gather.89.cloned.1.call-update) | async-done | bytes 3145744 | tf_op jit(solution)/shard_map/all_gather | solution.py:170
  1744.4 59.5 %all-gather.91.cloned.1.call-done = bf16[1,2048,768]{1,2,0:T(8,128)(2,1)} async-done(((bf16[1,2048,192]{1,2,0:T(8,128)(2,1)}), bf16[1,2048,768]{1,2,0:T(8,128)(2,1)}) %all-gather.91.cloned.1.call-update) | async-done | bytes 3145744 | tf_op jit(solution)/shard_map/all_gather | solution.py:171
  1807.4 60.2 %all-gather.93.cloned.1.call-done = bf16[1,768,2048]{2,1,0:T(8,128)(2,1)} async-done(((bf16[1,192,2048]{2,1,0:T(8,128)(2,1)}), bf16[1,768,2048]{2,1,0:T(8,128)(2,1)}) %all-gather.93.cloned.1.call-update) | async-done | bytes 3145744 | tf_op jit(solution)/shard_map/all_gather | solution.py:169
  1871.5 59.9 %all-gather.95.cloned.1.call-done = bf16[1,768,2048]{2,1,0:T(8,128)(2,1)} async-done(((bf16[1,192,2048]{2,1,0:T(8,128)(2,1)}), bf16[1,768,2048]{2,1,0:T(8,128)(2,1)}) %all-gather.95.cloned.1.call-update) | async-done | bytes 3145744 | tf_op jit(solution)/shard_map/all_gather | solution.py:170
  1935.4 59.7 %all-gather.97.cloned.1.call-done = bf16[1,2048,768]{1,2,0:T(8,128)(2,1)} async-done(((bf16[1,2048,192]{1,2,0:T(8,128)(2,1)}), bf16[1,2048,768]{1,2,0:T(8,128)(2,1)}) %all-gather.97.cloned.1.call-update) | async-done | bytes 3145744 | tf_op jit(solution)/shard_map/all_gather | solution.py:171
  1998.7 60.6 %all-gather.99.cloned.1.call-done = bf16[1,768,2048]{2,1,0:T(8,128)(2,1)} async-done(((bf16[1,192,2048]{2,1,0:T(8,128)(2,1)}), bf16[1,768,2048]{2,1,0:T(8,128)(2,1)}) %all-gather.99.cloned.1.call-update) | async-done | bytes 3145744 | tf_op jit(solution)/shard_map/all_gather | solution.py:169
  2063.2 59.8 %all-gather.101.cloned.1.call-done = bf16[1,768,2048]{2,1,0:T(8,128)(2,1)} async-done(((bf16[1,192,2048]{2,1,0:T(8,128)(2,1)}), bf16[1,768,2048]{2,1,0:T(8,128)(2,1)}) %all-gather.101.cloned.1.call-update) | async-done | bytes 3145744 | tf_op jit(solution)/shard_map/all_gather | solution.py:170
  2127.1 59.6 %all-gather.103.cloned.1.call-done = bf16[1,2048,768]{1,2,0:T(8,128)(2,1)} async-done(((bf16[1,2048,192]{1,2,0:T(8,128)(2,1)}), bf16[1,2048,768]{1,2,0:T(8,128)(2,1)}) %all-gather.103.cloned.1.call-update) | async-done | bytes 3145744 | tf_op jit(solution)/shard_map/all_gather | solution.py:171
  2229.2 46.8 all-to-all-done.1
  2323.0 75.4 %all_to_all.60 = bf16[8,8,24,2048]{3,2,1,0:T(8,128)(2,1)S(1)} all-to-all(bf16[8,8,24,2048]{3,2,1,0:T(8,128)(2,1)} %bitcast.697), channel_id=1, replica_groups=mesh['expert'=8,'shard'=4] {'expert'}, dimensions={0} | all-to-all | bytes 12582912 | tf_op jit(solution)/shard_map/all_to_all | solution.py:200
  2536.3 62.9 %all-to-all-done.3 = bf16[1,8,192,2048]{3,1,0,2:T(8,128)(2,1)} async-done(((bf16[1,8,192,2048]{3,1,0,2:T(8,128)(2,1)}), bf16[1,8,192,2048]{3,1,0,2:T(8,128)(2,1)}, u32[]{:S(2)}, u32[]{:S(2)}) %all-to-all-start.3) | async-done | bytes 6291488 | tf_op jit(solution)/shard_map/all_to_all | solution.py:244
  2843.7 60.5 %reduce-scatter.48.cloned.1.call-done = bf16[192,2048]{1,0:T(8,128)(2,1)} async-done(((bf16[768,2048]{1,0:T(8,128)(2,1)}), bf16[192,2048]{1,0:T(8,128)(2,1)}) %reduce-scatter.48.cloned.1.call-update) | async-done | bytes 786448 | tf_op jit(solution)/shard_map/reduce_scatter | solution.py:230
  2915.4 51.4 %reduce-scatter.50.cloned.1.call-done = bf16[192,2048]{1,0:T(8,128)(2,1)} async-done(((bf16[768,2048]{1,0:T(8,128)(2,1)}), bf16[192,2048]{1,0:T(8,128)(2,1)}) %reduce-scatter.50.cloned.1.call-update) | async-done | bytes 786448 | tf_op jit(solution)/shard_map/reduce_scatter | solution.py:233
  2968.9 60.4 %reduce-scatter.52.cloned.1.call-done = bf16[192,2048]{1,0:T(8,128)(2,1)} async-done(((bf16[768,2048]{1,0:T(8,128)(2,1)}), bf16[192,2048]{1,0:T(8,128)(2,1)}) %reduce-scatter.52.cloned.1.call-update) | async-done | bytes 786448 | tf_op jit(solution)/shard_map/reduce_scatter | solution.py:233
  3031.4 60.4 %reduce-scatter.54.cloned.1.call-done = bf16[192,2048]{1,0:T(8,128)(2,1)} async-done(((bf16[768,2048]{1,0:T(8,128)(2,1)}), bf16[192,2048]{1,0:T(8,128)(2,1)}) %reduce-scatter.54.cloned.1.call-update) | async-done | bytes 786448 | tf_op jit(solution)/shard_map/reduce_scatter | solution.py:233
  3093.9 60.5 %reduce-scatter.56.cloned.1.call-done = bf16[192,2048]{1,0:T(8,128)(2,1)} async-done(((bf16[768,2048]{1,0:T(8,128)(2,1)}), bf16[192,2048]{1,0:T(8,128)(2,1)}) %reduce-scatter.56.cloned.1.call-update) | async-done | bytes 786448 | tf_op jit(solution)/shard_map/reduce_scatter | solution.py:233
  3156.5 60.4 %reduce-scatter.58.cloned.1.call-done = bf16[192,2048]{1,0:T(8,128)(2,1)} async-done(((bf16[768,2048]{1,0:T(8,128)(2,1)}), bf16[192,2048]{1,0:T(8,128)(2,1)}) %reduce-scatter.58.cloned.1.call-update) | async-done | bytes 786448 | tf_op jit(solution)/shard_map/reduce_scatter | solution.py:233
  3219.0 60.5 %reduce-scatter.60.cloned.1.call-done = bf16[192,2048]{1,0:T(8,128)(2,1)} async-done(((bf16[768,2048]{1,0:T(8,128)(2,1)}), bf16[192,2048]{1,0:T(8,128)(2,1)}) %reduce-scatter.60.cloned.1.call-update) | async-done | bytes 786448 | tf_op jit(solution)/shard_map/reduce_scatter | solution.py:233
  3301.5 281.0 %reduce-scatter.30.cloned.1.call-done = bf16[1024,2048]{1,0:T(8,128)(2,1)} async-done(((bf16[4096,2048]{1,0:T(8,128)(2,1)}), bf16[1024,2048]{1,0:T(8,128)(2,1)}) %reduce-scatter.30.cloned.1.call-update) | async-done | bytes 4194320 | tf_op jit(solution)/shard_map/reduce_scatter | solution.py:338
  3582.5 350.2 %reduce-scatter.28.cloned.1.call-done = bf16[512,5120]{1,0:T(8,128)(2,1)} async-done(((bf16[2048,5120]{1,0:T(8,128)(2,1)}), bf16[512,5120]{1,0:T(8,128)(2,1)}) %reduce-scatter.28.cloned.1.call-update) | async-done | bytes 5242896 | tf_op jit(solution)/shard_map/reduce_scatter | solution.py:329
  3932.7 64.7 %reduce-scatter.62.cloned.1.call-done = bf16[192,2048]{1,0:T(8,128)(2,1)} async-done(((bf16[768,2048]{1,0:T(8,128)(2,1)}), bf16[192,2048]{1,0:T(8,128)(2,1)}) %reduce-scatter.62.cloned.1.call-update) | async-done | bytes 786448 | tf_op jit(solution)/shard_map/reduce_scatter | solution.py:233
  3999.5 61.1 %reduce-scatter.64.cloned.1.call-done = bf16[192,2048]{1,0:T(8,128)(2,1)} async-done(((bf16[768,2048]{1,0:T(8,128)(2,1)}), bf16[192,2048]{1,0:T(8,128)(2,1)}) %reduce-scatter.64.cloned.1.call-update) | async-done | bytes 786448 | tf_op jit(solution)/shard_map/reduce_scatter | solution.py:233
  4071.7 51.4 %reduce-scatter.66.cloned.1.call-done = bf16[2048,192]{0,1:T(8,128)(2,1)} async-done(((bf16[2048,768]{0,1:T(8,128)(2,1)}), bf16[2048,192]{0,1:T(8,128)(2,1)}) %reduce-scatter.66.cloned.1.call-update) | async-done | bytes 786448 | tf_op jit(solution)/shard_map/reduce_scatter | solution.py:236
  4125.2 60.5 %reduce-scatter.68.cloned.1.call-done = bf16[2048,192]{0,1:T(8,128)(2,1)} async-done(((bf16[2048,768]{0,1:T(8,128)(2,1)}), bf16[2048,192]{0,1:T(8,128)(2,1)}) %reduce-scatter.68.cloned.1.call-update) | async-done | bytes 786448 | tf_op jit(solution)/shard_map/reduce_scatter | solution.py:236
  4187.8 60.5 %reduce-scatter.70.cloned.1.call-done = bf16[2048,192]{0,1:T(8,128)(2,1)} async-done(((bf16[2048,768]{0,1:T(8,128)(2,1)}), bf16[2048,192]{0,1:T(8,128)(2,1)}) %reduce-scatter.70.cloned.1.call-update) | async-done | bytes 786448 | tf_op jit(solution)/shard_map/reduce_scatter | solution.py:236
  4250.3 60.5 %reduce-scatter.72.cloned.1.call-done = bf16[2048,192]{0,1:T(8,128)(2,1)} async-done(((bf16[2048,768]{0,1:T(8,128)(2,1)}), bf16[2048,192]{0,1:T(8,128)(2,1)}) %reduce-scatter.72.cloned.1.call-update) | async-done | bytes 786448 | tf_op jit(solution)/shard_map/reduce_scatter | solution.py:236
  4312.9 60.6 %reduce-scatter.74.cloned.1.call-done = bf16[2048,192]{0,1:T(8,128)(2,1)} async-done(((bf16[2048,768]{0,1:T(8,128)(2,1)}), bf16[2048,192]{0,1:T(8,128)(2,1)}) %reduce-scatter.74.cloned.1.call-update) | async-done | bytes 786448 | tf_op jit(solution)/shard_map/reduce_scatter | solution.py:236
  4375.6 60.5 %reduce-scatter.76.cloned.1.call-done = bf16[2048,192]{0,1:T(8,128)(2,1)} async-done(((bf16[2048,768]{0,1:T(8,128)(2,1)}), bf16[2048,192]{0,1:T(8,128)(2,1)}) %reduce-scatter.76.cloned.1.call-update) | async-done | bytes 786448 | tf_op jit(solution)/shard_map/reduce_scatter | solution.py:236
  4438.2 60.6 %reduce-scatter.78.cloned.1.call-done = bf16[2048,192]{0,1:T(8,128)(2,1)} async-done(((bf16[2048,768]{0,1:T(8,128)(2,1)}), bf16[2048,192]{0,1:T(8,128)(2,1)}) %reduce-scatter.78.cloned.1.call-update) | async-done | bytes 786448 | tf_op jit(solution)/shard_map/reduce_scatter | solution.py:236
  4500.9 60.5 %reduce-scatter.80.cloned.1.call-done = bf16[2048,192]{0,1:T(8,128)(2,1)} async-done(((bf16[2048,768]{0,1:T(8,128)(2,1)}), bf16[2048,192]{0,1:T(8,128)(2,1)}) %reduce-scatter.80.cloned.1.call-update) | async-done | bytes 786448 | tf_op jit(solution)/shard_map/reduce_scatter | solution.py:236
  4572.8 132.9 %all-reduce.14.cloned.1.call-done = (bf16[512,5120]{1,0:T(8,128)(2,1)}, bf16[1024,2048]{1,0:T(8,128)(2,1)}, bf16[512,64]{0,1:T(8,128)(2,1)}) async-done(((bf16[512,5120]{1,0:T(8,128)(2,1)}, bf16[1024,2048]{1,0:T(8,128)(2,1)}, bf16[512,64]{0,1:T(8,128)(2,1)}), (bf16[512,5120]{1,0:T(8,128)(2,1)}, bf16[1024,2048]{1,0:T(8,128)(2,1)}, bf16[512,64]{0,1:T(8,128)(2,1)})) %all-reduce.14.cloned.1.call-update) | async-done | bytes 9502736 | tf_op jit(solution)/shard_map/psum | solution.py:350
  (666 shorter events, 862.2 us)
Async XLA Ops:
  7.9 648.7 %all-gather.55.cloned.1.call-start = ((), (), s32[]{:S(2)}) async-start(), calls=%async_computation.32 | async-start | bytes 20971520 | tf_op jit(solution)/shard_map/all_gather | solution.py:83
  8.7 745.7 %all-gather.57.cloned.1.call-start = ((), (), s32[]{:S(2)}) async-start(), calls=%async_computation.60 | async-start | bytes 3932160 | tf_op jit(solution)/shard_map/all_gather | solution.py:169
  14.3 769.3 %all-gather.63.cloned.1.call-start = ((), (), s32[]{:S(2)}) async-start(), calls=%async_computation.63 | async-start | bytes 3932160 | tf_op jit(solution)/shard_map/all_gather | solution.py:169
  14.9 832.3 %all-gather.69.cloned.1.call-start = ((), (), s32[]{:S(2)}) async-start(), calls=%async_computation.66 | async-start | bytes 3932160 | tf_op jit(solution)/shard_map/all_gather | solution.py:169
  15.5 895.9 %all-gather.75.cloned.1.call-start = ((), (), s32[]{:S(2)}) async-start(), calls=%async_computation.69 | async-start | bytes 3932160 | tf_op jit(solution)/shard_map/all_gather | solution.py:169
  16.0 959.0 %all-gather.59.cloned.1.call-start = ((), (), s32[]{:S(2)}) async-start(), calls=%async_computation.61 | async-start | bytes 3932160 | tf_op jit(solution)/shard_map/all_gather | solution.py:170
  22.6 1016.2 %all-gather.65.cloned.1.call-start = ((), (), s32[]{:S(2)}) async-start(), calls=%async_computation.64 | async-start | bytes 3932160 | tf_op jit(solution)/shard_map/all_gather | solution.py:170
  23.4 1079.2 %all-gather.71.cloned.1.call-start = ((), (), s32[]{:S(2)}) async-start(), calls=%async_computation.67 | async-start | bytes 3932160 | tf_op jit(solution)/shard_map/all_gather | solution.py:170
  24.1 1142.1 %all-gather.61.cloned.1.call-start = ((), (), s32[]{:S(2)}) async-start(), calls=%async_computation.62 | async-start | bytes 3932160 | tf_op jit(solution)/shard_map/all_gather | solution.py:171
  30.6 1199.3 %all-gather.67.cloned.1.call-start = ((), (), s32[]{:S(2)}) async-start(), calls=%async_computation.65 | async-start | bytes 3932160 | tf_op jit(solution)/shard_map/all_gather | solution.py:171
  31.4 1262.2 %all-gather.73.cloned.1.call-start = ((), (), s32[]{:S(2)}) async-start(), calls=%async_computation.68 | async-start | bytes 3932160 | tf_op jit(solution)/shard_map/all_gather | solution.py:171
  31.9 1325.4 %all-gather.77.cloned.1.call-start = ((), (), s32[]{:S(2)}) async-start(), calls=%async_computation.70 | async-start | bytes 3932160 | tf_op jit(solution)/shard_map/all_gather | solution.py:170
  32.7 1388.2 %all-gather.79.cloned.1.call-start = ((), (), s32[]{:S(2)}) async-start(), calls=%async_computation.71 | async-start | bytes 3932160 | tf_op jit(solution)/shard_map/all_gather | solution.py:171
  33.3 1451.8 %all-gather.81.cloned.1.call-start = ((), (), s32[]{:S(2)}) async-start(), calls=%async_computation.72 | async-start | bytes 3932160 | tf_op jit(solution)/shard_map/all_gather | solution.py:169
  33.9 1514.9 %all-gather.83.cloned.1.call-start = ((), (), s32[]{:S(2)}) async-start(), calls=%async_computation.73 | async-start | bytes 3932160 | tf_op jit(solution)/shard_map/all_gather | solution.py:170
  34.4 1577.9 %all-gather.85.cloned.1.call-start = ((), (), s32[]{:S(2)}) async-start(), calls=%async_computation.74 | async-start | bytes 3932160 | tf_op jit(solution)/shard_map/all_gather | solution.py:171
  35.0 1641.5 %all-gather.87.cloned.1.call-start = ((), (), s32[]{:S(2)}) async-start(), calls=%async_computation.75 | async-start | bytes 3932160 | tf_op jit(solution)/shard_map/all_gather | solution.py:169
  35.6 1704.7 %all-gather.89.cloned.1.call-start = ((), (), s32[]{:S(2)}) async-start(), calls=%async_computation.76 | async-start | bytes 3932160 | tf_op jit(solution)/shard_map/all_gather | solution.py:170
  36.3 1767.5 %all-gather.91.cloned.1.call-start = ((), (), s32[]{:S(2)}) async-start(), calls=%async_computation.77 | async-start | bytes 3932160 | tf_op jit(solution)/shard_map/all_gather | solution.py:171
  36.9 1830.7 %all-gather.93.cloned.1.call-start = ((), (), s32[]{:S(2)}) async-start(), calls=%async_computation.78 | async-start | bytes 3932160 | tf_op jit(solution)/shard_map/all_gather | solution.py:169
  37.7 1893.7 %all-gather.95.cloned.1.call-start = ((), (), s32[]{:S(2)}) async-start(), calls=%async_computation.79 | async-start | bytes 3932160 | tf_op jit(solution)/shard_map/all_gather | solution.py:170
  38.4 1956.7 %all-gather.97.cloned.1.call-start = ((), (), s32[]{:S(2)}) async-start(), calls=%async_computation.80 | async-start | bytes 3932160 | tf_op jit(solution)/shard_map/all_gather | solution.py:171
  39.1 2020.2 %all-gather.99.cloned.1.call-start = ((), (), s32[]{:S(2)}) async-start(), calls=%async_computation.81 | async-start | bytes 3932160 | tf_op jit(solution)/shard_map/all_gather | solution.py:169
  677.8 1445.2 %all-gather.101.cloned.1.call-start = ((), (), s32[]{:S(2)}) async-start(), calls=%async_computation.82 | async-start | bytes 3932160 | tf_op jit(solution)/shard_map/all_gather | solution.py:170
  678.6 1508.1 %all-gather.103.cloned.1.call-start = ((), (), s32[]{:S(2)}) async-start(), calls=%async_computation.83 | async-start | bytes 3932160 | tf_op jit(solution)/shard_map/all_gather | solution.py:171
  2204.5 579.9 %reduce-scatter.34.cloned.1.call-start = ((), (), s32[]{:S(2)}) async-start(), calls=%async_computation.36 | async-start | bytes 3932160 | tf_op jit(solution)/shard_map/reduce_scatter | solution.py:230
  2446.3 395.3 %reduce-scatter.46.cloned.1.call-start = ((), (), s32[]{:S(2)}) async-start(), calls=%async_computation.42 | async-start | bytes 3932160 | tf_op jit(solution)/shard_map/reduce_scatter | solution.py:230
  2454.2 450.0 %reduce-scatter.48.cloned.1.call-start = ((), (), s32[]{:S(2)}) async-start(), calls=%async_computation.43 | async-start | bytes 3932160 | tf_op jit(solution)/shard_map/reduce_scatter | solution.py:230
  2462.2 504.6 %reduce-scatter.50.cloned.1.call-start = ((), (), s32[]{:S(2)}) async-start(), calls=%async_computation.44 | async-start | bytes 3932160 | tf_op jit(solution)/shard_map/reduce_scatter | solution.py:233
  2466.1 563.2 %reduce-scatter.52.cloned.1.call-start = ((), (), s32[]{:S(2)}) async-start(), calls=%async_computation.45 | async-start | bytes 3932160 | tf_op jit(solution)/shard_map/reduce_scatter | solution.py:233
  2470.1 621.7 %reduce-scatter.54.cloned.1.call-start = ((), (), s32[]{:S(2)}) async-start(), calls=%async_computation.46 | async-start | bytes 3932160 | tf_op jit(solution)/shard_map/reduce_scatter | solution.py:233
  2474.1 680.3 %reduce-scatter.56.cloned.1.call-start = ((), (), s32[]{:S(2)}) async-start(), calls=%async_computation.47 | async-start | bytes 3932160 | tf_op jit(solution)/shard_map/reduce_scatter | solution.py:233
  2478.2 738.7 %reduce-scatter.58.cloned.1.call-start = ((), (), s32[]{:S(2)}) async-start(), calls=%async_computation.48 | async-start | bytes 3932160 | tf_op jit(solution)/shard_map/reduce_scatter | solution.py:233
  2482.2 797.3 %reduce-scatter.60.cloned.1.call-start = ((), (), s32[]{:S(2)}) async-start(), calls=%async_computation.49 | async-start | bytes 3932160 | tf_op jit(solution)/shard_map/reduce_scatter | solution.py:233
  2527.7 773.8 %reduce-scatter.32.cloned.1.call-start = ((), (), s32[]{:S(2)}) async-start(), calls=%async_computation.35 | async-start | bytes 327680 | tf_op jit(solution)/shard_map/reduce_scatter | solution.py:344
  2528.8 1053.7 %reduce-scatter.30.cloned.1.call-start = ((), (), s32[]{:S(2)}) async-start(), calls=%async_computation.34 | async-start | bytes 20971520 | tf_op jit(solution)/shard_map/reduce_scatter | solution.py:338
  2638.0 1294.7 %reduce-scatter.28.cloned.1.call-start = ((), (), s32[]{:S(2)}) async-start(), calls=%async_computation.33 | async-start | bytes 26214400 | tf_op jit(solution)/shard_map/reduce_scatter | solution.py:329
  2703.8 1293.6 %reduce-scatter.62.cloned.1.call-start = ((), (), s32[]{:S(2)}) async-start(), calls=%async_computation.50 | async-start | bytes 3932160 | tf_op jit(solution)/shard_map/reduce_scatter | solution.py:233
  2706.6 1353.9 %reduce-scatter.64.cloned.1.call-start = ((), (), s32[]{:S(2)}) async-start(), calls=%async_computation.51 | async-start | bytes 3932160 | tf_op jit(solution)/shard_map/reduce_scatter | solution.py:233
  2710.3 1412.8 %reduce-scatter.66.cloned.1.call-start = ((), (), s32[]{:S(2)}) async-start(), calls=%async_computation.52 | async-start | bytes 3932160 | tf_op jit(solution)/shard_map/reduce_scatter | solution.py:236
  2714.2 1471.5 %reduce-scatter.68.cloned.1.call-start = ((), (), s32[]{:S(2)}) async-start(), calls=%async_computation.53 | async-start | bytes 3932160 | tf_op jit(solution)/shard_map/reduce_scatter | solution.py:236
  2718.1 1530.2 %reduce-scatter.70.cloned.1.call-start = ((), (), s32[]{:S(2)}) async-start(), calls=%async_computation.54 | async-start | bytes 3932160 | tf_op jit(solution)/shard_map/reduce_scatter | solution.py:236
  2722.0 1588.8 %reduce-scatter.72.cloned.1.call-start = ((), (), s32[]{:S(2)}) async-start(), calls=%async_computation.55 | async-start | bytes 3932160 | tf_op jit(solution)/shard_map/reduce_scatter | solution.py:236
  2726.0 1647.6 %reduce-scatter.74.cloned.1.call-start = ((), (), s32[]{:S(2)}) async-start(), calls=%async_computation.56 | async-start | bytes 3932160 | tf_op jit(solution)/shard_map/reduce_scatter | solution.py:236
  2729.8 1706.3 %reduce-scatter.76.cloned.1.call-start = ((), (), s32[]{:S(2)}) async-start(), calls=%async_computation.57 | async-start | bytes 3932160 | tf_op jit(solution)/shard_map/reduce_scatter | solution.py:236
  2733.7 1765.1 %reduce-scatter.78.cloned.1.call-start = ((), (), s32[]{:S(2)}) async-start(), calls=%async_computation.58 | async-start | bytes 3932160 | tf_op jit(solution)/shard_map/reduce_scatter | solution.py:236
  2737.7 1823.7 %reduce-scatter.80.cloned.1.call-start = ((), (), s32[]{:S(2)}) async-start(), calls=%async_computation.59 | async-start | bytes 3932160 | tf_op jit(solution)/shard_map/reduce_scatter | solution.py:236
  2741.9 1963.9 %all-reduce.14.cloned.1.call-start = ((), (), s32[]{:S(2)}) async-start(), calls=%async_computation.84 | async-start | bytes 19005440 | tf_op jit(solution)/shard_map/psum | solution.py:350
  (151 other events, 7148.8 us)
Sparse Core Ops, SparseCore 0:
  9.6 360.0 all-gather.52
  371.2 285.3 all-gather.54
  658.2 61.6 all-gather.56
  721.4 62.1 all-gather.62
  785.0 62.1 all-gather.68
  849.2 62.1 all-gather.74
  912.9 62.1 all-gather.58
  976.7 62.1 all-gather.64
  1040.4 62.1 all-gather.70
  1104.0 62.1 all-gather.60
  1167.8 62.1 all-gather.66
  1231.4 62.1 all-gather.72
  1295.1 62.1 all-gather.76
  1358.8 62.1 all-gather.78
  1422.9 62.1 all-gather.80
  1486.5 62.1 all-gather.82
  1550.1 62.1 all-gather.84
  1614.3 62.1 all-gather.86
  1678.1 62.1 all-gather.88
  1741.7 62.1 all-gather.90
  1805.4 62.1 all-gather.92
  1869.2 62.1 all-gather.94
  1932.9 62.1 all-gather.96
  1997.1 62.1 all-gather.98
  2060.9 62.1 all-gather.100
  2124.5 62.1 all-gather.102
  2467.7 60.2 reduce-scatter.35
  2530.4 60.2 reduce-scatter.37
  2592.8 60.2 reduce-scatter.39
  2655.5 60.2 reduce-scatter.41
  2718.1 60.9 reduce-scatter.43
  2781.2 60.3 reduce-scatter.45
  2843.9 60.2 reduce-scatter.47
  2906.5 60.2 reduce-scatter.49
  2969.0 60.2 reduce-scatter.51
  3031.5 60.2 reduce-scatter.53
  3094.1 60.2 reduce-scatter.55
  3156.6 60.2 reduce-scatter.57
  3219.2 60.2 reduce-scatter.59
  3304.0 278.4 reduce-scatter.29
  3584.7 347.9 reduce-scatter.27
  3935.7 61.6 reduce-scatter.61
  4062.8 60.2 reduce-scatter.65
  4125.4 60.2 reduce-scatter.67
  4250.5 60.2 reduce-scatter.71
  4313.2 60.2 reduce-scatter.73
  4501.1 60.2 reduce-scatter.79
  4565.9 139.7 all-reduce.13
  (6 shorter events, 317.5 us)
where the time goes:
time: 4730 us
  waiting for transfers between devices  3870 us (82%)
  matrix products  293 us (6%)
  local copies, waits for them, and re-layouts  231 us (5%)
  blocking collectives  187 us (4%)
  other arithmetic  105 us (2%)
    reduce_scatter x8, waiting for transfers between devices, per_device(): lax.psum_scatter(d_up_mat.astype(jnp.bfloat16), 'shard', scatter_dimensio...  479 us
    all_gather x8, waiting for transfers between devices, per_device(): lax.all_gather(w_up[expert_slot], 'shard', axis=0, tiled=True)  477 us
    all_gather x8, waiting for transfers between devices, per_device(): lax.all_gather(w_down[expert_slot], 'shard', axis=1, tiled=True)  477 us
    reduce_scatter x8, waiting for transfers between devices, per_device(): lax.psum_scatter(d_down.astype(jnp.bfloat16), 'shard', scatter_dimension=...  475 us
    all_gather x8, waiting for transfers between devices, per_device(): lax.all_gather(w_gate[expert_slot], 'shard', axis=0, tiled=True)  387 us
    reduce_scatter x1, waiting for transfers between devices, per_device(): lax.psum_scatter(d_qkv_weight.astype(jnp.bfloat16), 'shard', scatter_dime...  350 us
    reduce_scatter x1, waiting for transfers between devices, per_device(): lax.psum_scatter(d_out_weight.astype(jnp.bfloat16), 'shard', scatter_dime...  281 us
    all_gather x1, waiting for transfers between devices, per_device(): lax.all_gather(w_out, 'shard', axis=0, tiled=True)  269 us
  transfers between devices with their start and end apart: 57, of which 50 were waited for; matrix products, arithmetic and copies ran while one was open for 11% of the time, Pallas kernels for 0%

commit v1 on v0

v1 whole, which is shorter than its diff:
```python
import jax
import jax.numpy as jnp
from jax import lax
from jax.sharding import PartitionSpec as P

MODEL_WIDTH = 2048
QUERY_HEADS = 32
KEY_VALUE_HEADS = 4
HEAD_SIZE = 128
TOPK = 8
EXP_DEV = 8
TAIL = 128
GROUP_BLOCKS = 32

EPS = 1e-06
THETA = 1000000.0
LOW = jnp.bfloat16
FULL = jnp.float32


def unit_norm(values):
    inverse = lax.rsqrt(jnp.mean(values * values, axis=-1, keepdims=True) + EPS)
    return values * inverse, inverse


def norm_back(incoming, unit_rows, inverse, gain):
    inner = incoming * gain
    return inverse * (inner - unit_rows * jnp.mean(inner * unit_rows, axis=-1, keepdims=True))


def rotate(values, cosine, sine):
    half = values.shape[-1] // 2
    a, b = values[..., :half], values[..., half:]
    return jnp.concatenate([a * cosine - b * sine, b * cosine + a * sine], axis=-1)


def rotate_back(values, cosine, sine):
    half = values.shape[-1] // 2
    a, b = values[..., :half], values[..., half:]
    return jnp.concatenate([a * cosine + b * sine, b * cosine - a * sine], axis=-1)


def dot(spec, left, right):
    return jnp.einsum(spec, left, right, preferred_element_type=FULL)


def positions_of(segment_row):
    places = jnp.arange(segment_row.shape[0], dtype=jnp.int32)
    before = (segment_row[None, :] == segment_row[:, None]) & (places[None, :] < places[:, None])
    return jnp.sum(before.astype(jnp.int32), axis=1)


def columns(parts, rows):
    wide = jnp.concatenate([part.astype(LOW) for part in parts], axis=1)
    return jnp.pad(wide, ((0, rows - wide.shape[0]), (0, TAIL - wide.shape[1])))


def per_device(
    tokens,
    segments,
    routes,
    attn_gain,
    qkv_weight,
    query_gain,
    k_gain,
    w_out,
    ffn_gain,
    router,
    w_gate,
    w_up,
    w_down,
    d_out,
):
    owners = lax.axis_size("expert")
    planes = lax.axis_size("shard")
    me = lax.axis_index("expert")
    plane = lax.axis_index("shard")
    length = tokens.shape[0]
    blocks = owners * planes
    experts_all = router.shape[1]
    capacity = 3 * length * TOPK // (2 * experts_all)
    heads = QUERY_HEADS // owners
    query_cols = heads * HEAD_SIZE
    scaling = HEAD_SIZE ** (-0.5)
    both = ("expert", "shard")
    rows_in = qkv_weight.shape[0]

    kv_head = me * KEY_VALUE_HEADS // owners
    k_at = QUERY_HEADS * HEAD_SIZE + kv_head * HEAD_SIZE
    v_at = k_at + KEY_VALUE_HEADS * HEAD_SIZE
    gains = columns(
        [
            router,
            attn_gain[:, None],
            ffn_gain[:, None],
            jnp.pad(query_gain, (0, rows_in - query_gain.shape[0]))[:, None],
            jnp.pad(k_gain, (0, rows_in - k_gain.shape[0]))[:, None],
        ],
        rows_in,
    )
    mine = jnp.concatenate(
        [
            lax.dynamic_slice_in_dim(qkv_weight, me * query_cols, query_cols, 1),
            lax.dynamic_slice_in_dim(qkv_weight, k_at, HEAD_SIZE, 1),
            lax.dynamic_slice_in_dim(qkv_weight, v_at, HEAD_SIZE, 1),
            gains,
        ],
        axis=1,
    )
    gathered = lax.all_gather(mine, "shard", axis=0, tiled=True)
    qkv_cols = query_cols + 2 * HEAD_SIZE
    wqkv = gathered[:, :qkv_cols]
    router_full = gathered[:, qkv_cols : qkv_cols + experts_all]
    gain_cols = gathered[:, qkv_cols + experts_all :].astype(FULL)
    gain_one, gain_two = gain_cols[:, 0], gain_cols[:, 1]
    per = query_gain.shape[0]
    by_plane = gain_cols.reshape(planes, rows_in, -1)[:, :per]
    gain_query = by_plane[:, :, 2].reshape(-1)
    gain_key = by_plane[:, :, 3].reshape(-1)

    segment_row = segments[0]
    token_tail = columns(
        [segment_row[:, None], positions_of(segment_row)[:, None]], length
    )
    plane_rows = lax.all_gather(
        jnp.concatenate([tokens, token_tail], axis=1), "expert", axis=0, tiled=False
    )
    plane_tokens = plane_rows[:, :, :MODEL_WIDTH].astype(FULL)
    plane_segments = plane_rows[:, :, MODEL_WIDTH]
    plane_places = plane_rows[:, :, MODEL_WIDTH + 1].astype(FULL)

    out_rows = w_out.shape[0]
    first = me * query_cols
    offset = first - plane * out_rows
    if out_rows >= query_cols:
        held = (offset >= 0) & (offset < out_rows)
        piece = lax.dynamic_slice_in_dim(w_out, jnp.where(held, offset, 0), query_cols, 0)
        w_mine = lax.psum(jnp.where(held, piece, 0).astype(LOW), "shard")
    else:
        parts = query_cols // out_rows
        at = plane - me * parts
        held = (at >= 0) & (at < parts)
        spread = jnp.where(held & (jnp.arange(parts) == at)[:, None, None], w_out[None], 0)
        w_mine = lax.psum(spread.astype(LOW), "shard").reshape(query_cols, MODEL_WIDTH)

    d_tail = columns([routes], length)
    d_all = lax.all_gather(
        jnp.concatenate([d_out, d_tail], axis=1), both, axis=0, tiled=False
    )

    unit_plane, inverse_plane = unit_norm(plane_tokens)
    h1 = (unit_plane * gain_one).astype(LOW)
    projected = dot("bqd,df->bqf", h1, wqkv)
    half = HEAD_SIZE // 2
    frequency = THETA ** (-2.0 * jnp.arange(half, dtype=FULL) / HEAD_SIZE)
    angles = plane_places[:, :, None] * frequency
    cosine, sine = jnp.cos(angles), jnp.sin(angles)
    cosine_q, sine_q = cosine[:, :, None, :], sine[:, :, None, :]
    query_raw = projected[:, :, :query_cols].reshape(owners, length, heads, HEAD_SIZE)
    key_raw = projected[:, :, query_cols : query_cols + HEAD_SIZE]
    value = projected[:, :, query_cols + HEAD_SIZE :].astype(LOW)
    query_unit, query_inverse = unit_norm(query_raw)
    key_unit, key_inverse = unit_norm(key_raw)
    query = rotate(query_unit * gain_query, cosine_q, sine_q).astype(LOW)
    key = rotate(key_unit * gain_key, cosine, sine).astype(LOW)
    places = jnp.arange(length, dtype=jnp.int32)
    allowed = (plane_segments[:, :, None] == plane_segments[:, None, :]) & (
        places[None, :] <= places[:, None]
    )
    scores = dot("bqhd,bkd->bhqk", query, key) * scaling
    scores = jnp.where(allowed[:, None], scores, -1e30)
    highest = jnp.max(scores, axis=-1, keepdims=True)
    exponent = jnp.exp(scores - highest)
    probs = exponent / jnp.sum(exponent, axis=-1, keepdims=True)
    probs_low = probs.astype(LOW)
    mixed = dot("bhqk,bkd->bqhd", probs_low, value).astype(LOW)
    mixed = mixed.reshape(owners, length, query_cols)
    partial = dot("bqf,fd->bqd", mixed, w_mine).astype(LOW)
    branch = lax.psum_scatter(partial, "expert", scatter_dimension=0, tiled=False)

    middle = tokens.astype(FULL) + branch.astype(FULL)
    unit_two, inverse_two = unit_norm(middle)
    h2 = (unit_two * gain_two).astype(LOW)
    logits = dot("nd,de->ne", h2, router_full)
    chance = jax.nn.softmax(logits, axis=-1)
    named = jnp.sum(
        (routes[:, :, None] == jnp.arange(experts_all, dtype=jnp.int32)).astype(FULL), axis=1
    )
    chosen_sum = jnp.sum(named * chance, axis=1, keepdims=True)
    gates = named * chance / chosen_sum
    gates_high = gates.astype(LOW)
    gates_rest = (gates - gates_high.astype(FULL)).astype(LOW)
    h_all = lax.all_gather(
        jnp.concatenate([h2, gates_high, gates_rest], axis=1), both, axis=0, tiled=False
    )

    route_all = d_all[:, :, MODEL_WIDTH : MODEL_WIDTH + TOPK].astype(FULL)
    own_experts = (me * EXP_DEV + jnp.arange(EXP_DEV, dtype=jnp.int32)).astype(FULL)
    match = jnp.sum((route_all[:, :, :, None] == own_experts).astype(FULL), axis=2)
    earlier = (places[None, :] < places[:, None]).astype(LOW)
    rank = dot("ts,bsj->btj", earlier, match.astype(LOW))
    slot_ids = jnp.arange(capacity, dtype=jnp.int32).astype(FULL)
    place = jnp.where(match > 0, rank, -1.0).transpose(0, 2, 1)
    dispatch = (place[:, :, None, :] == slot_ids[:, None]).astype(LOW)

    def experts(h_rows, d_rows, gate_high, gate_rest, put):
        count = h_rows.shape[0]
        flat = put.reshape(count, EXP_DEV * capacity, length)
        x = dot("bst,btd->bsd", flat, h_rows).astype(LOW)
        dy = dot("bst,btd->bsd", flat, d_rows).astype(LOW)

        def by_expert(v):
            v = v.reshape(count, EXP_DEV, capacity, v.shape[-1])
            return v.transpose(1, 0, 2, 3).reshape(EXP_DEV, count * capacity, v.shape[-1])

        def by_block(v):
            v = v.reshape(EXP_DEV, count, capacity, v.shape[-1])
            return v.transpose(1, 0, 2, 3).reshape(count, EXP_DEV * capacity, v.shape[-1])

        x, dy = by_expert(x), by_expert(dy)
        gate_slot = dot("bjct,btj->jbc", put, gate_high) + dot("bjct,btj->jbc", put, gate_rest)
        gate_slot = gate_slot.reshape(EXP_DEV, count * capacity, 1)
        g = dot("erd,efd->erf", x, w_gate)
        u = dot("erd,efd->erf", x, w_up)
        da = dot("erd,edf->erf", dy, w_down)
        sigma = jax.nn.sigmoid(g)
        silu = g * sigma
        act = (silu * u).astype(LOW).astype(FULL)
        d_gate_slot = jnp.sum(act * da, axis=-1)
        act_gated = (act * gate_slot).astype(LOW)
        d_act = da * gate_slot
        dg = (d_act * u * sigma * (1.0 + g * (1.0 - sigma))).astype(LOW)
        du = (d_act * silu).astype(LOW)
        y = dot("erf,edf->erd", act_gated, w_down).astype(LOW)
        d_down = dot("erd,erf->edf", dy, act_gated)
        d_gate = dot("erf,erd->efd", dg, x)
        d_up = dot("erf,erd->efd", du, x)
        dx = (dot("erf,efd->erd", dg, w_gate) + dot("erf,efd->erd", du, w_up)).astype(LOW)
        mix = dot("bst,bsd->btd", flat, by_block(y)).astype(LOW)
        d_h = dot("bst,bsd->btd", flat, by_block(dx)).astype(LOW)
        d_g = dot(
            "bjct,jbc->btj", put.astype(FULL), d_gate_slot.reshape(EXP_DEV, count, capacity)
        )
        return mix, d_h, d_g, d_gate, d_up, d_down

    gate_cols = lax.dynamic_slice_in_dim(h_all, MODEL_WIDTH + me * EXP_DEV, EXP_DEV, 2)
    rest_cols = lax.dynamic_slice_in_dim(
        h_all, MODEL_WIDTH + experts_all + me * EXP_DEV, EXP_DEV, 2
    )
    step = min(blocks, GROUP_BLOCKS)
    mixes, d_hs, d_gs, totals = [], [], [], None
    for at in range(0, blocks, step):
        cut = slice(at, at + step)
        mix, d_h, d_g, *grads = experts(
            h_all[cut, :, :MODEL_WIDTH],
            d_all[cut, :, :MODEL_WIDTH],
            gate_cols[cut],
            rest_cols[cut],
            dispatch[cut],
        )
        mixes.append(mix)
        d_hs.append(d_h)
        d_gs.append(d_g)
        totals = grads if totals is None else [a + b for a, b in zip(totals, grads)]
    d_gate, d_up, d_down = totals
    d_g = jnp.concatenate(d_gs, axis=0)
    spread = jnp.zeros((blocks, length, TAIL), LOW)
    spread = lax.dynamic_update_slice_in_dim(spread, d_g.astype(LOW), me * EXP_DEV, 2)
    d_h_wide = jnp.concatenate([jnp.concatenate(d_hs, axis=0), spread], axis=2)

    def home(v):
        v = v.reshape(owners, planes, length, v.shape[-1])
        v = lax.psum_scatter(v, "expert", scatter_dimension=0, tiled=False)
        return lax.psum_scatter(v, "shard", scatter_dimension=0, tiled=False)

    d_home = home(d_h_wide)
    mixture = home(jnp.concatenate(mixes, axis=0))
    result = (middle + mixture.astype(FULL)).astype(LOW)

    upstream = d_out.astype(FULL)
    d_gates = d_home[:, MODEL_WIDTH : MODEL_WIDTH + experts_all].astype(FULL)
    d_chance = named * (d_gates - jnp.sum(d_gates * gates, axis=1, keepdims=True)) / chosen_sum
    d_logits = chance * (d_chance - jnp.sum(d_chance * chance, axis=1, keepdims=True))
    d_logits = d_logits.astype(LOW)
    d_h2 = d_home[:, :MODEL_WIDTH].astype(FULL) + dot("ne,de->nd", d_logits, router_full)
    d_gain_two = jnp.sum(d_h2 * unit_two, axis=0)
    d_middle = upstream + norm_back(d_h2, unit_two, inverse_two, gain_two)
    d_router = dot("nd,ne->de", h2, d_logits)

    d_branch = lax.all_gather(d_middle.astype(LOW), "expert", axis=0, tiled=False)
    d_w_out = dot("bqf,bqd->fd", mixed, d_branch).astype(LOW)
    d_mixed = dot("bqd,fd->bqf", d_branch, w_mine).astype(LOW)
    d_mixed = d_mixed.reshape(owners, length, heads, HEAD_SIZE)
    d_probs = dot("bqhd,bkd->bhqk", d_mixed, value)
    d_scores = probs * (d_probs - jnp.sum(d_probs * probs, axis=-1, keepdims=True))
    d_scores = d_scores.astype(LOW)
    d_query = dot("bhqk,bkd->bqhd", d_scores, key) * scaling
    d_key = dot("bhqk,bqhd->bkd", d_scores, query) * scaling
    d_value = dot("bhqk,bqhd->bkd", probs_low, d_mixed)
    d_query = rotate_back(d_query, cosine_q, sine_q)
    d_key = rotate_back(d_key, cosine, sine)
    d_gain_query = jnp.sum(d_query * query_unit, axis=(0, 1, 2))
    d_gain_key = jnp.sum(d_key * key_unit, axis=(0, 1))
    d_query = norm_back(d_query, query_unit, query_inverse, gain_query)
    d_key = norm_back(d_key, key_unit, key_inverse, gain_key)
    d_projected = jnp.concatenate(
        [d_query.reshape(owners, length, query_cols), d_key, d_value], axis=2
    ).astype(LOW)
    d_h1_part = dot("bqf,df->bqd", d_projected, wqkv).astype(LOW)
    d_h1 = lax.psum_scatter(d_h1_part, "expert", scatter_dimension=0, tiled=False).astype(FULL)
    resident = tokens.astype(FULL)
    unit_one, inverse_one = unit_norm(resident)
    d_gain_one = jnp.sum(d_h1 * unit_one, axis=0)
    d_tokens = (d_middle + norm_back(d_h1, unit_one, inverse_one, gain_one)).astype(LOW)

    d_wqkv = dot("bqd,bqf->df", h1, d_projected).astype(LOW)

    def by_rows(v):
        v = v.reshape(planes, per)
        return jnp.pad(v, ((0, 0), (0, rows_in - per))).reshape(-1)[:, None]

    d_tail = columns(
        [
            d_router,
            d_gain_one[:, None],
            d_gain_two[:, None],
            by_rows(d_gain_query),
            by_rows(d_gain_key),
        ],
        MODEL_WIDTH,
    )
    d_pack = lax.psum_scatter(
        jnp.concatenate([d_wqkv, d_tail], axis=1), "shard", scatter_dimension=0, tiled=True
    )
    d_pack = lax.all_gather(d_pack, "expert", axis=0, tiled=False).astype(FULL)
    d_q_cols = d_pack[:, :, :query_cols].transpose(1, 0, 2).reshape(rows_in, -1)
    d_kv = d_pack[:, :, query_cols:qkv_cols]
    d_kv = jnp.sum(d_kv.reshape(KEY_VALUE_HEADS, -1, rows_in, 2, HEAD_SIZE), axis=1)
    d_kv = d_kv.transpose(1, 2, 0, 3).reshape(rows_in, -1)
    d_qkv_weight = jnp.concatenate([d_q_cols, d_kv], axis=1)
    d_rest = jnp.sum(d_pack[:, :, qkv_cols:], axis=0)
    d_router_out = d_rest[:, :experts_all]
    d_gain_out = d_rest[:, experts_all:]

    d_w_out = d_w_out.reshape(query_cols, owners, -1)
    d_w_out = lax.all_to_all(d_w_out, "expert", split_axis=1, concat_axis=0, tiled=False)
    d_w_out = d_w_out.reshape(QUERY_HEADS * HEAD_SIZE, -1)
    d_w_out = lax.psum_scatter(d_w_out, "shard", scatter_dimension=0, tiled=True)
    d_w_out = lax.all_gather(d_w_out, "expert", axis=1, tiled=True).astype(FULL)

    return (
        result,
        d_tokens,
        d_gain_out[:, 0],
        d_qkv_weight,
        d_gain_out[:per, 2],
        d_gain_out[:per, 3],
        d_w_out,
        d_gain_out[:, 1],
        d_router_out,
        d_gate,
        d_up,
        d_down,
    )


def solution(mesh):
    placed = (
        P(("expert", "shard"), None),
        P(("expert", "shard"), None),
        P(("expert", "shard"), None),
        P("shard"),
        P("shard", None),
        P("shard"),
        P("shard"),
        P("shard", None),
        P("shard"),
        P("shard", None),
        P("expert", "shard", None),
        P("expert", "shard", None),
        P("expert", None, "shard"),
        P(("expert", "shard"), None),
    )
    return jax.shard_map(
        per_device,
        mesh=mesh,
        in_specs=placed,
        out_specs=(
            P(("expert", "shard"), None),
            P(("expert", "shard"), None),
            P("shard"),
            P("shard", None),
            P("shard"),
            P("shard"),
            P("shard", None),
            P("shard"),
            P("shard", None),
            P("expert", "shard", None),
            P("expert", "shard", None),
            P("expert", None, "shard"),
        ),
        check_vma=False,
    )
```

time: 4730 us -> 1480 us (0.31)
  waiting for transfers between devices: 3870 us -> 803 us
  blocking collectives: 187 us -> 29.9 us
    all_gather x26 -> x7, waiting for transfers between devices: 1840 us -> 356 us  [the longest x1 77.6 us: per_device(): lax.all_gather(jnp.concatenate([h2, gates_high, gates_rest], axis=1), bot...]
    reduce_scatter x27 -> x8, waiting for transfers between devices: 1710 us -> 416 us  [the longest x2 192 us: home(): v = lax.psum_scatter(v, 'expert', scatter_dimension=0, tiled=False)]
    all_to_all x3 -> x0, waiting for transfers between devices: 180 us -> none  [the longest x1 70.3 us: per_device(): lax.all_to_all(outgoing, 'expert', split_axis=0, concat_axis=2, tiled=True)]
    transpose x0 -> x7, local copies, waits for them, and re-layouts: none -> 105 us  [the longest x2 42.3 us: by_expert(): v.transpose(1, 0, 2, 3).reshape(EXP_DEV, count * capacity, v.shape[-1])]
    psum x1, waiting for transfers between devices: 133 us -> 31.7 us  [per_device(): w_mine = lax.psum(jnp.where(held, piece, 0).astype(LOW), 'shard')]
    all_gather x3 -> x0, blocking collectives: 68 us -> none  [the longest x1 28.3 us: per_device(): lax.all_gather(attn_gain, 'shard', axis=0, tiled=True)]
    gather x9 -> x0, local copies, waits for them, and re-layouts: 54.9 us -> none  [the longest x1 15.4 us: per_device(): d_padded[pair_of_slot].reshape(owners, EXP_DEV, capacity, MODEL_WIDTH)]
    dot_general x88 -> x31, matrix products: 293 us -> 287 us  [dot(): return jnp.einsum(spec, left, right, preferred_element_type=FULL)]
  transfers between devices with their start and end apart: 57 -> 16, of which waited for: 50 -> 15; matrix products, arithmetic and copies ran while one was open for 11% -> 17% of each run, Pallas kernels for 0% -> 0%
where the time goes in v1:
time: 1480 us; the launch traced here: 1470 us
  waiting for transfers between devices  803 us (54%)
  matrix products  289 us (20%)
  local copies, waits for them, and re-layouts  226 us (15%)
  other arithmetic  104 us (7%)
  blocking collectives  29.9 us (2%)
  between operations  17.2 us (1%)
    dot_general x31, matrix products, dot(): return jnp.einsum(spec, left, right, preferred_element_type=FULL)  287 us
    reduce_scatter x2, waiting for transfers between devices, home(): v = lax.psum_scatter(v, 'expert', scatter_dimension=0, tiled=False)  192 us
    all_gather x1, waiting for transfers between devices, per_device(): lax.all_gather(jnp.concatenate([h2, gates_high, gates_rest], axis=1), bot...  77.6 us
    reduce_scatter x1, waiting for transfers between devices, per_device(): lax.psum_scatter(jnp.concatenate([d_wqkv, d_tail], axis=1), 'shard', scat...  70.6 us
    all_gather x1, waiting for transfers between devices, per_device(): gathered = lax.all_gather(mine, 'shard', axis=0, tiled=True)  70 us
    all_gather x1, waiting for transfers between devices, per_device(): lax.all_gather(jnp.concatenate([d_out, d_tail], axis=1), both, axis=0, ti...  58.5 us
    reduce_scatter x1, waiting for transfers between devices, per_device(): lax.psum_scatter(partial, 'expert', scatter_dimension=0, tiled=False)  55.4 us
    unnamed x183, local copies, waits for them, and re-layouts  54.5 us
  transfers between devices with their start and end apart: 16, of which 15 were waited for; matrix products, arithmetic and copies ran while one was open for 17% of the time, Pallas kernels for 0%

profile of v1, /device:TPU:0, one launch (start us, length us, event | category | flops | bytes accessed | tf_op | source)
XLA Modules:
  0.0 1470.1 jit_solution(9671860820583538627)
XLA Ops:
  20.7 70.0 %all-gather.13.cloned.1.call-done = bf16[2048,896]{1,0:T(8,128)(2,1)} async-done(((bf16[512,896]{1,0:T(8,128)(2,1)}), bf16[2048,896]{1,0:T(8,128)(2,1)}) %all-gather.13.cloned.1.call-update) | async-done | bytes 3670032 | tf_op jit(solution)/shard_map/all_gather | solution.py:110
  93.3 36.4 %all-gather.17.cloned.1.call-done = bf16[1024,2176]{1,0:T(8,128)(2,1)} async-done(((bf16[128,2176]{1,0:T(8,128)(2,1)}), bf16[1024,2176]{1,0:T(8,128)(2,1)}) %all-gather.17.cloned.1.call-update) | async-done | bytes 4456464 | tf_op jit(solution)/shard_map/all_gather | solution.py:125
  135.6 6.8 copy.377
  146.4 6.7 fusion.13
  153.1 6.8 copy.311
  159.9 6.2 fusion.19
  186.9 31.7 %all-reduce.10.cloned.1.call-done = bf16[512,2048]{1,0:T(8,128)(2,1)} async-done(((bf16[512,2048]{1,0:T(8,128)(2,1)}), bf16[512,2048]{1,0:T(8,128)(2,1)}) %all-reduce.10.cloned.1.call-update) | async-done | bytes 2097168 | tf_op jit(solution)/shard_map/psum | solution.py:138
  218.6 6.3 convolution_convert_fusion.3
  227.0 55.4 %reduce-scatter.9.cloned.1.call-done = bf16[1,128,2048]{2,1,0:T(8,128)(2,1)} async-done(((bf16[8,128,2048]{2,1,0:T(8,128)(2,1)}), bf16[1,128,2048]{2,1,0:T(8,128)(2,1)}) %reduce-scatter.9.cloned.1.call-update) | async-done | bytes 524304 | tf_op jit(solution)/shard_map/reduce_scatter | solution.py:179
  288.6 58.5 %all-gather.19.cloned.1.call-done = bf16[4096,2176]{1,0:T(8,128)(2,1)} async-done(((bf16[128,2176]{1,0:T(8,128)(2,1)}), bf16[4096,2176]{1,0:T(8,128)(2,1)}) %all-gather.19.cloned.1.call-update) | async-done | bytes 17825808 | tf_op jit(solution)/shard_map/all_gather | solution.py:147
  349.7 19.8 %fusion.8 = bf16[32,192,2048]{2,1,0:T(8,128)(2,1)} fusion(pred[32,192,128]{2,1,0:T(32,128)(4,1)S(1)} %bitcast_compare_fusion, bf16[32,128,2176]{2,1,0:T(8,128)(2,1)} %bitcast.266), kind=kOutput, calls=%fused_computation.11 | convolution fusion | flops 3233808384 | bytes 42729472 | tf_op jit(solution)/shard_map/bst,btd->bsd/dot_general | solution.py:44
  369.5 21.1 %copy.326 = bf16[8,32,24,2048]{3,2,1,0:T(8,128)(2,1)} copy(bf16[8,32,24,2048]{3,2,0,1:T(8,128)(2,1)} %bitcast.248) | data formatting | bytes 50331648 | tf_op jit(solution)/shard_map/transpose | solution.py:214
  390.6 77.6 %all-gather.21.cloned.1.call-done = bf16[4096,2176]{1,0:T(8,128)(2,1)} async-done(((bf16[128,2176]{1,0:T(8,128)(2,1)}), bf16[4096,2176]{1,0:T(8,128)(2,1)}) %all-gather.21.cloned.1.call-update) | async-done | bytes 17825808 | tf_op jit(solution)/shard_map/all_gather | solution.py:193
  468.2 19.2 %fusion.5 = bf16[32,192,2048]{2,1,0:T(8,128)(2,1)} fusion(pred[32,192,128]{2,1,0:T(32,128)(4,1)S(1)} %bitcast_compare_fusion, bf16[32,128,2176]{2,1,0:T(8,128)(2,1)} %bitcast.263), kind=kOutput, calls=%fused_computation.10 | convolution fusion | flops 3233808384 | bytes 42729472 | tf_op jit(solution)/shard_map/bst,btd->bsd/dot_general | solution.py:44
  493.4 21.2 %copy.324 = bf16[8,32,24,2048]{3,2,1,0:T(8,128)(2,1)} copy(bf16[8,32,24,2048]{3,2,0,1:T(8,128)(2,1)} %bitcast.247) | data formatting | bytes 50331648 | tf_op jit(solution)/shard_map/transpose | solution.py:214
  514.6 16.4 %fusion.122 = f32[8,768,192]{1,2,0:T(8,128)} fusion(bf16[8,768,2048]{2,1,0:T(8,128)(2,1)} %bitcast.243, bf16[8,192,2048]{2,1,0:T(8,128)(2,1)} %param.25), kind=kOutput, calls=%fused_computation.228 | convolution fusion | flops 4831838208 | bytes 36175872 | tf_op jit(solution)/shard_map/erd,efd->erf/dot_general | solution.py:44
  531.0 16.6 %fusion.121 = f32[8,768,192]{1,2,0:T(8,128)} fusion(bf16[8,768,2048]{2,1,0:T(8,128)(2,1)} %bitcast.244, bf16[8,192,2048]{2,1,0:T(8,128)(2,1)} %param.24), kind=kOutput, calls=%fused_computation.227 | convolution fusion | flops 4831838208 | bytes 36175872 | tf_op jit(solution)/shard_map/erd,efd->erf/dot_general | solution.py:44
  547.5 19.8 %fusion.16 = (bf16[8,768]{1,0:T(8,128)(2,1)S(1)}, bf16[8,768,192]{1,2,0:T(8,128)(2,1)}, bf16[8,768,192]{1,2,0:T(8,128)(2,1)}, bf16[8,768,192]{1,2,0:T(8,128)(2,1)S(1)}) fusion(f32[8,768,192]{1,2,0:T(8,128)} %fusion.122, f32[8,768,192]{1,2,0:T(8,128)} %fusion.121, f32[8,768]{1,0:T(8,128)S(1)} %mul.480, bf16[8,768,2048]{2,1,0:T(8,128)(2,1)} %bitcast.249, ...), kind=kOutput, calls=%fused_computation.25 | convolution fusion | flops 4854245376 | bytes 48009216 | tf_op jit(solution)/shard_map/erd,edf->erf/dot_general | solution.py:44
  571.8 22.5 %fusion.123 = f32[8,768,2048]{2,1,0:T(8,128)} fusion(bf16[8,768,192]{1,2,0:T(8,128)(2,1)} %get-tuple-element.29, bf16[8,192,2048]{2,1,0:T(8,128)(2,1)} %param.24), kind=kOutput, calls=%fused_computation.229 | convolution fusion | flops 4831838208 | bytes 58982400 | tf_op jit(solution)/shard_map/erf,efd->erd/dot_general | solution.py:44
  594.3 27.4 %add_convert_fusion = bf16[8,768,2048]{2,1,0:T(8,128)(2,1)} fusion(f32[8,768,2048]{2,1,0:T(8,128)} %fusion.123, bf16[8,768,192]{1,2,0:T(8,128)(2,1)S(1)} %get-tuple-element.30, bf16[8,192,2048]{2,1,0:T(8,128)(2,1)} %param.25), kind=kOutput, calls=%fused_computation.1 | convolution fusion | flops 4857004032 | bytes 84148224 | tf_op jit(solution)/shard_map/erf,efd->erd/dot_general | solution.py:44
  621.7 21.0 %copy.327 = bf16[32,8,24,2048]{3,2,1,0:T(8,128)(2,1)} copy(bf16[32,8,24,2048]{3,2,0,1:T(8,128)(2,1)} %bitcast.254) | data formatting | bytes 50331648 | tf_op jit(solution)/shard_map/transpose | solution.py:218
  642.7 16.7 %convolution_convert_fusion.1 = bf16[32,128,2048]{2,1,0:T(8,128)(2,1)} fusion(pred[32,192,128]{2,1,0:T(32,128)(4,1)S(1)} %bitcast_compare_fusion, bf16[32,192,2048]{2,1,0:T(8,128)(2,1)} %bitcast.252), kind=kOutput, calls=%fused_computation.8 | convolution fusion | flops 3229614080 | bytes 42729472 | tf_op jit(solution)/shard_map/bst,bsd->btd/dot_general | solution.py:44
  663.5 14.2 pad_maximum_fusion
  677.9 125.4 %reduce-scatter.15.cloned.1.call-done = bf16[1,4,128,2176]{3,2,1,0:T(8,128)(2,1)} async-done(((bf16[8,4,128,2176]{3,2,1,0:T(8,128)(2,1)}), bf16[1,4,128,2176]{3,2,1,0:T(8,128)(2,1)}) %reduce-scatter.15.cloned.1.call-update) | async-done | bytes 2228240 | tf_op jit(solution)/shard_map/reduce_scatter | solution.py:273
  803.4 48.1 %reduce-scatter.17.cloned.1.call-done = bf16[1,128,2176]{2,1,0:T(8,128)(2,1)} async-done(((bf16[4,128,2176]{2,1,0:T(8,128)(2,1)}), bf16[1,128,2176]{2,1,0:T(8,128)(2,1)}) %reduce-scatter.17.cloned.1.call-update) | async-done | bytes 557072 | tf_op jit(solution)/shard_map/reduce_scatter | solution.py:274
  863.8 30.7 %all-gather.23.cloned.1.call-done = bf16[1024,2048]{1,0:T(8,128)(2,1)} async-done(((bf16[128,2048]{1,0:T(8,128)(2,1)}), bf16[1024,2048]{1,0:T(8,128)(2,1)}) %all-gather.23.cloned.1.call-update) | async-done | bytes 4194320 | tf_op jit(solution)/shard_map/all_gather | solution.py:290
  894.6 6.3 fusion.40
  932.4 16.4 %convolution_convert_fusion = bf16[8,768,2048]{2,1,0:T(8,128)(2,1)} fusion(bf16[8,2048,192]{1,2,0:T(8,128)(2,1)} %param.26, bf16[8,768,192]{1,2,0:T(8,128)(2,1)} %get-tuple-element.24, f32[8,768]{1,0:T(8,128)S(1)} %mul.480), kind=kOutput, calls=%fused_computation.7 | convolution fusion | flops 4847960064 | bytes 33841152 | tf_op jit(solution)/shard_map/erf,edf->erd/dot_general | solution.py:44
  948.8 21.2 %copy.325 = bf16[32,8,24,2048]{3,2,1,0:T(8,128)(2,1)} copy(bf16[32,8,24,2048]{3,2,0,1:T(8,128)(2,1)} %bitcast.253) | data formatting | bytes 50331648 | tf_op jit(solution)/shard_map/transpose | solution.py:218
  970.0 17.0 %convolution_convert_fusion.2 = bf16[32,128,2048]{2,1,0:T(8,128)(2,1)} fusion(pred[32,192,128]{2,1,0:T(32,128)(4,1)S(1)} %bitcast_compare_fusion, bf16[32,192,2048]{2,1,0:T(8,128)(2,1)} %bitcast.251), kind=kOutput, calls=%fused_computation.9 | convolution fusion | flops 3229614080 | bytes 42729472 | tf_op jit(solution)/shard_map/bst,bsd->btd/dot_general | solution.py:44
  993.1 29.9 %all_to_all.15 = bf16[1,512,8,256]{3,1,0,2:T(8,128)(2,1)} all-to-all(bf16[1,512,8,256]{3,1,0,2:T(8,128)(2,1)S(1)} %copy.348), channel_id=1, replica_groups=mesh['expert'=8,'shard'=4] {'expert'}, dimensions={2} | all-to-all | bytes 4194304 | tf_op jit(solution)/shard_map/all_to_all | solution.py:346
  1024.6 7.5 bitcast_convert_fusion
  1037.2 66.7 %reduce-scatter.11.cloned.1.call-done = bf16[1,4,128,2048]{3,2,1,0:T(8,128)(2,1)} async-done(((bf16[8,4,128,2048]{3,2,1,0:T(8,128)(2,1)}), bf16[1,4,128,2048]{3,2,1,0:T(8,128)(2,1)}) %reduce-scatter.11.cloned.1.call-update) | async-done | bytes 2097168 | tf_op jit(solution)/shard_map/reduce_scatter | solution.py:273
  1103.9 46.1 %reduce-scatter.23.cloned.1.call-done = bf16[1024,256]{1,0:T(8,128)(2,1)} async-done(((bf16[4096,256]{1,0:T(8,128)(2,1)}), bf16[1024,256]{1,0:T(8,128)(2,1)}) %reduce-scatter.23.cloned.1.call-update) | async-done | bytes 524304 | tf_op jit(solution)/shard_map/reduce_scatter | solution.py:348
  1150.1 70.6 %reduce-scatter.21.cloned.1.call-done = bf16[512,896]{0,1:T(8,128)(2,1)} async-done(((bf16[2048,896]{0,1:T(8,128)(2,1)}), bf16[512,896]{0,1:T(8,128)(2,1)}) %reduce-scatter.21.cloned.1.call-update) | async-done | bytes 917520 | tf_op jit(solution)/shard_map/reduce_scatter | solution.py:332
  1220.7 15.1 %fusion.124 = f32[8,192,2048]{2,1,0:T(8,128)} fusion(bf16[8,768,192]{1,2,0:T(8,128)(2,1)} %get-tuple-element.29, bf16[8,768,2048]{2,1,0:T(8,128)(2,1)} %bitcast.245), kind=kOutput, calls=%fused_computation.230 | convolution fusion | flops 4831838208 | bytes 40108032 | tf_op jit(solution)/shard_map/erf,erd->efd/dot_general | solution.py:44
  1235.7 13.8 fusion.125
  1249.6 14.1 fusion.34
  1269.9 36.0 %all-gather.15.cloned.1.call-done = bf16[1024,2048]{1,0:T(8,128)(2,1)} async-done(((bf16[1024,256]{1,0:T(8,128)(2,1)}), bf16[1024,2048]{1,0:T(8,128)(2,1)}) %all-gather.15.cloned.1.call-update) | async-done | bytes 4194320 | tf_op jit(solution)/shard_map/all_gather | solution.py:349
  1305.9 6.7 convert_element_type.341
  1312.5 46.6 %all-gather.25.cloned.1.call-done = bf16[4096,896]{0,1:T(8,128)(2,1)} async-done(((bf16[512,896]{0,1:T(8,128)(2,1)}), bf16[4096,896]{0,1:T(8,128)(2,1)}) %all-gather.25.cloned.1.call-update) | async-done | bytes 7340048 | tf_op jit(solution)/shard_map/all_gather | solution.py:335
  1359.1 10.2 convert_element_type.345
  1369.4 25.0 %copy.392 = f32[112,8,8,512]{3,2,1,0:T(8,128)} copy(f32[112,8,8,512]{3,1,2,0:T(8,128)} %bitcast.260) | data formatting | bytes 29360128
  1403.0 7.8 slice_bitcast_fusion
  1410.7 10.6 copy.345
  1421.4 14.8 %copy.393 = f32[64,8,8,512]{3,1,2,0:T(8,128)} copy(f32[64,8,8,512]{3,2,1,0:T(8,128)} %bitcast.262) | data formatting | bytes 16777216
  1442.2 7.9 reduce_sum.258
  1454.0 8.6 pad_maximum_fusion.1
  (340 shorter events, 151.5 us)
Async XLA Ops:
  8.0 82.7 %all-gather.13.cloned.1.call-start = ((), (), s32[]{:S(2)}) async-start(), calls=%async_computation.9 | async-start | bytes 4587520 | tf_op jit(solution)/shard_map/all_gather | solution.py:110
  15.8 113.9 %all-gather.17.cloned.1.call-start = ((), (), s32[]{:S(2)}) async-start(), calls=%async_computation.20 | async-start | bytes 5013504 | tf_op jit(solution)/shard_map/all_gather | solution.py:125
  17.0 201.5 %all-reduce.10.cloned.1.call-start = ((), (), s32[]{:S(2)}) async-start(), calls=%async_computation.10 | async-start | bytes 4194304 | tf_op jit(solution)/shard_map/psum | solution.py:138
  20.6 261.8 %reduce-scatter.9.cloned.1.call-start = ((), (), s32[]{:S(2)}) async-start(), calls=%async_computation.11 | async-start | bytes 4718592 | tf_op jit(solution)/shard_map/reduce_scatter | solution.py:179
  20.7 156.3 %copy-start.76 = (f32[64]{0:T(128)}, f32[64]{0:T(128)S(1)}, u32[]{:S(2)}) copy-start(f32[64]{0:T(128)S(1)} %multiply_power_fusion) | copy-start | bytes 772
  92.9 53.5 %copy-start.53 = (f32[2048]{0:T(1024)}, f32[2048]{0:T(1024)S(1)}, u32[]{:S(2)}) copy-start(f32[2048]{0:T(1024)S(1)} %get-tuple-element.19) | copy-start | bytes 24580
  92.9 190.8 %copy-start.51 = (f32[2048]{0:T(1024)}, f32[2048]{0:T(1024)S(1)}, u32[]{:S(2)}) copy-start(f32[2048]{0:T(1024)S(1)} %get-tuple-element.18) | copy-start | bytes 24580
  93.2 82.3 %copy-start.68 = (f32[128]{0:T(128)}, f32[128]{0:T(128)S(1)}, u32[]{:S(2)}) copy-start(f32[128]{0:T(128)S(1)} %mul.442) | copy-start | bytes 1540
  93.2 86.2 %copy-start.66 = (f32[128]{0:T(128)}, f32[128]{0:T(128)S(1)}, u32[]{:S(2)}) copy-start(f32[128]{0:T(128)S(1)} %mul.457) | copy-start | bytes 1540
  224.9 122.3 %all-gather.19.cloned.1.call-start = ((), (), s32[]{:S(2)}) async-start(), calls=%async_computation.21 | async-start | bytes 18382848 | tf_op jit(solution)/shard_map/all_gather | solution.py:147
  226.8 241.4 %all-gather.21.cloned.1.call-start = ((), (), s32[]{:S(2)}) async-start(), calls=%async_computation.22 | async-start | bytes 18382848 | tf_op jit(solution)/shard_map/all_gather | solution.py:193
  227.0 120.2 %copy-start.41 = (f32[128,64]{1,0:T(8,128)}, f32[128,64]{1,0:T(8,128)S(1)}, u32[]{:S(2)}) copy-start(f32[128,64]{1,0:T(8,128)S(1)} %copy.323) | copy-start | bytes 98308
  283.7 63.5 %copy-start.70 = (f32[128]{0:T(128)}, f32[128]{0:T(128)S(1)}, u32[]{:S(2)}) copy-start(f32[128]{0:T(128)S(1)} %add_rsqrt_fusion.4) | copy-start | bytes 1540
  285.0 63.8 %copy-start.19 = (bf16[128,2048]{1,0:T(8,128)(2,1)}, bf16[128,2048]{1,0:T(8,128)(2,1)S(1)}, u32[]{:S(2)}) copy-start(bf16[128,2048]{1,0:T(8,128)(2,1)S(1)} %multiply_convert_fusion.3) | copy-start | bytes 1572868
  286.7 62.3 %copy-start.37 = (f32[128,64]{1,0:T(8,128)}, f32[128,64]{1,0:T(8,128)S(1)}, u32[]{:S(2)}) copy-start(f32[128,64]{1,0:T(8,128)S(1)} %copy.322) | copy-start | bytes 98308
  287.1 61.4 %copy-start.64 = (f32[128]{0:T(128)}, f32[128]{0:T(128)S(1)}, u32[]{:S(2)}) copy-start(f32[128]{0:T(128)S(1)} %get-tuple-element.25) | copy-start | bytes 1540
  287.1 61.9 %copy-start.39 = (f32[128,64]{1,0:T(8,128)}, f32[128,64]{1,0:T(8,128)S(1)}, u32[]{:S(2)}) copy-start(f32[128,64]{1,0:T(8,128)S(1)} %get-tuple-element.26) | copy-start | bytes 98308
  288.5 514.8 %reduce-scatter.15.cloned.1.call-start = ((), (), s32[]{:S(2)}) async-start(), calls=%async_computation.14 | async-start | bytes 20054016 | tf_op jit(solution)/shard_map/reduce_scatter | solution.py:273
  567.4 27.0 %copy-start.7 = (bf16[8,768,192]{1,2,0:T(8,128)(2,1)}, bf16[8,768,192]{1,2,0:T(8,128)(2,1)S(1)}, u32[]{:S(2)}) copy-start(bf16[8,768,192]{1,2,0:T(8,128)(2,1)S(1)} %get-tuple-element.30) | copy-start | bytes 7077892
  677.7 173.8 %copy-start.40 = (f32[128,64]{1,0:T(8,128)S(1)}, f32[128,64]{1,0:T(8,128)}, u32[]{:S(2)}) copy-start(f32[128,64]{1,0:T(8,128)} %copy-done.39) | copy-start | bytes 98308
  677.7 173.8 %copy-start.65 = (f32[128]{0:T(128)S(1)}, f32[128]{0:T(128)}, u32[]{:S(2)}) copy-start(f32[128]{0:T(128)} %copy-done.64) | copy-start | bytes 1540
  677.7 174.7 %copy-start.38 = (f32[128,64]{1,0:T(8,128)S(1)}, f32[128,64]{1,0:T(8,128)}, u32[]{:S(2)}) copy-start(f32[128,64]{1,0:T(8,128)} %copy-done.37) | copy-start | bytes 98308
  677.7 174.8 %copy-start.42 = (f32[128,64]{1,0:T(8,128)S(1)}, f32[128,64]{1,0:T(8,128)}, u32[]{:S(2)}) copy-start(f32[128,64]{1,0:T(8,128)} %copy-done.41) | copy-start | bytes 98308
  677.7 174.8 %copy-start.63 = (f32[128]{0:T(128)S(1)}, f32[128]{0:T(128)}, u32[]{:S(2)}) copy-start(f32[128]{0:T(128)} %copy-done.62) | copy-start | bytes 1540
  677.7 174.8 %copy-start.73 = (f32[128]{0:T(128)S(1)}, f32[128]{0:T(128)}, u32[]{:S(2)}) copy-start(f32[128]{0:T(128)} %copy-done.72) | copy-start | bytes 1540
  677.7 175.7 %copy-start.2 = (bf16[128,2048]{1,0:T(8,128)(2,1)S(1)}, bf16[128,2048]{1,0:T(8,128)(2,1)}, u32[]{:S(2)}) copy-start(bf16[128,2048]{1,0:T(8,128)(2,1)} %param.14) | copy-start | bytes 1572868
  677.8 175.7 %copy-start.10 = (bf16[1,128,2048]{2,1,0:T(8,128)(2,1)S(1)}, bf16[1,128,2048]{2,1,0:T(8,128)(2,1)}, u32[]{:S(2)}) copy-start(bf16[1,128,2048]{2,1,0:T(8,128)(2,1)} %reduce-scatter.9.cloned.1.call-done) | copy-start | bytes 1572868
  677.8 175.7 %copy-start.52 = (f32[2048]{0:T(1024)S(1)}, f32[2048]{0:T(1024)}, u32[]{:S(2)}) copy-start(f32[2048]{0:T(1024)} %copy-done.51) | copy-start | bytes 24580
  677.8 175.7 %copy-start.71 = (f32[128]{0:T(128)S(1)}, f32[128]{0:T(128)}, u32[]{:S(2)}) copy-start(f32[128]{0:T(128)} %copy-done.70) | copy-start | bytes 1540
  677.8 173.7 %reduce-scatter.17.cloned.1.call-start = ((), (), s32[]{:S(2)}) async-start(), calls=%async_computation.15 | async-start | bytes 2785280 | tf_op jit(solution)/shard_map/reduce_scatter | solution.py:274
  803.3 53.7 %copy-start.17 = (bf16[128,2048]{1,0:T(8,128)(2,1)S(1)}, bf16[128,2048]{1,0:T(8,128)(2,1)}, u32[]{:S(2)}) copy-start(bf16[128,2048]{1,0:T(8,128)(2,1)} %param.27) | copy-start | bytes 1572868
  803.3 91.2 %all-gather.23.cloned.1.call-start = ((), (), s32[]{:S(2)}) async-start(), calls=%async_computation.23 | async-start | bytes 4718592 | tf_op jit(solution)/shard_map/all_gather | solution.py:290
  858.3 173.7 %reduce-scatter.19.cloned.1.call-start = ((), (), s32[]{:S(2)}) async-start(), calls=%async_computation.16 | async-start | bytes 4718592 | tf_op jit(solution)/shard_map/reduce_scatter | solution.py:310
  932.4 171.5 %reduce-scatter.11.cloned.1.call-start = ((), (), s32[]{:S(2)}) async-start(), calls=%async_computation.12 | async-start | bytes 18874368 | tf_op jit(solution)/shard_map/reduce_scatter | solution.py:273
  987.0 163.0 %reduce-scatter.23.cloned.1.call-start = ((), (), s32[]{:S(2)}) async-start(), calls=%async_computation.18 | async-start | bytes 2621440 | tf_op jit(solution)/shard_map/reduce_scatter | solution.py:348
  993.0 30.1 %copy-start.81 = (f32[128]{0:T(128)S(1)}, f32[128]{0:T(128)}, u32[]{:S(2)}) copy-start(f32[128]{0:T(128)} %get-tuple-element.22) | copy-start | bytes 1540
  993.0 30.1 %copy-start.20 = (bf16[128,2048]{1,0:T(8,128)(2,1)S(1)}, bf16[128,2048]{1,0:T(8,128)(2,1)}, u32[]{:S(2)}) copy-start(bf16[128,2048]{1,0:T(8,128)(2,1)} %copy-done.19) | copy-start | bytes 1572868
  993.0 30.1 %copy-start.43 = (f32[128,64]{1,0:T(8,128)S(1)}, f32[128,64]{1,0:T(8,128)}, u32[]{:S(2)}) copy-start(f32[128,64]{1,0:T(8,128)} %copy-done.41) | copy-start | bytes 98308
  993.0 30.1 %copy-start.75 = (f32[128]{0:T(128)S(1)}, f32[128]{0:T(128)}, u32[]{:S(2)}) copy-start(f32[128]{0:T(128)} %copy-done.74) | copy-start | bytes 1540
  993.1 30.1 %copy-start.79 = (f32[128]{0:T(128)S(1)}, f32[128]{0:T(128)}, u32[]{:S(2)}) copy-start(f32[128]{0:T(128)} %copy-done.78) | copy-start | bytes 1540
  993.1 31.5 %copy-start.35 = (bf16[8,128,512]{2,1,0:T(8,128)(2,1)S(1)}, bf16[8,128,512]{2,1,0:T(8,128)(2,1)}, u32[]{:S(2)}) copy-start(bf16[8,128,512]{2,1,0:T(8,128)(2,1)} %copy-done.34) | copy-start | bytes 3145732
  993.1 31.5 %copy-start.46 = (bf16[8,128,128]{2,1,0:T(8,128)(2,1)S(1)}, bf16[8,128,128]{2,1,0:T(8,128)(2,1)}, u32[]{:S(2)}) copy-start(bf16[8,128,128]{2,1,0:T(8,128)(2,1)} %multiply_convert_fusion.4) | copy-start | bytes 786436
  993.1 31.5 %copy-start.83 = (bf16[8,128,128]{2,1,0:T(8,128)(2,1)S(1)}, bf16[8,128,128]{2,1,0:T(8,128)(2,1)}, u32[]{:S(2)}) copy-start(bf16[8,128,128]{2,1,0:T(8,128)(2,1)} %fusion.48) | copy-start | bytes 786436
  1023.0 197.6 %reduce-scatter.21.cloned.1.call-start = ((), (), s32[]{:S(2)}) async-start(), calls=%async_computation.17 | async-start | bytes 4587520 | tf_op jit(solution)/shard_map/reduce_scatter | solution.py:332
  1037.1 229.9 %reduce-scatter.13.cloned.1.call-start = ((), (), s32[]{:S(2)}) async-start(), calls=%async_computation.13 | async-start | bytes 2621440 | tf_op jit(solution)/shard_map/reduce_scatter | solution.py:274
  1103.9 202.0 %all-gather.15.cloned.1.call-start = ((), (), s32[]{:S(2)}) async-start(), calls=%async_computation.19 | async-start | bytes 4718592 | tf_op jit(solution)/shard_map/all_gather | solution.py:349
  1150.0 209.1 %all-gather.25.cloned.1.call-start = ((), (), s32[]{:S(2)}) async-start(), calls=%async_computation.24 | async-start | bytes 8257536 | tf_op jit(solution)/shard_map/all_gather | solution.py:335
  1249.6 17.5 %copy-start.18 = (bf16[128,2048]{1,0:T(8,128)(2,1)S(1)}, bf16[128,2048]{1,0:T(8,128)(2,1)}, u32[]{:S(2)}) copy-start(bf16[128,2048]{1,0:T(8,128)(2,1)} %param.27) | copy-start | bytes 1572868
  (52 other events, 267.6 us)
Sparse Core Ops, SparseCore 0:
  15.9 74.7 all-gather.12
  93.2 36.4 all-gather.16
  132.0 86.5 all-reduce.9
  225.0 57.3 reduce-scatter.8
  677.9 125.3 reduce-scatter.14
  805.5 45.9 reduce-scatter.16
  858.4 36.1 all-gather.22
  932.5 51.3 reduce-scatter.18
  987.9 115.9 reduce-scatter.10
  1106.1 43.8 reduce-scatter.22
  1152.9 67.7 reduce-scatter.20
  1222.8 44.2 reduce-scatter.12
  1269.1 36.7 all-gather.14
  1307.8 51.2 all-gather.24
Sparse Core Ops, SparseCore 1:
  228.8 118.3 all-gather.18
  350.5 117.7 all-gather.20

commit v2 on v1

--- a/solution.py
+++ b/solution.py
@@ -1,6 +1,10 @@
+import functools
+
 import jax
 import jax.numpy as jnp
 from jax import lax
+from jax.experimental import pallas as pl
+from jax.experimental.pallas import tpu as pltpu
 from jax.sharding import PartitionSpec as P
 
 MODEL_WIDTH = 2048
@@ -11,6 +15,7 @@
 EXP_DEV = 8
 TAIL = 128
 GROUP_BLOCKS = 32
+RESIDENT = 20 << 20
 
 EPS = 1e-06
 THETA = 1000000.0
@@ -53,6 +58,601 @@
 def columns(parts, rows):
     wide = jnp.concatenate([part.astype(LOW) for part in parts], axis=1)
     return jnp.pad(wide, ((0, rows - wide.shape[0]), (0, TAIL - wide.shape[1])))
+
+
+MESH = pl.DeviceIdType.MESH
+ANY = pl.BlockSpec(memory_space=pl.ANY)
+VM = pl.BlockSpec(memory_space=pltpu.VMEM)
+DMA = pltpu.SemaphoreType.DMA
+VMEM_LIMIT = 58 << 20
+TILE = 512
+
+
+def neighbours():
+    e = lax.axis_index("expert")
+    core = e + 1 - 2 * (e % 2)
+    flip_x = e + 2 - 4 * ((e // 2) % 2)
+    flip_y = e + 4 - 8 * ((e // 4) % 2)
+    diagonal = flip_x + flip_y - e
+    return e, core, flip_x, flip_y, diagonal
+
+
+def greet(planes):
+    e, core, flip_x, flip_y, _ = neighbours()
+    s = lax.axis_index("shard")
+    barrier = pltpu.get_barrier_semaphore()
+    for other in (core, flip_x, flip_y):
+        pl.semaphore_signal(barrier, 1, device_id=(other, s), device_id_type=MESH)
+
+    @pl.when(s > 0)
+    def _():
+        pl.semaphore_signal(barrier, 1, device_id=(e, s - 1), device_id_type=MESH)
+
+    @pl.when(s < planes - 1)
+    def _():
+        pl.semaphore_signal(barrier, 1, device_id=(e, s + 1), device_id_type=MESH)
+
+    inner = (s > 0) & (s < planes - 1)
+
+    @pl.when(inner)
+    def _():
+        pl.semaphore_wait(barrier, 5)
+
+    @pl.when(jnp.logical_not(inner))
+    def _():
+        pl.semaphore_wait(barrier, 4)
+
+
+def send(source, target, send_sem, recv_sem, device):
+    return pltpu.make_async_remote_copy(
+        src_ref=source,
+        dst_ref=target,
+        send_sem=send_sem,
+        recv_sem=recv_sem,
+        device_id=device,
+        device_id_type=MESH,
+    )
+
+
+def one_hot_pair(place_ref, pair, hot_ref, slots):
+    rows = place_ref[pair]
+    at = lax.broadcasted_iota(jnp.int32, (slots, rows.shape[1]), 0).astype(FULL)
+    for j in range(EXP_DEV):
+        hot_ref[pl.ds(j * slots, slots), :] = (at == rows[j : j + 1, :]).astype(LOW)
+
+
+def gather_dispatch_kernel(
+    planes, slots, x_ref, d_ref, place_ref, outx_ref, outd_ref,
+    buf, hot, stage_x, stage_d, load_d,
+    z_send, z_recv, x_send, x_recv, y_send, y_recv, c_send, c_recv, out_x, out_d, in_d,
+):
+    e, core, flip_x, flip_y, diagonal = neighbours()
+    s = lax.axis_index("shard")
+    length = x_ref.shape[0]
+    half = length // 2
+    width = x_ref.shape[1]
+    low_half, high_half = pl.ds(0, half), pl.ds(half, half)
+    greet(planes)
+    buf[e, s] = x_ref[...]
+
+    def up(sp):
+        return send(buf.at[e, sp], buf.at[e, sp], z_send.at[0, sp], z_recv.at[sp], (e, s + 1))
+
+    def down(sp):
+        return send(buf.at[e, sp], buf.at[e, sp], z_send.at[1, sp], z_recv.at[sp], (e, s - 1))
+
+    def first(sp):
+        block = buf.at[e, sp]
+        return [
+            send(block, block, x_send.at[0, sp], x_recv.at[0, sp], (flip_x, s)),
+            send(block, block, y_send.at[0, sp], y_recv.at[0, sp], (flip_y, s)),
+            send(block, block, c_send.at[0, sp], c_recv.at[0, sp], (core, s)),
+        ]
+
+    def from_x(sp):
+        block = buf.at[flip_x, sp]
+        part = buf.at[flip_x, sp, low_half]
+        return [
+            send(part, part, y_send.at[1, sp], y_recv.at[1, sp], (flip_y, s)),
+            send(block, block, c_send.at[1, sp], c_recv.at[1, sp], (core, s)),
+        ]
+
+    def from_y(sp):
+        block = buf.at[flip_y, sp]
+        part = buf.at[flip_y, sp, high_half]
+        return [
+            send(part, part, x_send.at[1, sp], x_recv.at[1, sp], (flip_x, s)),
+            send(block, block, c_send.at[2, sp], c_recv.at[2, sp], (core, s)),
+        ]
+
+    def from_diagonal(sp):
+        block = buf.at[diagonal, sp]
+        return send(block, block, c_send.at[3, sp], c_recv.at[3, sp], (core, s))
+
+    def arrived(block, sem):
+        send(block, block, sem, sem, (core, s)).wait_recv()
+
+    def plane_at(i):
+        distance = (i + 1) // 2
+        sign = 2 * (i % 2) - 1
+        sp = s + sign * distance
+        return sp, (sp >= 0) & (sp < planes) & (i >= 0) & (i <= 2 * planes - 2)
+
+    def step_first(sp, i):
+        @pl.when(i > 0)
+        def _():
+            arrived(buf.at[e, sp], z_recv.at[sp])
+
+        @pl.when((sp <= s) & (s < planes - 1))
+        def _():
+            up(sp).start()
+
+        @pl.when((sp >= s) & (s > 0))
+        def _():
+            down(sp).start()
+
+        for copy in first(sp):
+            copy.start()
+
+    def step_second(sp):
+        arrived(buf.at[flip_x, sp], x_recv.at[0, sp])
+        for copy in from_x(sp):
+            copy.start()
+        arrived(buf.at[flip_y, sp], y_recv.at[0, sp])
+        for copy in from_y(sp):
+            copy.start()
+
+    def step_third(sp):
+        arrived(buf.at[diagonal, sp, low_half], y_recv.at[1, sp])
+        arrived(buf.at[diagonal, sp, high_half], x_recv.at[1, sp])
+        from_diagonal(sp).start()
+
+    def copy_out(stage, out, sem, q, sp):
+        rows = pl.ds(pl.multiple_of((q * planes + sp) * slots, 16), slots)
+        return pltpu.make_async_copy(stage.at[q], out.at[:, rows, :], sem.at[q])
+
+    def load(q, sp, k):
+        return pltpu.make_async_copy(
+            d_ref.at[2 * q + k, sp, :, pl.ds(0, MODEL_WIDTH)],
+            load_d.at[q, pl.ds(k * length, length), :],
+            in_d.at[q, k],
+        )
+
+    def start_loads(sp):
+        for q in range(4):
+            for k in range(2):
+                load(q, sp, k).start()
+
+    def dispatch(sp, i):
+        for k, other in enumerate((core, core + flip_x - e, core + flip_y - e, core + diagonal - e)):
+            arrived(buf.at[other, sp], c_recv.at[k, sp])
+
+        def one(q, carry):
+            one_hot_pair(place_ref, q * planes + sp, hot, slots)
+            d_wide = load_d.shape[2]
+
+            @pl.when(i > 0)
+            def _():
+                copy_out(stage_x, outx_ref, out_x, q, sp).wait()
+                copy_out(stage_d, outd_ref, out_d, q, sp).wait()
+
+            for k in range(2):
+                load(q, sp, k).wait()
+
+            def columns_of(at, wide, with_d):
+                rows = jnp.concatenate(
+                    [buf[2 * q, sp, :, at], buf[2 * q + 1, sp, :, at]], axis=0
+                )
+                got = jnp.dot(hot[...], rows, preferred_element_type=FULL).astype(LOW)
+                stage_x[q, :, :, at] = got.reshape(EXP_DEV, slots, wide)
+                if with_d:
+                    got = jnp.dot(
+                        hot[...], load_d[q, :, at], preferred_element_type=FULL
+                    ).astype(LOW)
+                    stage_d[q, :, :, at] = got.reshape(EXP_DEV, slots, wide)
+
+            def tile(t, inner):
+                columns_of(pl.ds(pl.multiple_of(t * TILE, TILE), TILE), TILE, True)
+                return inner
+
+            lax.fori_loop(0, MODEL_WIDTH // TILE, tile, 0)
+            if width > MODEL_WIDTH:
+                columns_of(pl.ds(MODEL_WIDTH, width - MODEL_WIDTH), width - MODEL_WIDTH, False)
+            copy_out(stage_x, outx_ref, out_x, q, sp).start()
+            copy_out(stage_d, outd_ref, out_d, q, sp).start()
+            return carry
+
+        lax.fori_loop(0, 4, one, 0)
+
+    def step(i, carry):
+        for lag, work in ((0, step_first), (1, step_second), (2, step_third), (3, dispatch)):
+            sp, there = plane_at(i - lag)
+
+            @pl.when(there)
+            def _(sp=sp, lag=lag, work=work):
+                if lag in (0, 3):
+                    work(sp, i - lag)
+                else:
+                    work(sp)
+
+        sp, there = plane_at(i - 2)
+
+        @pl.when(there)
+        def _():
+            start_loads(sp)
+
+        return carry
+
+    lax.fori_loop(0, 2 * planes + 2, step, 0)
+
+    def drain(sp, carry):
+        for copy in first(sp) + from_x(sp) + from_y(sp) + [from_diagonal(sp)]:
+            copy.wait_send()
+
+        @pl.when((sp <= s) & (s < planes - 1))
+        def _():
+            up(sp).wait_send()
+
+        @pl.when((sp >= s) & (s > 0))
+        def _():
+            down(sp).wait_send()
+
+        return carry
+
+    lax.fori_loop(0, planes, drain, 0)
+    for q in range(4):
+        copy_out(stage_x, outx_ref, out_x, q, 0).wait()
+        copy_out(stage_d, outd_ref, out_d, q, 0).wait()
+
+
+def gather_dispatch(rows, d_all, place, planes, slots, identity):
+    owners = lax.axis_size("expert")
+    length, width = rows.shape
+    total = place.shape[0] * slots
+    kernel = functools.partial(gather_dispatch_kernel, planes, slots)
+    return pl.pallas_call(
+        kernel,
+        out_shape=[
+            jax.ShapeDtypeStruct((EXP_DEV, total, width), LOW),
+            jax.ShapeDtypeStruct((EXP_DEV, total, MODEL_WIDTH), LOW),
+        ],
+        in_specs=[VM, ANY, VM],
+        out_specs=[ANY, ANY],
+        scratch_shapes=[
+            pltpu.VMEM((owners, planes, length, width), LOW),
+            pltpu.VMEM((EXP_DEV * slots, 2 * length), LOW),
+            pltpu.VMEM((4, EXP_DEV, slots, width), LOW),
+            pltpu.VMEM((4, EXP_DEV, slots, MODEL_WIDTH), LOW),
+            pltpu.VMEM((4, 2 * length, MODEL_WIDTH), LOW),
+            DMA((2, planes)),
+            DMA((planes,)),
+            DMA((2, planes)),
+            DMA((2, planes)),
+            DMA((2, planes)),
+            DMA((2, planes)),
+            DMA((4, planes)),
+            DMA((4, planes)),
+            DMA((4,)),
+            DMA((4,)),
+            DMA((4, 2)),
+        ],
+        compiler_params=pltpu.CompilerParams(
+            collective_id=identity, has_side_effects=True, vmem_limit_bytes=VMEM_LIMIT
+        ),
+    )(rows, d_all, place)
+
+
+def expert_kernel(
+    sel_ref, x_ref, dy_ref, wg_ref, wu_ref, wd_ref,
+    y_ref, dx_ref, dwg_ref, dwu_ref, dwd_ref, a_all, dg_all, du_all,
+):
+    rows = x_ref.shape[1]
+    step = 256
+    experts = sel_ref.shape[2] // 2
+    sel = sel_ref[0, 0:1, :]
+    lane = lax.broadcasted_iota(jnp.int32, sel.shape, 1)
+    high_sel = jnp.where(lane < experts, sel, 0.0)
+    rest_sel = sel - high_sel
+    nt = (((1,), (1,)), ((), ()))
+    tn = (((0,), (0,)), ((), ()))
+
+    def chunk(r, carry):
+        at = pl.ds(pl.multiple_of(r * step, step), step)
+        x = x_ref[0, at, :MODEL_WIDTH]
+        tail = x_ref[0, at, MODEL_WIDTH:].astype(FULL)
+        dy = dy_ref[0, at, :]
+        gate = jnp.sum(tail * sel, axis=1, keepdims=True)
+        g = lax.dot_general(x, wg_ref[0], nt, preferred_element_type=FULL)
+        u = lax.dot_general(x, wu_ref[0], nt, preferred_element_type=FULL)
+        da = jnp.dot(dy, wd_ref[0], preferred_element_type=FULL)
+        sigma = 1.0 / (1.0 + jnp.exp(-g))
+        silu = g * sigma
+        act = (silu * u).astype(LOW).astype(FULL)
+        d_gate = jnp.sum(act * da, axis=1, keepdims=True)
+        d_act = da * gate
+        a_all[at, :] = (act * gate).astype(LOW)
+        dg_all[at, :] = (d_act * u * sigma * (1.0 + g * (1.0 - sigma))).astype(LOW)
+        du_all[at, :] = (d_act * silu).astype(LOW)
+        high = d_gate.astype(LOW).astype(FULL)
+        dx_ref[0, at, MODEL_WIDTH:] = (high * high_sel + (d_gate - high) * rest_sel).astype(LOW)
+        y_ref[0, at, :] = lax.dot_general(
+            a_all[at, :], wd_ref[0], nt, preferred_element_type=FULL
+        ).astype(LOW)
+        dx_ref[0, at, :MODEL_WIDTH] = (
+            jnp.dot(dg_all[at, :], wg_ref[0], preferred_element_type=FULL)
+            + jnp.dot(du_all[at, :], wu_ref[0], preferred_element_type=FULL)
+        ).astype(LOW)
+        return carry
+
+    lax.fori_loop(0, rows // step, chunk, 0)
+
+    def tile(t, carry):
+        at = pl.ds(pl.multiple_of(t * TILE, TILE), TILE)
+        dwg_ref[0, :, at] = lax.dot_general(
+            dg_all[...], x_ref[0, :, at], tn, preferred_element_type=FULL
+        )
+        dwu_ref[0, :, at] = lax.dot_general(
+            du_all[...], x_ref[0, :, at], tn, preferred_element_type=FULL
+        )
+        dwd_ref[0, at, :] = lax.dot_general(
+            dy_ref[0, :, at], a_all[...], tn, preferred_element_type=FULL
+        )
+        return carry
+
+    lax.fori_loop(0, MODEL_WIDTH // TILE, tile, 0)
+
+
+def expert_pass(sel, x, dy, w_gate, w_up, w_down):
+    rows, width = x.shape[1:]
+    hidden = w_gate.shape[1]
+
+    def spec(*shape):
+        return pl.BlockSpec((1,) + shape, lambda j: (j, 0, 0))
+
+    def out(*shape, dtype=LOW):
+        return jax.ShapeDtypeStruct((EXP_DEV,) + shape, dtype)
+
+    return pl.pallas_call(
+        expert_kernel,
+        grid=(EXP_DEV,),
+        in_specs=[
+            spec(*sel.shape[1:]),
+            spec(rows, width),
+            spec(rows, MODEL_WIDTH),
+            spec(hidden, MODEL_WIDTH),
+            spec(hidden, MODEL_WIDTH),
+            spec(MODEL_WIDTH, hidden),
+        ],
+        out_specs=[
+            spec(rows, MODEL_WIDTH),
+            spec(rows, width),
+            spec(hidden, MODEL_WIDTH),
+            spec(hidden, MODEL_WIDTH),
+            spec(MODEL_WIDTH, hidden),
+        ],
+        out_shape=[
+            out(rows, MODEL_WIDTH),
+            out(rows, width),
+            out(hidden, MODEL_WIDTH, dtype=FULL),
+            out(hidden, MODEL_WIDTH, dtype=FULL),
+            out(MODEL_WIDTH, hidden, dtype=FULL),
+        ],
+        scratch_shapes=[pltpu.VMEM((rows, hidden), LOW)] * 3,
+        compiler_params=pltpu.CompilerParams(vmem_limit_bytes=VMEM_LIMIT),
+        cost_estimate=pl.CostEstimate(
+            flops=EXP_DEV * rows * MODEL_WIDTH * hidden * 18,
+            bytes_accessed=160 << 20,
+            transcendentals=EXP_DEV * rows * hidden,
+        ),
+    )(sel, x, dy, w_gate, w_up, w_down)
+
+
+def combine_home_kernel(
+    planes, slots, place_ref, v_ref, out_ref,
+    hot, load, mine, away, c_in, x_in, y_in, x_half, y_half, u_in, d_in,
+    in_sem, c_send, c_recv, x_send, x_recv, y_send, y_recv, z_send, z_recv,
+):
+    e, core, flip_x, flip_y, diagonal = neighbours()
+    s = lax.axis_index("shard")
+    q_own, q_x, q_y, q_d = e // 2, flip_x // 2, flip_y // 2, diagonal // 2
+    parity = e % 2
+    length, width = out_ref.shape
+    half = length // 2
+    low_half, high_half = pl.ds(0, half), pl.ds(half, half)
+
+    def fetch(q, sp):
+        rows = pl.ds(pl.multiple_of((q * planes + sp) * slots, 16), slots)
+        return pltpu.make_async_copy(v_ref.at[:, rows, :], load.at[q], in_sem.at[q])
+
+    def to_core(q, sp):
+        return send(away.at[q, sp], c_in.at[q, sp], c_send.at[q, sp], c_recv.at[q, sp], (core, s))
+
+    def halves(sp):
+        return [
+            send(
+                mine.at[q_d, sp, low_half], y_half.at[sp], y_send.at[0, sp], y_recv.at[0, sp],
+                (flip_y, s),
+            ),
+            send(
+                mine.at[q_d, sp, high_half], x_half.at[sp], x_send.at[0, sp], x_recv.at[0, sp],
+                (flip_x, s),
+            ),
+        ]
+
+    def to_x(sp):
+        return send(mine.at[q_x, sp], x_in.at[sp], x_send.at[1, sp], x_recv.at[1, sp], (flip_x, s))
+
+    def to_y(sp):
+        return send(mine.at[q_y, sp], y_in.at[sp], y_send.at[1, sp], y_recv.at[1, sp], (flip_y, s))
+
+    def up(sp):
+        return send(mine.at[q_own, sp], u_in.at[sp], z_send.at[0, sp], z_recv.at[0, sp], (e, s + 1))
+
+    def down(sp):
+        return send(mine.at[q_own, sp], d_in.at[sp], z_send.at[1, sp], z_recv.at[1, sp], (e, s - 1))
+
+    def arrived(block, sem):
+        send(block, block, sem, sem, (core, s)).wait_recv()
+
+    def plane_at(i):
+        back = 2 * planes - 2 - i
+        sp = s + (2 * (back % 2) - 1) * ((back + 1) // 2)
+        return sp, (sp >= 0) & (sp < planes) & (i >= 0) & (back >= 0)
+
+    def add(target, *others):
+        total = target[...].astype(FULL)
+        for other in others:
+            total = total + other[...].astype(FULL)
+        target[...] = total.astype(LOW)
+
+    def work(sp):
+        for q in range(4):
+            fetch(q, sp).start()
+
+        def one(q, carry):
+            one_hot_pair(place_ref, q * planes + sp, hot, slots)
+            fetch(q, sp).wait()
+
+            def part(at, wide):
+                rows = load[q, :, :, at].reshape(EXP_DEV * slots, wide)
+                got = lax.dot_general(
+                    hot[...], rows, (((0,), (0,)), ((), ())), preferred_element_type=FULL
+                ).astype(LOW)
+                got = got.reshape(2, length, wide)
+
+                @pl.when(parity == 0)
+                def _():
+                    mine[q, sp, :, at] = got[0]
+                    away[q, sp, :, at] = got[1]
+
+                @pl.when(parity == 1)
+                def _():
+                    mine[q, sp, :, at] = got[1]
+                    away[q, sp, :, at] = got[0]
+
+            def tile(t, inner):
+                part(pl.ds(pl.multiple_of(t * TILE, TILE), TILE), TILE)
+                return inner
+
+            lax.fori_loop(0, MODEL_WIDTH // TILE, tile, 0)
+            if width > MODEL_WIDTH:
+                part(pl.ds(MODEL_WIDTH, width - MODEL_WIDTH), width - MODEL_WIDTH)
+            to_core(q, sp).start()
+            return carry
+
+        lax.fori_loop(0, 4, one, 0)
+
+    def pairs(sp):
+        def one(q, carry):
+            arrived(c_in.at[q, sp], c_recv.at[q, sp])
+            add(mine.at[q, sp], c_in.at[q, sp])
+            return carry
+
+        one(q_d, 0)
+        for copy in halves(sp):
+            copy.start()
+        for q in (q_x, q_y, q_own):
+            one(q, 0)
+
+    def sides(sp):
+        arrived(y_half.at[sp], y_recv.at[0, sp])
+        add(mine.at[q_x, sp, low_half], y_half.at[sp])
+        to_x(sp).start()
+        arrived(x_half.at[sp], x_recv.at[0, sp])
+        add(mine.at[q_y, sp, high_half], x_half.at[sp])
+        to_y(sp).start()
+
+    def line(sp):
+        arrived(x_in.at[sp], x_recv.at[1, sp])
+        arrived(y_in.at[sp], y_recv.at[1, sp])
+        add(mine.at[q_own, sp], x_in.at[sp], y_in.at[sp])
+
+        @pl.when((sp >= s) & (s > 0))
+        def _():
+            arrived(u_in.at[sp], z_recv.at[0, sp])
+            add(mine.at[q_own, sp], u_in.at[sp])
+
+        @pl.when((sp <= s) & (s < planes - 1))
+        def _():
+            arrived(d_in.at[sp], z_recv.at[1, sp])
+            add(mine.at[q_own, sp], d_in.at[sp])
+
+        @pl.when(sp > s)
+        def _():
+            up(sp).start()
+
+        @pl.when(sp < s)
+        def _():
+            down(sp).start()
+
+    greet(planes)
+
+    def step(i, carry):
+        for lag, job in ((0, work), (1, pairs), (2, sides), (3, line)):
+            sp, there = plane_at(i - lag)
+
+            @pl.when(there)
+            def _(sp=sp, job=job):
+                job(sp)
+
+        return carry
+
+    lax.fori_loop(0, 2 * planes + 2, step, 0)
+    out_ref[...] = mine[q_own, s].astype(FULL)
+
+    def drain(sp, carry):
+        for q in range(4):
+            to_core(q, sp).wait_send()
+        for copy in halves(sp) + [to_x(sp), to_y(sp)]:
+            copy.wait_send()
+
+        @pl.when(sp > s)
+        def _():
+            up(sp).wait_send()
+
+        @pl.when(sp < s)
+        def _():
+            down(sp).wait_send()
+
+        return carry
+
+    lax.fori_loop(0, planes, drain, 0)
+
+
+def combine_home(place, v, length, planes, slots, identity):
+    width = v.shape[2]
+    block = (planes, length, width)
+    return pl.pallas_call(
+        functools.partial(combine_home_kernel, planes, slots),
+        out_shape=jax.ShapeDtypeStruct((length, width), FULL),
+        in_specs=[VM, ANY],
+        out_specs=VM,
+        scratch_shapes=[
+            pltpu.VMEM((EXP_DEV * slots, 2 * length), LOW),
+            pltpu.VMEM((4, EXP_DEV, slots, width), LOW),
+            pltpu.VMEM((4,) + block, LOW),
+            pltpu.VMEM((4,) + block, LOW),
+            pltpu.VMEM((4,) + block, LOW),
+            pltpu.VMEM(block, LOW),
+            pltpu.VMEM(block, LOW),
+            pltpu.VMEM((planes, length // 2, width), LOW),
+            pltpu.VMEM((planes, length // 2, width), LOW),
+            pltpu.VMEM(block, LOW),
+            pltpu.VMEM(block, LOW),
+            DMA((4,)),
+            DMA((4, planes)),
+            DMA((4, planes)),
+            DMA((2, planes)),
+            DMA((2, planes)),
+            DMA((2, planes)),
+            DMA((2, planes)),
+            DMA((2, planes)),
+            DMA((2, planes)),
+        ],
+        compiler_params=pltpu.CompilerParams(
+            collective_id=identity, has_side_effects=True, vmem_limit_bytes=VMEM_LIMIT
+        ),
+    )(place, v)
 
 
 def per_device(
@@ -190,9 +790,8 @@
     gates = named * chance / chosen_sum
     gates_high = gates.astype(LOW)
     gates_rest = (gates - gates_high.astype(FULL)).astype(LOW)
-    h_all = lax.all_gather(
-        jnp.concatenate([h2, gates_high, gates_rest], axis=1), both, axis=0, tiled=False
-    )
+    h_rows = jnp.concatenate([h2, gates_high, gates_rest], axis=1)
+    resident_pass = blocks * length * h_rows.shape[1] * 2 <= RESIDENT
 
     route_all = d_all[:, :, MODEL_WIDTH : MODEL_WIDTH + TOPK].astype(FULL)
     own_experts = (me * EXP_DEV + jnp.arange(EXP_DEV, dtype=jnp.int32)).astype(FULL)
@@ -201,84 +800,102 @@
     rank = dot("ts,bsj->btj", earlier, match.astype(LOW))
     slot_ids = jnp.arange(capacity, dtype=jnp.int32).astype(FULL)
     place = jnp.where(match > 0, rank, -1.0).transpose(0, 2, 1)
-    dispatch = (place[:, :, None, :] == slot_ids[:, None]).astype(LOW)
-
-    def experts(h_rows, d_rows, gate_high, gate_rest, put):
-        count = h_rows.shape[0]
-        flat = put.reshape(count, EXP_DEV * capacity, length)
-        x = dot("bst,btd->bsd", flat, h_rows).astype(LOW)
-        dy = dot("bst,btd->bsd", flat, d_rows).astype(LOW)
-
-        def by_expert(v):
-            v = v.reshape(count, EXP_DEV, capacity, v.shape[-1])
-            return v.transpose(1, 0, 2, 3).reshape(EXP_DEV, count * capacity, v.shape[-1])
-
-        def by_block(v):
-            v = v.reshape(EXP_DEV, count, capacity, v.shape[-1])
-            return v.transpose(1, 0, 2, 3).reshape(count, EXP_DEV * capacity, v.shape[-1])
-
-        x, dy = by_expert(x), by_expert(dy)
-        gate_slot = dot("bjct,btj->jbc", put, gate_high) + dot("bjct,btj->jbc", put, gate_rest)
-        gate_slot = gate_slot.reshape(EXP_DEV, count * capacity, 1)
-        g = dot("erd,efd->erf", x, w_gate)
-        u = dot("erd,efd->erf", x, w_up)
-        da = dot("erd,edf->erf", dy, w_down)
-        sigma = jax.nn.sigmoid(g)
-        silu = g * sigma
-        act = (silu * u).astype(LOW).astype(FULL)
-        d_gate_slot = jnp.sum(act * da, axis=-1)
-        act_gated = (act * gate_slot).astype(LOW)
-        d_act = da * gate_slot
-        dg = (d_act * u * sigma * (1.0 + g * (1.0 - sigma))).astype(LOW)
-        du = (d_act * silu).astype(LOW)
-        y = dot("erf,edf->erd", act_gated, w_down).astype(LOW)
-        d_down = dot("erd,erf->edf", dy, act_gated)
-        d_gate = dot("erf,erd->efd", dg, x)
-        d_up = dot("erf,erd->efd", du, x)
-        dx = (dot("erf,efd->erd", dg, w_gate) + dot("erf,efd->erd", du, w_up)).astype(LOW)
-        mix = dot("bst,bsd->btd", flat, by_block(y)).astype(LOW)
-        d_h = dot("bst,bsd->btd", flat, by_block(dx)).astype(LOW)
-        d_g = dot(
-            "bjct,jbc->btj", put.astype(FULL), d_gate_slot.reshape(EXP_DEV, count, capacity)
+    if resident_pass:
+        place = place.reshape(owners // 2, 2, planes, EXP_DEV, length)
+        offset = (capacity * jnp.arange(2, dtype=jnp.int32)).astype(FULL)
+        place = jnp.where(place >= 0, place + offset[:, None, None, None], -1.0)
+        place = place.transpose(0, 2, 3, 1, 4).reshape(blocks // 2, EXP_DEV, 2 * length)
+        lanes = jnp.arange(2 * experts_all, dtype=jnp.int32) % experts_all
+        own = (me * EXP_DEV + jnp.arange(EXP_DEV, dtype=jnp.int32))[:, None] == lanes
+        sel = jnp.broadcast_to(own.astype(FULL)[:, None, :], (EXP_DEV, 8, 2 * experts_all))
+        slots = 2 * capacity
+        x, dy = gather_dispatch(
+            h_rows, d_all.reshape(owners, planes, length, -1), place, planes, slots, 1
         )
-        return mix, d_h, d_g, d_gate, d_up, d_down
-
-    gate_cols = lax.dynamic_slice_in_dim(h_all, MODEL_WIDTH + me * EXP_DEV, EXP_DEV, 2)
-    rest_cols = lax.dynamic_slice_in_dim(
-        h_all, MODEL_WIDTH + experts_all + me * EXP_DEV, EXP_DEV, 2
-    )
-    step = min(blocks, GROUP_BLOCKS)
-    mixes, d_hs, d_gs, totals = [], [], [], None
-    for at in range(0, blocks, step):
-        cut = slice(at, at + step)
-        mix, d_h, d_g, *grads = experts(
-            h_all[cut, :, :MODEL_WIDTH],
-            d_all[cut, :, :MODEL_WIDTH],
-            gate_cols[cut],
-            rest_cols[cut],
-            dispatch[cut],
+        y, dx, d_gate, d_up, d_down = expert_pass(sel, x, dy, w_gate, w_up, w_down)
+        d_home = combine_home(place, dx, length, planes, slots, 2)
+        mixture = combine_home(place, y, length, planes, slots, 3)
+    else:
+        dispatch = (place[:, :, None, :] == slot_ids[:, None]).astype(LOW)
+
+        def experts(h_rows, d_rows, gate_high, gate_rest, put):
+            count = h_rows.shape[0]
+            flat = put.reshape(count, EXP_DEV * capacity, length)
+            x = dot("bst,btd->bsd", flat, h_rows).astype(LOW)
+            dy = dot("bst,btd->bsd", flat, d_rows).astype(LOW)
+
+            def by_expert(v):
+                v = v.reshape(count, EXP_DEV, capacity, v.shape[-1])
+                return v.transpose(1, 0, 2, 3).reshape(EXP_DEV, count * capacity, v.shape[-1])
+
+            def by_block(v):
+                v = v.reshape(EXP_DEV, count, capacity, v.shape[-1])
+                return v.transpose(1, 0, 2, 3).reshape(count, EXP_DEV * capacity, v.shape[-1])
+
+            x, dy = by_expert(x), by_expert(dy)
+            gate_slot = dot("bjct,btj->jbc", put, gate_high) + dot("bjct,btj->jbc", put, gate_rest)
+            gate_slot = gate_slot.reshape(EXP_DEV, count * capacity, 1)
+            g = dot("erd,efd->erf", x, w_gate)
+            u = dot("erd,efd->erf", x, w_up)
+            da = dot("erd,edf->erf", dy, w_down)
+            sigma = jax.nn.sigmoid(g)
+            silu = g * sigma
+            act = (silu * u).astype(LOW).astype(FULL)
+            d_gate_slot = jnp.sum(act * da, axis=-1)
+            act_gated = (act * gate_slot).astype(LOW)
+            d_act = da * gate_slot
+            dg = (d_act * u * sigma * (1.0 + g * (1.0 - sigma))).astype(LOW)
+            du = (d_act * silu).astype(LOW)
+            y = dot("erf,edf->erd", act_gated, w_down).astype(LOW)
+            d_down = dot("erd,erf->edf", dy, act_gated)
+            d_gate = dot("erf,erd->efd", dg, x)
+            d_up = dot("erf,erd->efd", du, x)
+            dx = (dot("erf,efd->erd", dg, w_gate) + dot("erf,efd->erd", du, w_up)).astype(LOW)
+            mix = dot("bst,bsd->btd", flat, by_block(y)).astype(LOW)
+            d_h = dot("bst,bsd->btd", flat, by_block(dx)).astype(LOW)
+            d_g = dot(
+                "bjct,jbc->btj", put.astype(FULL), d_gate_slot.reshape(EXP_DEV, count, capacity)
+            )
+            return mix, d_h, d_g, d_gate, d_up, d_down
+
+        h_all = lax.all_gather(h_rows, both, axis=0, tiled=False)
+        gate_cols = lax.dynamic_slice_in_dim(h_all, MODEL_WIDTH + me * EXP_DEV, EXP_DEV, 2)
+        rest_cols = lax.dynamic_slice_in_dim(
+            h_all, MODEL_WIDTH + experts_all + me * EXP_DEV, EXP_DEV, 2
         )
-        mixes.append(mix)
-        d_hs.append(d_h)
-        d_gs.append(d_g)
-        totals = grads if totals is None else [a + b for a, b in zip(totals, grads)]
-    d_gate, d_up, d_down = totals
-    d_g = jnp.concatenate(d_gs, axis=0)
-    spread = jnp.zeros((blocks, length, TAIL), LOW)
-    spread = lax.dynamic_update_slice_in_dim(spread, d_g.astype(LOW), me * EXP_DEV, 2)
-    d_h_wide = jnp.concatenate([jnp.concatenate(d_hs, axis=0), spread], axis=2)
-
-    def home(v):
-        v = v.reshape(owners, planes, length, v.shape[-1])
-        v = lax.psum_scatter(v, "expert", scatter_dimension=0, tiled=False)
-        return lax.psum_scatter(v, "shard", scatter_dimension=0, tiled=False)
-
-    d_home = home(d_h_wide)
-    mixture = home(jnp.concatenate(mixes, axis=0))
+        step = min(blocks, GROUP_BLOCKS)
+        mixes, d_hs, d_gs, totals = [], [], [], None
+        for at in range(0, blocks, step):
+            cut = slice(at, at + step)
+            mix, d_h, d_g, *grads = experts(
+                h_all[cut, :, :MODEL_WIDTH],
+                d_all[cut, :, :MODEL_WIDTH],
+                gate_cols[cut],
+                rest_cols[cut],
+                dispatch[cut],
+            )
+            mixes.append(mix)
+            d_hs.append(d_h)
+            d_gs.append(d_g)
+            totals = grads if totals is None else [a + b for a, b in zip(totals, grads)]
+        d_gate, d_up, d_down = totals
+        d_g = jnp.concatenate(d_gs, axis=0)
+        spread = jnp.zeros((blocks, length, 2 * experts_all), LOW)
+        spread = lax.dynamic_update_slice_in_dim(spread, d_g.astype(LOW), me * EXP_DEV, 2)
+        d_h_wide = jnp.concatenate([jnp.concatenate(d_hs, axis=0), spread], axis=2)
+
+        def home(v):
+            v = v.reshape(owners, planes, length, v.shape[-1])
+            v = lax.psum_scatter(v, "expert", scatter_dimension=0, tiled=False)
+            return lax.psum_scatter(v, "shard", scatter_dimension=0, tiled=False)
+
+        d_home = home(d_h_wide)
+        mixture = home(jnp.concatenate(mixes, axis=0))
     result = (middle + mixture.astype(FULL)).astype(LOW)
 
     upstream = d_out.astype(FULL)
-    d_gates = d_home[:, MODEL_WIDTH : MODEL_WIDTH + experts_all].astype(FULL)
+    d_gates = d_home[:, MODEL_WIDTH:].astype(FULL)
+    d_gates = d_gates[:, :experts_all] + d_gates[:, experts_all:]
     d_chance = named * (d_gates - jnp.sum(d_gates * gates, axis=1, keepdims=True)) / chosen_sum
     d_logits = chance * (d_chance - jnp.sum(d_chance * chance, axis=1, keepdims=True))
     d_logits = d_logits.astype(LOW)

time: 1480 us -> 1200 us (0.81)
  waiting for transfers between devices: 803 us -> 400 us
  Pallas kernels: 0 us -> 400 us
  matrix products: 289 us -> 54.9 us
  local copies, waits for them, and re-layouts: 226 us -> 167 us
    pallas_call x0 -> x4, Pallas kernels: none -> 400 us  [the longest x2 229 us: combine_home(): pl.pallas_call(functools.partial(combine_home_kernel, planes, slots), out...]
    reduce_scatter x4 -> x0, waiting for transfers between devices: 244 us -> none  [the longest x2 192 us: home(): v = lax.psum_scatter(v, 'expert', scatter_dimension=0, tiled=False)]
    dot_general x31 -> x15, matrix products: 287 us -> 50.6 us  [dot(): return jnp.einsum(spec, left, right, preferred_element_type=FULL)]
    transpose x4 -> x0, local copies, waits for them, and re-layouts: 84.5 us -> none  [the longest x2 42.3 us: by_expert(): v.transpose(1, 0, 2, 3).reshape(EXP_DEV, count * capacity, v.shape[-1])]
    all_gather x1 -> x0, waiting for transfers between devices: 77.6 us -> none  [per_device(): lax.all_gather(jnp.concatenate([h2, gates_high, gates_rest], axis=1), bot...]
    all_gather x1, waiting for transfers between devices: 46.6 us -> 0.01 us  [per_device(): d_pack = lax.all_gather(d_pack, 'expert', axis=0, tiled=False).astype(FULL)]
    all_gather x1, waiting for transfers between devices: 36 us -> 0.01 us  [per_device(): d_w_out = lax.all_gather(d_w_out, 'expert', axis=1, tiled=True).astype(FULL)]
    unnamed x183 -> x149, local copies, waits for them, and re-layouts: 54.5 us -> 86.9 us
  transfers between devices with their start and end apart: 16 -> 11, of which waited for: 15 -> 9; matrix products, arithmetic and copies ran while one was open for 17% -> 12% of each run, Pallas kernels for 0% -> 11%
where the time goes in v2:
time: 1200 us; the launch traced here: 1180 us
  waiting for transfers between devices  400 us (33%)
  Pallas kernels  400 us (33%)
  local copies, waits for them, and re-layouts  167 us (14%)
  other arithmetic  98.3 us (8%)
  matrix products  54.9 us (5%)
  blocking collectives  40.4 us (3%)
  between operations  17.2 us (1%)
    pallas_call x2, Pallas kernels, combine_home(): pl.pallas_call(functools.partial(combine_home_kernel, planes, slots), out...  229 us
    pallas_call x1, Pallas kernels, gather_dispatch(): pl.pallas_call(kernel, out_shape=[jax.ShapeDtypeStruct((EXP_DEV, total, w...  91.1 us
    unnamed x149, local copies, waits for them, and re-layouts  86.9 us
    pallas_call x1, Pallas kernels, expert_pass(): pl.pallas_call(expert_kernel, grid=(EXP_DEV,), in_specs=[spec(*sel.shape[...  80.8 us
    reduce_scatter x1, waiting for transfers between devices, per_device(): lax.psum_scatter(jnp.concatenate([d_wqkv, d_tail], axis=1), 'shard', scat...  70.6 us
    all_gather x1, waiting for transfers between devices, per_device(): gathered = lax.all_gather(mine, 'shard', axis=0, tiled=True)  70 us
    all_gather x1, waiting for transfers between devices, per_device(): lax.all_gather(jnp.concatenate([d_out, d_tail], axis=1), both, axis=0, ti...  53.9 us
    dot_general x15, matrix products, dot(): return jnp.einsum(spec, left, right, preferred_element_type=FULL)  50.6 us
  transfers between devices with their start and end apart: 11, of which 9 were waited for; matrix products, arithmetic and copies ran while one was open for 12% of the time, Pallas kernels for 11%

profile of v2, /device:TPU:0, one launch (start us, length us, event | category | flops | bytes accessed | tf_op | source)
XLA Modules:
  0.0 1178.7 jit_solution(14502212340204760660)
XLA Ops:
  17.1 3.4 dynamic-slice_select_fusion
  20.7 70.0 %all-gather.11.cloned.1.call-done = bf16[2048,896]{1,0:T(8,128)(2,1)} async-done(((bf16[512,896]{1,0:T(8,128)(2,1)}), bf16[2048,896]{1,0:T(8,128)(2,1)}) %all-gather.11.cloned.1.call-update) | async-done | bytes 3670032 | tf_op jit(solution)/shard_map/all_gather | solution.py:710
  93.6 36.1 %all-gather.15.cloned.1.call-done = bf16[1024,2176]{1,0:T(8,128)(2,1)} async-done(((bf16[128,2176]{1,0:T(8,128)(2,1)}), bf16[1024,2176]{1,0:T(8,128)(2,1)}) %all-gather.15.cloned.1.call-update) | async-done | bytes 4456464 | tf_op jit(solution)/shard_map/all_gather | solution.py:725
  129.7 4.8 slice.144
  135.7 7.0 copy.325
  142.7 3.9 fusion.1
  146.6 6.7 fusion.3
  153.3 6.7 copy.266
  160.1 6.2 fusion.6
  168.7 2.9 reshape.285
  171.6 2.8 multiply_reduce_fusion.1
  182.2 4.3 fusion.93
  186.5 3.3 convolution_convert_fusion.3
  189.8 29.4 %all-reduce.10.cloned.1.call-done = bf16[512,2048]{1,0:T(8,128)(2,1)} async-done(((bf16[512,2048]{1,0:T(8,128)(2,1)}), bf16[512,2048]{1,0:T(8,128)(2,1)}) %all-reduce.10.cloned.1.call-update) | async-done | bytes 2097168 | tf_op jit(solution)/shard_map/psum | solution.py:738
  219.2 6.3 convolution_convert_fusion
  227.6 11.3 copy.281.wd_ref
  240.7 42.3 %reduce-scatter.5.cloned.1.call-done = bf16[1,128,2048]{2,1,0:T(8,128)(2,1)} async-done(((bf16[8,128,2048]{2,1,0:T(8,128)(2,1)}), bf16[1,128,2048]{2,1,0:T(8,128)(2,1)}) %reduce-scatter.5.cloned.1.call-update) | async-done | bytes 524304 | tf_op jit(solution)/shard_map/reduce_scatter | solution.py:779
  293.9 53.9 %all-gather.17.cloned.1.call-done = bf16[4096,2176]{1,0:T(8,128)(2,1)} async-done(((bf16[128,2176]{1,0:T(8,128)(2,1)}), bf16[4096,2176]{1,0:T(8,128)(2,1)}) %all-gather.17.cloned.1.call-update) | async-done | bytes 17825808 | tf_op jit(solution)/shard_map/all_gather | solution.py:747
  355.5 91.1 %shard_map.229 = (bf16[8,768,2176]{2,1,0:T(8,128)(2,1)}, bf16[8,768,2048]{2,1,0:T(8,128)(2,1)}) custom-call(bf16[128,2176]{1,0:T(8,128)(2,1)} %concatenate.54.x_ref, bf16[8,4,128,2176]{3,2,1,0:T(8,128)(2,1)} %bitcast.189, f32[16,8,256]{2,1,0:T(8,128)} %bitcast.197), custom_call_target="tpu_custom_call" | custom-call | tf_op jit(solution)/shard_map/pallas_call | solution.py:313
  447.2 80.8 %shard_map.230 = (bf16[8,768,2048]{2,1,0:T(8,128)(2,1)}, bf16[8,768,2176]{2,1,0:T(8,128)(2,1)}, f32[8,192,2048]{2,1,0:T(8,128)}, f32[8,192,2048]{2,1,0:T(8,128)}, f32[8,2048,192]{2,1,0:T(8,128)}) custom-call(f32[8,8,128]{2,1,0:T(8,128)} %broadcast_in_dim.42.sel_ref, bf16[8,768,2176]{2,1,0:T(8,128)(2,1)} %get-tuple-element.19.x_ref, ...), custom_call_target="tpu_custom_call" | custom-call | flops 43486543872 | bytes 167772160 | tf_op jit(solution)/shard_map/pallas_call | solution.py:415
  528.1 101.1 %shard_map.232 = f32[128,2176]{1,0:T(8,128)} custom-call(f32[16,8,256]{2,1,0:T(8,128)} %bitcast.198, bf16[8,768,2176]{2,1,0:T(8,128)(2,1)} %get-tuple-element.22.v_ref), custom_call_target="tpu_custom_call" | custom-call | tf_op jit(solution)/shard_map/pallas_call | solution.py:625
  637.5 3.3 mul.420.clone
  640.8 3.0 mul.455
  643.9 50.5 %all-gather.19.cloned.1.call-done = bf16[1024,2048]{1,0:T(8,128)(2,1)} async-done(((bf16[128,2048]{1,0:T(8,128)(2,1)}), bf16[1024,2048]{1,0:T(8,128)(2,1)}) %all-gather.19.cloned.1.call-update) | async-done | bytes 4194320 | tf_op jit(solution)/shard_map/all_gather | solution.py:907
  694.4 6.2 fusion.20
  719.7 3.9 fusion.57
  725.8 3.0 fusion.10
  729.8 5.2 convolution_convert_fusion.1
  735.1 4.8 bitcast_convert_fusion.1
  741.1 40.4 %all_to_all.15 = bf16[1,512,8,256]{3,1,0,2:T(8,128)(2,1)} all-to-all(bf16[1,512,8,256]{3,1,0,2:T(8,128)(2,1)S(1)} %copy.302), channel_id=1, replica_groups=mesh['expert'=8,'shard'=4] {'expert'}, dimensions={2} | all-to-all | bytes 4194304 | tf_op jit(solution)/shard_map/all_to_all | solution.py:963
  783.1 7.4 bitcast_convert_fusion
  790.5 6.2 reduce-scatter.7.cloned.1.call-done
  798.4 3.4 fusion.5
  801.9 41.1 %reduce-scatter.11.cloned.1.call-done = bf16[1024,256]{1,0:T(8,128)(2,1)} async-done(((bf16[4096,256]{1,0:T(8,128)(2,1)}), bf16[1024,256]{1,0:T(8,128)(2,1)}) %reduce-scatter.11.cloned.1.call-update) | async-done | bytes 524304 | tf_op jit(solution)/shard_map/reduce_scatter | solution.py:965
  843.1 70.6 %reduce-scatter.9.cloned.1.call-done = bf16[512,896]{0,1:T(8,128)(2,1)} async-done(((bf16[2048,896]{0,1:T(8,128)(2,1)}), bf16[512,896]{0,1:T(8,128)(2,1)}) %reduce-scatter.9.cloned.1.call-update) | async-done | bytes 917520 | tf_op jit(solution)/shard_map/reduce_scatter | solution.py:949
  913.7 127.4 %shard_map.231 = f32[128,2048]{1,0:T(8,128)} custom-call(f32[16,8,256]{2,1,0:T(8,128)} %bitcast.199, bf16[8,768,2048]{2,1,0:T(8,128)(2,1)} %get-tuple-element.21.v_ref), custom_call_target="tpu_custom_call" | custom-call | tf_op jit(solution)/shard_map/pallas_call | solution.py:625
  1041.2 16.5 %copy.303 = f32[8,2048,192]{1,2,0:T(8,128)} copy(f32[8,2048,192]{2,1,0:T(8,128)} %get-tuple-element.109) | data formatting | bytes 25165824
  1057.7 3.0 fusion.33
  1060.7 6.7 convert_element_type.277
  1067.3 10.3 convert_element_type.280
  1077.6 25.1 %copy.340 = f32[112,8,8,512]{3,2,1,0:T(8,128)} copy(f32[112,8,8,512]{3,1,2,0:T(8,128)} %bitcast.185) | data formatting | bytes 29360128
  1102.7 7.8 slice_bitcast_fusion
  1110.5 4.6 slice.169
  1119.0 10.7 copy.299
  1129.7 14.7 %copy.341 = f32[64,8,8,512]{3,1,2,0:T(8,128)} copy(f32[64,8,8,512]{3,2,1,0:T(8,128)} %bitcast.187) | data formatting | bytes 16777216
  1144.4 6.0 reshape.294
  1150.4 7.9 reduce_sum.248
  1162.2 8.6 pad_maximum_fusion
  (265 shorter events, 89.1 us)
Async XLA Ops:
  8.0 82.7 %all-gather.11.cloned.1.call-start = ((), (), s32[]{:S(2)}) async-start(), calls=%async_computation.5 | async-start | bytes 4587520 | tf_op jit(solution)/shard_map/all_gather | solution.py:710
  13.4 2.4 copy-start.64
  13.4 2.8 copy-start.1
  15.8 113.9 %all-gather.15.cloned.1.call-start = ((), (), s32[]{:S(2)}) async-start(), calls=%async_computation.12 | async-start | bytes 5013504 | tf_op jit(solution)/shard_map/all_gather | solution.py:725
  17.1 202.1 %all-reduce.10.cloned.1.call-start = ((), (), s32[]{:S(2)}) async-start(), calls=%async_computation.6 | async-start | bytes 4194304 | tf_op jit(solution)/shard_map/psum | solution.py:738
  20.6 262.4 %reduce-scatter.5.cloned.1.call-start = ((), (), s32[]{:S(2)}) async-start(), calls=%async_computation.7 | async-start | bytes 4718592 | tf_op jit(solution)/shard_map/reduce_scatter | solution.py:779
  20.7 155.8 %copy-start.62 = (f32[64]{0:T(128)}, f32[64]{0:T(128)S(1)}, u32[]{:S(2)}) copy-start(f32[64]{0:T(128)S(1)} %multiply_power_fusion) | copy-start | bytes 772
  93.2 53.4 %copy-start.36 = (f32[2048]{0:T(1024)}, f32[2048]{0:T(1024)S(1)}, u32[]{:S(2)}) copy-start(f32[2048]{0:T(1024)S(1)} %get-tuple-element.117) | copy-start | bytes 24580
  93.5 81.5 %copy-start.55 = (f32[128]{0:T(128)}, f32[128]{0:T(128)S(1)}, u32[]{:S(2)}) copy-start(f32[128]{0:T(128)S(1)} %mul.407) | copy-start | bytes 1540
  93.6 85.5 %copy-start.53 = (f32[128]{0:T(128)}, f32[128]{0:T(128)S(1)}, u32[]{:S(2)}) copy-start(f32[128]{0:T(128)S(1)} %mul.422) | copy-start | bytes 1540
  142.7 3.9 copy-start
  166.2 2.4 copy-start.2
  168.6 6.5 copy-start.38
  174.6 5.1 copy-start.40
  179.1 3.2 copy-start.21
  186.5 3.3 copy-start.42
  225.5 122.3 %all-gather.17.cloned.1.call-start = ((), (), s32[]{:S(2)}) async-start(), calls=%async_computation.13 | async-start | bytes 18382848 | tf_op jit(solution)/shard_map/all_gather | solution.py:747
  227.4 467.0 %all-gather.19.cloned.1.call-start = ((), (), s32[]{:S(2)}) async-start(), calls=%async_computation.14 | async-start | bytes 4718592 | tf_op jit(solution)/shard_map/all_gather | solution.py:907
  227.6 56.7 %copy-start.33 = (f32[2048]{0:T(1024)S(1)}, f32[2048]{0:T(1024)}, u32[]{:S(2)}) copy-start(f32[2048]{0:T(1024)} %get-tuple-element.116) | copy-start | bytes 24580
  284.3 4.0 copy-start.57
  285.6 64.5 %copy-start.5 = (bf16[128,2048]{1,0:T(8,128)(2,1)}, bf16[128,2048]{1,0:T(8,128)(2,1)S(1)}, u32[]{:S(2)}) copy-start(bf16[128,2048]{1,0:T(8,128)(2,1)S(1)} %multiply_convert_fusion) | copy-start | bytes 1572868
  355.5 91.1 %copy-start.44 = (f32[8,128]{1,0:T(8,128)S(1)}, f32[8,128]{1,0:T(8,128)}, u32[]{:S(2)}) copy-start(f32[8,128]{1,0:T(8,128)} %compare_convert_fusion) | copy-start | bytes 12292
  528.0 101.2 %copy-start.27 = (f32[128,64]{1,0:T(8,128)S(1)}, f32[128,64]{1,0:T(8,128)}, u32[]{:S(2)}) copy-start(f32[128,64]{1,0:T(8,128)} %copy-done.26) | copy-start | bytes 98308
  528.0 101.2 %copy-start.52 = (f32[128]{0:T(128)S(1)}, f32[128]{0:T(128)}, u32[]{:S(2)}) copy-start(f32[128]{0:T(128)} %copy-done.51) | copy-start | bytes 1540
  528.0 102.3 %copy-start.46 = (f32[128]{0:T(128)S(1)}, f32[128]{0:T(128)}, u32[]{:S(2)}) copy-start(f32[128]{0:T(128)} %get-tuple-element.155) | copy-start | bytes 1540
  528.0 102.3 %copy-start.49 = (f32[128]{0:T(128)S(1)}, f32[128]{0:T(128)}, u32[]{:S(2)}) copy-start(f32[128]{0:T(128)} %copy-done.48) | copy-start | bytes 1540
  528.0 104.1 %copy-start.4 = (bf16[1,128,2048]{2,1,0:T(8,128)(2,1)S(1)}, bf16[1,128,2048]{2,1,0:T(8,128)(2,1)}, u32[]{:S(2)}) copy-start(bf16[1,128,2048]{2,1,0:T(8,128)(2,1)} %reduce-scatter.5.cloned.1.call-done) | copy-start | bytes 1572868
  528.0 104.1 %copy-start.34 = (f32[2048]{0:T(1024)S(1)}, f32[2048]{0:T(1024)}, u32[]{:S(2)}) copy-start(f32[2048]{0:T(1024)} %get-tuple-element.116) | copy-start | bytes 24580
  528.0 104.1 %copy-start.58 = (f32[128]{0:T(128)S(1)}, f32[128]{0:T(128)}, u32[]{:S(2)}) copy-start(f32[128]{0:T(128)} %copy-done.57) | copy-start | bytes 1540
  631.5 2.7 copy-start.60
  631.5 3.7 copy-start.13
  636.4 160.3 %reduce-scatter.7.cloned.1.call-start = ((), (), s32[]{:S(2)}) async-start(), calls=%async_computation.8 | async-start | bytes 4718592 | tf_op jit(solution)/shard_map/reduce_scatter | solution.py:927
  702.9 2.7 copy-start.20
  717.8 5.8 copy-start.39
  717.8 5.8 copy-start.56
  719.7 5.6 copy-start.3
  725.8 4.0 copy-start.28
  725.8 4.0 copy-start.65
  735.0 108.0 %reduce-scatter.11.cloned.1.call-start = ((), (), s32[]{:S(2)}) async-start(), calls=%async_computation.10 | async-start | bytes 2621440 | tf_op jit(solution)/shard_map/reduce_scatter | solution.py:965
  781.5 132.1 %reduce-scatter.9.cloned.1.call-start = ((), (), s32[]{:S(2)}) async-start(), calls=%async_computation.9 | async-start | bytes 4587520 | tf_op jit(solution)/shard_map/reduce_scatter | solution.py:949
  783.1 13.6 %copy-start.37 = (f32[2048]{0:T(1024)S(1)}, f32[2048]{0:T(1024)}, u32[]{:S(2)}) copy-start(f32[2048]{0:T(1024)} %copy-done.36) | copy-start | bytes 24580
  801.8 258.9 %all-gather.13.cloned.1.call-start = ((), (), s32[]{:S(2)}) async-start(), calls=%async_computation.11 | async-start | bytes 4718592 | tf_op jit(solution)/shard_map/all_gather | solution.py:966
  843.0 224.3 %all-gather.21.cloned.1.call-start = ((), (), s32[]{:S(2)}) async-start(), calls=%async_computation.15 | async-start | bytes 8257536 | tf_op jit(solution)/shard_map/all_gather | solution.py:952
  1041.1 16.5 %copy-start.14 = (bf16[128,2048]{1,0:T(8,128)(2,1)S(1)}, bf16[128,2048]{1,0:T(8,128)(2,1)}, u32[]{:S(2)}) copy-start(bf16[128,2048]{1,0:T(8,128)(2,1)} %param.27) | copy-start | bytes 1572868
  1041.1 16.5 %copy-start.17 = (f32[128,2048]{1,0:T(8,128)S(1)}, f32[128,2048]{1,0:T(8,128)}, u32[]{:S(2)}) copy-start(f32[128,2048]{1,0:T(8,128)} %shard_map.231) | copy-start | bytes 3145732
  1041.1 16.5 %copy-start.19 = (bf16[1,128,2048]{2,1,0:T(8,128)(2,1)S(1)}, bf16[1,128,2048]{2,1,0:T(8,128)(2,1)}, u32[]{:S(2)}) copy-start(bf16[1,128,2048]{2,1,0:T(8,128)(2,1)} %reduce-scatter.7.cloned.1.call-done) | copy-start | bytes 1572868
  1041.1 16.5 %copy-start.35 = (f32[2048]{0:T(1024)S(1)}, f32[2048]{0:T(1024)}, u32[]{:S(2)}) copy-start(f32[2048]{0:T(1024)} %get-tuple-element.116) | copy-start | bytes 24580
  1041.1 16.5 %copy-start.59 = (f32[128]{0:T(128)S(1)}, f32[128]{0:T(128)}, u32[]{:S(2)}) copy-start(f32[128]{0:T(128)} %copy-done.57) | copy-start | bytes 1540
  (29 other events, 38.4 us)
Sparse Core Ops, SparseCore 0:
  15.9 74.7 all-gather.10
  93.2 36.4 all-gather.14
  132.6 86.5 all-reduce.9
  225.6 57.3 reduce-scatter.4
  636.6 57.7 all-gather.18
  735.2 61.5 reduce-scatter.6
  799.1 43.8 reduce-scatter.10
  845.9 67.7 reduce-scatter.8
  915.5 53.9 all-gather.12
  971.2 75.4 all-gather.20
Sparse Core Ops, SparseCore 1:
  229.4 118.3 all-gather.16

commit v3 on v2

--- a/solution.py
+++ b/solution.py
@@ -364,7 +364,7 @@
         gate = jnp.sum(tail * sel, axis=1, keepdims=True)
         g = lax.dot_general(x, wg_ref[0], nt, preferred_element_type=FULL)
         u = lax.dot_general(x, wu_ref[0], nt, preferred_element_type=FULL)
-        da = jnp.dot(dy, wd_ref[0], preferred_element_type=FULL)
+        da = lax.dot_general(dy, wd_ref[0], nt, preferred_element_type=FULL)
         sigma = 1.0 / (1.0 + jnp.exp(-g))
         silu = g * sigma
         act = (silu * u).astype(LOW).astype(FULL)
@@ -375,8 +375,8 @@
         du_all[at, :] = (d_act * silu).astype(LOW)
         high = d_gate.astype(LOW).astype(FULL)
         dx_ref[0, at, MODEL_WIDTH:] = (high * high_sel + (d_gate - high) * rest_sel).astype(LOW)
-        y_ref[0, at, :] = lax.dot_general(
-            a_all[at, :], wd_ref[0], nt, preferred_element_type=FULL
+        y_ref[0, at, :] = jnp.dot(
+            a_all[at, :], wd_ref[0], preferred_element_type=FULL
         ).astype(LOW)
         dx_ref[0, at, :MODEL_WIDTH] = (
             jnp.dot(dg_all[at, :], wg_ref[0], preferred_element_type=FULL)
@@ -394,8 +394,8 @@
         dwu_ref[0, :, at] = lax.dot_general(
             du_all[...], x_ref[0, :, at], tn, preferred_element_type=FULL
         )
-        dwd_ref[0, at, :] = lax.dot_general(
-            dy_ref[0, :, at], a_all[...], tn, preferred_element_type=FULL
+        dwd_ref[0, :, at] = lax.dot_general(
+            a_all[...], dy_ref[0, :, at], tn, preferred_element_type=FULL
         )
         return carry
 
@@ -421,21 +421,21 @@
             spec(rows, MODEL_WIDTH),
             spec(hidden, MODEL_WIDTH),
             spec(hidden, MODEL_WIDTH),
-            spec(MODEL_WIDTH, hidden),
+            spec(hidden, MODEL_WIDTH),
         ],
         out_specs=[
             spec(rows, MODEL_WIDTH),
             spec(rows, width),
             spec(hidden, MODEL_WIDTH),
             spec(hidden, MODEL_WIDTH),
-            spec(MODEL_WIDTH, hidden),
+            spec(hidden, MODEL_WIDTH),
         ],
         out_shape=[
             out(rows, MODEL_WIDTH),
             out(rows, width),
             out(hidden, MODEL_WIDTH, dtype=FULL),
             out(hidden, MODEL_WIDTH, dtype=FULL),
-            out(MODEL_WIDTH, hidden, dtype=FULL),
+            out(hidden, MODEL_WIDTH, dtype=FULL),
         ],
         scratch_shapes=[pltpu.VMEM((rows, hidden), LOW)] * 3,
         compiler_params=pltpu.CompilerParams(vmem_limit_bytes=VMEM_LIMIT),
@@ -448,9 +448,9 @@
 
 
 def combine_home_kernel(
-    planes, slots, place_ref, v_ref, out_ref,
-    hot, load, mine, away, c_in, x_in, y_in, x_half, y_half, u_in, d_in,
-    in_sem, c_send, c_recv, x_send, x_recv, y_send, y_recv, z_send, z_recv,
+    planes, slots, place_ref, v_ref, m_ref, out_ref, mix_ref,
+    hot, load, load_m, stage, mine, away, c_in, x_in, y_in, x_half, y_half, u_in, d_in,
+    in_sem, m_sem, stage_sem, c_send, c_recv, x_send, x_recv, y_send, y_recv, z_send, z_recv,
 ):
     e, core, flip_x, flip_y, diagonal = neighbours()
     s = lax.axis_index("shard")
@@ -463,6 +463,40 @@
     def fetch(q, sp):
         rows = pl.ds(pl.multiple_of((q * planes + sp) * slots, 16), slots)
         return pltpu.make_async_copy(v_ref.at[:, rows, :], load.at[q], in_sem.at[q])
+
+    def fetch_mix(q, sp):
+        rows = pl.ds(pl.multiple_of((q * planes + sp) * slots, 16), slots)
+        return pltpu.make_async_copy(m_ref.at[:, rows, :], load_m.at[q % 2], m_sem.at[q % 2])
+
+    def store_mix(q, sp):
+        return pltpu.make_async_copy(
+            stage.at[q % 2], mix_ref.at[q, :, sp], stage_sem.at[q % 2]
+        )
+
+    def mix(sp):
+        for q in range(2):
+            fetch_mix(q, sp).start()
+        for q in range(4):
+            one_hot_pair(place_ref, q * planes + sp, hot, slots)
+            fetch_mix(q, sp).wait()
+            if q >= 2:
+                store_mix(q - 2, sp).wait()
+
+            def tile(t, inner, q=q):
+                at = pl.ds(pl.multiple_of(t * TILE, TILE), TILE)
+                rows = load_m[q % 2, :, :, at].reshape(EXP_DEV * slots, TILE)
+                got = lax.dot_general(
+                    hot[...], rows, (((0,), (0,)), ((), ())), preferred_element_type=FULL
+                ).astype(LOW)
+                stage[q % 2, :, :, at] = got.reshape(2, length, TILE)
+                return inner
+
+            lax.fori_loop(0, MODEL_WIDTH // TILE, tile, 0)
+            store_mix(q, sp).start()
+            if q < 2:
+                fetch_mix(q + 2, sp).start()
+        for q in (2, 3):
+            store_mix(q, sp).wait()
 
     def to_core(q, sp):
         return send(away.at[q, sp], c_in.at[q, sp], c_send.at[q, sp], c_recv.at[q, sp], (core, s))
@@ -588,7 +622,7 @@
     greet(planes)
 
     def step(i, carry):
-        for lag, job in ((0, work), (1, pairs), (2, sides), (3, line)):
+        for lag, job in ((0, work), (1, pairs), (2, sides), (3, line), (0, mix)):
             sp, there = plane_at(i - lag)
 
             @pl.when(there)
@@ -619,17 +653,23 @@
     lax.fori_loop(0, planes, drain, 0)
 
 
-def combine_home(place, v, length, planes, slots, identity):
+def combine_home(place, v, m, length, planes, slots, identity):
     width = v.shape[2]
     block = (planes, length, width)
+    pairs = place.shape[0] // planes
     return pl.pallas_call(
         functools.partial(combine_home_kernel, planes, slots),
-        out_shape=jax.ShapeDtypeStruct((length, width), FULL),
-        in_specs=[VM, ANY],
-        out_specs=VM,
+        out_shape=[
+            jax.ShapeDtypeStruct((length, width), FULL),
+            jax.ShapeDtypeStruct((pairs, 2, planes, length, MODEL_WIDTH), LOW),
+        ],
+        in_specs=[VM, ANY, ANY],
+        out_specs=[VM, ANY],
         scratch_shapes=[
             pltpu.VMEM((EXP_DEV * slots, 2 * length), LOW),
             pltpu.VMEM((4, EXP_DEV, slots, width), LOW),
+            pltpu.VMEM((2, EXP_DEV, slots, MODEL_WIDTH), LOW),
+            pltpu.VMEM((2, 2, length, MODEL_WIDTH), LOW),
             pltpu.VMEM((4,) + block, LOW),
             pltpu.VMEM((4,) + block, LOW),
             pltpu.VMEM((4,) + block, LOW),
@@ -640,6 +680,8 @@
             pltpu.VMEM(block, LOW),
             pltpu.VMEM(block, LOW),
             DMA((4,)),
+            DMA((2,)),
+            DMA((2,)),
             DMA((4, planes)),
             DMA((4, planes)),
             DMA((2, planes)),
@@ -652,7 +694,758 @@
         compiler_params=pltpu.CompilerParams(
             collective_id=identity, has_side_effects=True, vmem_limit_bytes=VMEM_LIMIT
         ),
-    )(place, v)
+    )(place, v, m)
+
+
+def greet_plane(planes, owners):
+    e, s = lax.axis_index("expert"), lax.axis_index("shard")
+    barrier = pltpu.get_barrier_semaphore()
+    for o in range(1, owners):
+        pl.semaphore_signal(
+            barrier, 1, device_id=(lax.rem(e + o, owners), s), device_id_type=MESH
+        )
+
+    @pl.when(s > 0)
+    def _():
+        pl.semaphore_signal(barrier, 1, device_id=(e, s - 1), device_id_type=MESH)
+
+    @pl.when(s < planes - 1)
+    def _():
+        pl.semaphore_signal(barrier, 1, device_id=(e, s + 1), device_id_type=MESH)
+
+    inner = (s > 0) & (s < planes - 1)
+
+    @pl.when(inner)
+    def _():
+        pl.semaphore_wait(barrier, owners + 1)
+
+    @pl.when(jnp.logical_not(inner))
+    def _():
+        pl.semaphore_wait(barrier, owners)
+
+
+def share_kernel(
+    planes, owners, head_ref, rest_ref, rows_ref, out_rows, out_head, out_rest,
+    acc_rows, acc_head, acc_rest, u_rows, u_head, u_rest, d_rows, d_head, d_rest,
+    load_sem, a_send, a_recv, z_send, z_recv, x_send, x_recv, y_send, y_recv, c_send, c_recv, own_sem,
+):
+    e, core, flip_x, flip_y, diagonal = neighbours()
+    s = lax.axis_index("shard")
+    lanes = owners // planes
+    share = rows_ref.shape[1] // owners
+    acc = (acc_rows, acc_head, acc_rest)
+    up_in, down_in = (u_rows, u_head, u_rest), (d_rows, d_head, d_rest)
+    outs = (out_rows, out_head, out_rest)
+    sources = (None, head_ref, rest_ref)
+
+    def load(k, sp):
+        return pltpu.make_async_copy(sources[k].at[sp], acc[k].at[sp], load_sem.at[k - 1, sp])
+
+    for k in (1, 2):
+        for sp in range(planes):
+            load(k, sp).start()
+
+    def part(sp):
+        return acc_rows.at[pl.ds(sp * lanes, lanes)]
+
+    def chunk(k, sp):
+        return part(sp) if k == 0 else acc[k].at[sp]
+
+    def spread(o):
+        other = lax.rem(e + o, owners)
+        at = pl.ds(pl.multiple_of(other * share, share), share)
+        return send(
+            rows_ref.at[:, at], acc_rows.at[e], a_send.at[o], a_recv.at[e], (other, s)
+        )
+
+    def arrived(block, sem):
+        send(block, block, sem, sem, (core, s)).wait_recv()
+
+    greet_plane(planes, owners)
+    for o in range(1, owners):
+        spread(o).start()
+    acc_rows[e] = rows_ref[:, pl.ds(pl.multiple_of(e * share, share), share)]
+
+    def add(target, other):
+        count = target.shape[1] // 128
+        for lead in range(target.shape[0]):
+
+            def one(r, carry, lead=lead):
+                at = pl.ds(pl.multiple_of(r * 128, 128), 128)
+                target[lead, at, :] = (
+                    target[lead, at, :].astype(FULL) + other[lead, at, :].astype(FULL)
+                ).astype(LOW)
+                return carry
+
+            lax.fori_loop(0, count, one, 0)
+
+    def up(k, sp):
+        return send(
+            chunk(k, sp), up_in[k].at[sp], z_send.at[k, 0, sp], z_recv.at[k, 0, sp], (e, s + 1)
+        )
+
+    def down(k, sp):
+        return send(
+            chunk(k, sp), down_in[k].at[sp], z_send.at[k, 1, sp], z_recv.at[k, 1, sp], (e, s - 1)
+        )
+
+    def line(k, sp):
+        if k == 0:
+            for lane in range(lanes):
+                source = sp * lanes + lane
+
+                @pl.when(source != e)
+                def _(source=source):
+                    arrived(acc_rows.at[source], a_recv.at[source])
+
+        else:
+            load(k, sp).wait()
+
+        @pl.when((sp >= s) & (s > 0))
+        def _():
+            arrived(up_in[k].at[sp], z_recv.at[k, 0, sp])
+            add(chunk(k, sp), up_in[k].at[sp])
+
+        @pl.when((sp <= s) & (s < planes - 1))
+        def _():
+            arrived(down_in[k].at[sp], z_recv.at[k, 1, sp])
+            add(chunk(k, sp), down_in[k].at[sp])
+
+        @pl.when(sp > s)
+        def _():
+            up(k, sp).start()
+
+        @pl.when(sp < s)
+        def _():
+            down(k, sp).start()
+
+    def others(k):
+        def one(i, carry):
+            back = 2 * planes - 2 - i
+            sp = s + (2 * (back % 2) - 1) * ((back + 1) // 2)
+
+            @pl.when((sp >= 0) & (sp < planes))
+            def _():
+                line(k, sp)
+
+            return carry
+
+        lax.fori_loop(0, 2 * planes - 2, one, 0)
+
+    def first(k):
+        block = chunk(k, s)
+        target = outs[k].at[e]
+        return [
+            send(block, target, x_send.at[k, 0], x_recv.at[k, 0], (flip_x, s)),
+            send(block, target, y_send.at[k, 0], y_recv.at[k, 0], (flip_y, s)),
+            send(block, target, c_send.at[k, 0], c_recv.at[k, 0], (core, s)),
+        ]
+
+    def half(k, lane, at):
+        count = outs[k].shape[1] // 2
+        return outs[k].at[lane, pl.ds(at * count, count)]
+
+    def from_x(k):
+        block, piece = outs[k].at[flip_x], half(k, flip_x, 0)
+        return [
+            send(piece, piece, y_send.at[k, 1], y_recv.at[k, 1], (flip_y, s)),
+            send(block, block, c_send.at[k, 1], c_recv.at[k, 1], (core, s)),
+        ]
+
+    def from_y(k):
+        block, piece = outs[k].at[flip_y], half(k, flip_y, 1)
+        return [
+            send(piece, piece, x_send.at[k, 1], x_recv.at[k, 1], (flip_x, s)),
+            send(block, block, c_send.at[k, 2], c_recv.at[k, 2], (core, s)),
+        ]
+
+    def from_diagonal(k):
+        block = outs[k].at[diagonal]
+        return send(block, block, c_send.at[k, 3], c_recv.at[k, 3], (core, s))
+
+    def keep(k):
+        return pltpu.make_async_copy(chunk(k, s), outs[k].at[e], own_sem.at[k])
+
+    def own(k):
+        line(k, s)
+        for copy in first(k):
+            copy.start()
+        keep(k).start()
+
+    def second(k):
+        arrived(outs[k].at[flip_x], x_recv.at[k, 0])
+        for copy in from_x(k):
+            copy.start()
+        arrived(outs[k].at[flip_y], y_recv.at[k, 0])
+        for copy in from_y(k):
+            copy.start()
+
+    def third(k):
+        arrived(half(k, diagonal, 0), y_recv.at[k, 1])
+        arrived(half(k, diagonal, 1), x_recv.at[k, 1])
+        from_diagonal(k).start()
+
+    a, b, c = 1, 0, 2
+    others(a)
+    others(b)
+    own(a)
+    others(c)
+    second(a)
+    own(b)
+    third(a)
+    own(c)
+    second(b)
+    third(b)
+    second(c)
+    third(c)
+    for k in range(3):
+        keep(k).wait()
+        for j, lane in enumerate(
+            (core, core + flip_x - e, core + flip_y - e, core + diagonal - e)
+        ):
+            arrived(outs[k].at[lane], c_recv.at[k, j])
+        for copy in first(k) + from_x(k) + from_y(k) + [from_diagonal(k)]:
+            copy.wait_send()
+    for o in range(1, owners):
+        spread(o).wait_send()
+
+    def drain(sp, carry):
+        for k in range(3):
+
+            @pl.when(sp > s)
+            def _(k=k):
+                up(k, sp).wait_send()
+
+            @pl.when(sp < s)
+            def _(k=k):
+                down(k, sp).wait_send()
+
+        return carry
+
+    lax.fori_loop(0, planes, drain, 0)
+
+
+def share_grads(head, rest, rows, planes, owners, identity):
+    share = rows.shape[1] // owners
+    shapes = (
+        (owners // planes, rows.shape[0], share),
+        head.shape[1:],
+        rest.shape[1:],
+    )
+    acc = [pltpu.VMEM((owners,) + shapes[0][1:], LOW)]
+    acc += [pltpu.VMEM((planes,) + shape, LOW) for shape in shapes[1:]]
+    landing = [pltpu.VMEM((planes,) + shape, LOW) for shape in shapes]
+    return pl.pallas_call(
+        functools.partial(share_kernel, planes, owners),
+        out_shape=[jax.ShapeDtypeStruct((owners,) + shape, LOW) for shape in shapes],
+        in_specs=[ANY, ANY, VM],
+        out_specs=[ANY, ANY, ANY],
+        scratch_shapes=acc
+        + landing
+        + landing
+        + [
+            DMA((2, planes)),
+            DMA((owners,)),
+            DMA((owners,)),
+            DMA((3, 2, planes)),
+            DMA((3, 2, planes)),
+            DMA((3, 2)),
+            DMA((3, 2)),
+            DMA((3, 2)),
+            DMA((3, 2)),
+            DMA((3, 4)),
+            DMA((3, 4)),
+            DMA((3,)),
+        ],
+        compiler_params=pltpu.CompilerParams(
+            collective_id=identity, has_side_effects=True, vmem_limit_bytes=VMEM_LIMIT
+        ),
+    )(head, rest, rows)
+
+
+def finish_kernel(owners, rows_ref, head_ref, kv_ref, tail_ref, out_rows, out_qkv, out_tail):
+    i = pl.program_id(0)
+
+    @pl.when(i < owners)
+    def _():
+        out_rows[...] = rows_ref[0].astype(FULL)
+        out_qkv[...] = head_ref[0].astype(FULL)
+
+    @pl.when(i >= owners)
+    def _():
+        each = owners // KEY_VALUE_HEADS
+        for h in range(KEY_VALUE_HEADS):
+            total = kv_ref[h * each].astype(FULL)
+            for j in range(1, each):
+                total = total + kv_ref[h * each + j].astype(FULL)
+            out_qkv[:, h * HEAD_SIZE : (h + 1) * HEAD_SIZE] = total
+
+    @pl.when(i == 0)
+    def _():
+        total = tail_ref[0].astype(FULL)
+        for lane in range(1, owners):
+            total = total + tail_ref[lane].astype(FULL)
+        out_tail[...] = total
+
+
+def finish_grads(rows, head, rest, owners):
+    rows = rows.reshape(owners, -1, rows.shape[-1])
+    head = head.reshape(owners, -1, head.shape[-1])
+    rest = rest.reshape(owners, -1, rest.shape[-1])
+    count, share = rows.shape[1:]
+    height, wide = head.shape[1:]
+    last = owners - 1
+    return pl.pallas_call(
+        functools.partial(finish_kernel, owners),
+        grid=(owners + 2,),
+        in_specs=[
+            pl.BlockSpec((1, count, share), lambda i: (jnp.minimum(i, last), 0, 0)),
+            pl.BlockSpec((1, height, wide), lambda i: (jnp.minimum(i, last), 0, 0)),
+            pl.BlockSpec((owners, height, HEAD_SIZE), lambda i: (0, 0, i // (owners + 1))),
+            pl.BlockSpec((owners, height, TAIL), lambda i: (0, 0, 2)),
+        ],
+        out_specs=[
+            pl.BlockSpec((count, share), lambda i: (0, jnp.minimum(i, last))),
+            pl.BlockSpec((height, wide), lambda i: (0, i)),
+            pl.BlockSpec((height, TAIL), lambda i: (0, 0)),
+        ],
+        out_shape=[
+            jax.ShapeDtypeStruct((count, owners * share), FULL),
+            jax.ShapeDtypeStruct((height, (owners + 2) * wide), FULL),
+            jax.ShapeDtypeStruct((height, TAIL), FULL),
+        ],
+        compiler_params=pltpu.CompilerParams(vmem_limit_bytes=VMEM_LIMIT),
+    )(rows, head, rest, rest)
+
+
+def gather_steps(at, cut, source, x_send, x_recv, y_send, y_recv, c_send, c_recv):
+    e, core, flip_x, flip_y, diagonal = neighbours()
+    s = lax.axis_index("shard")
+
+    def arrived(block, sem):
+        send(block, block, sem, sem, (core, s)).wait_recv()
+
+    def first():
+        return [
+            send(source, at(e), x_send(0), x_recv(0), (flip_x, s)),
+            send(source, at(e), y_send(0), y_recv(0), (flip_y, s)),
+            send(source, at(e), c_send(0), c_recv(0), (core, s)),
+        ]
+
+    def from_x():
+        return [
+            send(cut(flip_x, 0), cut(flip_x, 0), y_send(1), y_recv(1), (flip_y, s)),
+            send(at(flip_x), at(flip_x), c_send(1), c_recv(1), (core, s)),
+        ]
+
+    def from_y():
+        return [
+            send(cut(flip_y, 1), cut(flip_y, 1), x_send(1), x_recv(1), (flip_x, s)),
+            send(at(flip_y), at(flip_y), c_send(2), c_recv(2), (core, s)),
+        ]
+
+    def from_diagonal():
+        return [send(at(diagonal), at(diagonal), c_send(3), c_recv(3), (core, s))]
+
+    def begin():
+        for copy in first():
+            copy.start()
+
+    def second():
+        arrived(at(flip_x), x_recv(0))
+        for copy in from_x():
+            copy.start()
+        arrived(at(flip_y), y_recv(0))
+        for copy in from_y():
+            copy.start()
+
+    def third():
+        arrived(cut(diagonal, 0), y_recv(1))
+        arrived(cut(diagonal, 1), x_recv(1))
+        for copy in from_diagonal():
+            copy.start()
+
+    def last():
+        for k, lane in enumerate((core, core + flip_x - e, core + flip_y - e, core + diagonal - e)):
+            arrived(at(lane), c_recv(k))
+
+    def sent():
+        for copy in first() + from_x() + from_y() + from_diagonal():
+            copy.wait_send()
+
+    return begin, second, third, last, sent
+
+
+def start_kernel(
+    planes, owners, w_ref, tok_ref, out_ref, d_ref, w_all, tok_all, w_out_mine, d_all,
+    o_rows, keep_sem, w_send, w_recv, o_send, o_recv, z_send, z_recv,
+    tx_send, tx_recv, ty_send, ty_recv, tc_send, tc_recv,
+    dx_send, dx_recv, dy_send, dy_recv, dc_send, dc_recv,
+):
+    e, core, _, _, _ = neighbours()
+    s = lax.axis_index("shard")
+    lanes = owners // planes
+    home = e // lanes
+    length = tok_ref.shape[0]
+    half = length // 2
+    count = w_out_mine.shape[0]
+    pieces = 4
+    out_part = count // pieces
+
+    def arrived(block, sem):
+        send(block, block, sem, sem, (core, s)).wait_recv()
+
+    def w_copy(sp, way):
+        block = w_all.at[sp]
+        return send(block, block, w_send.at[way, sp], w_recv.at[sp], (e, s + 1 - 2 * way))
+
+    def d_copy(sp, way):
+        block = d_all.at[e, sp]
+        return send(block, block, z_send.at[way, sp], z_recv.at[sp], (e, s + 1 - 2 * way))
+
+    def o_copy(k, way):
+        block = w_out_mine.at[pl.ds(k * out_part, out_part)]
+        return send(block, block, o_send.at[way, k], o_recv.at[k], (e, s + 1 - 2 * way))
+
+    def tokens():
+        return gather_steps(
+            lambda lane: tok_all.at[lane],
+            lambda lane, k: tok_all.at[lane, pl.ds(k * half, half)],
+            tok_ref,
+            lambda k: tx_send.at[k],
+            lambda k: tx_recv.at[k],
+            lambda k: ty_send.at[k],
+            lambda k: ty_recv.at[k],
+            lambda k: tc_send.at[k],
+            lambda k: tc_recv.at[k],
+        )
+
+    def d_rows(sp):
+        return gather_steps(
+            lambda lane: d_all.at[lane, sp],
+            lambda lane, k: d_all.at[lane, sp, pl.ds(k * half, half)],
+            d_all.at[e, sp],
+            lambda k: dx_send.at[k, sp],
+            lambda k: dx_recv.at[k, sp],
+            lambda k: dy_send.at[k, sp],
+            lambda k: dy_recv.at[k, sp],
+            lambda k: dc_send.at[k, sp],
+            lambda k: dc_recv.at[k, sp],
+        )
+
+    keep_w = pltpu.make_async_copy(w_ref, w_all.at[s], keep_sem.at[0])
+    keep_t = pltpu.make_async_copy(tok_ref, tok_all.at[e], keep_sem.at[1])
+    keep_d = pltpu.make_async_copy(d_ref, d_all.at[e, s], keep_sem.at[2])
+    rows = pl.ds(pl.multiple_of((e - home * lanes) * count, 16), count)
+    load_o = pltpu.make_async_copy(out_ref.at[rows], o_rows, keep_sem.at[3])
+    keep_o = pltpu.make_async_copy(o_rows, w_out_mine, keep_sem.at[3])
+    keep_w.start()
+    keep_t.start()
+    keep_d.start()
+
+    @pl.when(s == home)
+    def _():
+        load_o.start()
+
+    greet(planes)
+
+    def both_ways(copy, sp):
+        @pl.when((sp <= s) & (s < planes - 1))
+        def _():
+            copy(sp, 0).start()
+
+        @pl.when((sp >= s) & (s > 0))
+        def _():
+            copy(sp, 1).start()
+
+    tokens()[0]()
+    keep_w.wait()
+    both_ways(w_copy, s)
+    keep_d.wait()
+    both_ways(d_copy, s)
+    d_rows(s)[0]()
+
+    def out_step(k):
+        @pl.when(s != home)
+        def _():
+            arrived(w_out_mine.at[pl.ds(k * out_part, out_part)], o_recv.at[k])
+
+        @pl.when((s >= home) & (s < planes - 1))
+        def _():
+            o_copy(k, 0).start()
+
+        @pl.when((s <= home) & (s > 0))
+        def _():
+            o_copy(k, 1).start()
+
+    @pl.when(s == home)
+    def _():
+        load_o.wait()
+        keep_o.start()
+        keep_o.wait()
+        for k in range(pieces):
+            out_step(k)
+
+    def plane_at(i):
+        sp = s + (2 * (i % 2) - 1) * ((i + 1) // 2)
+        return sp, (sp >= 0) & (sp < planes) & (i >= 0) & (i <= 2 * planes - 2)
+
+    def step(i, carry):
+        sp, there = plane_at(i)
+
+        @pl.when(there & (i > 0))
+        def _():
+            arrived(w_all.at[sp], w_recv.at[sp])
+            both_ways(w_copy, sp)
+            arrived(d_all.at[e, sp], z_recv.at[sp])
+            both_ways(d_copy, sp)
+            d_rows(sp)[0]()
+
+        @pl.when(i == 1)
+        def _():
+            tokens()[1]()
+
+        @pl.when(i == 2)
+        def _():
+            tokens()[2]()
+
+        @pl.when((i > 0) & ((2 * (s - home) == i) | (2 * (home - s) == i)))
+        def _():
+            for k in range(pieces):
+                out_step(k)
+
+        for lag in (1, 2):
+            sp, there = plane_at(i - lag)
+
+            @pl.when(there)
+            def _(sp=sp, lag=lag):
+                d_rows(sp)[lag]()
+
+        return carry
+
+    lax.fori_loop(0, 2 * planes + 1, step, 0)
+    tokens()[3]()
+    tokens()[4]()
+    keep_t.wait()
+
+    def finish(copy, sp):
+        @pl.when((sp <= s) & (s < planes - 1))
+        def _():
+            copy(sp, 0).wait_send()
+
+        @pl.when((sp >= s) & (s > 0))
+        def _():
+            copy(sp, 1).wait_send()
+
+    def drain(sp, carry):
+        d_rows(sp)[3]()
+        d_rows(sp)[4]()
+        finish(w_copy, sp)
+        finish(d_copy, sp)
+        return carry
+
+    lax.fori_loop(0, planes, drain, 0)
+    for k in range(pieces):
+
+        @pl.when((s >= home) & (s < planes - 1))
+        def _(k=k):
+            o_copy(k, 0).wait_send()
+
+        @pl.when((s <= home) & (s > 0))
+        def _(k=k):
+            o_copy(k, 1).wait_send()
+
+
+def start_gather(w, tokens, w_out, d_rows, planes, owners, identity):
+    def out(*shape):
+        return jax.ShapeDtypeStruct(shape, LOW)
+
+    count = w_out.shape[0] * planes // owners
+    return pl.pallas_call(
+        functools.partial(start_kernel, planes, owners),
+        out_shape=[
+            out(planes, *w.shape),
+            out(owners, *tokens.shape),
+            out(count, w_out.shape[1]),
+            out(owners, planes, *d_rows.shape),
+        ],
+        in_specs=[VM, VM, ANY, VM],
+        out_specs=[ANY] * 4,
+        scratch_shapes=[
+            pltpu.VMEM((count, w_out.shape[1]), LOW),
+            DMA((4,)),
+            DMA((2, planes)),
+            DMA((planes,)),
+            DMA((2, 4)),
+            DMA((4,)),
+            DMA((2, planes)),
+            DMA((planes,)),
+            DMA((2,)),
+            DMA((2,)),
+            DMA((2,)),
+            DMA((2,)),
+            DMA((4,)),
+            DMA((4,)),
+            DMA((2, planes)),
+            DMA((2, planes)),
+            DMA((2, planes)),
+            DMA((2, planes)),
+            DMA((4, planes)),
+            DMA((4, planes)),
+        ],
+        compiler_params=pltpu.CompilerParams(collective_id=identity, has_side_effects=True),
+    )(w, tokens, w_out, d_rows)
+
+
+def greet_near():
+    e, core, flip_x, flip_y, _ = neighbours()
+    s = lax.axis_index("shard")
+    barrier = pltpu.get_barrier_semaphore()
+    for other in (core, flip_x, flip_y):
+        pl.semaphore_signal(barrier, 1, device_id=(other, s), device_id_type=MESH)
+    pl.semaphore_wait(barrier, 3)
+
+
+def plane_gather_kernel(rows_ref, all_ref, keep_sem, xs, xr, ys, yr, cs, cr):
+    e = lax.axis_index("expert")
+    half = rows_ref.shape[0] // 2
+    keep = pltpu.make_async_copy(rows_ref, all_ref.at[e], keep_sem)
+    keep.start()
+    greet_near()
+    begin, second, third, last, sent = gather_steps(
+        lambda lane: all_ref.at[lane],
+        lambda lane, k: all_ref.at[lane, pl.ds(k * half, half)],
+        rows_ref,
+        lambda k: xs.at[k],
+        lambda k: xr.at[k],
+        lambda k: ys.at[k],
+        lambda k: yr.at[k],
+        lambda k: cs.at[k],
+        lambda k: cr.at[k],
+    )
+    begin()
+    second()
+    third()
+    last()
+    sent()
+    keep.wait()
+
+
+def plane_gather(rows, owners, identity):
+    return pl.pallas_call(
+        plane_gather_kernel,
+        out_shape=jax.ShapeDtypeStruct((owners,) + rows.shape, LOW),
+        in_specs=[VM],
+        out_specs=ANY,
+        scratch_shapes=[DMA(()), DMA((2,)), DMA((2,)), DMA((2,)), DMA((2,)), DMA((4,)), DMA((4,))],
+        compiler_params=pltpu.CompilerParams(collective_id=identity, has_side_effects=True),
+    )(rows)
+
+
+def project_home_kernel(
+    turned, rows_ref, w_ref, out_ref, mine, away, c_in, x_in, y_in, x_half, y_half,
+    cs, cr, xs, xr, ys, yr,
+):
+    e, core, flip_x, flip_y, diagonal = neighbours()
+    s = lax.axis_index("shard")
+    q_own, q_x, q_y, q_d = e // 2, flip_x // 2, flip_y // 2, diagonal // 2
+    parity = e % 2
+    half = out_ref.shape[0] // 2
+    low_half, high_half = pl.ds(0, half), pl.ds(half, half)
+    across = (((1,), (1 if turned else 0,)), ((), ()))
+
+    def arrived(block, sem):
+        send(block, block, sem, sem, (core, s)).wait_recv()
+
+    def add(target, *others):
+        total = target[...].astype(FULL)
+        for other in others:
+            total = total + other[...].astype(FULL)
+        target[...] = total.astype(LOW)
+
+    def to_core(q):
+        return send(away.at[q], c_in.at[q], cs.at[q], cr.at[q], (core, s))
+
+    def compute(q, lane, into):
+        rows = rows_ref[2 * q + lane]
+
+        def tile(t, carry):
+            at = pl.ds(pl.multiple_of(t * TILE, TILE), TILE)
+            w = w_ref[at, :] if turned else w_ref[:, at]
+            into[q, :, at] = lax.dot_general(
+                rows, w, across, preferred_element_type=FULL
+            ).astype(LOW)
+            return carry
+
+        lax.fori_loop(0, MODEL_WIDTH // TILE, tile, 0)
+
+    halves = [
+        send(mine.at[q_d, low_half], y_half, ys.at[0], yr.at[0], (flip_y, s)),
+        send(mine.at[q_d, high_half], x_half, xs.at[0], xr.at[0], (flip_x, s)),
+    ]
+    to_x = send(mine.at[q_x], x_in, xs.at[1], xr.at[1], (flip_x, s))
+    to_y = send(mine.at[q_y], y_in, ys.at[1], yr.at[1], (flip_y, s))
+    greet_near()
+    order = (q_d, q_x, q_y, q_own)
+    for q in order:
+        compute(q, 1 - parity, away)
+        to_core(q).start()
+    for q in order:
+        compute(q, parity, mine)
+
+    def joined(q):
+        arrived(c_in.at[q], cr.at[q])
+        add(mine.at[q], c_in.at[q])
+
+    joined(q_d)
+    for copy in halves:
+        copy.start()
+    joined(q_x)
+    joined(q_y)
+    arrived(y_half, yr.at[0])
+    add(mine.at[q_x, low_half], y_half)
+    to_x.start()
+    arrived(x_half, xr.at[0])
+    add(mine.at[q_y, high_half], x_half)
+    to_y.start()
+    joined(q_own)
+    arrived(x_in, xr.at[1])
+    arrived(y_in, yr.at[1])
+    out_ref[...] = mine[q_own].astype(FULL) + x_in[...].astype(FULL) + y_in[...].astype(FULL)
+    for q in order:
+        to_core(q).wait_send()
+    for copy in halves + [to_x, to_y]:
+        copy.wait_send()
+
+
+def project_home(rows, w, turned, identity):
+    length = rows.shape[1]
+    block = (length, MODEL_WIDTH)
+    part = (length // 2, MODEL_WIDTH)
+    return pl.pallas_call(
+        functools.partial(project_home_kernel, turned),
+        out_shape=jax.ShapeDtypeStruct(block, FULL),
+        in_specs=[VM, VM],
+        out_specs=VM,
+        scratch_shapes=[
+            pltpu.VMEM((4,) + block, LOW),
+            pltpu.VMEM((4,) + block, LOW),
+            pltpu.VMEM((4,) + block, LOW),
+            pltpu.VMEM(block, LOW),
+            pltpu.VMEM(block, LOW),
+            pltpu.VMEM(part, LOW),
+            pltpu.VMEM(part, LOW),
+            DMA((4,)),
+            DMA((4,)),
+            DMA((2,)),
+            DMA((2,)),
+            DMA((2,)),
+            DMA((2,)),
+        ],
+        compiler_params=pltpu.CompilerParams(
+            collective_id=identity, has_side_effects=True, vmem_limit_bytes=VMEM_LIMIT
+        ),
+    )(rows, w)
 
 
 def per_device(
@@ -685,6 +1478,8 @@
     both = ("expert", "shard")
     rows_in = qkv_weight.shape[0]
 
+    resident_pass = blocks * length * (MODEL_WIDTH + 2 * experts_all) * 2 <= RESIDENT
+
     kv_head = me * KEY_VALUE_HEADS // owners
     k_at = QUERY_HEADS * HEAD_SIZE + kv_head * HEAD_SIZE
     v_at = k_at + KEY_VALUE_HEADS * HEAD_SIZE
@@ -707,7 +1502,35 @@
         ],
         axis=1,
     )
-    gathered = lax.all_gather(mine, "shard", axis=0, tiled=True)
+    segment_row = segments[0]
+    token_tail = columns(
+        [segment_row[:, None], positions_of(segment_row)[:, None]], length
+    )
+    token_rows = jnp.concatenate([tokens, token_tail], axis=1)
+    d_rows = jnp.concatenate([d_out, columns([routes], length)], axis=1)
+    if resident_pass:
+        gathered, plane_rows, w_mine, d_all = start_gather(
+            mine, token_rows, w_out, d_rows, planes, owners, 5
+        )
+        gathered = gathered.reshape(MODEL_WIDTH, -1)
+        d_all = d_all.reshape(blocks, length, -1)
+    else:
+        gathered = lax.all_gather(mine, "shard", axis=0, tiled=True)
+        plane_rows = lax.all_gather(token_rows, "expert", axis=0, tiled=False)
+        d_all = lax.all_gather(d_rows, both, axis=0, tiled=False)
+        out_rows = w_out.shape[0]
+        first = me * query_cols
+        offset = first - plane * out_rows
+        if out_rows >= query_cols:
+            held = (offset >= 0) & (offset < out_rows)
+            piece = lax.dynamic_slice_in_dim(w_out, jnp.where(held, offset, 0), query_cols, 0)
+            w_mine = lax.psum(jnp.where(held, piece, 0).astype(LOW), "shard")
+        else:
+            parts = query_cols // out_rows
+            at = plane - me * parts
+            held = (at >= 0) & (at < parts)
+            spread = jnp.where(held & (jnp.arange(parts) == at)[:, None, None], w_out[None], 0)
+            w_mine = lax.psum(spread.astype(LOW), "shard").reshape(query_cols, MODEL_WIDTH)
     qkv_cols = query_cols + 2 * HEAD_SIZE
     wqkv = gathered[:, :qkv_cols]
     router_full = gathered[:, qkv_cols : qkv_cols + experts_all]
@@ -717,36 +1540,9 @@
     by_plane = gain_cols.reshape(planes, rows_in, -1)[:, :per]
     gain_query = by_plane[:, :, 2].reshape(-1)
     gain_key = by_plane[:, :, 3].reshape(-1)
-
-    segment_row = segments[0]
-    token_tail = columns(
-        [segment_row[:, None], positions_of(segment_row)[:, None]], length
-    )
-    plane_rows = lax.all_gather(
-        jnp.concatenate([tokens, token_tail], axis=1), "expert", axis=0, tiled=False
-    )
     plane_tokens = plane_rows[:, :, :MODEL_WIDTH].astype(FULL)
     plane_segments = plane_rows[:, :, MODEL_WIDTH]
     plane_places = plane_rows[:, :, MODEL_WIDTH + 1].astype(FULL)
-
-    out_rows = w_out.shape[0]
-    first = me * query_cols
-    offset = first - plane * out_rows
-    if out_rows >= query_cols:
-        held = (offset >= 0) & (offset < out_rows)
-        piece = lax.dynamic_slice_in_dim(w_out, jnp.where(held, offset, 0), query_cols, 0)
-        w_mine = lax.psum(jnp.where(held, piece, 0).astype(LOW), "shard")
-    else:
-        parts = query_cols // out_rows
-        at = plane - me * parts
-        held = (at >= 0) & (at < parts)
-        spread = jnp.where(held & (jnp.arange(parts) == at)[:, None, None], w_out[None], 0)
-        w_mine = lax.psum(spread.astype(LOW), "shard").reshape(query_cols, MODEL_WIDTH)
-
-    d_tail = columns([routes], length)
-    d_all = lax.all_gather(
-        jnp.concatenate([d_out, d_tail], axis=1), both, axis=0, tiled=False
-    )
 
     unit_plane, inverse_plane = unit_norm(plane_tokens)
     h1 = (unit_plane * gain_one).astype(LOW)
@@ -775,23 +1571,11 @@
     probs_low = probs.astype(LOW)
     mixed = dot("bhqk,bkd->bqhd", probs_low, value).astype(LOW)
     mixed = mixed.reshape(owners, length, query_cols)
-    partial = dot("bqf,fd->bqd", mixed, w_mine).astype(LOW)
-    branch = lax.psum_scatter(partial, "expert", scatter_dimension=0, tiled=False)
-
-    middle = tokens.astype(FULL) + branch.astype(FULL)
-    unit_two, inverse_two = unit_norm(middle)
-    h2 = (unit_two * gain_two).astype(LOW)
-    logits = dot("nd,de->ne", h2, router_full)
-    chance = jax.nn.softmax(logits, axis=-1)
-    named = jnp.sum(
-        (routes[:, :, None] == jnp.arange(experts_all, dtype=jnp.int32)).astype(FULL), axis=1
-    )
-    chosen_sum = jnp.sum(named * chance, axis=1, keepdims=True)
-    gates = named * chance / chosen_sum
-    gates_high = gates.astype(LOW)
-    gates_rest = (gates - gates_high.astype(FULL)).astype(LOW)
-    h_rows = jnp.concatenate([h2, gates_high, gates_rest], axis=1)
-    resident_pass = blocks * length * h_rows.shape[1] * 2 <= RESIDENT
+    if resident_pass:
+        branch = project_home(mixed, w_mine, False, 6)
+    else:
+        partial = dot("bqf,fd->bqd", mixed, w_mine).astype(LOW)
+        branch = lax.psum_scatter(partial, "expert", scatter_dimension=0, tiled=False)
 
     route_all = d_all[:, :, MODEL_WIDTH : MODEL_WIDTH + TOPK].astype(FULL)
     own_experts = (me * EXP_DEV + jnp.arange(EXP_DEV, dtype=jnp.int32)).astype(FULL)
@@ -809,12 +1593,32 @@
         own = (me * EXP_DEV + jnp.arange(EXP_DEV, dtype=jnp.int32))[:, None] == lanes
         sel = jnp.broadcast_to(own.astype(FULL)[:, None, :], (EXP_DEV, 8, 2 * experts_all))
         slots = 2 * capacity
+
+    middle = tokens.astype(FULL) + branch.astype(FULL)
+    unit_two, inverse_two = unit_norm(middle)
+    h2 = (unit_two * gain_two).astype(LOW)
+    logits = dot("nd,de->ne", h2, router_full)
+    chance = jax.nn.softmax(logits, axis=-1)
+    named = jnp.sum(
+        (routes[:, :, None] == jnp.arange(experts_all, dtype=jnp.int32)).astype(FULL), axis=1
+    )
+    chosen_sum = jnp.sum(named * chance, axis=1, keepdims=True)
+    gates = named * chance / chosen_sum
+    gates_high = gates.astype(LOW)
+    gates_rest = (gates - gates_high.astype(FULL)).astype(LOW)
+    h_rows = jnp.concatenate([h2, gates_high, gates_rest], axis=1)
+
+    if resident_pass:
         x, dy = gather_dispatch(
             h_rows, d_all.reshape(owners, planes, length, -1), place, planes, slots, 1
         )
-        y, dx, d_gate, d_up, d_down = expert_pass(sel, x, dy, w_gate, w_up, w_down)
-        d_home = combine_home(place, dx, length, planes, slots, 2)
-        mixture = combine_home(place, y, length, planes, slots, 3)
+        y, dx, d_gate, d_up, d_down = expert_pass(
+            sel, x, dy, w_gate, w_up, w_down.swapaxes(1, 2)
+        )
+        d_down = d_down.swapaxes(1, 2)
+        d_home, mixture = combine_home(place, dx, y, length, planes, slots, 2)
+        mixture = mixture.reshape(owners, planes, length, MODEL_WIDTH)
+        mixture = lax.psum_scatter(mixture, "expert", scatter_dimension=0, tiled=False)
     else:
         dispatch = (place[:, :, None, :] == slot_ids[:, None]).astype(LOW)
 
@@ -891,8 +1695,6 @@
 
         d_home = home(d_h_wide)
         mixture = home(jnp.concatenate(mixes, axis=0))
-    result = (middle + mixture.astype(FULL)).astype(LOW)
-
     upstream = d_out.astype(FULL)
     d_gates = d_home[:, MODEL_WIDTH:].astype(FULL)
     d_gates = d_gates[:, :experts_all] + d_gates[:, experts_all:]
@@ -904,7 +1706,10 @@
     d_middle = upstream + norm_back(d_h2, unit_two, inverse_two, gain_two)
     d_router = dot("nd,ne->de", h2, d_logits)
 
-    d_branch = lax.all_gather(d_middle.astype(LOW), "expert", axis=0, tiled=False)
+    if resident_pass:
+        d_branch = plane_gather(d_middle.astype(LOW), owners, 7)
+    else:
+        d_branch = lax.all_gather(d_middle.astype(LOW), "expert", axis=0, tiled=False)
     d_w_out = dot("bqf,bqd->fd", mixed, d_branch).astype(LOW)
     d_mixed = dot("bqd,fd->bqf", d_branch, w_mine).astype(LOW)
     d_mixed = d_mixed.reshape(owners, length, heads, HEAD_SIZE)
@@ -923,12 +1728,19 @@
     d_projected = jnp.concatenate(
         [d_query.reshape(owners, length, query_cols), d_key, d_value], axis=2
     ).astype(LOW)
-    d_h1_part = dot("bqf,df->bqd", d_projected, wqkv).astype(LOW)
-    d_h1 = lax.psum_scatter(d_h1_part, "expert", scatter_dimension=0, tiled=False).astype(FULL)
+    if resident_pass:
+        d_h1 = project_home(d_projected, wqkv, True, 8)
+        mixture, d_h1 = lax.optimization_barrier((mixture, d_h1))
+        mixture = lax.psum_scatter(mixture, "shard", scatter_dimension=0, tiled=False)
+    else:
+        d_h1 = dot("bqf,df->bqd", d_projected, wqkv).astype(LOW)
+        d_h1 = lax.psum_scatter(d_h1, "expert", scatter_dimension=0, tiled=False).astype(FULL)
     resident = tokens.astype(FULL)
     unit_one, inverse_one = unit_norm(resident)
     d_gain_one = jnp.sum(d_h1 * unit_one, axis=0)
     d_tokens = (d_middle + norm_back(d_h1, unit_one, inverse_one, gain_one)).astype(LOW)
+
+    result = (middle + mixture.astype(FULL)).astype(LOW)
 
     d_wqkv = dot("bqd,bqf->df", h1, d_projected).astype(LOW)
 
@@ -946,24 +1758,35 @@
         ],
         MODEL_WIDTH,
     )
-    d_pack = lax.psum_scatter(
-        jnp.concatenate([d_wqkv, d_tail], axis=1), "shard", scatter_dimension=0, tiled=True
-    )
-    d_pack = lax.all_gather(d_pack, "expert", axis=0, tiled=False).astype(FULL)
-    d_q_cols = d_pack[:, :, :query_cols].transpose(1, 0, 2).reshape(rows_in, -1)
-    d_kv = d_pack[:, :, query_cols:qkv_cols]
-    d_kv = jnp.sum(d_kv.reshape(KEY_VALUE_HEADS, -1, rows_in, 2, HEAD_SIZE), axis=1)
-    d_kv = d_kv.transpose(1, 2, 0, 3).reshape(rows_in, -1)
-    d_qkv_weight = jnp.concatenate([d_q_cols, d_kv], axis=1)
-    d_rest = jnp.sum(d_pack[:, :, qkv_cols:], axis=0)
+    d_pack = jnp.concatenate([d_wqkv, d_tail], axis=1)
+    if resident_pass:
+        shape = (planes, 2, rows_in // 2)
+        parts = share_grads(
+            d_pack[:, :query_cols].reshape(shape + (query_cols,)),
+            d_pack[:, query_cols:].reshape(shape + (-1,)),
+            d_w_out,
+            planes,
+            owners,
+            4,
+        )
+        d_w_out, d_qkv_weight, d_rest = finish_grads(*parts, owners)
+    else:
+        d_pack = lax.psum_scatter(d_pack, "shard", scatter_dimension=0, tiled=True)
+        d_pack = lax.all_gather(d_pack, "expert", axis=0, tiled=False).astype(FULL)
+        d_q_cols = d_pack[:, :, :query_cols].transpose(1, 0, 2).reshape(rows_in, -1)
+        d_kv = d_pack[:, :, query_cols:qkv_cols]
+        d_kv = jnp.sum(d_kv.reshape(KEY_VALUE_HEADS, -1, rows_in, 2, HEAD_SIZE), axis=1)
+        d_kv = d_kv.transpose(1, 2, 0, 3).reshape(rows_in, -1)
+        d_qkv_weight = jnp.concatenate([d_q_cols, d_kv], axis=1)
+        d_rest = jnp.sum(d_pack[:, :, qkv_cols:], axis=0)
+
+        d_w_out = d_w_out.reshape(query_cols, owners, -1)
+        d_w_out = lax.all_to_all(d_w_out, "expert", split_axis=1, concat_axis=0, tiled=False)
+        d_w_out = d_w_out.reshape(QUERY_HEADS * HEAD_SIZE, -1)
+        d_w_out = lax.psum_scatter(d_w_out, "shard", scatter_dimension=0, tiled=True)
+        d_w_out = lax.all_gather(d_w_out, "expert", axis=1, tiled=True).astype(FULL)
     d_router_out = d_rest[:, :experts_all]
     d_gain_out = d_rest[:, experts_all:]
-
-    d_w_out = d_w_out.reshape(query_cols, owners, -1)
-    d_w_out = lax.all_to_all(d_w_out, "expert", split_axis=1, concat_axis=0, tiled=False)
-    d_w_out = d_w_out.reshape(QUERY_HEADS * HEAD_SIZE, -1)
-    d_w_out = lax.psum_scatter(d_w_out, "shard", scatter_dimension=0, tiled=True)
-    d_w_out = lax.all_gather(d_w_out, "expert", axis=1, tiled=True).astype(FULL)
 
     return (
         result,

time: 1200 us -> 937 us (0.78)
  waiting for transfers between devices: 400 us -> 23.9 us
  Pallas kernels: 400 us -> 730 us
  local copies, waits for them, and re-layouts: 167 us -> 62.6 us
  other arithmetic: 98.3 us -> 47.5 us
  blocking collectives: 40.4 us -> 0 us
  matrix products: 54.9 us -> 39.1 us
    pallas_call x0 -> x6, Pallas kernels: none -> 448 us  [the longest x1 169 us: start_gather(): pl.pallas_call(functools.partial(start_kernel, planes, owners), out_shape...]
    all_gather x6 -> x0, waiting for transfers between devices: 211 us -> none  [the longest x1 70 us: per_device(): gathered = lax.all_gather(mine, 'shard', axis=0, tiled=True)]
    reduce_scatter x4 -> x2, waiting for transfers between devices: 160 us -> 23.9 us  [the longest x1 23.8 us: per_device(): lax.psum_scatter(mixture, 'expert', scatter_dimension=0, tiled=False)]
    pallas_call x2 -> x1, Pallas kernels: 229 us -> 115 us  [combine_home(): pl.pallas_call(functools.partial(combine_home_kernel, planes, slots), out...]
    unnamed x149 -> x169, local copies, waits for them, and re-layouts: 86.9 us -> 18.9 us
    all_to_all x1 -> x0, blocking collectives: 40.4 us -> none  [per_device(): lax.all_to_all(d_w_out, 'expert', split_axis=1, concat_axis=0, tiled=False)]
    psum x1 -> x0, waiting for transfers between devices: 29.4 us -> none  [per_device(): w_mine = lax.psum(jnp.where(held, piece, 0).astype(LOW), 'shard')]
    convert_element_type x4 -> x1, other arithmetic: 25 us -> 1.15 us  [per_device(): d_branch = plane_gather(d_middle.astype(LOW), owners, 7)]
  transfers between devices with their start and end apart: 11 -> 2, of which waited for: 9 -> 1; matrix products, arithmetic and copies ran while one was open for 12% -> 7% of each run, Pallas kernels for 11% -> 27%
where the time goes in v3:
time: 937 us; the launch traced here: 919 us
  Pallas kernels  730 us (78%)
  local copies, waits for them, and re-layouts  62.6 us (7%)
  other arithmetic  47.5 us (5%)
  matrix products  39.1 us (4%)
  waiting for transfers between devices  23.9 us (3%)
  between operations  15.4 us (2%)
    pallas_call x1, Pallas kernels, start_gather(): pl.pallas_call(functools.partial(start_kernel, planes, owners), out_shape...  169 us
    pallas_call x1, Pallas kernels, share_grads(): pl.pallas_call(functools.partial(share_kernel, planes, owners), out_shape...  156 us
    pallas_call x1, Pallas kernels, combine_home(): pl.pallas_call(functools.partial(combine_home_kernel, planes, slots), out...  115 us
    pallas_call x1, Pallas kernels, gather_dispatch(): pl.pallas_call(kernel, out_shape=[jax.ShapeDtypeStruct((EXP_DEV, total, w...  89.8 us
    pallas_call x2, Pallas kernels, project_home(): pl.pallas_call(functools.partial(project_home_kernel, turned), out_shape=...  85.1 us
    pallas_call x1, Pallas kernels, expert_pass(): pl.pallas_call(expert_kernel, grid=(EXP_DEV,), in_specs=[spec(*sel.shape[...  77.9 us
    dot_general x13, matrix products, dot(): return jnp.einsum(spec, left, right, preferred_element_type=FULL)  34.8 us
    reduce_scatter x1, waiting for transfers between devices, per_device(): lax.psum_scatter(mixture, 'expert', scatter_dimension=0, tiled=False)  23.8 us
  transfers between devices with their start and end apart: 2, of which 1 were waited for; matrix products, arithmetic and copies ran while one was open for 7% of the time, Pallas kernels for 27%

profile of v3, /device:TPU:0, one launch (start us, length us, event | category | flops | bytes accessed | tf_op | source)
XLA Modules:
  0.0 918.8 jit_solution(6355594105841427417)
XLA Ops:
  18.6 169.2 %shard_map.229 = (bf16[4,512,896]{2,1,0:T(8,128)(2,1)}, bf16[8,128,2176]{2,1,0:T(8,128)(2,1)}, bf16[512,2048]{1,0:T(8,128)(2,1)}, bf16[8,4,128,2176]{3,2,1,0:T(8,128)(2,1)}) custom-call(bf16[512,896]{1,0:T(8,128)(2,1)} %fusion.43.w_ref, bf16[128,2176]{1,0:T(8,128)(2,1)} %get-tuple-element.176.tok_ref, bf16[1024,2048]{1,0:T(8,128)(2,1)} %out_ref.1, ...), custom_call_target="tpu_custom_call" | custom-call | tf_op jit(solution)/shard_map/pallas_call | solution.py:1264
  187.8 3.2 fusion.1
  191.0 1.6 convert_reduce_fusion.1
  193.8 3.5 fusion.4
  197.5 2.1 fusion.91
  201.8 2.9 reshape.295
  204.7 2.8 multiply_reduce_fusion.1
  209.9 3.0 fusion.56
  214.0 2.1 subtract_convert_fusion
  216.1 4.3 fusion.92
  220.4 2.3 convolution_convert_fusion.1
  222.6 1.3 copy.271.rows_ref
  224.0 34.4 %shard_map.230 = f32[128,2048]{1,0:T(8,128)} custom-call(bf16[8,128,512]{2,1,0:T(8,128)(2,1)} %copy.271.rows_ref, bf16[512,2048]{1,0:T(8,128)(2,1)} %get-tuple-element.35.w_ref), custom_call_target="tpu_custom_call" | custom-call | tf_op jit(solution)/shard_map/pallas_call | solution.py:1425
  258.4 2.0 multiply_reduce_fusion.4
  261.4 1.9 fusion.93
  264.2 2.3 slice.152
  266.6 2.2 copy.278
  268.7 1.5 convert_element_type.223
  275.1 1.8 concatenate.51.x_ref
  277.0 1.6 add_select_fusion
  278.6 89.8 %shard_map.231 = (bf16[8,768,2176]{2,1,0:T(8,128)(2,1)}, bf16[8,768,2048]{2,1,0:T(8,128)(2,1)}) custom-call(bf16[128,2176]{1,0:T(8,128)(2,1)} %concatenate.51.x_ref, bf16[8,4,128,2176]{3,2,1,0:T(8,128)(2,1)} %get-tuple-element.36.d_ref, f32[16,8,256]{2,1,0:T(8,128)} %bitcast.156), custom_call_target="tpu_custom_call" | custom-call | tf_op jit(solution)/shard_map/pallas_call | solution.py:313
  369.2 77.9 %shard_map.232 = (bf16[8,768,2048]{2,1,0:T(8,128)(2,1)}, bf16[8,768,2176]{2,1,0:T(8,128)(2,1)}, f32[8,192,2048]{2,1,0:T(8,128)}, f32[8,192,2048]{2,1,0:T(8,128)}, f32[8,192,2048]{2,1,0:T(8,128)}) custom-call(f32[8,8,128]{2,1,0:T(8,128)} %broadcast_in_dim.38.sel_ref, bf16[8,768,2176]{2,1,0:T(8,128)(2,1)} %get-tuple-element.37.x_ref, ...), custom_call_target="tpu_custom_call" | custom-call | flops 43486543872 | bytes 167772160 | tf_op jit(solution)/shard_map/pallas_call | solution.py:415
  447.1 114.8 %shard_map.233 = (f32[128,2176]{1,0:T(8,128)}, bf16[4,2,4,128,2048]{4,3,2,1,0:T(8,128)(2,1)}) custom-call(f32[16,8,256]{2,1,0:T(8,128)} %bitcast.157, bf16[8,768,2176]{2,1,0:T(8,128)(2,1)} %get-tuple-element.39.v_ref, bf16[8,768,2048]{2,1,0:T(8,128)(2,1)} %get-tuple-element.40.m_ref), custom_call_target="tpu_custom_call" | custom-call | tf_op jit(solution)/shard_map/pallas_call | solution.py:660
  563.7 3.8 slice.142.w_ref
  568.0 2.2 multiply_reduce_fusion.2
  572.3 23.7 %shard_map.234 = bf16[8,128,2048]{2,1,0:T(8,128)(2,1)} custom-call(bf16[128,2048]{1,0:T(8,128)(2,1)} %fusion.88.rows_ref), custom_call_target="tpu_custom_call" | custom-call | tf_op jit(solution)/shard_map/pallas_call | solution.py:1335
  596.1 7.4 fusion.22
  603.5 2.6 copy.282
  606.1 3.3 fusion.13
  613.9 2.6 fusion.52
  617.6 2.2 mul.465
  619.8 1.9 mul.466
  621.6 3.1 mul.416.clone
  624.8 3.5 mul.439
  628.4 2.2 fusion.28
  630.6 2.2 fusion.59
  639.7 50.8 %shard_map.235 = f32[128,2048]{1,0:T(8,128)} custom-call(bf16[8,128,768]{2,1,0:T(8,128)(2,1)} %pad_maximum_fusion.1.rows_ref, bf16[2048,768]{1,0:T(8,128)(2,1)} %slice.142.w_ref), custom_call_target="tpu_custom_call" | custom-call | tf_op jit(solution)/shard_map/pallas_call | solution.py:1425
  690.5 23.8 %reduce-scatter.3.cloned.1.call-done = bf16[1,4,128,2048]{3,2,1,0:T(8,128)(2,1)} async-done(((bf16[8,4,128,2048]{3,2,1,0:T(8,128)(2,1)}), bf16[1,4,128,2048]{3,2,1,0:T(8,128)(2,1)}) %reduce-scatter.3.cloned.1.call-update) | async-done | bytes 2097168 | tf_op jit(solution)/shard_map/reduce_scatter | solution.py:1621
  716.4 6.2 bitcast_convert_fusion
  722.6 1.5 slice.159
  726.9 3.6 bitcast_convert_fusion.1.rows_ref
  731.4 2.5 fusion.21
  733.9 156.4 %shard_map.236 = (bf16[8,2,512,256]{3,2,1,0:T(8,128)(2,1)}, bf16[8,2,256,512]{3,2,1,0:T(8,128)(2,1)}, bf16[8,2,256,384]{3,2,1,0:T(8,128)(2,1)}) custom-call(bf16[4,2,256,512]{3,2,1,0:T(8,128)(2,1)} %bitcast.145, bf16[4,2,256,384]{3,2,1,0:T(8,128)(2,1)} %bitcast.146, bf16[512,2048]{1,0:T(8,128)(2,1)} %bitcast_convert_fusion.1.rows_ref), custom_call_target="tpu_custom_call" | custom-call | tf_op jit(solution)/shard_map/pallas_call | solution.py:938
  890.3 13.4 %shard_map.237 = (f32[1024,2048]{1,0:T(8,128)}, f32[512,5120]{1,0:T(8,128)}, f32[512,128]{1,0:T(8,128)}) custom-call(bf16[8,1024,256]{2,1,0:T(8,128)(2,1)} %bitcast.152, bf16[8,512,512]{2,1,0:T(8,128)(2,1)} %bitcast.153, bf16[8,512,384]{2,1,0:T(8,128)(2,1)} %bitcast.142, bf16[8,512,384]{2,1,0:T(8,128)(2,1)} %bitcast.143), custom_call_target="tpu_custom_call" | custom-call | tf_op jit(solution)/shard_map/pallas_call | solution.py:998
  903.7 1.7 copy.254
  905.5 1.5 slice_reduce_fusion.7
  906.9 2.0 slice_reduce_fusion.2
  909.0 2.8 fusion.36
  (248 shorter events, 48.0 us)
Async XLA Ops:
  7.2 707.1 %reduce-scatter.3.cloned.1.call-start = ((), (), s32[]{:S(2)}) async-start(), calls=%async_computation.2 | async-start | bytes 18874368 | tf_op jit(solution)/shard_map/reduce_scatter | solution.py:1621
  14.0 3.5 copy-start.12
  187.8 4.9 copy-start.16
  187.8 6.0 copy-start.17
  192.6 17.3 %copy-start.44 = (f32[8,128]{1,0:T(8,128)}, f32[8,128]{1,0:T(8,128)S(1)}, u32[]{:S(2)}) copy-start(f32[8,128]{1,0:T(8,128)S(1)} %convert_reduce_fusion.1) | copy-start | bytes 12292
  192.6 17.3 %copy-start.71 = (f32[64]{0:T(128)}, f32[64]{0:T(128)S(1)}, u32[]{:S(2)}) copy-start(f32[64]{0:T(128)S(1)} %multiply_power_fusion) | copy-start | bytes 772
  193.8 3.5 copy-start.70
  201.5 6.3 copy-start.42
  201.8 6.0 copy-start.63
  207.7 5.9 copy-start.40
  207.7 5.9 copy-start.38
  207.8 5.8 copy-start.61
  224.0 34.4 %copy-start.13 = (bf16[128,2048]{1,0:T(8,128)(2,1)S(1)}, bf16[128,2048]{1,0:T(8,128)(2,1)}, u32[]{:S(2)}) copy-start(bf16[128,2048]{1,0:T(8,128)(2,1)} %param.14) | copy-start | bytes 1572868
  264.2 10.1 %copy-start.33 = (f32[128,64]{1,0:T(8,128)}, f32[128,64]{1,0:T(8,128)S(1)}, u32[]{:S(2)}) copy-start(f32[128,64]{1,0:T(8,128)S(1)} %copy.235) | copy-start | bytes 98308
  278.6 89.8 %copy-start.78 = (s32[128]{0:T(128)S(1)}, s32[128]{0:T(128)}, u32[]{:S(2)}) copy-start(s32[128]{0:T(128)} %and_select_fusion) | copy-start | bytes 1540
  278.6 89.9 %copy-start.79 = (s32[8]{0:T(128)S(1)}, s32[8]{0:T(128)}, u32[]{:S(2)}) copy-start(s32[8]{0:T(128)} %get-tuple-element.178) | copy-start | bytes 100
  561.9 347.0 %reduce-scatter.5.cloned.1.call-start = ((), (), s32[]{:S(2)}) async-start(), calls=%async_computation.3 | async-start | bytes 2621440 | tf_op jit(solution)/shard_map/reduce_scatter | solution.py:1734
  563.6 3.9 copy-start.28
  563.6 3.9 copy-start.36
  563.6 3.9 copy-start.60
  563.6 4.1 copy-start.34
  563.6 4.1 copy-start.49
  563.7 4.1 copy-start.57
  563.7 4.3 copy-start.66
  606.1 3.8 copy-start.26
  606.1 3.8 copy-start.52
  624.8 3.5 copy-start.3
  624.8 3.5 copy-start.24
  628.3 4.4 copy-start.1
  628.3 4.4 copy-start.43
  628.3 4.4 copy-start.64
  690.4 25.3 %copy-start.55 = (bf16[2048]{0:T(1024)(128)(2,1)S(1)}, bf16[2048]{0:T(1024)(128)(2,1)}, u32[]{:S(2)}) copy-start(bf16[2048]{0:T(1024)(128)(2,1)} %get-tuple-element.128) | copy-start | bytes 12292
  716.4 8.9 copy-start.77
  716.4 8.9 copy-start.50
  716.4 8.9 copy-start.58
  716.4 8.9 copy-start.69
  716.4 9.3 %copy-start.31 = (bf16[8,128,4,128]{3,1,2,0:T(8,128)(2,1)S(1)}, bf16[8,128,4,128]{3,1,2,0:T(8,128)(2,1)}, u32[]{:S(2)}) copy-start(bf16[8,128,4,128]{3,1,2,0:T(8,128)(2,1)} %copy-done.30) | copy-start | bytes 3145732
  722.6 4.2 copy-start.25
  725.3 5.2 copy-start.75
  726.8 3.6 copy-start.6
  726.8 3.7 copy-start.14
  726.8 4.1 copy-start.46
  726.8 4.1 copy-start.47
  726.8 4.1 copy-start.48
  890.3 18.7 %copy-start.5 = (f32[128,2048]{1,0:T(8,128)S(1)}, f32[128,2048]{1,0:T(8,128)}, u32[]{:S(2)}) copy-start(f32[128,2048]{1,0:T(8,128)} %copy-done.4) | copy-start | bytes 3145732
  890.3 18.7 %copy-start.67 = (f32[128]{0:T(128)S(1)}, f32[128]{0:T(128)}, u32[]{:S(2)}) copy-start(f32[128]{0:T(128)} %copy-done.65) | copy-start | bytes 1540
  890.3 18.7 %copy-start.74 = (f32[128]{0:T(128)S(1)}, f32[128]{0:T(128)}, u32[]{:S(2)}) copy-start(f32[128]{0:T(128)} %copy-done.73) | copy-start | bytes 1540
  890.3 18.7 %copy-start.76 = (f32[128]{0:T(128)S(1)}, f32[128]{0:T(128)}, u32[]{:S(2)}) copy-start(f32[128]{0:T(128)} %copy-done.75) | copy-start | bytes 1540
  (34 other events, 61.2 us)
Sparse Core Ops, SparseCore 0:
  562.0 152.2 reduce-scatter.2
  716.6 80.5 reduce-scatter.4

commit v4 on v2

--- a/solution.py
+++ b/solution.py
@@ -14,6 +14,7 @@
 TOPK = 8
 EXP_DEV = 8
 TAIL = 128
+GAIN_ONE = 67
 GROUP_BLOCKS = 32
 RESIDENT = 20 << 20
 
@@ -364,7 +365,7 @@
         gate = jnp.sum(tail * sel, axis=1, keepdims=True)
         g = lax.dot_general(x, wg_ref[0], nt, preferred_element_type=FULL)
         u = lax.dot_general(x, wu_ref[0], nt, preferred_element_type=FULL)
-        da = jnp.dot(dy, wd_ref[0], preferred_element_type=FULL)
+        da = lax.dot_general(dy, wd_ref[0], nt, preferred_element_type=FULL)
         sigma = 1.0 / (1.0 + jnp.exp(-g))
         silu = g * sigma
         act = (silu * u).astype(LOW).astype(FULL)
@@ -375,8 +376,8 @@
         du_all[at, :] = (d_act * silu).astype(LOW)
         high = d_gate.astype(LOW).astype(FULL)
         dx_ref[0, at, MODEL_WIDTH:] = (high * high_sel + (d_gate - high) * rest_sel).astype(LOW)
-        y_ref[0, at, :] = lax.dot_general(
-            a_all[at, :], wd_ref[0], nt, preferred_element_type=FULL
+        y_ref[0, at, :] = jnp.dot(
+            a_all[at, :], wd_ref[0], preferred_element_type=FULL
         ).astype(LOW)
         dx_ref[0, at, :MODEL_WIDTH] = (
             jnp.dot(dg_all[at, :], wg_ref[0], preferred_element_type=FULL)
@@ -394,8 +395,8 @@
         dwu_ref[0, :, at] = lax.dot_general(
             du_all[...], x_ref[0, :, at], tn, preferred_element_type=FULL
         )
-        dwd_ref[0, at, :] = lax.dot_general(
-            dy_ref[0, :, at], a_all[...], tn, preferred_element_type=FULL
+        dwd_ref[0, :, at] = lax.dot_general(
+            a_all[...], dy_ref[0, :, at], tn, preferred_element_type=FULL
         )
         return carry
 
@@ -421,21 +422,21 @@
             spec(rows, MODEL_WIDTH),
             spec(hidden, MODEL_WIDTH),
             spec(hidden, MODEL_WIDTH),
-            spec(MODEL_WIDTH, hidden),
+            spec(hidden, MODEL_WIDTH),
         ],
         out_specs=[
             spec(rows, MODEL_WIDTH),
             spec(rows, width),
             spec(hidden, MODEL_WIDTH),
             spec(hidden, MODEL_WIDTH),
-            spec(MODEL_WIDTH, hidden),
+            spec(hidden, MODEL_WIDTH),
         ],
         out_shape=[
             out(rows, MODEL_WIDTH),
             out(rows, width),
             out(hidden, MODEL_WIDTH, dtype=FULL),
             out(hidden, MODEL_WIDTH, dtype=FULL),
-            out(MODEL_WIDTH, hidden, dtype=FULL),
+            out(hidden, MODEL_WIDTH, dtype=FULL),
         ],
         scratch_shapes=[pltpu.VMEM((rows, hidden), LOW)] * 3,
         compiler_params=pltpu.CompilerParams(vmem_limit_bytes=VMEM_LIMIT),
@@ -448,9 +449,9 @@
 
 
 def combine_home_kernel(
-    planes, slots, place_ref, v_ref, out_ref,
-    hot, load, mine, away, c_in, x_in, y_in, x_half, y_half, u_in, d_in,
-    in_sem, c_send, c_recv, x_send, x_recv, y_send, y_recv, z_send, z_recv,
+    planes, slots, place_ref, v_ref, m_ref, out_ref, mix_ref,
+    hot, hot_t, load, mine, away, c_in, x_in, y_in, x_half, y_half, u_in, d_in,
+    in_sem, free, c_send, c_recv, x_send, x_recv, y_send, y_recv, z_send, z_recv,
 ):
     e, core, flip_x, flip_y, diagonal = neighbours()
     s = lax.axis_index("shard")
@@ -459,37 +460,71 @@
     length, width = out_ref.shape
     half = length // 2
     low_half, high_half = pl.ds(0, half), pl.ds(half, half)
-
-    def fetch(q, sp):
-        rows = pl.ds(pl.multiple_of((q * planes + sp) * slots, 16), slots)
-        return pltpu.make_async_copy(v_ref.at[:, rows, :], load.at[q], in_sem.at[q])
-
-    def to_core(q, sp):
-        return send(away.at[q, sp], c_in.at[q, sp], c_send.at[q, sp], c_recv.at[q, sp], (core, s))
-
-    def halves(sp):
+    order = (q_d, q_x, q_y, q_own)
+
+    def fetch(kind, k, sp):
+        rows = pl.ds(pl.multiple_of((order[k] * planes + sp) * slots, 16), slots)
+        if kind == 0:
+            return pltpu.make_async_copy(v_ref.at[:, rows, :], load.at[k % 2], in_sem.at[k % 2])
+        return pltpu.make_async_copy(
+            m_ref.at[:, rows, :], load.at[k % 2, :, :, pl.ds(0, MODEL_WIDTH)], in_sem.at[k % 2]
+        )
+
+    def to_core(kind, q, sp):
+        return send(
+            away.at[q, sp], c_in.at[q, sp], c_send.at[kind, q, sp], c_recv.at[kind, q, sp],
+            (core, s),
+        )
+
+    def halves(kind, sp):
         return [
             send(
-                mine.at[q_d, sp, low_half], y_half.at[sp], y_send.at[0, sp], y_recv.at[0, sp],
-                (flip_y, s),
+                mine.at[q_d, sp, low_half], y_half.at[kind, sp],
+                y_send.at[kind, 0, sp], y_recv.at[kind, 0, sp], (flip_y, s),
             ),
             send(
-                mine.at[q_d, sp, high_half], x_half.at[sp], x_send.at[0, sp], x_recv.at[0, sp],
-                (flip_x, s),
+                mine.at[q_d, sp, high_half], x_half.at[kind, sp],
+                x_send.at[kind, 0, sp], x_recv.at[kind, 0, sp], (flip_x, s),
             ),
         ]
 
-    def to_x(sp):
-        return send(mine.at[q_x, sp], x_in.at[sp], x_send.at[1, sp], x_recv.at[1, sp], (flip_x, s))
-
-    def to_y(sp):
-        return send(mine.at[q_y, sp], y_in.at[sp], y_send.at[1, sp], y_recv.at[1, sp], (flip_y, s))
-
-    def up(sp):
-        return send(mine.at[q_own, sp], u_in.at[sp], z_send.at[0, sp], z_recv.at[0, sp], (e, s + 1))
-
-    def down(sp):
-        return send(mine.at[q_own, sp], d_in.at[sp], z_send.at[1, sp], z_recv.at[1, sp], (e, s - 1))
+    def to_x(kind, sp):
+        return send(
+            mine.at[q_x, sp], x_in.at[kind, sp], x_send.at[kind, 1, sp], x_recv.at[kind, 1, sp],
+            (flip_x, s),
+        )
+
+    def to_y(kind, sp):
+        return send(
+            mine.at[q_y, sp], y_in.at[kind, sp], y_send.at[kind, 1, sp], y_recv.at[kind, 1, sp],
+            (flip_y, s),
+        )
+
+    def up(kind, sp):
+        return send(
+            mine.at[q_own, sp], u_in.at[kind, sp], z_send.at[kind, 0, sp], z_recv.at[kind, 0, sp],
+            (e, s + 1),
+        )
+
+    def down(kind, sp):
+        return send(
+            mine.at[q_own, sp], d_in.at[kind, sp], z_send.at[kind, 1, sp], z_recv.at[kind, 1, sp],
+            (e, s - 1),
+        )
+
+    def settled(kind, sp):
+        for q in range(4):
+            to_core(kind, q, sp).wait_send()
+        for copy in halves(kind, sp) + [to_x(kind, sp), to_y(kind, sp)]:
+            copy.wait_send()
+
+        @pl.when(sp > s)
+        def _():
+            up(kind, sp).wait_send()
+
+        @pl.when(sp < s)
+        def _():
+            down(kind, sp).wait_send()
 
     def arrived(block, sem):
         send(block, block, sem, sem, (core, s)).wait_recv()
@@ -505,19 +540,20 @@
             total = total + other[...].astype(FULL)
         target[...] = total.astype(LOW)
 
-    def work(sp):
-        for q in range(4):
-            fetch(q, sp).start()
-
-        def one(q, carry):
+    def work(kind, sp):
+        if kind == 1:
+            settled(0, sp)
+            pl.semaphore_wait(free.at[sp], 1)
+        for k in range(2):
+            fetch(kind, k, sp).start()
+        for k, q in enumerate(order):
             one_hot_pair(place_ref, q * planes + sp, hot, slots)
-            fetch(q, sp).wait()
-
-            def part(at, wide):
-                rows = load[q, :, :, at].reshape(EXP_DEV * slots, wide)
-                got = lax.dot_general(
-                    hot[...], rows, (((0,), (0,)), ((), ())), preferred_element_type=FULL
-                ).astype(LOW)
+            hot_t[...] = hot[...].T
+            fetch(kind, k, sp).wait()
+
+            def part(at, wide, q=q, k=k):
+                rows = load[k % 2, :, :, at].reshape(EXP_DEV * slots, wide)
+                got = jnp.dot(hot_t[...], rows, preferred_element_type=FULL).astype(LOW)
                 got = got.reshape(2, length, wide)
 
                 @pl.when(parity == 0)
@@ -530,132 +566,1181 @@
                     mine[q, sp, :, at] = got[1]
                     away[q, sp, :, at] = got[0]
 
-            def tile(t, inner):
+            def tile(t, inner, part=part):
                 part(pl.ds(pl.multiple_of(t * TILE, TILE), TILE), TILE)
                 return inner
 
             lax.fori_loop(0, MODEL_WIDTH // TILE, tile, 0)
-            if width > MODEL_WIDTH:
+            if kind == 0 and width > MODEL_WIDTH:
                 part(pl.ds(MODEL_WIDTH, width - MODEL_WIDTH), width - MODEL_WIDTH)
-            to_core(q, sp).start()
-            return carry
-
-        lax.fori_loop(0, 4, one, 0)
-
-    def pairs(sp):
-        def one(q, carry):
-            arrived(c_in.at[q, sp], c_recv.at[q, sp])
+            to_core(kind, q, sp).start()
+            if k < 2:
+                fetch(kind, k + 2, sp).start()
+
+    def pairs(kind, sp):
+        for k, q in enumerate(order):
+            arrived(c_in.at[q, sp], c_recv.at[kind, q, sp])
             add(mine.at[q, sp], c_in.at[q, sp])
-            return carry
-
-        one(q_d, 0)
-        for copy in halves(sp):
-            copy.start()
-        for q in (q_x, q_y, q_own):
-            one(q, 0)
-
-    def sides(sp):
-        arrived(y_half.at[sp], y_recv.at[0, sp])
-        add(mine.at[q_x, sp, low_half], y_half.at[sp])
-        to_x(sp).start()
-        arrived(x_half.at[sp], x_recv.at[0, sp])
-        add(mine.at[q_y, sp, high_half], x_half.at[sp])
-        to_y(sp).start()
-
-    def line(sp):
-        arrived(x_in.at[sp], x_recv.at[1, sp])
-        arrived(y_in.at[sp], y_recv.at[1, sp])
-        add(mine.at[q_own, sp], x_in.at[sp], y_in.at[sp])
+            if k == 0:
+                for copy in halves(kind, sp):
+                    copy.start()
+        if kind == 0:
+            pl.semaphore_signal(free.at[sp], 1, device_id=(core, s), device_id_type=MESH)
+
+    def sides(kind, sp):
+        arrived(y_half.at[kind, sp], y_recv.at[kind, 0, sp])
+        add(mine.at[q_x, sp, low_half], y_half.at[kind, sp])
+        to_x(kind, sp).start()
+        arrived(x_half.at[kind, sp], x_recv.at[kind, 0, sp])
+        add(mine.at[q_y, sp, high_half], x_half.at[kind, sp])
+        to_y(kind, sp).start()
+
+    def line(kind, sp):
+        arrived(x_in.at[kind, sp], x_recv.at[kind, 1, sp])
+        arrived(y_in.at[kind, sp], y_recv.at[kind, 1, sp])
+        add(mine.at[q_own, sp], x_in.at[kind, sp], y_in.at[kind, sp])
 
         @pl.when((sp >= s) & (s > 0))
         def _():
-            arrived(u_in.at[sp], z_recv.at[0, sp])
-            add(mine.at[q_own, sp], u_in.at[sp])
+            arrived(u_in.at[kind, sp], z_recv.at[kind, 0, sp])
+            add(mine.at[q_own, sp], u_in.at[kind, sp])
 
         @pl.when((sp <= s) & (s < planes - 1))
         def _():
-            arrived(d_in.at[sp], z_recv.at[1, sp])
-            add(mine.at[q_own, sp], d_in.at[sp])
+            arrived(d_in.at[kind, sp], z_recv.at[kind, 1, sp])
+            add(mine.at[q_own, sp], d_in.at[kind, sp])
 
         @pl.when(sp > s)
         def _():
-            up(sp).start()
+            up(kind, sp).start()
 
         @pl.when(sp < s)
         def _():
-            down(sp).start()
+            down(kind, sp).start()
+
+        @pl.when(sp == s)
+        def _():
+            if kind == 0:
+                out_ref[...] = mine[q_own, sp].astype(FULL)
+            else:
+                mix_ref[...] = mine[q_own, sp, :, :MODEL_WIDTH].astype(FULL)
 
     greet(planes)
-
-    def step(i, carry):
+    span = 2 * planes - 1
+
+    def step(t, carry):
         for lag, job in ((0, work), (1, pairs), (2, sides), (3, line)):
-            sp, there = plane_at(i - lag)
-
-            @pl.when(there)
-            def _(sp=sp, job=job):
-                job(sp)
+            for kind in range(2):
+                sp, there = plane_at(t - lag - kind * span)
+
+                @pl.when(there)
+                def _(sp=sp, job=job, kind=kind):
+                    job(kind, sp)
 
         return carry
 
-    lax.fori_loop(0, 2 * planes + 2, step, 0)
-    out_ref[...] = mine[q_own, s].astype(FULL)
+    lax.fori_loop(0, 2 * span + 3, step, 0)
 
     def drain(sp, carry):
-        for q in range(4):
-            to_core(q, sp).wait_send()
-        for copy in halves(sp) + [to_x(sp), to_y(sp)]:
-            copy.wait_send()
-
-        @pl.when(sp > s)
-        def _():
-            up(sp).wait_send()
-
-        @pl.when(sp < s)
-        def _():
-            down(sp).wait_send()
-
+        settled(1, sp)
         return carry
 
     lax.fori_loop(0, planes, drain, 0)
 
 
-def combine_home(place, v, length, planes, slots, identity):
+def combine_home(place, v, m, length, planes, slots, identity):
     width = v.shape[2]
     block = (planes, length, width)
+    part = (planes, length // 2, width)
     return pl.pallas_call(
         functools.partial(combine_home_kernel, planes, slots),
-        out_shape=jax.ShapeDtypeStruct((length, width), FULL),
-        in_specs=[VM, ANY],
-        out_specs=VM,
+        out_shape=[
+            jax.ShapeDtypeStruct((length, width), FULL),
+            jax.ShapeDtypeStruct((length, MODEL_WIDTH), FULL),
+        ],
+        in_specs=[VM, ANY, ANY],
+        out_specs=[VM, VM],
         scratch_shapes=[
             pltpu.VMEM((EXP_DEV * slots, 2 * length), LOW),
-            pltpu.VMEM((4, EXP_DEV, slots, width), LOW),
+            pltpu.VMEM((2 * length, EXP_DEV * slots), LOW),
+            pltpu.VMEM((2, EXP_DEV, slots, width), LOW),
+            pltpu.VMEM((4,) + block, LOW),
+            pltpu.VMEM((4,) + block, LOW),
+            pltpu.VMEM((4,) + block, LOW),
+            pltpu.VMEM((2,) + block, LOW),
+            pltpu.VMEM((2,) + block, LOW),
+            pltpu.VMEM((2,) + part, LOW),
+            pltpu.VMEM((2,) + part, LOW),
+            pltpu.VMEM((2,) + block, LOW),
+            pltpu.VMEM((2,) + block, LOW),
+            DMA((2,)),
+            pltpu.SemaphoreType.REGULAR((planes,)),
+            DMA((2, 4, planes)),
+            DMA((2, 4, planes)),
+            DMA((2, 2, planes)),
+            DMA((2, 2, planes)),
+            DMA((2, 2, planes)),
+            DMA((2, 2, planes)),
+            DMA((2, 2, planes)),
+            DMA((2, 2, planes)),
+        ],
+        compiler_params=pltpu.CompilerParams(
+            collective_id=identity, has_side_effects=True, vmem_limit_bytes=VMEM_LIMIT
+        ),
+    )(place, v, m)
+
+
+def greet_plane(planes, owners):
+    e, s = lax.axis_index("expert"), lax.axis_index("shard")
+    barrier = pltpu.get_barrier_semaphore()
+    for o in range(1, owners):
+        pl.semaphore_signal(
+            barrier, 1, device_id=(lax.rem(e + o, owners), s), device_id_type=MESH
+        )
+
+    @pl.when(s > 0)
+    def _():
+        pl.semaphore_signal(barrier, 1, device_id=(e, s - 1), device_id_type=MESH)
+
+    @pl.when(s < planes - 1)
+    def _():
+        pl.semaphore_signal(barrier, 1, device_id=(e, s + 1), device_id_type=MESH)
+
+    inner = (s > 0) & (s < planes - 1)
+
+    @pl.when(inner)
+    def _():
+        pl.semaphore_wait(barrier, owners + 1)
+
+    @pl.when(jnp.logical_not(inner))
+    def _():
+        pl.semaphore_wait(barrier, owners)
+
+
+def finish_kernel(owners, rows_ref, head_ref, kv_ref, tail_ref, out_rows, out_qkv, out_tail):
+    i = pl.program_id(0)
+
+    @pl.when(i < owners)
+    def _():
+        out_rows[...] = rows_ref[0].astype(FULL)
+        out_qkv[...] = head_ref[0].astype(FULL)
+
+    @pl.when(i >= owners)
+    def _():
+        each = owners // KEY_VALUE_HEADS
+        for h in range(KEY_VALUE_HEADS):
+            total = kv_ref[h * each].astype(FULL)
+            for j in range(1, each):
+                total = total + kv_ref[h * each + j].astype(FULL)
+            out_qkv[:, h * HEAD_SIZE : (h + 1) * HEAD_SIZE] = total
+
+    @pl.when(i == 0)
+    def _():
+        total = tail_ref[0].astype(FULL)
+        for lane in range(1, owners):
+            total = total + tail_ref[lane].astype(FULL)
+        out_tail[...] = total
+
+
+def finish_grads(rows, head, rest, owners):
+    rows = rows.reshape(owners, -1, rows.shape[-1])
+    head = head.reshape(owners, -1, head.shape[-1])
+    rest = rest.reshape(owners, -1, rest.shape[-1])
+    count, share = rows.shape[1:]
+    height, wide = head.shape[1:]
+    last = owners - 1
+    return pl.pallas_call(
+        functools.partial(finish_kernel, owners),
+        grid=(owners + 2,),
+        in_specs=[
+            pl.BlockSpec((1, count, share), lambda i: (jnp.minimum(i, last), 0, 0)),
+            pl.BlockSpec((1, height, wide), lambda i: (jnp.minimum(i, last), 0, 0)),
+            pl.BlockSpec((owners, height, HEAD_SIZE), lambda i: (0, 0, i // (owners + 1))),
+            pl.BlockSpec((owners, height, TAIL), lambda i: (0, 0, 2)),
+        ],
+        out_specs=[
+            pl.BlockSpec((count, share), lambda i: (0, jnp.minimum(i, last))),
+            pl.BlockSpec((height, wide), lambda i: (0, i)),
+            pl.BlockSpec((height, TAIL), lambda i: (0, 0)),
+        ],
+        out_shape=[
+            jax.ShapeDtypeStruct((count, owners * share), FULL),
+            jax.ShapeDtypeStruct((height, (owners + 2) * wide), FULL),
+            jax.ShapeDtypeStruct((height, TAIL), FULL),
+        ],
+        compiler_params=pltpu.CompilerParams(vmem_limit_bytes=VMEM_LIMIT),
+    )(rows, head, rest, rest)
+
+
+def gather_steps(at, cut, source, x_send, x_recv, y_send, y_recv, c_send, c_recv):
+    e, core, flip_x, flip_y, diagonal = neighbours()
+    s = lax.axis_index("shard")
+
+    def arrived(block, sem):
+        send(block, block, sem, sem, (core, s)).wait_recv()
+
+    def first():
+        return [
+            send(source, at(e), x_send(0), x_recv(0), (flip_x, s)),
+            send(source, at(e), y_send(0), y_recv(0), (flip_y, s)),
+            send(source, at(e), c_send(0), c_recv(0), (core, s)),
+        ]
+
+    def from_x():
+        return [
+            send(cut(flip_x, 0), cut(flip_x, 0), y_send(1), y_recv(1), (flip_y, s)),
+            send(at(flip_x), at(flip_x), c_send(1), c_recv(1), (core, s)),
+        ]
+
+    def from_y():
+        return [
+            send(cut(flip_y, 1), cut(flip_y, 1), x_send(1), x_recv(1), (flip_x, s)),
+            send(at(flip_y), at(flip_y), c_send(2), c_recv(2), (core, s)),
+        ]
+
+    def from_diagonal():
+        return [send(at(diagonal), at(diagonal), c_send(3), c_recv(3), (core, s))]
+
+    def begin():
+        for copy in first():
+            copy.start()
+
+    def second():
+        arrived(at(flip_x), x_recv(0))
+        for copy in from_x():
+            copy.start()
+        arrived(at(flip_y), y_recv(0))
+        for copy in from_y():
+            copy.start()
+
+    def third():
+        arrived(cut(diagonal, 0), y_recv(1))
+        arrived(cut(diagonal, 1), x_recv(1))
+        for copy in from_diagonal():
+            copy.start()
+
+    def last():
+        for k, lane in enumerate((core, core + flip_x - e, core + flip_y - e, core + diagonal - e)):
+            arrived(at(lane), c_recv(k))
+
+    def sent():
+        for copy in first() + from_x() + from_y() + from_diagonal():
+            copy.wait_send()
+
+    return begin, second, third, last, sent
+
+
+def rope_tables(places, frequency):
+    angles = places * frequency
+    lane = lax.broadcasted_iota(jnp.int32, angles.shape, 1)
+    sine = jnp.sin(angles)
+    return jnp.cos(angles), jnp.where(lane < HEAD_SIZE // 2, -sine, sine)
+
+
+def half_turn(v):
+    return pltpu.roll(v, HEAD_SIZE // 2, 1)
+
+
+def front_kernel(
+    planes, owners, w_ref, gain_ref, tok_ref, d_ref, freq_ref, out_ref,
+    d_all, w_out_all, w_all_out, gains, tail_ref, h1_ref, proj_ref, probs_ref, mixed_ref, branch_ref,
+    w_all, tok_all, w_mine, q_rows, mine, away, c_in, x_in, y_in, x_half, y_half,
+    keep_sem, w_send, w_recv, g_send, g_recv, o_send, o_recv, z_send, z_recv,
+    tx_send, tx_recv, ty_send, ty_recv, tc_send, tc_recv,
+    dx_send, dx_recv, dy_send, dy_recv, dc_send, dc_recv,
+    px_send, px_recv, py_send, py_recv, pc_send, pc_recv,
+):
+    e, core, flip_x, flip_y, diagonal = neighbours()
+    s = lax.axis_index("shard")
+    lanes = owners // planes
+    home = e // lanes
+    length = tok_ref.shape[0]
+    half = length // 2
+    count = w_mine.shape[0]
+    heads = count // HEAD_SIZE
+    pieces = 4
+    out_part = count // pieces
+    deep = w_ref.shape[0]
+    qkv_cols = proj_ref.shape[2]
+
+    def arrived(block, sem):
+        send(block, block, sem, sem, (core, s)).wait_recv()
+
+    def w_copy(sp, way):
+        block = w_all.at[sp]
+        return send(block, block, w_send.at[way, sp], w_recv.at[sp], (e, s + 1 - 2 * way))
+
+    def g_copy(sp, way):
+        block = gains.at[sp]
+        return send(block, block, g_send.at[way, sp], g_recv.at[sp], (e, s + 1 - 2 * way))
+
+    def d_copy(sp, way):
+        block = d_all.at[e, sp]
+        return send(block, block, z_send.at[way, sp], z_recv.at[sp], (e, s + 1 - 2 * way))
+
+    def o_copy(k, way):
+        block = w_mine.at[pl.ds(k * out_part, out_part)]
+        return send(block, block, o_send.at[way, k], o_recv.at[k], (e, s + 1 - 2 * way))
+
+    t_begin, t_second, t_third, t_last, t_sent = gather_steps(
+        lambda lane: tok_all.at[lane],
+        lambda lane, k: tok_all.at[lane, pl.ds(k * half, half)],
+        tok_ref,
+        lambda k: tx_send.at[k],
+        lambda k: tx_recv.at[k],
+        lambda k: ty_send.at[k],
+        lambda k: ty_recv.at[k],
+        lambda k: tc_send.at[k],
+        lambda k: tc_recv.at[k],
+    )
+
+    def d_rows(sp):
+        return gather_steps(
+            lambda lane: d_all.at[lane, sp],
+            lambda lane, k: d_all.at[lane, sp, pl.ds(k * half, half)],
+            d_all.at[e, sp],
+            lambda k: dx_send.at[k, sp],
+            lambda k: dx_recv.at[k, sp],
+            lambda k: dy_send.at[k, sp],
+            lambda k: dy_recv.at[k, sp],
+            lambda k: dc_send.at[k, sp],
+            lambda k: dc_recv.at[k, sp],
+        )
+
+    keep_d = pltpu.make_async_copy(d_ref, d_all.at[e, s], keep_sem.at[0])
+    rows = pl.ds(pl.multiple_of((e - home * lanes) * count, 16), count)
+    load_o = pltpu.make_async_copy(out_ref.at[rows], w_mine, keep_sem.at[1])
+    keep_w = pltpu.make_async_copy(w_all, w_all_out, keep_sem.at[2])
+    keep_o = pltpu.make_async_copy(w_mine, w_out_all, keep_sem.at[3])
+    keep_d.start()
+
+    @pl.when(s == home)
+    def _():
+        load_o.start()
+
+    w_all[s] = w_ref[...]
+    gains[s] = gain_ref[...]
+    tok_all[e] = tok_ref[...]
+    greet(planes)
+
+    def both_ways(copy, sp):
+        @pl.when((sp <= s) & (s < planes - 1))
+        def _():
+            copy(sp, 0).start()
+
+        @pl.when((sp >= s) & (s > 0))
+        def _():
+            copy(sp, 1).start()
+
+    def plane_at(i):
+        sp = s + (2 * (i % 2) - 1) * ((i + 1) // 2)
+        return sp, (sp >= 0) & (sp < planes) & (i >= 0) & (i <= 2 * planes - 2)
+
+    def out_step(k):
+        @pl.when(s != home)
+        def _():
+            arrived(w_mine.at[pl.ds(k * out_part, out_part)], o_recv.at[k])
+
+        @pl.when((s >= home) & (s < planes - 1))
+        def _():
+            o_copy(k, 0).start()
+
+        @pl.when((s <= home) & (s > 0))
+        def _():
+            o_copy(k, 1).start()
+
+    t_begin()
+    both_ways(g_copy, s)
+    both_ways(w_copy, s)
+
+    keep_d.wait()
+    d_rows(s)[0]()
+
+    def weights(i, carry):
+        sp, there = plane_at(i)
+
+        @pl.when(there & (i > 0))
+        def _():
+            arrived(gains.at[sp], g_recv.at[sp])
+            both_ways(g_copy, sp)
+            arrived(w_all.at[sp], w_recv.at[sp])
+            both_ways(w_copy, sp)
+
+        @pl.when(i == 1)
+        def _():
+            t_second()
+
+        @pl.when(i == 2)
+        def _():
+            t_third()
+            d_rows(s)[1]()
+
+        @pl.when(i == 3)
+        def _():
+            d_rows(s)[2]()
+
+        @pl.when((i == 2) & (s == home))
+        def _():
+            load_o.wait()
+            for k in range(pieces):
+                out_step(k)
+
+        return carry
+
+    lax.fori_loop(1, 2 * planes - 1, weights, 0)
+    t_last()
+    keep_w.start()
+
+    def far(n):
+        for i in (2 * n - 1, 2 * n):
+            sp, there = plane_at(i)
+
+            @pl.when(there)
+            def _(sp=sp):
+                arrived(d_all.at[e, sp], z_recv.at[sp])
+                both_ways(d_copy, sp)
+                d_rows(sp)[0]()
+
+    def rows_onward(n):
+        @pl.when((s - home == n) | (home - s == n))
+        def _():
+            for k in range(pieces):
+                out_step(k)
+
+    def near(n, stage):
+        for i in (2 * n - 1, 2 * n):
+            sp, there = plane_at(i)
+
+            @pl.when(there)
+            def _(sp=sp):
+                d_rows(sp)[stage]()
+
+    gain_query = gains[0, 2:3, :HEAD_SIZE].astype(FULL)
+    gain_key = gains[0, 3:4, :HEAD_SIZE].astype(FULL)
+    for sp in range(1, planes):
+        gain_query = gain_query + gains[sp, 2:3, :HEAD_SIZE].astype(FULL)
+        gain_key = gain_key + gains[sp, 3:4, :HEAD_SIZE].astype(FULL)
+    row = lax.broadcasted_iota(jnp.int32, (length, length), 0).astype(FULL)
+    column = lax.broadcasted_iota(jnp.int32, (length, length), 1).astype(FULL)
+
+    def attend(b, carry):
+        x = tok_all[b, :, :MODEL_WIDTH].astype(FULL)
+        inverse = lax.rsqrt(jnp.mean(x * x, axis=1, keepdims=True) + EPS)
+        total = jnp.zeros((length, qkv_cols), FULL)
+        for sp in range(planes):
+            at = slice(sp * deep, (sp + 1) * deep)
+            part = x[:, at] * inverse * gains[sp, 0:1, :].astype(FULL)
+            part = part.astype(LOW)
+            h1_ref[b, :, at] = part
+            total = total + jnp.dot(part, w_all[sp, :, :qkv_cols], preferred_element_type=FULL)
+        proj_ref[b] = total
+        tail_ref[b] = tok_all[b, :, MODEL_WIDTH:]
+        places = tok_all[b, :, MODEL_WIDTH:].astype(FULL)[:, 1:2]
+        cosine, sine = rope_tables(places, freq_ref[0:1, :])
+
+        def normed(v, gain):
+            v = v * lax.rsqrt(jnp.mean(v * v, axis=1, keepdims=True) + EPS) * gain
+            return (v * cosine + half_turn(v) * sine).astype(LOW)
+
+        for h in range(heads):
+            at = slice(h * HEAD_SIZE, (h + 1) * HEAD_SIZE)
+            q_rows[h * length : (h + 1) * length, :] = normed(total[:, at], gain_query)
+        key = normed(total[:, count : count + HEAD_SIZE], gain_key)
+        value = total[:, count + HEAD_SIZE :].astype(LOW)
+        scores = lax.dot_general(
+            q_rows[...], key, (((1,), (1,)), ((), ())), preferred_element_type=FULL
+        ) * (HEAD_SIZE**-0.5)
+        allowed = (column <= row) & (column >= row - places)
+        scores = jnp.where(jnp.concatenate([allowed] * heads, axis=0), scores, -1e30)
+        exponent = jnp.exp(scores - jnp.max(scores, axis=1, keepdims=True))
+        probs = (exponent / jnp.sum(exponent, axis=1, keepdims=True)).astype(LOW)
+        probs_ref[b] = probs
+        mixed = jnp.dot(probs, value, preferred_element_type=FULL).astype(LOW)
+        for h in range(heads):
+            at = slice(h * HEAD_SIZE, (h + 1) * HEAD_SIZE)
+            mixed_ref[b, :, at] = mixed[h * length : (h + 1) * length]
+
+        for k in range(pieces):
+
+            @pl.when((b == 2 * k) & ((s - home == 1) | (home - s == 1)))
+            def _(k=k):
+                out_step(k)
+
+        return carry
+
+    lax.fori_loop(0, owners, attend, 0)
+    both_ways(d_copy, s)
+    rows_onward(2)
+    far(1)
+    for n in range(3, planes):
+        rows_onward(n)
+    keep_o.start()
+    begin, middle, finish, sent = project_steps(
+        False, mixed_ref, w_mine, branch_ref, mine, away, c_in, x_in, y_in, x_half, y_half,
+        pc_send, pc_recv, px_send, px_recv, py_send, py_recv,
+    )
+    begin()
+    near(1, 1)
+    far(2)
+    middle()
+    near(1, 2)
+    near(2, 1)
+    for n in range(3, planes):
+        far(n)
+    finish()
+    near(2, 2)
+    for n in range(3, planes):
+        near(n, 1)
+    for n in range(3, planes):
+        near(n, 2)
+    t_sent()
+    sent()
+
+    def settled(copy, sp):
+        @pl.when((sp <= s) & (s < planes - 1))
+        def _():
+            copy(sp, 0).wait_send()
+
+        @pl.when((sp >= s) & (s > 0))
+        def _():
+            copy(sp, 1).wait_send()
+
+    def drain(sp, carry):
+        d_rows(sp)[3]()
+        d_rows(sp)[4]()
+        settled(w_copy, sp)
+        settled(g_copy, sp)
+        settled(d_copy, sp)
+        return carry
+
+    lax.fori_loop(0, planes, drain, 0)
+    for k in range(pieces):
+
+        @pl.when((s >= home) & (s < planes - 1))
+        def _(k=k):
+            o_copy(k, 0).wait_send()
+
+        @pl.when((s <= home) & (s > 0))
+        def _(k=k):
+            o_copy(k, 1).wait_send()
+
+    keep_w.wait()
+    keep_o.wait()
+
+
+def front(w, gain_rows, tokens, w_out, d_rows, frequency, planes, owners, identity):
+    def out(*shape, dtype=LOW):
+        return jax.ShapeDtypeStruct(shape, dtype)
+
+    length = tokens.shape[0]
+    count = w_out.shape[0] * planes // owners
+    qkv_cols = count + 2 * HEAD_SIZE
+    block = (length, MODEL_WIDTH)
+    part = (length // 2, MODEL_WIDTH)
+    return pl.pallas_call(
+        functools.partial(front_kernel, planes, owners),
+        out_shape=[
+            out(owners, planes, *d_rows.shape),
+            out(count, MODEL_WIDTH),
+            out(planes, *w.shape),
+            out(planes, *gain_rows.shape),
+            out(owners, length, TAIL),
+            out(owners, length, MODEL_WIDTH),
+            out(owners, length, qkv_cols, dtype=FULL),
+            out(owners, length * count // HEAD_SIZE, length),
+            out(owners, length, count),
+            out(length, MODEL_WIDTH, dtype=FULL),
+        ],
+        in_specs=[VM, VM, VM, VM, VM, ANY],
+        out_specs=[ANY, ANY, ANY, VM, VM, VM, VM, VM, VM, VM],
+        scratch_shapes=[
+            pltpu.VMEM((planes,) + w.shape, LOW),
+            pltpu.VMEM((owners,) + tokens.shape, LOW),
+            pltpu.VMEM((count, MODEL_WIDTH), LOW),
+            pltpu.VMEM((length * count // HEAD_SIZE, HEAD_SIZE), LOW),
             pltpu.VMEM((4,) + block, LOW),
             pltpu.VMEM((4,) + block, LOW),
             pltpu.VMEM((4,) + block, LOW),
             pltpu.VMEM(block, LOW),
             pltpu.VMEM(block, LOW),
-            pltpu.VMEM((planes, length // 2, width), LOW),
-            pltpu.VMEM((planes, length // 2, width), LOW),
-            pltpu.VMEM(block, LOW),
-            pltpu.VMEM(block, LOW),
+            pltpu.VMEM(part, LOW),
+            pltpu.VMEM(part, LOW),
             DMA((4,)),
-            DMA((4, planes)),
-            DMA((4, planes)),
+            DMA((2, planes)),
+            DMA((planes,)),
+            DMA((2, planes)),
+            DMA((planes,)),
+            DMA((2, 4)),
+            DMA((4,)),
+            DMA((2, planes)),
+            DMA((planes,)),
+            DMA((2,)),
+            DMA((2,)),
+            DMA((2,)),
+            DMA((2,)),
+            DMA((4,)),
+            DMA((4,)),
             DMA((2, planes)),
             DMA((2, planes)),
             DMA((2, planes)),
             DMA((2, planes)),
+            DMA((4, planes)),
+            DMA((4, planes)),
+            DMA((2,)),
+            DMA((2,)),
+            DMA((2,)),
+            DMA((2,)),
+            DMA((4,)),
+            DMA((4,)),
+        ],
+        compiler_params=pltpu.CompilerParams(
+            collective_id=identity, has_side_effects=True, vmem_limit_bytes=VMEM_LIMIT
+        ),
+    )(w, gain_rows, tokens, d_rows, frequency, w_out)
+
+
+def project_steps(
+    turned, rows_ref, w_ref, out_ref, mine, away, c_in, x_in, y_in, x_half, y_half,
+    cs, cr, xs, xr, ys, yr,
+):
+    e, core, flip_x, flip_y, diagonal = neighbours()
+    s = lax.axis_index("shard")
+    q_own, q_x, q_y, q_d = e // 2, flip_x // 2, flip_y // 2, diagonal // 2
+    parity = e % 2
+    half = out_ref.shape[0] // 2
+    low_half, high_half = pl.ds(0, half), pl.ds(half, half)
+    across = (((1,), (1 if turned else 0,)), ((), ()))
+    order = (q_d, q_x, q_y, q_own)
+
+    def arrived(block, sem):
+        send(block, block, sem, sem, (core, s)).wait_recv()
+
+    def add(target, *others):
+        total = target[...].astype(FULL)
+        for other in others:
+            total = total + other[...].astype(FULL)
+        target[...] = total.astype(LOW)
+
+    def to_core(q):
+        return send(away.at[q], c_in.at[q], cs.at[q], cr.at[q], (core, s))
+
+    def compute(q, lane, into):
+        rows = rows_ref[2 * q + lane]
+
+        def tile(t, carry):
+            at = pl.ds(pl.multiple_of(t * TILE, TILE), TILE)
+            if turned:
+                deep = w_ref.shape[1]
+                w = w_ref[t * TILE // deep, :, : rows.shape[1]]
+            else:
+                w = w_ref[:, at]
+            into[q, :, at] = lax.dot_general(
+                rows, w, across, preferred_element_type=FULL
+            ).astype(LOW)
+            return carry
+
+        lax.fori_loop(0, MODEL_WIDTH // TILE, tile, 0)
+
+    halves = [
+        send(mine.at[q_d, low_half], y_half, ys.at[0], yr.at[0], (flip_y, s)),
+        send(mine.at[q_d, high_half], x_half, xs.at[0], xr.at[0], (flip_x, s)),
+    ]
+    to_x = send(mine.at[q_x], x_in, xs.at[1], xr.at[1], (flip_x, s))
+    to_y = send(mine.at[q_y], y_in, ys.at[1], yr.at[1], (flip_y, s))
+
+    def joined(q):
+        arrived(c_in.at[q], cr.at[q])
+        add(mine.at[q], c_in.at[q])
+
+    def begin():
+        for q in order:
+            compute(q, 1 - parity, away)
+            to_core(q).start()
+        for k, q in enumerate(order):
+            compute(q, parity, mine)
+            if k == 0:
+                joined(q_d)
+                for copy in halves:
+                    copy.start()
+
+    def middle():
+        joined(q_x)
+        arrived(y_half, yr.at[0])
+        add(mine.at[q_x, low_half], y_half)
+        to_x.start()
+        joined(q_y)
+        arrived(x_half, xr.at[0])
+        add(mine.at[q_y, high_half], x_half)
+        to_y.start()
+
+    def finish():
+        joined(q_own)
+        arrived(x_in, xr.at[1])
+        arrived(y_in, yr.at[1])
+        out_ref[...] = (
+            mine[q_own].astype(FULL) + x_in[...].astype(FULL) + y_in[...].astype(FULL)
+        )
+
+    def sent():
+        for q in order:
+            to_core(q).wait_send()
+        for copy in halves + [to_x, to_y]:
+            copy.wait_send()
+
+    return begin, middle, finish, sent
+
+
+def back_kernel(
+    planes, owners, dm_ref, w_ref, mixed_ref, proj_ref, probs_ref, tail_ref, gain_ref, freq_ref,
+    dproj_ref, sum_ref, dgain_ref,
+    dm_all, mixed_t, rows, acc, up_in, down_in, q_rows, dm_rows,
+    keep_sem, xs, xr, ys, yr, cs, cr, a_send, a_recv, z_send, z_recv,
+):
+    e, core, _, _, _ = neighbours()
+    s = lax.axis_index("shard")
+    lanes = owners // planes
+    length = dm_ref.shape[0]
+    half = length // 2
+    count = w_ref.shape[0]
+    heads = count // HEAD_SIZE
+    share = acc.shape[2]
+    scaling = HEAD_SIZE**-0.5
+    nt = (((1,), (1,)), ((), ()))
+    tn = (((0,), (0,)), ((), ()))
+
+    def arrived(block, sem):
+        send(block, block, sem, sem, (core, s)).wait_recv()
+
+    greet_plane(planes, owners)
+    begin, second, third, last, sent = gather_steps(
+        lambda lane: dm_all.at[lane],
+        lambda lane, k: dm_all.at[lane, pl.ds(k * half, half)],
+        dm_ref,
+        lambda k: xs.at[k],
+        lambda k: xr.at[k],
+        lambda k: ys.at[k],
+        lambda k: yr.at[k],
+        lambda k: cs.at[k],
+        lambda k: cr.at[k],
+    )
+    begin()
+    dm_all[e] = dm_ref[...]
+    for b in range(owners):
+        mixed_t[:, b * length : (b + 1) * length] = mixed_ref[b].T
+    second()
+    third()
+    last()
+
+    def spread(other):
+        return send(
+            rows.at[:, pl.ds(other * share, share)], acc.at[e], a_send.at[other], a_recv.at[e],
+            (other, s),
+        )
+
+    for other in range(owners):
+        at = pl.ds(other * share, share)
+        got = jnp.dot(
+            mixed_t[...],
+            dm_all[:, :, at].reshape(owners * length, share),
+            preferred_element_type=FULL,
+        ).astype(LOW)
+        rows[:, at] = got
+
+        @pl.when(other != e)
+        def _(other=other):
+            spread(other).start()
+
+        @pl.when(other == e)
+        def _(got=got):
+            acc[e] = got
+
+    def chunk(sp):
+        return acc.at[pl.ds(sp * lanes, lanes)]
+
+    def up(sp):
+        return send(chunk(sp), up_in.at[sp], z_send.at[0, sp], z_recv.at[0, sp], (e, s + 1))
+
+    def down(sp):
+        return send(chunk(sp), down_in.at[sp], z_send.at[1, sp], z_recv.at[1, sp], (e, s - 1))
+
+    def line(sp):
+        for lane in range(lanes):
+            source = sp * lanes + lane
+
+            @pl.when(source != e)
+            def _(source=source):
+                arrived(acc.at[source], a_recv.at[source])
+
+        @pl.when((sp >= s) & (s > 0))
+        def _():
+            arrived(up_in.at[sp], z_recv.at[0, sp])
+            add_blocks(chunk(sp), up_in.at[sp])
+
+        @pl.when((sp <= s) & (s < planes - 1))
+        def _():
+            arrived(down_in.at[sp], z_recv.at[1, sp])
+            add_blocks(chunk(sp), down_in.at[sp])
+
+        @pl.when(sp > s)
+        def _():
+            up(sp).start()
+
+        @pl.when(sp < s)
+        def _():
+            down(sp).start()
+
+    dgain_ref[...] = jnp.zeros_like(dgain_ref)
+    gain_query = gain_ref[0, 2:3, :HEAD_SIZE].astype(FULL)
+    gain_key = gain_ref[0, 3:4, :HEAD_SIZE].astype(FULL)
+    for sp in range(1, planes):
+        gain_query = gain_query + gain_ref[sp, 2:3, :HEAD_SIZE].astype(FULL)
+        gain_key = gain_key + gain_ref[sp, 3:4, :HEAD_SIZE].astype(FULL)
+
+    def attend(b, carry):
+        places = tail_ref[b].astype(FULL)[:, 1:2]
+        cosine, sine = rope_tables(places, freq_ref[0:1, :])
+
+        def unit(v):
+            inverse = lax.rsqrt(jnp.mean(v * v, axis=1, keepdims=True) + EPS)
+            return v * inverse, inverse
+
+        def turned(v):
+            return (v * cosine + half_turn(v) * sine).astype(LOW)
+
+        def back(v, units, inverse, gain, row):
+            v = v * cosine - half_turn(v) * sine
+            dgain_ref[row : row + 1, :] += jnp.sum(v * units, axis=0, keepdims=True)
+            v = v * gain
+            return inverse * (v - units * jnp.mean(v * units, axis=1, keepdims=True))
+
+        d_mixed = lax.dot_general(
+            dm_all[b], w_ref[...], nt, preferred_element_type=FULL
+        ).astype(LOW)
+        for h in range(heads):
+            at = slice(h * HEAD_SIZE, (h + 1) * HEAD_SIZE)
+            here = slice(h * length, (h + 1) * length)
+            dm_rows[here, :] = d_mixed[:, at]
+            units, _ = unit(proj_ref[b, :, at])
+            q_rows[here, :] = turned(units * gain_query)
+        key_units, key_inverse = unit(proj_ref[b, :, count : count + HEAD_SIZE])
+        key = turned(key_units * gain_key)
+        value = proj_ref[b, :, count + HEAD_SIZE :].astype(LOW)
+        probs = probs_ref[b]
+        wide = probs.astype(FULL)
+        d_probs = lax.dot_general(dm_rows[...], value, nt, preferred_element_type=FULL)
+        d_scores = wide * (d_probs - jnp.sum(d_probs * wide, axis=1, keepdims=True))
+        d_scores = d_scores.astype(LOW)
+        d_query = jnp.dot(d_scores, key, preferred_element_type=FULL) * scaling
+        d_key = lax.dot_general(d_scores, q_rows[...], tn, preferred_element_type=FULL) * scaling
+        d_value = lax.dot_general(probs, dm_rows[...], tn, preferred_element_type=FULL)
+        for h in range(heads):
+            at = slice(h * HEAD_SIZE, (h + 1) * HEAD_SIZE)
+            units, inverse = unit(proj_ref[b, :, at])
+            got = back(d_query[h * length : (h + 1) * length], units, inverse, gain_query, 0)
+            dproj_ref[b, :, at] = got.astype(LOW)
+        got = back(d_key, key_units, key_inverse, gain_key, 1)
+        dproj_ref[b, :, count : count + HEAD_SIZE] = got.astype(LOW)
+        dproj_ref[b, :, count + HEAD_SIZE :] = d_value.astype(LOW)
+
+        i = b - (owners - 2 * planes + 2)
+        distance = (2 * planes - 2 - i + 1) // 2
+        sp = s + (2 * (i % 2) - 1) * (0 - distance)
+
+        @pl.when((i >= 0) & (sp >= 0) & (sp < planes))
+        def _():
+            line(sp)
+
+        return carry
+
+    lax.fori_loop(0, owners, attend, 0)
+    line(s)
+    sum_ref[...] = chunk(s)[...]
+    sent()
+    for other in range(owners):
+
+        @pl.when(other != e)
+        def _(other=other):
+            spread(other).wait_send()
+
+    def drain(sp, carry):
+        @pl.when(sp > s)
+        def _():
+            up(sp).wait_send()
+
+        @pl.when(sp < s)
+        def _():
+            down(sp).wait_send()
+
+        return carry
+
+    lax.fori_loop(0, planes, drain, 0)
+
+
+def add_blocks(target, other):
+    step = min(128, target.shape[1])
+    for lead in range(target.shape[0]):
+
+        def one(r, carry, lead=lead):
+            at = pl.ds(pl.multiple_of(r * step, step), step)
+            target[lead, at, :] = (
+                target[lead, at, :].astype(FULL) + other[lead, at, :].astype(FULL)
+            ).astype(LOW)
+            return carry
+
+        lax.fori_loop(0, target.shape[1] // step, one, 0)
+
+
+def back(dm, w, mixed, proj, probs, tail, gains, frequency, planes, owners, identity):
+    length = dm.shape[0]
+    count = w.shape[0]
+    share = MODEL_WIDTH // owners
+    lanes = owners // planes
+    return pl.pallas_call(
+        functools.partial(back_kernel, planes, owners),
+        out_shape=[
+            jax.ShapeDtypeStruct(proj.shape, LOW),
+            jax.ShapeDtypeStruct((lanes, count, share), LOW),
+            jax.ShapeDtypeStruct((8, HEAD_SIZE), FULL),
+        ],
+        in_specs=[VM] * 8,
+        out_specs=[VM] * 3,
+        scratch_shapes=[
+            pltpu.VMEM((owners, length, MODEL_WIDTH), LOW),
+            pltpu.VMEM((count, owners * length), LOW),
+            pltpu.VMEM((count, MODEL_WIDTH), LOW),
+            pltpu.VMEM((owners, count, share), LOW),
+            pltpu.VMEM((planes, lanes, count, share), LOW),
+            pltpu.VMEM((planes, lanes, count, share), LOW),
+            pltpu.VMEM((length * count // HEAD_SIZE, HEAD_SIZE), LOW),
+            pltpu.VMEM((length * count // HEAD_SIZE, HEAD_SIZE), LOW),
+            DMA(()),
+            DMA((2,)),
+            DMA((2,)),
+            DMA((2,)),
+            DMA((2,)),
+            DMA((4,)),
+            DMA((4,)),
+            DMA((owners,)),
+            DMA((owners,)),
             DMA((2, planes)),
             DMA((2, planes)),
         ],
         compiler_params=pltpu.CompilerParams(
             collective_id=identity, has_side_effects=True, vmem_limit_bytes=VMEM_LIMIT
         ),
-    )(place, v)
-
-
-def per_device(
+    )(dm, w, mixed, proj, probs, tail, gains, frequency)
+
+
+def share_kernel(
+    planes, owners, h1_ref, dproj_ref, w_ref, unit_ref, tail_ref, sum_ref,
+    out_rows, out_head, out_rest, dh1_ref,
+    acc_head, acc_rest, u_head, u_rest, d_head, d_rest, column, mine, away, c_in, x_in, y_in, x_half, y_half,
+    z_send, z_recv, x_send, x_recv, y_send, y_recv, c_send, c_recv, own_sem,
+    pc_send, pc_recv, px_send, px_recv, py_send, py_recv,
+):
+    e, core, flip_x, flip_y, diagonal = neighbours()
+    s = lax.axis_index("shard")
+    deep = acc_head.shape[1] * acc_head.shape[2]
+    half = deep // 2
+    wide = acc_head.shape[3]
+    acc = (None, acc_head, acc_rest)
+    up_in = (None, u_head, u_rest)
+    down_in = (None, d_head, d_rest)
+    outs = (out_rows, out_head, out_rest)
+    tn = (((0,), (0,)), ((), ()))
+
+    def arrived(block, sem):
+        send(block, block, sem, sem, (core, s)).wait_recv()
+
+    greet(planes)
+
+    def chunk(k, sp):
+        return sum_ref if k == 0 else acc[k].at[sp]
+
+    def make(k, sp):
+        at = pl.ds(pl.multiple_of(sp * deep, deep), deep)
+        left = h1_ref[:, :, at].reshape(-1, deep)
+        columns_at = slice(0, wide) if k == 1 else slice(wide, None)
+        right = dproj_ref[:, :, columns_at]
+        right = right.reshape(-1, right.shape[-1])
+        got = lax.dot_general(left, right, tn, preferred_element_type=FULL).astype(LOW)
+        got = got.reshape(2, half, got.shape[-1])
+        if k == 1:
+            acc_head[sp] = got
+        else:
+            acc_rest[sp, :, :, : got.shape[-1]] = got
+            at = pl.ds(pl.multiple_of(sp * deep, deep), deep)
+            row = jnp.sum(dh1_ref[:, at] * unit_ref[:, at], axis=0, keepdims=True)
+            column[GAIN_ONE : GAIN_ONE + 1, :] = row
+            extra = column[...].T.reshape(2, half, TAIL)
+            acc_rest[sp, :, :, got.shape[-1] :] = (tail_ref[sp].astype(FULL) + extra).astype(LOW)
+
+    def up(k, sp):
+        return send(
+            chunk(k, sp), up_in[k].at[sp], z_send.at[k, 0, sp], z_recv.at[k, 0, sp], (e, s + 1)
+        )
+
+    def down(k, sp):
+        return send(
+            chunk(k, sp), down_in[k].at[sp], z_send.at[k, 1, sp], z_recv.at[k, 1, sp], (e, s - 1)
+        )
+
+    def line(k, sp):
+        make(k, sp)
+
+        @pl.when((sp >= s) & (s > 0))
+        def _():
+            arrived(up_in[k].at[sp], z_recv.at[k, 0, sp])
+            add_blocks(chunk(k, sp), up_in[k].at[sp])
+
+        @pl.when((sp <= s) & (s < planes - 1))
+        def _():
+            arrived(down_in[k].at[sp], z_recv.at[k, 1, sp])
+            add_blocks(chunk(k, sp), down_in[k].at[sp])
+
+        @pl.when(sp > s)
+        def _():
+            up(k, sp).start()
+
+        @pl.when(sp < s)
+        def _():
+            down(k, sp).start()
+
+    def pair(k, n):
+        for i in (2 * n, 2 * n - 1):
+            sp = s + (2 * (i % 2) - 1) * n
+
+            @pl.when((sp >= 0) & (sp < planes))
+            def _(sp=sp):
+                line(k, sp)
+
+    def steps(k):
+        count = outs[k].shape[1] // 2
+        return gather_steps(
+            lambda lane: outs[k].at[lane],
+            lambda lane, at: outs[k].at[lane, pl.ds(at * count, count)],
+            chunk(k, s),
+            lambda n: x_send.at[k, n],
+            lambda n: x_recv.at[k, n],
+            lambda n: y_send.at[k, n],
+            lambda n: y_recv.at[k, n],
+            lambda n: c_send.at[k, n],
+            lambda n: c_recv.at[k, n],
+        )
+
+    def keep(k):
+        return pltpu.make_async_copy(chunk(k, s), outs[k].at[e], own_sem.at[k])
+
+    def share(k):
+        steps(k)[0]()
+        keep(k).start()
+
+    p_begin, p_middle, p_finish, p_sent = project_steps(
+        True, dproj_ref, w_ref, dh1_ref, mine, away, c_in, x_in, y_in, x_half, y_half,
+        pc_send, pc_recv, px_send, px_recv, py_send, py_recv,
+    )
+    share(0)
+    column[...] = jnp.zeros_like(column)
+    pair(1, planes - 1)
+    p_begin()
+    for n in range(planes - 2, 1, -1):
+        pair(1, n)
+    p_middle()
+    pair(1, 1)
+    p_finish()
+    pair(2, planes - 1)
+    steps(0)[1]()
+    line(1, s)
+    share(1)
+    for n in range(planes - 2, 1, -1):
+        pair(2, n)
+    steps(0)[2]()
+    pair(2, 1)
+    steps(1)[1]()
+    line(2, s)
+    share(2)
+    steps(1)[2]()
+    steps(2)[1]()
+    steps(2)[2]()
+    for k in range(3):
+        keep(k).wait()
+        steps(k)[3]()
+        steps(k)[4]()
+    p_sent()
+
+    def drain(sp, carry):
+        for k in (1, 2):
+
+            @pl.when(sp > s)
+            def _(k=k):
+                up(k, sp).wait_send()
+
+            @pl.when(sp < s)
+            def _(k=k):
+                down(k, sp).wait_send()
+
+        return carry
+
+    lax.fori_loop(0, planes, drain, 0)
+
+
+def share_grads(h1, dproj, w_all, units, tail, row_sum, planes, owners, identity):
+    length = h1.shape[1]
+    deep = MODEL_WIDTH // planes
+    query_cols = dproj.shape[2] - 2 * HEAD_SIZE
+    head = (2, deep // 2, query_cols)
+    rest = (2, deep // 2, 2 * HEAD_SIZE + tail.shape[-1])
+    tail = tail.reshape(planes, 2, deep // 2, -1)
+    block = (length, MODEL_WIDTH)
+    part = (length // 2, MODEL_WIDTH)
+
+    def per_plane(*shapes):
+        return [pltpu.VMEM((planes,) + shape, LOW) for shape in shapes]
+
+    return pl.pallas_call(
+        functools.partial(share_kernel, planes, owners),
+        out_shape=[
+            jax.ShapeDtypeStruct((owners,) + shape, LOW)
+            for shape in (row_sum.shape, head, rest)
+        ]
+        + [jax.ShapeDtypeStruct(block, FULL)],
+        in_specs=[VM] * 6,
+        out_specs=[ANY, ANY, ANY, VM],
+        scratch_shapes=per_plane(head, rest)
+        + per_plane(head, rest)
+        + per_plane(head, rest)
+        + [
+            pltpu.VMEM((TAIL, deep), FULL),
+            pltpu.VMEM((4,) + block, LOW),
+            pltpu.VMEM((4,) + block, LOW),
+            pltpu.VMEM((4,) + block, LOW),
+            pltpu.VMEM(block, LOW),
+            pltpu.VMEM(block, LOW),
+            pltpu.VMEM(part, LOW),
+            pltpu.VMEM(part, LOW),
+            DMA((3, 2, planes)),
+            DMA((3, 2, planes)),
+            DMA((3, 2)),
+            DMA((3, 2)),
+            DMA((3, 2)),
+            DMA((3, 2)),
+            DMA((3, 4)),
+            DMA((3, 4)),
+            DMA((3,)),
+            DMA((4,)),
+            DMA((4,)),
+            DMA((2,)),
+            DMA((2,)),
+            DMA((2,)),
+            DMA((2,)),
+        ],
+        compiler_params=pltpu.CompilerParams(
+            collective_id=identity, has_side_effects=True, vmem_limit_bytes=VMEM_LIMIT
+        ),
+    )(h1, dproj, w_all, units, tail, row_sum)
+
+
+def gathered_layer(
     tokens,
     segments,
     routes,
@@ -790,8 +1875,9 @@
     gates = named * chance / chosen_sum
     gates_high = gates.astype(LOW)
     gates_rest = (gates - gates_high.astype(FULL)).astype(LOW)
-    h_rows = jnp.concatenate([h2, gates_high, gates_rest], axis=1)
-    resident_pass = blocks * length * h_rows.shape[1] * 2 <= RESIDENT
+    h_all = lax.all_gather(
+        jnp.concatenate([h2, gates_high, gates_rest], axis=1), both, axis=0, tiled=False
+    )
 
     route_all = d_all[:, :, MODEL_WIDTH : MODEL_WIDTH + TOPK].astype(FULL)
     own_experts = (me * EXP_DEV + jnp.arange(EXP_DEV, dtype=jnp.int32)).astype(FULL)
@@ -800,102 +1886,84 @@
     rank = dot("ts,bsj->btj", earlier, match.astype(LOW))
     slot_ids = jnp.arange(capacity, dtype=jnp.int32).astype(FULL)
     place = jnp.where(match > 0, rank, -1.0).transpose(0, 2, 1)
-    if resident_pass:
-        place = place.reshape(owners // 2, 2, planes, EXP_DEV, length)
-        offset = (capacity * jnp.arange(2, dtype=jnp.int32)).astype(FULL)
-        place = jnp.where(place >= 0, place + offset[:, None, None, None], -1.0)
-        place = place.transpose(0, 2, 3, 1, 4).reshape(blocks // 2, EXP_DEV, 2 * length)
-        lanes = jnp.arange(2 * experts_all, dtype=jnp.int32) % experts_all
-        own = (me * EXP_DEV + jnp.arange(EXP_DEV, dtype=jnp.int32))[:, None] == lanes
-        sel = jnp.broadcast_to(own.astype(FULL)[:, None, :], (EXP_DEV, 8, 2 * experts_all))
-        slots = 2 * capacity
-        x, dy = gather_dispatch(
-            h_rows, d_all.reshape(owners, planes, length, -1), place, planes, slots, 1
+    dispatch = (place[:, :, None, :] == slot_ids[:, None]).astype(LOW)
+
+    def experts(h_rows, d_rows, gate_high, gate_rest, put):
+        count = h_rows.shape[0]
+        flat = put.reshape(count, EXP_DEV * capacity, length)
+        x = dot("bst,btd->bsd", flat, h_rows).astype(LOW)
+        dy = dot("bst,btd->bsd", flat, d_rows).astype(LOW)
+
+        def by_expert(v):
+            v = v.reshape(count, EXP_DEV, capacity, v.shape[-1])
+            return v.transpose(1, 0, 2, 3).reshape(EXP_DEV, count * capacity, v.shape[-1])
+
+        def by_block(v):
+            v = v.reshape(EXP_DEV, count, capacity, v.shape[-1])
+            return v.transpose(1, 0, 2, 3).reshape(count, EXP_DEV * capacity, v.shape[-1])
+
+        x, dy = by_expert(x), by_expert(dy)
+        gate_slot = dot("bjct,btj->jbc", put, gate_high) + dot("bjct,btj->jbc", put, gate_rest)
+        gate_slot = gate_slot.reshape(EXP_DEV, count * capacity, 1)
+        g = dot("erd,efd->erf", x, w_gate)
+        u = dot("erd,efd->erf", x, w_up)
+        da = dot("erd,edf->erf", dy, w_down)
+        sigma = jax.nn.sigmoid(g)
+        silu = g * sigma
+        act = (silu * u).astype(LOW).astype(FULL)
+        d_gate_slot = jnp.sum(act * da, axis=-1)
+        act_gated = (act * gate_slot).astype(LOW)
+        d_act = da * gate_slot
+        dg = (d_act * u * sigma * (1.0 + g * (1.0 - sigma))).astype(LOW)
+        du = (d_act * silu).astype(LOW)
+        y = dot("erf,edf->erd", act_gated, w_down).astype(LOW)
+        d_down = dot("erd,erf->edf", dy, act_gated)
+        d_gate = dot("erf,erd->efd", dg, x)
+        d_up = dot("erf,erd->efd", du, x)
+        dx = (dot("erf,efd->erd", dg, w_gate) + dot("erf,efd->erd", du, w_up)).astype(LOW)
+        mix = dot("bst,bsd->btd", flat, by_block(y)).astype(LOW)
+        d_h = dot("bst,bsd->btd", flat, by_block(dx)).astype(LOW)
+        d_g = dot(
+            "bjct,jbc->btj", put.astype(FULL), d_gate_slot.reshape(EXP_DEV, count, capacity)
         )
-        y, dx, d_gate, d_up, d_down = expert_pass(sel, x, dy, w_gate, w_up, w_down)
-        d_home = combine_home(place, dx, length, planes, slots, 2)
-        mixture = combine_home(place, y, length, planes, slots, 3)
-    else:
-        dispatch = (place[:, :, None, :] == slot_ids[:, None]).astype(LOW)
-
-        def experts(h_rows, d_rows, gate_high, gate_rest, put):
-            count = h_rows.shape[0]
-            flat = put.reshape(count, EXP_DEV * capacity, length)
-            x = dot("bst,btd->bsd", flat, h_rows).astype(LOW)
-            dy = dot("bst,btd->bsd", flat, d_rows).astype(LOW)
-
-            def by_expert(v):
-                v = v.reshape(count, EXP_DEV, capacity, v.shape[-1])
-                return v.transpose(1, 0, 2, 3).reshape(EXP_DEV, count * capacity, v.shape[-1])
-
-            def by_block(v):
-                v = v.reshape(EXP_DEV, count, capacity, v.shape[-1])
-                return v.transpose(1, 0, 2, 3).reshape(count, EXP_DEV * capacity, v.shape[-1])
-
-            x, dy = by_expert(x), by_expert(dy)
-            gate_slot = dot("bjct,btj->jbc", put, gate_high) + dot("bjct,btj->jbc", put, gate_rest)
-            gate_slot = gate_slot.reshape(EXP_DEV, count * capacity, 1)
-            g = dot("erd,efd->erf", x, w_gate)
-            u = dot("erd,efd->erf", x, w_up)
-            da = dot("erd,edf->erf", dy, w_down)
-            sigma = jax.nn.sigmoid(g)
-            silu = g * sigma
-            act = (silu * u).astype(LOW).astype(FULL)
-            d_gate_slot = jnp.sum(act * da, axis=-1)
-            act_gated = (act * gate_slot).astype(LOW)
-            d_act = da * gate_slot
-            dg = (d_act * u * sigma * (1.0 + g * (1.0 - sigma))).astype(LOW)
-            du = (d_act * silu).astype(LOW)
-            y = dot("erf,edf->erd", act_gated, w_down).astype(LOW)
-            d_down = dot("erd,erf->edf", dy, act_gated)
-            d_gate = dot("erf,erd->efd", dg, x)
-            d_up = dot("erf,erd->efd", du, x)
-            dx = (dot("erf,efd->erd", dg, w_gate) + dot("erf,efd->erd", du, w_up)).astype(LOW)
-            mix = dot("bst,bsd->btd", flat, by_block(y)).astype(LOW)
-            d_h = dot("bst,bsd->btd", flat, by_block(dx)).astype(LOW)
-            d_g = dot(
-                "bjct,jbc->btj", put.astype(FULL), d_gate_slot.reshape(EXP_DEV, count, capacity)
-            )
-            return mix, d_h, d_g, d_gate, d_up, d_down
-
-        h_all = lax.all_gather(h_rows, both, axis=0, tiled=False)
-        gate_cols = lax.dynamic_slice_in_dim(h_all, MODEL_WIDTH + me * EXP_DEV, EXP_DEV, 2)
-        rest_cols = lax.dynamic_slice_in_dim(
-            h_all, MODEL_WIDTH + experts_all + me * EXP_DEV, EXP_DEV, 2
+        return mix, d_h, d_g, d_gate, d_up, d_down
+
+    gate_cols = lax.dynamic_slice_in_dim(h_all, MODEL_WIDTH + me * EXP_DEV, EXP_DEV, 2)
+    rest_cols = lax.dynamic_slice_in_dim(
+        h_all, MODEL_WIDTH + experts_all + me * EXP_DEV, EXP_DEV, 2
+    )
+    step = min(blocks, GROUP_BLOCKS)
+    mixes, d_hs, d_gs, totals = [], [], [], None
+    for at in range(0, blocks, step):
+        cut = slice(at, at + step)
+        mix, d_h, d_g, *grads = experts(
+            h_all[cut, :, :MODEL_WIDTH],
+            d_all[cut, :, :MODEL_WIDTH],
+            gate_cols[cut],
+            rest_cols[cut],
+            dispatch[cut],
         )
-        step = min(blocks, GROUP_BLOCKS)
-        mixes, d_hs, d_gs, totals = [], [], [], None
-        for at in range(0, blocks, step):
-            cut = slice(at, at + step)
-            mix, d_h, d_g, *grads = experts(
-                h_all[cut, :, :MODEL_WIDTH],
-                d_all[cut, :, :MODEL_WIDTH],
-                gate_cols[cut],
-                rest_cols[cut],
-                dispatch[cut],
-            )
-            mixes.append(mix)
-            d_hs.append(d_h)
-            d_gs.append(d_g)
-            totals = grads if totals is None else [a + b for a, b in zip(totals, grads)]
-        d_gate, d_up, d_down = totals
-        d_g = jnp.concatenate(d_gs, axis=0)
-        spread = jnp.zeros((blocks, length, 2 * experts_all), LOW)
-        spread = lax.dynamic_update_slice_in_dim(spread, d_g.astype(LOW), me * EXP_DEV, 2)
-        d_h_wide = jnp.concatenate([jnp.concatenate(d_hs, axis=0), spread], axis=2)
-
-        def home(v):
-            v = v.reshape(owners, planes, length, v.shape[-1])
-            v = lax.psum_scatter(v, "expert", scatter_dimension=0, tiled=False)
-            return lax.psum_scatter(v, "shard", scatter_dimension=0, tiled=False)
-
-        d_home = home(d_h_wide)
-        mixture = home(jnp.concatenate(mixes, axis=0))
+        mixes.append(mix)
+        d_hs.append(d_h)
+        d_gs.append(d_g)
+        totals = grads if totals is None else [a + b for a, b in zip(totals, grads)]
+    d_gate, d_up, d_down = totals
+    d_g = jnp.concatenate(d_gs, axis=0)
+    spread = jnp.zeros((blocks, length, TAIL), LOW)
+    spread = lax.dynamic_update_slice_in_dim(spread, d_g.astype(LOW), me * EXP_DEV, 2)
+    d_h_wide = jnp.concatenate([jnp.concatenate(d_hs, axis=0), spread], axis=2)
+
+    def home(v):
+        v = v.reshape(owners, planes, length, v.shape[-1])
+        v = lax.psum_scatter(v, "expert", scatter_dimension=0, tiled=False)
+        return lax.psum_scatter(v, "shard", scatter_dimension=0, tiled=False)
+
+    d_home = home(d_h_wide)
+    mixture = home(jnp.concatenate(mixes, axis=0))
     result = (middle + mixture.astype(FULL)).astype(LOW)
 
     upstream = d_out.astype(FULL)
-    d_gates = d_home[:, MODEL_WIDTH:].astype(FULL)
-    d_gates = d_gates[:, :experts_all] + d_gates[:, experts_all:]
+    d_gates = d_home[:, MODEL_WIDTH : MODEL_WIDTH + experts_all].astype(FULL)
     d_chance = named * (d_gates - jnp.sum(d_gates * gates, axis=1, keepdims=True)) / chosen_sum
     d_logits = chance * (d_chance - jnp.sum(d_chance * chance, axis=1, keepdims=True))
     d_logits = d_logits.astype(LOW)
@@ -981,6 +2049,157 @@
     )
 
 
+def resident_layer(
+    tokens,
+    segments,
+    routes,
+    attn_gain,
+    qkv_weight,
+    query_gain,
+    k_gain,
+    w_out,
+    ffn_gain,
+    router,
+    w_gate,
+    w_up,
+    w_down,
+    d_out,
+):
+    owners = lax.axis_size("expert")
+    planes = lax.axis_size("shard")
+    me = lax.axis_index("expert")
+    plane = lax.axis_index("shard")
+    length = tokens.shape[0]
+    blocks = owners * planes
+    experts_all = router.shape[1]
+    capacity = 3 * length * TOPK // (2 * experts_all)
+    slots = 2 * capacity
+    heads = QUERY_HEADS // owners
+    query_cols = heads * HEAD_SIZE
+    qkv_cols = query_cols + 2 * HEAD_SIZE
+    scaling = HEAD_SIZE ** (-0.5)
+    rows_in = qkv_weight.shape[0]
+    per = query_gain.shape[0]
+
+    kv_head = me * KEY_VALUE_HEADS // owners
+    k_at = QUERY_HEADS * HEAD_SIZE + kv_head * HEAD_SIZE
+    v_at = k_at + KEY_VALUE_HEADS * HEAD_SIZE
+    mine = jnp.concatenate(
+        [
+            lax.dynamic_slice_in_dim(qkv_weight, me * query_cols, query_cols, 1),
+            lax.dynamic_slice_in_dim(qkv_weight, k_at, HEAD_SIZE, 1),
+            lax.dynamic_slice_in_dim(qkv_weight, v_at, HEAD_SIZE, 1),
+            columns([router], rows_in),
+        ],
+        axis=1,
+    )
+    gain_rows = jnp.zeros((16, rows_in), LOW).at[0].set(attn_gain).at[1].set(ffn_gain)
+    gain_rows = lax.dynamic_update_slice(gain_rows, query_gain[None], (2, plane * per))
+    gain_rows = lax.dynamic_update_slice(gain_rows, k_gain[None], (3, plane * per))
+    segment_row = segments[0]
+    token_tail = columns([segment_row[:, None], positions_of(segment_row)[:, None]], length)
+    token_rows = jnp.concatenate([tokens, token_tail], axis=1)
+    d_rows = jnp.concatenate([d_out, columns([routes], length)], axis=1)
+    half = HEAD_SIZE // 2
+    frequency = THETA ** (-2.0 * jnp.arange(half, dtype=FULL) / HEAD_SIZE)
+    frequency = jnp.broadcast_to(jnp.tile(frequency, 2)[None, :], (8, HEAD_SIZE))
+    d_all, w_mine, w_all, gain_all, tail, h1, projected, probs_low, mixed, branch = front(
+        mine, gain_rows, token_rows, w_out, d_rows, frequency, planes, owners, 5
+    )
+    gains = gain_all.astype(FULL)
+    gain_one, gain_two = gains[:, 0].reshape(-1), gains[:, 1].reshape(-1)
+    router_full = w_all[:, :, qkv_cols : qkv_cols + experts_all].reshape(MODEL_WIDTH, -1)
+
+    places = jnp.arange(length, dtype=jnp.int32)
+    route_all = d_all[..., MODEL_WIDTH : MODEL_WIDTH + TOPK].reshape(blocks, length, TOPK)
+    own_experts = (me * EXP_DEV + jnp.arange(EXP_DEV, dtype=jnp.int32)).astype(FULL)
+    match = jnp.sum((route_all.astype(FULL)[:, :, :, None] == own_experts).astype(FULL), axis=2)
+    earlier = (places[None, :] < places[:, None]).astype(LOW)
+    rank = dot("ts,bsj->btj", earlier, match.astype(LOW))
+    place = jnp.where(match > 0, rank, -1.0).transpose(0, 2, 1)
+    place = place.reshape(owners // 2, 2, planes, EXP_DEV, length)
+    offset = (capacity * jnp.arange(2, dtype=jnp.int32)).astype(FULL)
+    place = jnp.where(place >= 0, place + offset[:, None, None, None], -1.0)
+    place = place.transpose(0, 2, 3, 1, 4).reshape(blocks // 2, EXP_DEV, 2 * length)
+    lanes = jnp.arange(2 * experts_all, dtype=jnp.int32) % experts_all
+    own = (me * EXP_DEV + jnp.arange(EXP_DEV, dtype=jnp.int32))[:, None] == lanes
+    sel = jnp.broadcast_to(own.astype(FULL)[:, None, :], (EXP_DEV, 8, 2 * experts_all))
+
+    middle = tokens.astype(FULL) + branch
+    unit_two, inverse_two = unit_norm(middle)
+    h2 = (unit_two * gain_two).astype(LOW)
+    logits = dot("nd,de->ne", h2, router_full)
+    chance = jax.nn.softmax(logits, axis=-1)
+    named = jnp.sum(
+        (routes[:, :, None] == jnp.arange(experts_all, dtype=jnp.int32)).astype(FULL), axis=1
+    )
+    chosen_sum = jnp.sum(named * chance, axis=1, keepdims=True)
+    gates = named * chance / chosen_sum
+    gates_high = gates.astype(LOW)
+    gates_rest = (gates - gates_high.astype(FULL)).astype(LOW)
+    h_rows = jnp.concatenate([h2, gates_high, gates_rest], axis=1)
+
+    x, dy = gather_dispatch(h_rows, d_all, place, planes, slots, 1)
+    y, dx, d_gate, d_up, d_down = expert_pass(sel, x, dy, w_gate, w_up, w_down.swapaxes(1, 2))
+    d_down = d_down.swapaxes(1, 2)
+    d_home, mixture = combine_home(place, dx, y, length, planes, slots, 2)
+
+    upstream = d_out.astype(FULL)
+    d_gates = d_home[:, MODEL_WIDTH:]
+    d_gates = d_gates[:, :experts_all] + d_gates[:, experts_all:]
+    d_chance = named * (d_gates - jnp.sum(d_gates * gates, axis=1, keepdims=True)) / chosen_sum
+    d_logits = chance * (d_chance - jnp.sum(d_chance * chance, axis=1, keepdims=True))
+    d_logits = d_logits.astype(LOW)
+    d_h2 = d_home[:, :MODEL_WIDTH] + dot("ne,de->nd", d_logits, router_full)
+    d_gain_two = jnp.sum(d_h2 * unit_two, axis=0)
+    d_middle = upstream + norm_back(d_h2, unit_two, inverse_two, gain_two)
+    d_router = dot("nd,ne->de", h2, d_logits)
+
+    d_projected, row_sum, d_gains = back(
+        d_middle.astype(LOW), w_mine, mixed, projected, probs_low, tail, gain_all, frequency,
+        planes, owners, 7,
+    )
+    resident = tokens.astype(FULL)
+    unit_one, inverse_one = unit_norm(resident)
+
+    def by_rows(v):
+        v = v.reshape(planes, per)
+        return jnp.pad(v, ((0, 0), (0, rows_in - per))).reshape(-1)[:, None]
+
+    d_tail = columns(
+        [d_router, d_gain_two[:, None], by_rows(d_gains[0]), by_rows(d_gains[1])], MODEL_WIDTH
+    )
+    *parts, d_h1 = share_grads(
+        h1, d_projected, w_all, unit_one, d_tail, row_sum, planes, owners, 4
+    )
+    d_w_out, d_qkv_weight, d_rest = finish_grads(*parts, owners)
+    result = (middle + mixture).astype(LOW)
+    d_tokens = (d_middle + norm_back(d_h1, unit_one, inverse_one, gain_one)).astype(LOW)
+    d_gain_out = d_rest[:, experts_all:]
+    return (
+        result,
+        d_tokens,
+        d_gain_out[:, GAIN_ONE - experts_all],
+        d_qkv_weight,
+        d_gain_out[:per, 1],
+        d_gain_out[:per, 2],
+        d_w_out,
+        d_gain_out[:, 0],
+        d_rest[:, :experts_all],
+        d_gate,
+        d_up,
+        d_down,
+    )
+
+
+def per_device(*args):
+    blocks = lax.axis_size("expert") * lax.axis_size("shard")
+    row_bytes = 2 * (MODEL_WIDTH + TAIL)
+    if blocks * args[0].shape[0] * row_bytes <= RESIDENT:
+        return resident_layer(*args)
+    return gathered_layer(*args)
+
+
 def solution(mesh):
     placed = (
         P(("expert", "shard"), None),

time: 1200 us -> 826 us (0.69); the launches traced: 1180 us -> 817 us
  waiting for transfers between devices: 400 us -> 0 us
  Pallas kernels: 400 us -> 774 us
  local copies, waits for them, and re-layouts: 167 us -> 20 us
  other arithmetic: 98.3 us -> 18.1 us
  matrix products: 54.9 us -> 3.43 us
  blocking collectives: 40.4 us -> 0 us
  between operations: 17.2 us -> 1.42 us
    pallas_call x0 -> x4, Pallas kernels: none -> 411 us  [the longest x1 205 us: front(): pl.pallas_call(functools.partial(front_kernel, planes, owners), out_shape...]
    all_gather x6 -> x0, waiting for transfers between devices: 211 us -> none  [the longest x1 70 us: per_device(): gathered = lax.all_gather(mine, 'shard', axis=0, tiled=True)]
    reduce_scatter x4 -> x0, waiting for transfers between devices: 160 us -> none  [the longest x1 70.6 us: per_device(): lax.psum_scatter(jnp.concatenate([d_wqkv, d_tail], axis=1), 'shard', scat...]
    unnamed x149 -> x27, local copies, waits for them, and re-layouts: 86.9 us -> 3.06 us
    dot_general x15 -> x4, matrix products: 50.6 us -> 3.43 us  [dot(): return jnp.einsum(spec, left, right, preferred_element_type=FULL)]
    pallas_call x2 -> x1, Pallas kernels: 229 us -> 181 us  [combine_home(): pl.pallas_call(functools.partial(combine_home_kernel, planes, slots), out...]
    all_to_all x1 -> x0, blocking collectives: 40.4 us -> none  [per_device(): lax.all_to_all(d_w_out, 'expert', split_axis=1, concat_axis=0, tiled=False)]
    convert_element_type x12 -> x7, other arithmetic: 33.8 us -> 3.22 us  [the longest x1 1.45 us: resident_layer(): (d_middle + norm_back(d_h1, unit_one, inverse_one, gain_one)).astype(LOW)]
  transfers between devices with their start and end apart: 11 -> 0, of which waited for: 9 -> 0; matrix products, arithmetic and copies ran while one was open for 12% -> 0% of each run, Pallas kernels for 11% -> 0%
where the time goes in v4:
time: 826 us; the launch traced here: 817 us
  Pallas kernels  774 us (94%)
  local copies, waits for them, and re-layouts  20 us (2%)
  other arithmetic  18.1 us (2%)
    pallas_call x1, Pallas kernels, front(): pl.pallas_call(functools.partial(front_kernel, planes, owners), out_shape...  205 us
    pallas_call x1, Pallas kernels, combine_home(): pl.pallas_call(functools.partial(combine_home_kernel, planes, slots), out...  181 us
    pallas_call x1, Pallas kernels, gather_dispatch(): pl.pallas_call(kernel, out_shape=[jax.ShapeDtypeStruct((EXP_DEV, total, w...  104 us
    pallas_call x1, Pallas kernels, back(): pl.pallas_call(functools.partial(back_kernel, planes, owners), out_shape=...  99.1 us
    pallas_call x1, Pallas kernels, share_grads(): pl.pallas_call(functools.partial(share_kernel, planes, owners), out_shape...  93.6 us
    pallas_call x1, Pallas kernels, expert_pass(): pl.pallas_call(expert_kernel, grid=(EXP_DEV,), in_specs=[spec(*sel.shape[...  77.9 us

profile of v4, /device:TPU:0, one launch (start us, length us, event | category | flops | bytes accessed | tf_op | source)
XLA Modules:
  0.0 817.1 jit_solution(13925453772117348238)
XLA Ops:
  0.7 0.9 convert_reduce_fusion.2
  1.6 0.7 convert_bitcast_fusion.1
  2.3 1.3 fusion.3
  3.7 0.7 reshape.248
  4.4 0.7 reshape.249
  5.1 0.7 convert_element_type.167
  5.9 0.6 broadcast_in_dim.25.freq_ref
  6.5 0.8 dynamic_update_slice.6
  7.3 0.8 dynamic_update_slice.7.gain_ref
  8.1 0.6 broadcast_in_dim.28.sel_ref
  9.0 0.7 convert_reduce_fusion.1
  9.8 1.0 copy.66
  10.8 1.0 constant_dynamic-slice_fusion.1
  11.8 1.1 constant_dynamic-slice_fusion.2
  12.9 1.0 fusion.4.w_ref
  13.9 1.1 fusion.5
  15.0 205.2 %shard_map.229 = (bf16[8,4,128,2176]{3,2,1,0:T(8,128)(2,1)}, bf16[512,2048]{1,0:T(8,128)(2,1)}, bf16[4,512,896]{2,1,0:T(8,128)(2,1)}, bf16[4,16,512]{2,1,0:T(8,1...) custom-call(bf16[512,896]{1,0:T(8,128)(2,1)} %fusion.4.w_ref, ...), custom_call_target="tpu_custom_call" | custom-call | tf_op jit(solution)/shard_map/pallas_call | solution.py:1140
  220.2 0.8 fusion.19
  221.0 1.9 slice.83
  222.9 1.3 slice.81
  224.2 0.3 bitcast_convert_fusion
  224.5 0.6 copy.69
  225.1 0.2 convert_reduce_fusion
  225.4 0.7 add_select_fusion
  226.2 2.6 multiply_reduce_fusion.3
  228.9 0.4 fusion.20
  229.4 0.2 fusion.12
  229.5 0.2 fusion.17
  229.9 0.9 concatenate.26.x_ref
  230.8 103.7 %shard_map.230 = (bf16[8,768,2176]{2,1,0:T(8,128)(2,1)}, bf16[8,768,2048]{2,1,0:T(8,128)(2,1)}) custom-call(bf16[128,2176]{1,0:T(8,128)(2,1)} %concatenate.26.x_ref, bf16[8,4,128,2176]{3,2,1,0:T(8,128)(2,1)} %get-tuple-element.66.d_ref, f32[16,8,256]{2,1,0:T(8,128)} %bitcast.51), custom_call_target="tpu_custom_call" | custom-call | tf_op jit(solution)/shard_map/pallas_call | solution.py:314
  334.5 77.9 %shard_map.231 = (bf16[8,768,2048]{2,1,0:T(8,128)(2,1)}, bf16[8,768,2176]{2,1,0:T(8,128)(2,1)}, f32[8,192,2048]{2,1,0:T(8,128)}, f32[8,192,2048]{2,1,0:T(8,128)}, f32[8,192,2048]{2,1,0:T(8,128)}) custom-call(f32[8,8,128]{2,1,0:T(8,128)} %broadcast_in_dim.28.sel_ref, bf16[8,768,2176]{2,1,0:T(8,128)(2,1)} %get-tuple-element.69.x_ref, ...), custom_call_target="tpu_custom_call" | custom-call | flops 43486543872 | bytes 167772160 | tf_op jit(solution)/shard_map/pallas_call | solution.py:416
  412.5 181.4 %shard_map.232 = (f32[128,2176]{1,0:T(8,128)}, f32[128,2048]{1,0:T(8,128)}) custom-call(f32[16,8,256]{2,1,0:T(8,128)} %bitcast.52, bf16[8,768,2176]{2,1,0:T(8,128)(2,1)} %get-tuple-element.71.v_ref, bf16[8,768,2048]{2,1,0:T(8,128)(2,1)} %get-tuple-element.72.m_ref), custom_call_target="tpu_custom_call" | custom-call | tf_op jit(solution)/shard_map/pallas_call | solution.py:655
  593.9 1.1 multiply_reduce_fusion.5
  595.0 1.2 multiply_reduce_fusion.4
  596.1 1.8 multiply_reduce_fusion.1
  598.0 1.1 convolution_convert_fusion
  599.1 1.1 fusion.16.dm_ref
  600.2 99.1 %shard_map.233 = (bf16[8,128,768]{2,1,0:T(8,128)(2,1)}, bf16[2,512,256]{2,1,0:T(8,128)(2,1)}, f32[8,128]{1,0:T(8,128)}) custom-call(bf16[128,2048]{1,0:T(8,128)(2,1)} %fusion.16.dm_ref, bf16[512,2048]{1,0:T(8,128)(2,1)} %get-tuple-element.76.w_ref, bf16[8,128,512]{2,1,0:T(8,128)(2,1)} %get-tuple-element.77.mixed_ref, ...), custom_call_target="tpu_custom_call" | custom-call | tf_op jit(solution)/shard_map/pallas_call | solution.py:1498
  699.3 0.7 convert.11
  700.3 0.3 copy.77
  700.6 0.9 pad.35.clone
  701.5 93.6 %shard_map.234 = (bf16[8,2,512,256]{3,2,1,0:T(8,128)(2,1)}, bf16[8,2,256,512]{3,2,1,0:T(8,128)(2,1)}, bf16[8,2,256,384]{3,2,1,0:T(8,128)(2,1)}, f32[128,2048]{1,0:T(8,128)}) custom-call(bf16[8,128,2048]{2,1,0:T(8,128)(2,1)} %get-tuple-element.75.h1_ref, bf16[8,128,768]{2,1,0:T(8,128)(2,1)} %get-tuple-element.81.dproj_ref, ...), custom_call_target="tpu_custom_call" | custom-call | tf_op jit(solution)/shard_map/pallas_call | solution.py:1700
  795.1 1.6 multiply_reduce_fusion
  796.7 1.4 add_convert_fusion
  798.2 13.3 %shard_map.235 = (f32[1024,2048]{1,0:T(8,128)}, f32[512,5120]{1,0:T(8,128)}, f32[512,128]{1,0:T(8,128)}) custom-call(bf16[8,1024,256]{2,1,0:T(8,128)(2,1)} %bitcast.47, bf16[8,512,512]{2,1,0:T(8,128)(2,1)} %bitcast.48, bf16[8,512,384]{2,1,0:T(8,128)(2,1)} %bitcast.43, bf16[8,512,384]{2,1,0:T(8,128)(2,1)} %bitcast.44), custom_call_target="tpu_custom_call" | custom-call | tf_op jit(solution)/shard_map/pallas_call | solution.py:752
  811.5 1.5 slice_reduce_fusion.2
  813.0 2.0 slice_reduce_fusion
  815.0 1.7 copy.76
  (51 shorter events, 1.5 us)
Async XLA Ops:
  2.3 11.6 %copy-start = (bf16[128,2048]{1,0:T(8,128)(2,1)S(1)}, bf16[128,2048]{1,0:T(8,128)(2,1)}, u32[]{:S(2)}) copy-start(bf16[128,2048]{1,0:T(8,128)(2,1)} %param.18) | copy-start | bytes 1572868
  2.3 11.6 %copy-start.1 = (bf16[128,2048]{1,0:T(8,128)(2,1)S(1)}, bf16[128,2048]{1,0:T(8,128)(2,1)}, u32[]{:S(2)}) copy-start(bf16[128,2048]{1,0:T(8,128)(2,1)} %param.31) | copy-start | bytes 1572868
  8.1 6.9 copy-start.9
  226.2 2.7 copy-start.4
  412.5 183.7 %copy-start.5 = (bf16[4,512,64]{2,1,0:T(8,128)(2,1)S(1)}, bf16[4,512,64]{2,1,0:T(8,128)(2,1)}, u32[]{:S(2)}) copy-start(bf16[4,512,64]{2,1,0:T(8,128)(2,1)} %slice.83) | copy-start | bytes 786436
  596.1 2.9 copy-start.2
  600.2 100.0 %copy-start.7 = (bf16[2048,64]{0,1:T(8,128)(2,1)S(1)}, bf16[2048,64]{0,1:T(8,128)(2,1)}, u32[]{:S(2)}) copy-start(bf16[2048,64]{0,1:T(8,128)(2,1)} %convolution_convert_fusion) | copy-start | bytes 786436
  701.5 95.2 %copy-start.3 = (bf16[128,2048]{1,0:T(8,128)(2,1)S(1)}, bf16[128,2048]{1,0:T(8,128)(2,1)}, u32[]{:S(2)}) copy-start(bf16[128,2048]{1,0:T(8,128)(2,1)} %param.31) | copy-start | bytes 1572868
  701.5 95.2 %copy-start.8 = (f32[128,2048]{1,0:T(8,128)S(1)}, f32[128,2048]{1,0:T(8,128)}, u32[]{:S(2)}) copy-start(f32[128,2048]{1,0:T(8,128)} %get-tuple-element.73) | copy-start | bytes 3145732
  795.1 1.7 copy-start.6

commit v5 on v4

--- a/solution.py
+++ b/solution.py
@@ -14,7 +14,7 @@
 TOPK = 8
 EXP_DEV = 8
 TAIL = 128
-GAIN_ONE = 67
+GAIN_QUERY, GAIN_KEY, GAIN_ONE = 65, 66, 67
 GROUP_BLOCKS = 32
 RESIDENT = 20 << 20
 
@@ -345,17 +345,16 @@
 
 def expert_kernel(
     sel_ref, x_ref, dy_ref, wg_ref, wu_ref, wd_ref,
-    y_ref, dx_ref, dwg_ref, dwu_ref, dwd_ref, a_all, dg_all, du_all,
+    y_ref, dx_ref, dwg_ref, dwu_ref, dwd_ref, a_all, dg_all, du_all, a_t, d_t,
 ):
     rows = x_ref.shape[1]
-    step = 256
+    step = rows
     experts = sel_ref.shape[2] // 2
     sel = sel_ref[0, 0:1, :]
     lane = lax.broadcasted_iota(jnp.int32, sel.shape, 1)
     high_sel = jnp.where(lane < experts, sel, 0.0)
     rest_sel = sel - high_sel
     nt = (((1,), (1,)), ((), ()))
-    tn = (((0,), (0,)), ((), ()))
 
     def chunk(r, carry):
         at = pl.ds(pl.multiple_of(r * step, step), step)
@@ -386,18 +385,18 @@
         return carry
 
     lax.fori_loop(0, rows // step, chunk, 0)
+    hidden = a_t.shape[0]
+    a_t[...] = a_all[...].T
+    d_t[:hidden, :] = dg_all[...].T
+    d_t[hidden:, :] = du_all[...].T
 
     def tile(t, carry):
         at = pl.ds(pl.multiple_of(t * TILE, TILE), TILE)
-        dwg_ref[0, :, at] = lax.dot_general(
-            dg_all[...], x_ref[0, :, at], tn, preferred_element_type=FULL
-        )
-        dwu_ref[0, :, at] = lax.dot_general(
-            du_all[...], x_ref[0, :, at], tn, preferred_element_type=FULL
-        )
-        dwd_ref[0, :, at] = lax.dot_general(
-            a_all[...], dy_ref[0, :, at], tn, preferred_element_type=FULL
-        )
+        x = x_ref[0, :, at]
+        got = jnp.dot(d_t[...], x, preferred_element_type=FULL)
+        dwg_ref[0, :, at] = got[:hidden]
+        dwu_ref[0, :, at] = got[hidden:]
+        dwd_ref[0, :, at] = jnp.dot(a_t[...], dy_ref[0, :, at], preferred_element_type=FULL)
         return carry
 
     lax.fori_loop(0, MODEL_WIDTH // TILE, tile, 0)
@@ -438,7 +437,8 @@
             out(hidden, MODEL_WIDTH, dtype=FULL),
             out(hidden, MODEL_WIDTH, dtype=FULL),
         ],
-        scratch_shapes=[pltpu.VMEM((rows, hidden), LOW)] * 3,
+        scratch_shapes=[pltpu.VMEM((rows, hidden), LOW)] * 3
+        + [pltpu.VMEM((hidden, rows), LOW), pltpu.VMEM((2 * hidden, rows), LOW)],
         compiler_params=pltpu.CompilerParams(vmem_limit_bytes=VMEM_LIMIT),
         cost_estimate=pl.CostEstimate(
             flops=EXP_DEV * rows * MODEL_WIDTH * hidden * 18,
@@ -449,9 +449,9 @@
 
 
 def combine_home_kernel(
-    planes, slots, place_ref, v_ref, m_ref, out_ref, mix_ref,
-    hot, hot_t, load, mine, away, c_in, x_in, y_in, x_half, y_half, u_in, d_in,
-    in_sem, free, c_send, c_recv, x_send, x_recv, y_send, y_recv, z_send, z_recv,
+    planes, slots, hot_ref, v_ref, m_ref, out_ref, mix_ref,
+    hot, load, mine, away, c_in, x_in, y_in, x_half, y_half, u_in, d_in,
+    hot_sem, in_sem, free, c_send, c_recv, x_send, x_recv, y_send, y_recv, z_send, z_recv,
 ):
     e, core, flip_x, flip_y, diagonal = neighbours()
     s = lax.axis_index("shard")
@@ -461,6 +461,7 @@
     half = length // 2
     low_half, high_half = pl.ds(0, half), pl.ds(half, half)
     order = (q_d, q_x, q_y, q_own)
+    spans = (pl.ds(0, width), pl.ds(0, MODEL_WIDTH))
 
     def fetch(kind, k, sp):
         rows = pl.ds(pl.multiple_of((order[k] * planes + sp) * slots, 16), slots)
@@ -470,45 +471,50 @@
             m_ref.at[:, rows, :], load.at[k % 2, :, :, pl.ds(0, MODEL_WIDTH)], in_sem.at[k % 2]
         )
 
+    def fetch_hot(k, sp):
+        return pltpu.make_async_copy(
+            hot_ref.at[order[k] * planes + sp], hot.at[k % 2], hot_sem.at[k % 2]
+        )
+
     def to_core(kind, q, sp):
         return send(
-            away.at[q, sp], c_in.at[q, sp], c_send.at[kind, q, sp], c_recv.at[kind, q, sp],
+            away.at[q, sp, :, spans[kind]], c_in.at[q, sp, :, spans[kind]], c_send.at[kind, q, sp], c_recv.at[kind, q, sp],
             (core, s),
         )
 
     def halves(kind, sp):
         return [
             send(
-                mine.at[q_d, sp, low_half], y_half.at[kind, sp],
+                mine.at[q_d, sp, low_half, spans[kind]], y_half.at[kind, sp, :, spans[kind]],
                 y_send.at[kind, 0, sp], y_recv.at[kind, 0, sp], (flip_y, s),
             ),
             send(
-                mine.at[q_d, sp, high_half], x_half.at[kind, sp],
+                mine.at[q_d, sp, high_half, spans[kind]], x_half.at[kind, sp, :, spans[kind]],
                 x_send.at[kind, 0, sp], x_recv.at[kind, 0, sp], (flip_x, s),
             ),
         ]
 
     def to_x(kind, sp):
         return send(
-            mine.at[q_x, sp], x_in.at[kind, sp], x_send.at[kind, 1, sp], x_recv.at[kind, 1, sp],
+            mine.at[q_x, sp, :, spans[kind]], x_in.at[kind, sp, :, spans[kind]], x_send.at[kind, 1, sp], x_recv.at[kind, 1, sp],
             (flip_x, s),
         )
 
     def to_y(kind, sp):
         return send(
-            mine.at[q_y, sp], y_in.at[kind, sp], y_send.at[kind, 1, sp], y_recv.at[kind, 1, sp],
+            mine.at[q_y, sp, :, spans[kind]], y_in.at[kind, sp, :, spans[kind]], y_send.at[kind, 1, sp], y_recv.at[kind, 1, sp],
             (flip_y, s),
         )
 
     def up(kind, sp):
         return send(
-            mine.at[q_own, sp], u_in.at[kind, sp], z_send.at[kind, 0, sp], z_recv.at[kind, 0, sp],
+            mine.at[q_own, sp, :, spans[kind]], u_in.at[kind, sp, :, spans[kind]], z_send.at[kind, 0, sp], z_recv.at[kind, 0, sp],
             (e, s + 1),
         )
 
     def down(kind, sp):
         return send(
-            mine.at[q_own, sp], d_in.at[kind, sp], z_send.at[kind, 1, sp], z_recv.at[kind, 1, sp],
+            mine.at[q_own, sp, :, spans[kind]], d_in.at[kind, sp, :, spans[kind]], z_send.at[kind, 1, sp], z_recv.at[kind, 1, sp],
             (e, s - 1),
         )
 
@@ -535,6 +541,9 @@
         return sp, (sp >= 0) & (sp < planes) & (i >= 0) & (back >= 0)
 
     def add(target, *others):
+        if len(others) == 1:
+            target[...] = target[...] + others[0][...]
+            return
         total = target[...].astype(FULL)
         for other in others:
             total = total + other[...].astype(FULL)
@@ -545,15 +554,15 @@
             settled(0, sp)
             pl.semaphore_wait(free.at[sp], 1)
         for k in range(2):
+            fetch_hot(k, sp).start()
             fetch(kind, k, sp).start()
         for k, q in enumerate(order):
-            one_hot_pair(place_ref, q * planes + sp, hot, slots)
-            hot_t[...] = hot[...].T
+            fetch_hot(k, sp).wait()
             fetch(kind, k, sp).wait()
 
             def part(at, wide, q=q, k=k):
                 rows = load[k % 2, :, :, at].reshape(EXP_DEV * slots, wide)
-                got = jnp.dot(hot_t[...], rows, preferred_element_type=FULL).astype(LOW)
+                got = jnp.dot(hot[k % 2], rows, preferred_element_type=FULL).astype(LOW)
                 got = got.reshape(2, length, wide)
 
                 @pl.when(parity == 0)
@@ -575,12 +584,13 @@
                 part(pl.ds(MODEL_WIDTH, width - MODEL_WIDTH), width - MODEL_WIDTH)
             to_core(kind, q, sp).start()
             if k < 2:
+                fetch_hot(k + 2, sp).start()
                 fetch(kind, k + 2, sp).start()
 
     def pairs(kind, sp):
         for k, q in enumerate(order):
-            arrived(c_in.at[q, sp], c_recv.at[kind, q, sp])
-            add(mine.at[q, sp], c_in.at[q, sp])
+            arrived(c_in.at[q, sp, :, spans[kind]], c_recv.at[kind, q, sp])
+            add(mine.at[q, sp, :, spans[kind]], c_in.at[q, sp, :, spans[kind]])
             if k == 0:
                 for copy in halves(kind, sp):
                     copy.start()
@@ -588,27 +598,31 @@
             pl.semaphore_signal(free.at[sp], 1, device_id=(core, s), device_id_type=MESH)
 
     def sides(kind, sp):
-        arrived(y_half.at[kind, sp], y_recv.at[kind, 0, sp])
-        add(mine.at[q_x, sp, low_half], y_half.at[kind, sp])
+        arrived(y_half.at[kind, sp, :, spans[kind]], y_recv.at[kind, 0, sp])
+        add(mine.at[q_x, sp, low_half, spans[kind]], y_half.at[kind, sp, :, spans[kind]])
         to_x(kind, sp).start()
-        arrived(x_half.at[kind, sp], x_recv.at[kind, 0, sp])
-        add(mine.at[q_y, sp, high_half], x_half.at[kind, sp])
+        arrived(x_half.at[kind, sp, :, spans[kind]], x_recv.at[kind, 0, sp])
+        add(mine.at[q_y, sp, high_half, spans[kind]], x_half.at[kind, sp, :, spans[kind]])
         to_y(kind, sp).start()
 
     def line(kind, sp):
-        arrived(x_in.at[kind, sp], x_recv.at[kind, 1, sp])
-        arrived(y_in.at[kind, sp], y_recv.at[kind, 1, sp])
-        add(mine.at[q_own, sp], x_in.at[kind, sp], y_in.at[kind, sp])
+        arrived(x_in.at[kind, sp, :, spans[kind]], x_recv.at[kind, 1, sp])
+        arrived(y_in.at[kind, sp, :, spans[kind]], y_recv.at[kind, 1, sp])
+        add(
+            mine.at[q_own, sp, :, spans[kind]],
+            x_in.at[kind, sp, :, spans[kind]],
+            y_in.at[kind, sp, :, spans[kind]],
+        )
 
         @pl.when((sp >= s) & (s > 0))
         def _():
-            arrived(u_in.at[kind, sp], z_recv.at[kind, 0, sp])
-            add(mine.at[q_own, sp], u_in.at[kind, sp])
+            arrived(u_in.at[kind, sp, :, spans[kind]], z_recv.at[kind, 0, sp])
+            add(mine.at[q_own, sp, :, spans[kind]], u_in.at[kind, sp, :, spans[kind]])
 
         @pl.when((sp <= s) & (s < planes - 1))
         def _():
-            arrived(d_in.at[kind, sp], z_recv.at[kind, 1, sp])
-            add(mine.at[q_own, sp], d_in.at[kind, sp])
+            arrived(d_in.at[kind, sp, :, spans[kind]], z_recv.at[kind, 1, sp])
+            add(mine.at[q_own, sp, :, spans[kind]], d_in.at[kind, sp, :, spans[kind]])
 
         @pl.when(sp > s)
         def _():
@@ -648,7 +662,7 @@
     lax.fori_loop(0, planes, drain, 0)
 
 
-def combine_home(place, v, m, length, planes, slots, identity):
+def combine_home(hot, v, m, length, planes, slots, identity):
     width = v.shape[2]
     block = (planes, length, width)
     part = (planes, length // 2, width)
@@ -658,11 +672,10 @@
             jax.ShapeDtypeStruct((length, width), FULL),
             jax.ShapeDtypeStruct((length, MODEL_WIDTH), FULL),
         ],
-        in_specs=[VM, ANY, ANY],
+        in_specs=[ANY, ANY, ANY],
         out_specs=[VM, VM],
         scratch_shapes=[
-            pltpu.VMEM((EXP_DEV * slots, 2 * length), LOW),
-            pltpu.VMEM((2 * length, EXP_DEV * slots), LOW),
+            pltpu.VMEM((2,) + hot.shape[1:], LOW),
             pltpu.VMEM((2, EXP_DEV, slots, width), LOW),
             pltpu.VMEM((4,) + block, LOW),
             pltpu.VMEM((4,) + block, LOW),
@@ -673,6 +686,7 @@
             pltpu.VMEM((2,) + part, LOW),
             pltpu.VMEM((2,) + block, LOW),
             pltpu.VMEM((2,) + block, LOW),
+            DMA((2,)),
             DMA((2,)),
             pltpu.SemaphoreType.REGULAR((planes,)),
             DMA((2, 4, planes)),
@@ -687,7 +701,7 @@
         compiler_params=pltpu.CompilerParams(
             collective_id=identity, has_side_effects=True, vmem_limit_bytes=VMEM_LIMIT
         ),
-    )(place, v, m)
+    )(hot, v, m)
 
 
 def greet_plane(planes, owners):
@@ -717,61 +731,6 @@
         pl.semaphore_wait(barrier, owners)
 
 
-def finish_kernel(owners, rows_ref, head_ref, kv_ref, tail_ref, out_rows, out_qkv, out_tail):
-    i = pl.program_id(0)
-
-    @pl.when(i < owners)
-    def _():
-        out_rows[...] = rows_ref[0].astype(FULL)
-        out_qkv[...] = head_ref[0].astype(FULL)
-
-    @pl.when(i >= owners)
-    def _():
-        each = owners // KEY_VALUE_HEADS
-        for h in range(KEY_VALUE_HEADS):
-            total = kv_ref[h * each].astype(FULL)
-            for j in range(1, each):
-                total = total + kv_ref[h * each + j].astype(FULL)
-            out_qkv[:, h * HEAD_SIZE : (h + 1) * HEAD_SIZE] = total
-
-    @pl.when(i == 0)
-    def _():
-        total = tail_ref[0].astype(FULL)
-        for lane in range(1, owners):
-            total = total + tail_ref[lane].astype(FULL)
-        out_tail[...] = total
-
-
-def finish_grads(rows, head, rest, owners):
-    rows = rows.reshape(owners, -1, rows.shape[-1])
-    head = head.reshape(owners, -1, head.shape[-1])
-    rest = rest.reshape(owners, -1, rest.shape[-1])
-    count, share = rows.shape[1:]
-    height, wide = head.shape[1:]
-    last = owners - 1
-    return pl.pallas_call(
-        functools.partial(finish_kernel, owners),
-        grid=(owners + 2,),
-        in_specs=[
-            pl.BlockSpec((1, count, share), lambda i: (jnp.minimum(i, last), 0, 0)),
-            pl.BlockSpec((1, height, wide), lambda i: (jnp.minimum(i, last), 0, 0)),
-            pl.BlockSpec((owners, height, HEAD_SIZE), lambda i: (0, 0, i // (owners + 1))),
-            pl.BlockSpec((owners, height, TAIL), lambda i: (0, 0, 2)),
-        ],
-        out_specs=[
-            pl.BlockSpec((count, share), lambda i: (0, jnp.minimum(i, last))),
-            pl.BlockSpec((height, wide), lambda i: (0, i)),
-            pl.BlockSpec((height, TAIL), lambda i: (0, 0)),
-        ],
-        out_shape=[
-            jax.ShapeDtypeStruct((count, owners * share), FULL),
-            jax.ShapeDtypeStruct((height, (owners + 2) * wide), FULL),
-            jax.ShapeDtypeStruct((height, TAIL), FULL),
-        ],
-        compiler_params=pltpu.CompilerParams(vmem_limit_bytes=VMEM_LIMIT),
-    )(rows, head, rest, rest)
-
-
 def gather_steps(at, cut, source, x_send, x_recv, y_send, y_recv, c_send, c_recv):
     e, core, flip_x, flip_y, diagonal = neighbours()
     s = lax.axis_index("shard")
@@ -842,10 +801,11 @@
 
 
 def front_kernel(
-    planes, owners, w_ref, gain_ref, tok_ref, d_ref, freq_ref, out_ref,
-    d_all, w_out_all, w_all_out, gains, tail_ref, h1_ref, proj_ref, probs_ref, mixed_ref, branch_ref,
+    planes, owners, w_ref, router_ref, gain_ref, tok_ref, d_ref, freq_ref, out_ref,
+    d_all, w_out_all, w_all_out, r_all, gains, tail_ref, h1_ref, proj_ref, probs_ref, mixed_ref, branch_ref,
     w_all, tok_all, w_mine, q_rows, mine, away, c_in, x_in, y_in, x_half, y_half,
-    keep_sem, w_send, w_recv, g_send, g_recv, o_send, o_recv, z_send, z_recv,
+    keep_sem, w_send, w_recv, v_send, v_recv, k_send, k_recv, r_send, r_recv, g_send, g_recv,
+    o_send, o_recv, z_send, z_recv, rx_send, rx_recv, ry_send, ry_recv, rc_send, rc_recv,
     tx_send, tx_recv, ty_send, ty_recv, tc_send, tc_recv,
     dx_send, dx_recv, dy_send, dy_recv, dc_send, dc_recv,
     px_send, px_recv, py_send, py_recv, pc_send, pc_recv,
@@ -858,17 +818,30 @@
     half = length // 2
     count = w_mine.shape[0]
     heads = count // HEAD_SIZE
-    pieces = 4
+    pieces = 8
     out_part = count // pieces
     deep = w_ref.shape[0]
-    qkv_cols = proj_ref.shape[2]
+    query_cols = count
+    kv_at = pl.ds(pl.multiple_of(count + HEAD_SIZE * (e % 2), HEAD_SIZE), HEAD_SIZE)
 
     def arrived(block, sem):
         send(block, block, sem, sem, (core, s)).wait_recv()
 
     def w_copy(sp, way):
-        block = w_all.at[sp]
+        block = w_all.at[sp, :, pl.ds(0, query_cols)]
         return send(block, block, w_send.at[way, sp], w_recv.at[sp], (e, s + 1 - 2 * way))
+
+    def v_copy(sp, way):
+        block = w_all.at[sp, :, kv_at]
+        return send(block, block, v_send.at[way, sp], v_recv.at[sp], (e, s + 1 - 2 * way))
+
+    def r_copy(sp, way):
+        block = r_all.at[e, sp]
+        return send(block, block, r_send.at[way, sp], r_recv.at[sp], (e, s + 1 - 2 * way))
+
+    def k_copy(sp):
+        block = w_all.at[sp, :, kv_at]
+        return send(block, block, k_send.at[sp], k_recv.at[sp], (core, s))
 
     def g_copy(sp, way):
         block = gains.at[sp]
@@ -892,6 +865,19 @@
         lambda k: ty_recv.at[k],
         lambda k: tc_send.at[k],
         lambda k: tc_recv.at[k],
+    )
+
+    r_half = planes // 2
+    r_begin, r_second, r_third, r_last, r_sent = gather_steps(
+        lambda lane: r_all.at[lane],
+        lambda lane, k: r_all.at[lane, pl.ds(k * r_half, r_half)],
+        r_all.at[e],
+        lambda k: rx_send.at[k],
+        lambda k: rx_recv.at[k],
+        lambda k: ry_send.at[k],
+        lambda k: ry_recv.at[k],
+        lambda k: rc_send.at[k],
+        lambda k: rc_recv.at[k],
     )
 
     def d_rows(sp):
@@ -918,7 +904,9 @@
     def _():
         load_o.start()
 
-    w_all[s] = w_ref[...]
+    w_all[s, :, :query_cols] = w_ref[:, :query_cols]
+    w_all[s, :, kv_at] = w_ref[:, query_cols:]
+    r_all[e, s] = router_ref[...]
     gains[s] = gain_ref[...]
     tok_all[e] = tok_ref[...]
     greet(planes)
@@ -951,9 +939,12 @@
 
     t_begin()
     both_ways(g_copy, s)
+    keep_d.wait()
+    both_ways(d_copy, s)
     both_ways(w_copy, s)
-
-    keep_d.wait()
+    both_ways(v_copy, s)
+    both_ways(r_copy, s)
+    k_copy(s).start()
     d_rows(s)[0]()
 
     def weights(i, carry):
@@ -963,8 +954,16 @@
         def _():
             arrived(gains.at[sp], g_recv.at[sp])
             both_ways(g_copy, sp)
-            arrived(w_all.at[sp], w_recv.at[sp])
+            arrived(d_all.at[e, sp], z_recv.at[sp])
+            both_ways(d_copy, sp)
+            d_rows(sp)[0]()
+            arrived(w_all.at[sp, :, pl.ds(0, query_cols)], w_recv.at[sp])
             both_ways(w_copy, sp)
+            arrived(w_all.at[sp, :, kv_at], v_recv.at[sp])
+            both_ways(v_copy, sp)
+            k_copy(sp).start()
+            arrived(r_all.at[e, sp], r_recv.at[sp])
+            both_ways(r_copy, sp)
 
         @pl.when(i == 1)
         def _():
@@ -973,13 +972,8 @@
         @pl.when(i == 2)
         def _():
             t_third()
-            d_rows(s)[1]()
-
-        @pl.when(i == 3)
-        def _():
-            d_rows(s)[2]()
-
-        @pl.when((i == 2) & (s == home))
+
+        @pl.when((i == 4) & (s == home))
         def _():
             load_o.wait()
             for k in range(pieces):
@@ -988,32 +982,15 @@
         return carry
 
     lax.fori_loop(1, 2 * planes - 1, weights, 0)
+    r_begin()
     t_last()
+    other_kv = pl.ds(pl.multiple_of(count + HEAD_SIZE * (1 - e % 2), HEAD_SIZE), HEAD_SIZE)
+    for sp in range(planes):
+        arrived(w_all.at[sp, :, other_kv], k_recv.at[sp])
     keep_w.start()
 
-    def far(n):
-        for i in (2 * n - 1, 2 * n):
-            sp, there = plane_at(i)
-
-            @pl.when(there)
-            def _(sp=sp):
-                arrived(d_all.at[e, sp], z_recv.at[sp])
-                both_ways(d_copy, sp)
-                d_rows(sp)[0]()
-
-    def rows_onward(n):
-        @pl.when((s - home == n) | (home - s == n))
-        def _():
-            for k in range(pieces):
-                out_step(k)
-
-    def near(n, stage):
-        for i in (2 * n - 1, 2 * n):
-            sp, there = plane_at(i)
-
-            @pl.when(there)
-            def _(sp=sp):
-                d_rows(sp)[stage]()
+    def distant(n):
+        return (s - home == n) | (home - s == n)
 
     gain_query = gains[0, 2:3, :HEAD_SIZE].astype(FULL)
     gain_key = gains[0, 3:4, :HEAD_SIZE].astype(FULL)
@@ -1026,13 +1003,13 @@
     def attend(b, carry):
         x = tok_all[b, :, :MODEL_WIDTH].astype(FULL)
         inverse = lax.rsqrt(jnp.mean(x * x, axis=1, keepdims=True) + EPS)
-        total = jnp.zeros((length, qkv_cols), FULL)
+        total = jnp.zeros((length, w_all.shape[2]), FULL)
         for sp in range(planes):
             at = slice(sp * deep, (sp + 1) * deep)
             part = x[:, at] * inverse * gains[sp, 0:1, :].astype(FULL)
             part = part.astype(LOW)
             h1_ref[b, :, at] = part
-            total = total + jnp.dot(part, w_all[sp, :, :qkv_cols], preferred_element_type=FULL)
+            total = total + jnp.dot(part, w_all[sp], preferred_element_type=FULL)
         proj_ref[b] = total
         tail_ref[b] = tok_all[b, :, MODEL_WIDTH:]
         places = tok_all[b, :, MODEL_WIDTH:].astype(FULL)[:, 1:2]
@@ -1060,40 +1037,61 @@
             at = slice(h * HEAD_SIZE, (h + 1) * HEAD_SIZE)
             mixed_ref[b, :, at] = mixed[h * length : (h + 1) * length]
 
+        for lag, stage in ((0, 1), (2, 2)):
+            sp, there = plane_at(b - lag)
+
+            @pl.when(there)
+            def _(sp=sp, stage=stage):
+                d_rows(sp)[stage]()
+
         for k in range(pieces):
 
-            @pl.when((b == 2 * k) & ((s - home == 1) | (home - s == 1)))
+            @pl.when((b == k) & distant(1))
             def _(k=k):
                 out_step(k)
 
+        for k in range(5):
+
+            @pl.when((b == 3 + k) & distant(2))
+            def _(k=k):
+                out_step(k)
+
         return carry
 
     lax.fori_loop(0, owners, attend, 0)
-    both_ways(d_copy, s)
-    rows_onward(2)
-    far(1)
+    for i in range(owners - 2, 2 * planes - 1):
+        sp, there = plane_at(i)
+
+        @pl.when(there)
+        def _(sp=sp):
+            d_rows(sp)[2]()
+
+
+    @pl.when(distant(2))
+    def _():
+        for k in range(5, pieces):
+            out_step(k)
+
+    r_second()
     for n in range(3, planes):
-        rows_onward(n)
+
+        @pl.when(distant(n))
+        def _():
+            for k in range(pieces):
+                out_step(k)
+
     keep_o.start()
     begin, middle, finish, sent = project_steps(
         False, mixed_ref, w_mine, branch_ref, mine, away, c_in, x_in, y_in, x_half, y_half,
         pc_send, pc_recv, px_send, px_recv, py_send, py_recv,
     )
     begin()
-    near(1, 1)
-    far(2)
+    r_third()
     middle()
-    near(1, 2)
-    near(2, 1)
-    for n in range(3, planes):
-        far(n)
     finish()
-    near(2, 2)
-    for n in range(3, planes):
-        near(n, 1)
-    for n in range(3, planes):
-        near(n, 2)
+    r_last()
     t_sent()
+    r_sent()
     sent()
 
     def settled(copy, sp):
@@ -1109,6 +1107,9 @@
         d_rows(sp)[3]()
         d_rows(sp)[4]()
         settled(w_copy, sp)
+        settled(v_copy, sp)
+        settled(r_copy, sp)
+        k_copy(sp).wait_send()
         settled(g_copy, sp)
         settled(d_copy, sp)
         return carry
@@ -1128,7 +1129,7 @@
     keep_o.wait()
 
 
-def front(w, gain_rows, tokens, w_out, d_rows, frequency, planes, owners, identity):
+def front(w, router, gain_rows, tokens, w_out, d_rows, frequency, planes, owners, identity):
     def out(*shape, dtype=LOW):
         return jax.ShapeDtypeStruct(shape, dtype)
 
@@ -1142,7 +1143,8 @@
         out_shape=[
             out(owners, planes, *d_rows.shape),
             out(count, MODEL_WIDTH),
-            out(planes, *w.shape),
+            out(planes, w.shape[0], qkv_cols),
+            out(owners, planes, *router.shape),
             out(planes, *gain_rows.shape),
             out(owners, length, TAIL),
             out(owners, length, MODEL_WIDTH),
@@ -1151,10 +1153,10 @@
             out(owners, length, count),
             out(length, MODEL_WIDTH, dtype=FULL),
         ],
-        in_specs=[VM, VM, VM, VM, VM, ANY],
-        out_specs=[ANY, ANY, ANY, VM, VM, VM, VM, VM, VM, VM],
+        in_specs=[VM, VM, VM, VM, VM, VM, ANY],
+        out_specs=[ANY, ANY, ANY, VM, VM, VM, VM, VM, VM, VM, VM],
         scratch_shapes=[
-            pltpu.VMEM((planes,) + w.shape, LOW),
+            pltpu.VMEM((planes, w.shape[0], qkv_cols), LOW),
             pltpu.VMEM((owners,) + tokens.shape, LOW),
             pltpu.VMEM((count, MODEL_WIDTH), LOW),
             pltpu.VMEM((length * count // HEAD_SIZE, HEAD_SIZE), LOW),
@@ -1170,10 +1172,22 @@
             DMA((planes,)),
             DMA((2, planes)),
             DMA((planes,)),
-            DMA((2, 4)),
-            DMA((4,)),
+            DMA((planes,)),
+            DMA((planes,)),
             DMA((2, planes)),
             DMA((planes,)),
+            DMA((2, planes)),
+            DMA((planes,)),
+            DMA((2, 8)),
+            DMA((8,)),
+            DMA((2, planes)),
+            DMA((planes,)),
+            DMA((2,)),
+            DMA((2,)),
+            DMA((2,)),
+            DMA((2,)),
+            DMA((4,)),
+            DMA((4,)),
             DMA((2,)),
             DMA((2,)),
             DMA((2,)),
@@ -1196,7 +1210,7 @@
         compiler_params=pltpu.CompilerParams(
             collective_id=identity, has_side_effects=True, vmem_limit_bytes=VMEM_LIMIT
         ),
-    )(w, gain_rows, tokens, d_rows, frequency, w_out)
+    )(w, router, gain_rows, tokens, d_rows, frequency, w_out)
 
 
 def project_steps(
@@ -1290,23 +1304,46 @@
     return begin, middle, finish, sent
 
 
+def add_blocks(target, other):
+    step = min(128, target.shape[1])
+    for lead in range(target.shape[0]):
+
+        def one(r, carry, lead=lead):
+            at = pl.ds(pl.multiple_of(r * step, step), step)
+            target[lead, at, :] = (
+                target[lead, at, :].astype(FULL) + other[lead, at, :].astype(FULL)
+            ).astype(LOW)
+            return carry
+
+        lax.fori_loop(0, target.shape[1] // step, one, 0)
+
+
 def back_kernel(
-    planes, owners, dm_ref, w_ref, mixed_ref, proj_ref, probs_ref, tail_ref, gain_ref, freq_ref,
-    dproj_ref, sum_ref, dgain_ref,
-    dm_all, mixed_t, rows, acc, up_in, down_in, q_rows, dm_rows,
-    keep_sem, xs, xr, ys, yr, cs, cr, a_send, a_recv, z_send, z_recv,
+    planes, owners, dm_ref, w_out_ref, mixed_ref, proj_ref, probs_ref, places_ref, gain_ref,
+    freq_ref, h1_ref, w_ref, unit_ref, tail_ref,
+    out_rows, out_head, out_rest, dh1_ref,
+    dm_all, mixed_t, rows, q_rows, dm_rows, dproj, column,
+    acc_rows, acc_head, acc_rest, sibling, u_rows, u_head, u_rest, d_rows, d_head, d_rest, pair_in,
+    mine, away, c_in, x_in, y_in, x_half, y_half,
+    gxs, gxr, gys, gyr, gcs, gcr, a_send, a_recv, s_send, s_recv, z_send, z_recv,
+    x_send, x_recv, y_send, y_recv, c_send, c_recv, own_sem,
+    pc_send, pc_recv, px_send, px_recv, py_send, py_recv,
 ):
     e, core, _, _, _ = neighbours()
     s = lax.axis_index("shard")
+    parity = e % 2
     lanes = owners // planes
     length = dm_ref.shape[0]
     half = length // 2
-    count = w_ref.shape[0]
+    count = w_out_ref.shape[0]
     heads = count // HEAD_SIZE
-    share = acc.shape[2]
+    share_cols = acc_rows.shape[2]
+    deep = acc_head.shape[1] * acc_head.shape[2]
     scaling = HEAD_SIZE**-0.5
     nt = (((1,), (1,)), ((), ()))
     tn = (((0,), (0,)), ((), ()))
+    up_in, down_in = (u_rows, u_head, u_rest), (d_rows, d_head, d_rest)
+    outs = (out_rows, out_head, out_rest)
 
     def arrived(block, sem):
         send(block, block, sem, sem, (core, s)).wait_recv()
@@ -1316,12 +1353,12 @@
         lambda lane: dm_all.at[lane],
         lambda lane, k: dm_all.at[lane, pl.ds(k * half, half)],
         dm_ref,
-        lambda k: xs.at[k],
-        lambda k: xr.at[k],
-        lambda k: ys.at[k],
-        lambda k: yr.at[k],
-        lambda k: cs.at[k],
-        lambda k: cr.at[k],
+        lambda k: gxs.at[k],
+        lambda k: gxr.at[k],
+        lambda k: gys.at[k],
+        lambda k: gyr.at[k],
+        lambda k: gcs.at[k],
+        lambda k: gcr.at[k],
     )
     begin()
     dm_all[e] = dm_ref[...]
@@ -1333,15 +1370,15 @@
 
     def spread(other):
         return send(
-            rows.at[:, pl.ds(other * share, share)], acc.at[e], a_send.at[other], a_recv.at[e],
-            (other, s),
+            rows.at[:, pl.ds(other * share_cols, share_cols)], acc_rows.at[e],
+            a_send.at[other], a_recv.at[e], (other, s),
         )
 
     for other in range(owners):
-        at = pl.ds(other * share, share)
+        at = pl.ds(other * share_cols, share_cols)
         got = jnp.dot(
             mixed_t[...],
-            dm_all[:, :, at].reshape(owners * length, share),
+            dm_all[:, :, at].reshape(owners * length, share_cols),
             preferred_element_type=FULL,
         ).astype(LOW)
         rows[:, at] = got
@@ -1352,44 +1389,9 @@
 
         @pl.when(other == e)
         def _(got=got):
-            acc[e] = got
-
-    def chunk(sp):
-        return acc.at[pl.ds(sp * lanes, lanes)]
-
-    def up(sp):
-        return send(chunk(sp), up_in.at[sp], z_send.at[0, sp], z_recv.at[0, sp], (e, s + 1))
-
-    def down(sp):
-        return send(chunk(sp), down_in.at[sp], z_send.at[1, sp], z_recv.at[1, sp], (e, s - 1))
-
-    def line(sp):
-        for lane in range(lanes):
-            source = sp * lanes + lane
-
-            @pl.when(source != e)
-            def _(source=source):
-                arrived(acc.at[source], a_recv.at[source])
-
-        @pl.when((sp >= s) & (s > 0))
-        def _():
-            arrived(up_in.at[sp], z_recv.at[0, sp])
-            add_blocks(chunk(sp), up_in.at[sp])
-
-        @pl.when((sp <= s) & (s < planes - 1))
-        def _():
-            arrived(down_in.at[sp], z_recv.at[1, sp])
-            add_blocks(chunk(sp), down_in.at[sp])
-
-        @pl.when(sp > s)
-        def _():
-            up(sp).start()
-
-        @pl.when(sp < s)
-        def _():
-            down(sp).start()
-
-    dgain_ref[...] = jnp.zeros_like(dgain_ref)
+            acc_rows[e] = got
+
+    column[...] = jnp.zeros_like(column)
     gain_query = gain_ref[0, 2:3, :HEAD_SIZE].astype(FULL)
     gain_key = gain_ref[0, 3:4, :HEAD_SIZE].astype(FULL)
     for sp in range(1, planes):
@@ -1397,7 +1399,7 @@
         gain_key = gain_key + gain_ref[sp, 3:4, :HEAD_SIZE].astype(FULL)
 
     def attend(b, carry):
-        places = tail_ref[b].astype(FULL)[:, 1:2]
+        places = places_ref[b].astype(FULL)[:, 1:2]
         cosine, sine = rope_tables(places, freq_ref[0:1, :])
 
         def unit(v):
@@ -1409,12 +1411,12 @@
 
         def back(v, units, inverse, gain, row):
             v = v * cosine - half_turn(v) * sine
-            dgain_ref[row : row + 1, :] += jnp.sum(v * units, axis=0, keepdims=True)
+            column[row : row + 1, :HEAD_SIZE] += jnp.sum(v * units, axis=0, keepdims=True)
             v = v * gain
             return inverse * (v - units * jnp.mean(v * units, axis=1, keepdims=True))
 
         d_mixed = lax.dot_general(
-            dm_all[b], w_ref[...], nt, preferred_element_type=FULL
+            dm_all[b], w_out_ref[...], nt, preferred_element_type=FULL
         ).astype(LOW)
         for h in range(heads):
             at = slice(h * HEAD_SIZE, (h + 1) * HEAD_SIZE)
@@ -1436,25 +1438,169 @@
         for h in range(heads):
             at = slice(h * HEAD_SIZE, (h + 1) * HEAD_SIZE)
             units, inverse = unit(proj_ref[b, :, at])
-            got = back(d_query[h * length : (h + 1) * length], units, inverse, gain_query, 0)
-            dproj_ref[b, :, at] = got.astype(LOW)
-        got = back(d_key, key_units, key_inverse, gain_key, 1)
-        dproj_ref[b, :, count : count + HEAD_SIZE] = got.astype(LOW)
-        dproj_ref[b, :, count + HEAD_SIZE :] = d_value.astype(LOW)
-
-        i = b - (owners - 2 * planes + 2)
-        distance = (2 * planes - 2 - i + 1) // 2
-        sp = s + (2 * (i % 2) - 1) * (0 - distance)
-
-        @pl.when((i >= 0) & (sp >= 0) & (sp < planes))
-        def _():
-            line(sp)
-
+            got = back(
+                d_query[h * length : (h + 1) * length], units, inverse, gain_query, GAIN_QUERY
+            )
+            dproj[b, :, at] = got.astype(LOW)
+        got = back(d_key, key_units, key_inverse, gain_key, GAIN_KEY)
+        dproj[b, :, count : count + HEAD_SIZE] = got.astype(LOW)
+        dproj[b, :, count + HEAD_SIZE :] = d_value.astype(LOW)
         return carry
 
     lax.fori_loop(0, owners, attend, 0)
-    line(s)
-    sum_ref[...] = chunk(s)[...]
+
+    def left_of(sp):
+        at = pl.ds(pl.multiple_of(sp * deep, deep), deep)
+        return h1_ref[:, :, at].reshape(-1, deep)
+
+    def make_head(sp):
+        right = dproj[:, :, :count].reshape(-1, count)
+        got = lax.dot_general(left_of(sp), right, tn, preferred_element_type=FULL).astype(LOW)
+        acc_head[sp] = got.reshape(acc_head.shape[1:])
+
+    def to_sibling(sp):
+        return send(sibling.at[sp], pair_in.at[sp], s_send.at[sp], s_recv.at[sp], (core, s))
+
+    def make_rest(sp):
+        right = dproj[:, :, count:].reshape(-1, 2 * HEAD_SIZE)
+        got = lax.dot_general(left_of(sp), right, tn, preferred_element_type=FULL).astype(LOW)
+        key, value = got[:, :HEAD_SIZE], got[:, HEAD_SIZE:]
+        at = pl.ds(pl.multiple_of(sp * deep, deep), deep)
+        column[GAIN_ONE : GAIN_ONE + 1, :] = jnp.sum(
+            dh1_ref[:, at] * unit_ref[:, at], axis=0, keepdims=True
+        )
+        extra = (tail_ref[sp].astype(FULL) + column[...].T).astype(LOW)
+        top, low = extra[: deep // 2], extra[deep // 2 :]
+
+        def put(into, kv, part):
+            into[sp, :4] = kv.reshape(4, deep // 4, HEAD_SIZE)
+            into[sp, 4:] = part.reshape(2, deep // 4, HEAD_SIZE)
+
+        @pl.when(parity == 0)
+        def _():
+            put(acc_rest, key, top)
+            put(sibling, value, low)
+
+        @pl.when(parity == 1)
+        def _():
+            put(acc_rest, value, low)
+            put(sibling, key, top)
+
+        to_sibling(sp).start()
+
+    def chunk(k, sp):
+        if k == 0:
+            return acc_rows.at[pl.ds(sp * lanes, lanes)]
+        return acc_head.at[sp] if k == 1 else acc_rest.at[sp]
+
+    def ready(k, sp):
+        if k == 0:
+            for lane in range(lanes):
+                source = sp * lanes + lane
+
+                @pl.when(source != e)
+                def _(source=source):
+                    arrived(acc_rows.at[source], a_recv.at[source])
+
+        elif k == 1:
+            make_head(sp)
+        else:
+            arrived(pair_in.at[sp], s_recv.at[sp])
+            add_blocks(acc_rest.at[sp], pair_in.at[sp])
+
+    def up(k, sp):
+        return send(
+            chunk(k, sp), up_in[k].at[sp], z_send.at[k, 0, sp], z_recv.at[k, 0, sp], (e, s + 1)
+        )
+
+    def down(k, sp):
+        return send(
+            chunk(k, sp), down_in[k].at[sp], z_send.at[k, 1, sp], z_recv.at[k, 1, sp], (e, s - 1)
+        )
+
+    def line(k, sp):
+        ready(k, sp)
+
+        @pl.when((sp >= s) & (s > 0))
+        def _():
+            arrived(up_in[k].at[sp], z_recv.at[k, 0, sp])
+            add_blocks(chunk(k, sp), up_in[k].at[sp])
+
+        @pl.when((sp <= s) & (s < planes - 1))
+        def _():
+            arrived(down_in[k].at[sp], z_recv.at[k, 1, sp])
+            add_blocks(chunk(k, sp), down_in[k].at[sp])
+
+        @pl.when(sp > s)
+        def _():
+            up(k, sp).start()
+
+        @pl.when(sp < s)
+        def _():
+            down(k, sp).start()
+
+    def pair(k, n):
+        for i in (2 * n, 2 * n - 1):
+            sp = s + (2 * (i % 2) - 1) * n
+
+            @pl.when((sp >= 0) & (sp < planes))
+            def _(sp=sp):
+                line(k, sp)
+
+    def steps(k):
+        size = outs[k].shape[1] // 2
+        return gather_steps(
+            lambda lane: outs[k].at[lane],
+            lambda lane, at: outs[k].at[lane, pl.ds(at * size, size)],
+            chunk(k, s),
+            lambda n: x_send.at[k, n],
+            lambda n: x_recv.at[k, n],
+            lambda n: y_send.at[k, n],
+            lambda n: y_recv.at[k, n],
+            lambda n: c_send.at[k, n],
+            lambda n: c_recv.at[k, n],
+        )
+
+    def keep(k):
+        return pltpu.make_async_copy(chunk(k, s), outs[k].at[e], own_sem.at[k])
+
+    def own(k):
+        line(k, s)
+        steps(k)[0]()
+        keep(k).start()
+
+    p_begin, p_middle, p_finish, p_sent = project_steps(
+        True, dproj, w_ref, dh1_ref, mine, away, c_in, x_in, y_in, x_half, y_half,
+        pc_send, pc_recv, px_send, px_recv, py_send, py_recv,
+    )
+    pair(1, planes - 1)
+    p_begin()
+    for n in range(planes - 2, 0, -1):
+        pair(1, n)
+    p_middle()
+    pair(0, planes - 1)
+    p_finish()
+    for sp in range(planes):
+        make_rest(sp)
+    for n in range(planes - 2, 0, -1):
+        pair(0, n)
+    own(1)
+    pair(2, planes - 1)
+    steps(1)[1]()
+    for n in range(planes - 2, 0, -1):
+        pair(2, n)
+    own(0)
+    steps(1)[2]()
+    own(2)
+    steps(0)[1]()
+    steps(2)[1]()
+    steps(0)[2]()
+    steps(2)[2]()
+    for k in range(3):
+        keep(k).wait()
+        steps(k)[3]()
+        steps(k)[4]()
+    p_sent()
     sent()
     for other in range(owners):
 
@@ -1463,57 +1609,70 @@
             spread(other).wait_send()
 
     def drain(sp, carry):
-        @pl.when(sp > s)
-        def _():
-            up(sp).wait_send()
-
-        @pl.when(sp < s)
-        def _():
-            down(sp).wait_send()
+        to_sibling(sp).wait_send()
+        for k in range(3):
+
+            @pl.when(sp > s)
+            def _(k=k):
+                up(k, sp).wait_send()
+
+            @pl.when(sp < s)
+            def _(k=k):
+                down(k, sp).wait_send()
 
         return carry
 
     lax.fori_loop(0, planes, drain, 0)
 
 
-def add_blocks(target, other):
-    step = min(128, target.shape[1])
-    for lead in range(target.shape[0]):
-
-        def one(r, carry, lead=lead):
-            at = pl.ds(pl.multiple_of(r * step, step), step)
-            target[lead, at, :] = (
-                target[lead, at, :].astype(FULL) + other[lead, at, :].astype(FULL)
-            ).astype(LOW)
-            return carry
-
-        lax.fori_loop(0, target.shape[1] // step, one, 0)
-
-
-def back(dm, w, mixed, proj, probs, tail, gains, frequency, planes, owners, identity):
+def back(dm, w_out, mixed, proj, probs, places, gains, frequency, h1, w, units, tail, planes, owners, identity):
     length = dm.shape[0]
-    count = w.shape[0]
-    share = MODEL_WIDTH // owners
-    lanes = owners // planes
+    count = w_out.shape[0]
+    share_cols = MODEL_WIDTH // owners
+    deep = MODEL_WIDTH // planes
+    shapes = (
+        (owners // planes, count, share_cols),
+        (2, deep // 2, count),
+        (6, deep // 4, HEAD_SIZE),
+    )
+    stack = (length * count // HEAD_SIZE, HEAD_SIZE)
+    block = (length, MODEL_WIDTH)
+    part = (length // 2, MODEL_WIDTH)
+
+    def vmem(*shape, dtype=LOW):
+        return pltpu.VMEM(shape, dtype)
+
+    per_plane = [vmem(planes, *shape) for shape in shapes]
     return pl.pallas_call(
         functools.partial(back_kernel, planes, owners),
-        out_shape=[
-            jax.ShapeDtypeStruct(proj.shape, LOW),
-            jax.ShapeDtypeStruct((lanes, count, share), LOW),
-            jax.ShapeDtypeStruct((8, HEAD_SIZE), FULL),
-        ],
-        in_specs=[VM] * 8,
-        out_specs=[VM] * 3,
+        out_shape=[jax.ShapeDtypeStruct((owners,) + shape, LOW) for shape in shapes]
+        + [jax.ShapeDtypeStruct(block, FULL)],
+        in_specs=[VM] * 12,
+        out_specs=[ANY, ANY, ANY, VM],
         scratch_shapes=[
-            pltpu.VMEM((owners, length, MODEL_WIDTH), LOW),
-            pltpu.VMEM((count, owners * length), LOW),
-            pltpu.VMEM((count, MODEL_WIDTH), LOW),
-            pltpu.VMEM((owners, count, share), LOW),
-            pltpu.VMEM((planes, lanes, count, share), LOW),
-            pltpu.VMEM((planes, lanes, count, share), LOW),
-            pltpu.VMEM((length * count // HEAD_SIZE, HEAD_SIZE), LOW),
-            pltpu.VMEM((length * count // HEAD_SIZE, HEAD_SIZE), LOW),
-            DMA(()),
+            vmem(owners, *block),
+            vmem(count, owners * length),
+            vmem(count, MODEL_WIDTH),
+            vmem(*stack),
+            vmem(*stack),
+            vmem(*proj.shape),
+            vmem(TAIL, deep, dtype=FULL),
+            vmem(owners, count, share_cols),
+            per_plane[1],
+            per_plane[2],
+            per_plane[2],
+        ]
+        + per_plane
+        + per_plane
+        + [
+            per_plane[2],
+            vmem(4, *block),
+            vmem(4, *block),
+            vmem(4, *block),
+            vmem(*block),
+            vmem(*block),
+            vmem(*part),
+            vmem(*part),
             DMA((2,)),
             DMA((2,)),
             DMA((2,)),
@@ -1522,202 +1681,8 @@
             DMA((4,)),
             DMA((owners,)),
             DMA((owners,)),
-            DMA((2, planes)),
-            DMA((2, planes)),
-        ],
-        compiler_params=pltpu.CompilerParams(
-            collective_id=identity, has_side_effects=True, vmem_limit_bytes=VMEM_LIMIT
-        ),
-    )(dm, w, mixed, proj, probs, tail, gains, frequency)
-
-
-def share_kernel(
-    planes, owners, h1_ref, dproj_ref, w_ref, unit_ref, tail_ref, sum_ref,
-    out_rows, out_head, out_rest, dh1_ref,
-    acc_head, acc_rest, u_head, u_rest, d_head, d_rest, column, mine, away, c_in, x_in, y_in, x_half, y_half,
-    z_send, z_recv, x_send, x_recv, y_send, y_recv, c_send, c_recv, own_sem,
-    pc_send, pc_recv, px_send, px_recv, py_send, py_recv,
-):
-    e, core, flip_x, flip_y, diagonal = neighbours()
-    s = lax.axis_index("shard")
-    deep = acc_head.shape[1] * acc_head.shape[2]
-    half = deep // 2
-    wide = acc_head.shape[3]
-    acc = (None, acc_head, acc_rest)
-    up_in = (None, u_head, u_rest)
-    down_in = (None, d_head, d_rest)
-    outs = (out_rows, out_head, out_rest)
-    tn = (((0,), (0,)), ((), ()))
-
-    def arrived(block, sem):
-        send(block, block, sem, sem, (core, s)).wait_recv()
-
-    greet(planes)
-
-    def chunk(k, sp):
-        return sum_ref if k == 0 else acc[k].at[sp]
-
-    def make(k, sp):
-        at = pl.ds(pl.multiple_of(sp * deep, deep), deep)
-        left = h1_ref[:, :, at].reshape(-1, deep)
-        columns_at = slice(0, wide) if k == 1 else slice(wide, None)
-        right = dproj_ref[:, :, columns_at]
-        right = right.reshape(-1, right.shape[-1])
-        got = lax.dot_general(left, right, tn, preferred_element_type=FULL).astype(LOW)
-        got = got.reshape(2, half, got.shape[-1])
-        if k == 1:
-            acc_head[sp] = got
-        else:
-            acc_rest[sp, :, :, : got.shape[-1]] = got
-            at = pl.ds(pl.multiple_of(sp * deep, deep), deep)
-            row = jnp.sum(dh1_ref[:, at] * unit_ref[:, at], axis=0, keepdims=True)
-            column[GAIN_ONE : GAIN_ONE + 1, :] = row
-            extra = column[...].T.reshape(2, half, TAIL)
-            acc_rest[sp, :, :, got.shape[-1] :] = (tail_ref[sp].astype(FULL) + extra).astype(LOW)
-
-    def up(k, sp):
-        return send(
-            chunk(k, sp), up_in[k].at[sp], z_send.at[k, 0, sp], z_recv.at[k, 0, sp], (e, s + 1)
-        )
-
-    def down(k, sp):
-        return send(
-            chunk(k, sp), down_in[k].at[sp], z_send.at[k, 1, sp], z_recv.at[k, 1, sp], (e, s - 1)
-        )
-
-    def line(k, sp):
-        make(k, sp)
-
-        @pl.when((sp >= s) & (s > 0))
-        def _():
-            arrived(up_in[k].at[sp], z_recv.at[k, 0, sp])
-            add_blocks(chunk(k, sp), up_in[k].at[sp])
-
-        @pl.when((sp <= s) & (s < planes - 1))
-        def _():
-            arrived(down_in[k].at[sp], z_recv.at[k, 1, sp])
-            add_blocks(chunk(k, sp), down_in[k].at[sp])
-
-        @pl.when(sp > s)
-        def _():
-            up(k, sp).start()
-
-        @pl.when(sp < s)
-        def _():
-            down(k, sp).start()
-
-    def pair(k, n):
-        for i in (2 * n, 2 * n - 1):
-            sp = s + (2 * (i % 2) - 1) * n
-
-            @pl.when((sp >= 0) & (sp < planes))
-            def _(sp=sp):
-                line(k, sp)
-
-    def steps(k):
-        count = outs[k].shape[1] // 2
-        return gather_steps(
-            lambda lane: outs[k].at[lane],
-            lambda lane, at: outs[k].at[lane, pl.ds(at * count, count)],
-            chunk(k, s),
-            lambda n: x_send.at[k, n],
-            lambda n: x_recv.at[k, n],
-            lambda n: y_send.at[k, n],
-            lambda n: y_recv.at[k, n],
-            lambda n: c_send.at[k, n],
-            lambda n: c_recv.at[k, n],
-        )
-
-    def keep(k):
-        return pltpu.make_async_copy(chunk(k, s), outs[k].at[e], own_sem.at[k])
-
-    def share(k):
-        steps(k)[0]()
-        keep(k).start()
-
-    p_begin, p_middle, p_finish, p_sent = project_steps(
-        True, dproj_ref, w_ref, dh1_ref, mine, away, c_in, x_in, y_in, x_half, y_half,
-        pc_send, pc_recv, px_send, px_recv, py_send, py_recv,
-    )
-    share(0)
-    column[...] = jnp.zeros_like(column)
-    pair(1, planes - 1)
-    p_begin()
-    for n in range(planes - 2, 1, -1):
-        pair(1, n)
-    p_middle()
-    pair(1, 1)
-    p_finish()
-    pair(2, planes - 1)
-    steps(0)[1]()
-    line(1, s)
-    share(1)
-    for n in range(planes - 2, 1, -1):
-        pair(2, n)
-    steps(0)[2]()
-    pair(2, 1)
-    steps(1)[1]()
-    line(2, s)
-    share(2)
-    steps(1)[2]()
-    steps(2)[1]()
-    steps(2)[2]()
-    for k in range(3):
-        keep(k).wait()
-        steps(k)[3]()
-        steps(k)[4]()
-    p_sent()
-
-    def drain(sp, carry):
-        for k in (1, 2):
-
-            @pl.when(sp > s)
-            def _(k=k):
-                up(k, sp).wait_send()
-
-            @pl.when(sp < s)
-            def _(k=k):
-                down(k, sp).wait_send()
-
-        return carry
-
-    lax.fori_loop(0, planes, drain, 0)
-
-
-def share_grads(h1, dproj, w_all, units, tail, row_sum, planes, owners, identity):
-    length = h1.shape[1]
-    deep = MODEL_WIDTH // planes
-    query_cols = dproj.shape[2] - 2 * HEAD_SIZE
-    head = (2, deep // 2, query_cols)
-    rest = (2, deep // 2, 2 * HEAD_SIZE + tail.shape[-1])
-    tail = tail.reshape(planes, 2, deep // 2, -1)
-    block = (length, MODEL_WIDTH)
-    part = (length // 2, MODEL_WIDTH)
-
-    def per_plane(*shapes):
-        return [pltpu.VMEM((planes,) + shape, LOW) for shape in shapes]
-
-    return pl.pallas_call(
-        functools.partial(share_kernel, planes, owners),
-        out_shape=[
-            jax.ShapeDtypeStruct((owners,) + shape, LOW)
-            for shape in (row_sum.shape, head, rest)
-        ]
-        + [jax.ShapeDtypeStruct(block, FULL)],
-        in_specs=[VM] * 6,
-        out_specs=[ANY, ANY, ANY, VM],
-        scratch_shapes=per_plane(head, rest)
-        + per_plane(head, rest)
-        + per_plane(head, rest)
-        + [
-            pltpu.VMEM((TAIL, deep), FULL),
-            pltpu.VMEM((4,) + block, LOW),
-            pltpu.VMEM((4,) + block, LOW),
-            pltpu.VMEM((4,) + block, LOW),
-            pltpu.VMEM(block, LOW),
-            pltpu.VMEM(block, LOW),
-            pltpu.VMEM(part, LOW),
-            pltpu.VMEM(part, LOW),
+            DMA((planes,)),
+            DMA((planes,)),
             DMA((3, 2, planes)),
             DMA((3, 2, planes)),
             DMA((3, 2)),
@@ -1737,7 +1702,61 @@
         compiler_params=pltpu.CompilerParams(
             collective_id=identity, has_side_effects=True, vmem_limit_bytes=VMEM_LIMIT
         ),
-    )(h1, dproj, w_all, units, tail, row_sum)
+    )(dm, w_out, mixed, proj, probs, places, gains, frequency, h1, w, units, tail)
+
+
+def finish_kernel(owners, rows_ref, head_ref, rest_ref, out_rows, out_qkv, out_tail):
+    i = pl.program_id(0)
+
+    @pl.when(i < owners)
+    def _():
+        out_rows[...] = rows_ref[0].astype(FULL)
+        out_qkv[...] = head_ref[0].astype(FULL)
+
+    for at in range(2):
+
+        @pl.when(i == owners + at)
+        def _(at=at):
+            for h in range(KEY_VALUE_HEADS):
+                got = rest_ref[2 * h + at, :4].reshape(-1, HEAD_SIZE)
+                out_qkv[:, h * HEAD_SIZE : (h + 1) * HEAD_SIZE] = got.astype(FULL)
+
+    @pl.when(i == 0)
+    def _():
+        height = out_tail.shape[0] // 2
+        for at in range(2):
+            total = jnp.zeros((height, TAIL), FULL)
+            for lane in range(at, owners, 2):
+                total = total + rest_ref[lane, 4:].reshape(-1, TAIL).astype(FULL)
+            out_tail[at * height : (at + 1) * height, :] = total
+
+
+def finish_grads(rows, head, rest, owners):
+    rows = rows.reshape(owners, -1, rows.shape[-1])
+    head = head.reshape(owners, -1, head.shape[-1])
+    count, share = rows.shape[1:]
+    height, wide = head.shape[1:]
+    last = owners - 1
+    return pl.pallas_call(
+        functools.partial(finish_kernel, owners),
+        grid=(owners + 2,),
+        in_specs=[
+            pl.BlockSpec((1, count, share), lambda i: (jnp.minimum(i, last), 0, 0)),
+            pl.BlockSpec((1, height, wide), lambda i: (jnp.minimum(i, last), 0, 0)),
+            pl.BlockSpec(rest.shape, lambda i: (0, 0, 0, 0)),
+        ],
+        out_specs=[
+            pl.BlockSpec((count, share), lambda i: (0, jnp.minimum(i, last))),
+            pl.BlockSpec((height, wide), lambda i: (0, i)),
+            pl.BlockSpec((height, TAIL), lambda i: (0, 0)),
+        ],
+        out_shape=[
+            jax.ShapeDtypeStruct((count, owners * share), FULL),
+            jax.ShapeDtypeStruct((height, (owners + 2) * wide), FULL),
+            jax.ShapeDtypeStruct((height, TAIL), FULL),
+        ],
+        compiler_params=pltpu.CompilerParams(vmem_limit_bytes=VMEM_LIMIT),
+    )(rows, head, rest)
 
 
 def gathered_layer(
@@ -2076,7 +2095,6 @@
     slots = 2 * capacity
     heads = QUERY_HEADS // owners
     query_cols = heads * HEAD_SIZE
-    qkv_cols = query_cols + 2 * HEAD_SIZE
     scaling = HEAD_SIZE ** (-0.5)
     rows_in = qkv_weight.shape[0]
     per = query_gain.shape[0]
@@ -2087,12 +2105,13 @@
     mine = jnp.concatenate(
         [
             lax.dynamic_slice_in_dim(qkv_weight, me * query_cols, query_cols, 1),
-            lax.dynamic_slice_in_dim(qkv_weight, k_at, HEAD_SIZE, 1),
-            lax.dynamic_slice_in_dim(qkv_weight, v_at, HEAD_SIZE, 1),
-            columns([router], rows_in),
+            lax.dynamic_slice_in_dim(qkv_weight, jnp.where(me % 2 == 0, k_at, v_at), HEAD_SIZE, 1),
         ],
         axis=1,
     )
+    router_rows = rows_in // owners
+    router_part = lax.dynamic_slice_in_dim(router, me * router_rows, router_rows, 0)
+    router_part = columns([router_part], router_rows)
     gain_rows = jnp.zeros((16, rows_in), LOW).at[0].set(attn_gain).at[1].set(ffn_gain)
     gain_rows = lax.dynamic_update_slice(gain_rows, query_gain[None], (2, plane * per))
     gain_rows = lax.dynamic_update_slice(gain_rows, k_gain[None], (3, plane * per))
@@ -2103,12 +2122,12 @@
     half = HEAD_SIZE // 2
     frequency = THETA ** (-2.0 * jnp.arange(half, dtype=FULL) / HEAD_SIZE)
     frequency = jnp.broadcast_to(jnp.tile(frequency, 2)[None, :], (8, HEAD_SIZE))
-    d_all, w_mine, w_all, gain_all, tail, h1, projected, probs_low, mixed, branch = front(
-        mine, gain_rows, token_rows, w_out, d_rows, frequency, planes, owners, 5
+    d_all, w_mine, w_all, router_all, gain_all, tail, h1, projected, probs_low, mixed, branch = front(
+        mine, router_part, gain_rows, token_rows, w_out, d_rows, frequency, planes, owners, 5
     )
     gains = gain_all.astype(FULL)
     gain_one, gain_two = gains[:, 0].reshape(-1), gains[:, 1].reshape(-1)
-    router_full = w_all[:, :, qkv_cols : qkv_cols + experts_all].reshape(MODEL_WIDTH, -1)
+    router_full = router_all.transpose(1, 0, 2, 3).reshape(MODEL_WIDTH, -1)[:, :experts_all]
 
     places = jnp.arange(length, dtype=jnp.int32)
     route_all = d_all[..., MODEL_WIDTH : MODEL_WIDTH + TOPK].reshape(blocks, length, TOPK)
@@ -2116,11 +2135,15 @@
     match = jnp.sum((route_all.astype(FULL)[:, :, :, None] == own_experts).astype(FULL), axis=2)
     earlier = (places[None, :] < places[:, None]).astype(LOW)
     rank = dot("ts,bsj->btj", earlier, match.astype(LOW))
-    place = jnp.where(match > 0, rank, -1.0).transpose(0, 2, 1)
-    place = place.reshape(owners // 2, 2, planes, EXP_DEV, length)
     offset = (capacity * jnp.arange(2, dtype=jnp.int32)).astype(FULL)
+    place = jnp.where(match > 0, rank, -1.0).reshape(owners // 2, 2, planes, length, EXP_DEV)
     place = jnp.where(place >= 0, place + offset[:, None, None, None], -1.0)
-    place = place.transpose(0, 2, 3, 1, 4).reshape(blocks // 2, EXP_DEV, 2 * length)
+    by_token = place.transpose(0, 2, 1, 3, 4).reshape(blocks // 2, 2 * length, EXP_DEV)
+    place = by_token.transpose(0, 2, 1)
+    slot_ids = jnp.arange(EXP_DEV * slots, dtype=jnp.int32)
+    widen = (slot_ids // slots == jnp.arange(EXP_DEV, dtype=jnp.int32)[:, None]).astype(LOW)
+    hot = dot("ptj,js->pts", by_token.astype(LOW), widen)
+    hot = (hot == (slot_ids % slots).astype(FULL)).astype(LOW)
     lanes = jnp.arange(2 * experts_all, dtype=jnp.int32) % experts_all
     own = (me * EXP_DEV + jnp.arange(EXP_DEV, dtype=jnp.int32))[:, None] == lanes
     sel = jnp.broadcast_to(own.astype(FULL)[:, None, :], (EXP_DEV, 8, 2 * experts_all))
@@ -2142,7 +2165,7 @@
     x, dy = gather_dispatch(h_rows, d_all, place, planes, slots, 1)
     y, dx, d_gate, d_up, d_down = expert_pass(sel, x, dy, w_gate, w_up, w_down.swapaxes(1, 2))
     d_down = d_down.swapaxes(1, 2)
-    d_home, mixture = combine_home(place, dx, y, length, planes, slots, 2)
+    d_home, mixture = combine_home(hot, dx, y, length, planes, slots, 2)
 
     upstream = d_out.astype(FULL)
     d_gates = d_home[:, MODEL_WIDTH:]
@@ -2155,36 +2178,25 @@
     d_middle = upstream + norm_back(d_h2, unit_two, inverse_two, gain_two)
     d_router = dot("nd,ne->de", h2, d_logits)
 
-    d_projected, row_sum, d_gains = back(
-        d_middle.astype(LOW), w_mine, mixed, projected, probs_low, tail, gain_all, frequency,
-        planes, owners, 7,
-    )
     resident = tokens.astype(FULL)
     unit_one, inverse_one = unit_norm(resident)
-
-    def by_rows(v):
-        v = v.reshape(planes, per)
-        return jnp.pad(v, ((0, 0), (0, rows_in - per))).reshape(-1)[:, None]
-
-    d_tail = columns(
-        [d_router, d_gain_two[:, None], by_rows(d_gains[0]), by_rows(d_gains[1])], MODEL_WIDTH
-    )
-    *parts, d_h1 = share_grads(
-        h1, d_projected, w_all, unit_one, d_tail, row_sum, planes, owners, 4
+    d_tail = columns([d_router, d_gain_two[:, None]], MODEL_WIDTH)
+    *parts, d_h1 = back(
+        d_middle.astype(LOW), w_mine, mixed, projected, probs_low, tail, gain_all, frequency, h1,
+        w_all, unit_one, d_tail.reshape(planes, rows_in, -1), planes, owners, 4,
     )
     d_w_out, d_qkv_weight, d_rest = finish_grads(*parts, owners)
     result = (middle + mixture).astype(LOW)
     d_tokens = (d_middle + norm_back(d_h1, unit_one, inverse_one, gain_one)).astype(LOW)
-    d_gain_out = d_rest[:, experts_all:]
     return (
         result,
         d_tokens,
-        d_gain_out[:, GAIN_ONE - experts_all],
+        d_rest[:, GAIN_ONE],
         d_qkv_weight,
-        d_gain_out[:per, 1],
-        d_gain_out[:per, 2],
+        lax.dynamic_slice_in_dim(d_rest[:, GAIN_QUERY], plane * per, per, 0),
+        lax.dynamic_slice_in_dim(d_rest[:, GAIN_KEY], plane * per, per, 0),
         d_w_out,
-        d_gain_out[:, 0],
+        d_rest[:, experts_all],
         d_rest[:, :experts_all],
         d_gate,
         d_up,

time: 826 us -> 744 us (0.901)
  Pallas kernels: 774 us -> 686 us
    pallas_call x1 -> x0, Pallas kernels: 93.6 us -> none  [share_grads(): pl.pallas_call(functools.partial(share_kernel, planes, owners), out_shape...]
    pallas_call x1, Pallas kernels: 99.1 us -> 179 us  [back(): pl.pallas_call(functools.partial(back_kernel, planes, owners), out_shape=...]
    pallas_call x1, Pallas kernels: 205 us -> 162 us  [front(): pl.pallas_call(functools.partial(front_kernel, planes, owners), out_shape...]
    pallas_call x1, Pallas kernels: 104 us -> 88.9 us  [gather_dispatch(): pl.pallas_call(kernel, out_shape=[jax.ShapeDtypeStruct((EXP_DEV, total, w...]
where the time goes in v5:
time: 744 us; the launch traced here: 732 us
  Pallas kernels  686 us (92%)
  local copies, waits for them, and re-layouts  21.5 us (3%)
  other arithmetic  18.2 us (2%)
    pallas_call x1, Pallas kernels, back(): pl.pallas_call(functools.partial(back_kernel, planes, owners), out_shape=...  179 us
    pallas_call x1, Pallas kernels, combine_home(): pl.pallas_call(functools.partial(combine_home_kernel, planes, slots), out...  173 us
    pallas_call x1, Pallas kernels, front(): pl.pallas_call(functools.partial(front_kernel, planes, owners), out_shape...  162 us
    pallas_call x1, Pallas kernels, gather_dispatch(): pl.pallas_call(kernel, out_shape=[jax.ShapeDtypeStruct((EXP_DEV, total, w...  88.9 us
    pallas_call x1, Pallas kernels, expert_pass(): pl.pallas_call(expert_kernel, grid=(EXP_DEV,), in_specs=[spec(*sel.shape[...  71.6 us

profile of v5, /device:TPU:0, one launch (start us, length us, event | category | flops | bytes accessed | tf_op | source)
XLA Modules:
  0.0 732.3 jit_solution(4848895654744838428)
XLA Ops:
  0.7 1.0 constant_dynamic-slice_fusion.1
  1.7 1.1 constant_dynamic-slice_fusion.2
  2.8 0.9 pad_maximum_fusion.w_ref
  3.9 0.6 pad.21.router_ref
  4.5 0.7 reshape.244
  5.2 0.7 reshape.245
  5.9 0.8 dynamic_update_slice.6
  6.7 0.8 dynamic_update_slice.7.gain_ref
  7.5 0.9 convert_reduce_fusion.2
  8.5 0.7 convert_bitcast_fusion.1
  9.3 0.7 convert_element_type.154
  10.1 1.1 fusion.4
  11.3 0.6 broadcast_in_dim.25.freq_ref
  11.9 161.5 %shard_map.229 = (bf16[8,4,128,2176]{3,2,1,0:T(8,128)(2,1)}, bf16[512,2048]{1,0:T(8,128)(2,1)}, bf16[4,512,768]{2,1,0:T(8,128)(2,1)}, bf16[8,4,64,128]{3,2,1,0:T...) custom-call(bf16[512,640]{1,0:T(8,128)(2,1)} %pad_maximum_fusion.w_r, ...), custom_call_target="tpu_custom_call" | custom-call | tf_op jit(solution)/shard_map/pallas_call | solution.py:1141
  173.4 0.2 fusion.3
  173.6 2.5 multiply_reduce_fusion.3
  176.1 0.8 fusion.33
  177.0 0.2 multiply_convert_fusion
  177.2 0.4 fusion.34
  177.7 0.2 fusion.15
  178.0 0.2 fusion.31
  178.3 0.9 concatenate.26.x_ref
  179.3 1.3 slice.68
  180.6 1.6 bitcast_convert_fusion
  182.2 2.2 copy.72
  184.4 0.2 convert_reduce_fusion
  184.5 0.2 fusion
  184.7 0.7 add_select_fusion
  185.5 88.9 %shard_map.230 = (bf16[8,768,2176]{2,1,0:T(8,128)(2,1)}, bf16[8,768,2048]{2,1,0:T(8,128)(2,1)}) custom-call(bf16[128,2176]{1,0:T(8,128)(2,1)} %concatenate.26.x_ref, bf16[8,4,128,2176]{3,2,1,0:T(8,128)(2,1)} %get-tuple-element.64.d_ref, f32[16,8,256]{2,1,0:T(8,128)} %bitcast.44), custom_call_target="tpu_custom_call" | custom-call | tf_op jit(solution)/shard_map/pallas_call | solution.py:314
  274.4 0.6 broadcast_in_dim.28.sel_ref
  275.0 71.6 %shard_map.231 = (bf16[8,768,2048]{2,1,0:T(8,128)(2,1)}, bf16[8,768,2176]{2,1,0:T(8,128)(2,1)}, f32[8,192,2048]{2,1,0:T(8,128)}, f32[8,192,2048]{2,1,0:T(8,128)}, f32[8,192,2048]{2,1,0:T(8,128)}) custom-call(f32[8,8,128]{2,1,0:T(8,128)} %broadcast_in_dim.28.sel_ref, bf16[8,768,2176]{2,1,0:T(8,128)(2,1)} %get-tuple-element.67.x_ref, ...), custom_call_target="tpu_custom_call" | custom-call | flops 43486543872 | bytes 167772160 | tf_op jit(solution)/shard_map/pallas_call | solution.py:415
  346.7 2.7 compare_convert_fusion.hot_ref
  349.4 173.2 %shard_map.232 = (f32[128,2176]{1,0:T(8,128)}, f32[128,2048]{1,0:T(8,128)}) custom-call(bf16[16,256,384]{2,1,0:T(8,128)(2,1)} %compare_convert_fusion.hot_ref, bf16[8,768,2176]{2,1,0:T(8,128)(2,1)} %get-tuple-element.69.v_ref, bf16[8,768,2048]{2,1,0:T(8,128)(2,1)} %get-tuple-element.70.m_ref), custom_call_target="tpu_custom_call" | custom-call | tf_op jit(solution)/shard_map/pallas_call | solution.py:669
  522.6 1.1 multiply_reduce_fusion.5
  523.7 1.2 multiply_reduce_fusion.4
  524.8 0.4 convolution_convert_fusion
  525.2 1.8 multiply_reduce_fusion.1
  527.0 1.0 copy.82
  528.1 1.9 pad.24.clone
  530.0 1.1 fusion.30.dm_ref
  531.1 178.5 %shard_map.233 = (bf16[8,2,512,256]{3,2,1,0:T(8,128)(2,1)}, bf16[8,2,256,512]{3,2,1,0:T(8,128)(2,1)}, bf16[8,6,128,128]{3,2,1,0:T(8,128)(2,1)}, f32[128,2048]{1,0:T(8,128)}) custom-call(bf16[128,2048]{1,0:T(8,128)(2,1)} %fusion.30.dm_ref, bf16[512,2048]{1,0:T(8,128)(2,1)} %get-tuple-element.73.w_out_ref, bf16[8,128,512]{2,1,0:T(8,128)(2,1)} %get-tuple-element.74.mixed_ref, ...), custom_call_target="tpu_custom_call" | custom-call | tf_op jit(solution)/shard_map/pallas_call | solution.py:1646
  709.7 12.0 %shard_map.234 = (f32[1024,2048]{1,0:T(8,128)}, f32[512,5120]{1,0:T(8,128)}, f32[512,128]{1,0:T(8,128)}) custom-call(bf16[8,1024,256]{2,1,0:T(8,128)(2,1)} %bitcast.41, bf16[8,512,512]{2,1,0:T(8,128)(2,1)} %bitcast.42, bf16[8,6,128,128]{3,2,1,0:T(8,128)(2,1)} %get-tuple-element.83.rest_ref), custom_call_target="tpu_custom_call" | custom-call | tf_op jit(solution)/shard_map/pallas_call | solution.py:1740
  721.7 2.6 slice_reduce_fusion
  724.3 0.6 dynamic-slice_reduce_fusion
  724.9 0.6 dynamic-slice_reduce_fusion.1
  725.5 1.7 copy.80
  727.2 1.5 multiply_reduce_fusion
  728.8 3.0 add_convert_fusion
  (47 shorter events, 1.1 us)
Async XLA Ops:
  0.6 3.1 copy-start
  0.7 9.4 %copy-start.2 = (bf16[128,2048]{1,0:T(8,128)(2,1)S(1)}, bf16[128,2048]{1,0:T(8,128)(2,1)}, u32[]{:S(2)}) copy-start(bf16[128,2048]{1,0:T(8,128)(2,1)} %param.18) | copy-start | bytes 1572868
  0.7 9.4 %copy-start.3 = (bf16[128,2048]{1,0:T(8,128)(2,1)S(1)}, bf16[128,2048]{1,0:T(8,128)(2,1)}, u32[]{:S(2)}) copy-start(bf16[128,2048]{1,0:T(8,128)(2,1)} %param.31) | copy-start | bytes 1572868
  7.5 4.4 copy-start.8
  173.4 3.7 copy-start.7
  173.6 4.2 copy-start.9
  177.2 5.0 copy-start.4
  275.0 71.6 %copy-start.6 = (f32[4,2,4,128,8]{3,4,1,2,0:T(8,128)S(1)}, f32[4,2,4,128,8]{3,4,1,2,0:T(8,128)}, u32[]{:S(2)}) copy-start(f32[4,2,4,128,8]{3,4,1,2,0:T(8,128)} %add_select_fusion) | copy-start | bytes 393220
  349.4 175.8 %copy-start.5 = (bf16[4,8,64,128]{3,2,1,0:T(8,128)(2,1)S(1)}, bf16[4,8,64,128]{3,2,1,0:T(8,128)(2,1)}, u32[]{:S(2)}) copy-start(bf16[4,8,64,128]{3,2,1,0:T(8,128)(2,1)} %copy-done.4) | copy-start | bytes 1572868
  728.8 3.0 copy-start.1

commit v6 on v5

--- a/solution.py
+++ b/solution.py
@@ -14,7 +14,7 @@
 TOPK = 8
 EXP_DEV = 8
 TAIL = 128
-GAIN_QUERY, GAIN_KEY, GAIN_ONE = 65, 66, 67
+GAIN_TWO, GAIN_QUERY, GAIN_KEY, GAIN_ONE = 64, 65, 66, 67
 GROUP_BLOCKS = 32
 RESIDENT = 20 << 20
 
@@ -115,17 +115,10 @@
     )
 
 
-def one_hot_pair(place_ref, pair, hot_ref, slots):
-    rows = place_ref[pair]
-    at = lax.broadcasted_iota(jnp.int32, (slots, rows.shape[1]), 0).astype(FULL)
-    for j in range(EXP_DEV):
-        hot_ref[pl.ds(j * slots, slots), :] = (at == rows[j : j + 1, :]).astype(LOW)
-
-
 def gather_dispatch_kernel(
-    planes, slots, x_ref, d_ref, place_ref, outx_ref, outd_ref,
-    buf, hot, stage_x, stage_d, load_d,
-    z_send, z_recv, x_send, x_recv, y_send, y_recv, c_send, c_recv, out_x, out_d, in_d,
+    planes, slots, x_ref, d_ref, outx_ref, outd_ref, outh_ref,
+    buf, hot, place, stage_x, stage_d, stage_h, load_d,
+    z_send, z_recv, x_send, x_recv, y_send, y_recv, c_send, c_recv, out_x, out_d, out_h, in_d,
 ):
     e, core, flip_x, flip_y, diagonal = neighbours()
     s = lax.axis_index("shard")
@@ -214,7 +207,7 @@
 
     def load(q, sp, k):
         return pltpu.make_async_copy(
-            d_ref.at[2 * q + k, sp, :, pl.ds(0, MODEL_WIDTH)],
+            d_ref.at[2 * q + k, sp],
             load_d.at[q, pl.ds(k * length, length), :],
             in_d.at[q, k],
         )
@@ -224,59 +217,97 @@
             for k in range(2):
                 load(q, sp, k).start()
 
+    def copy_hot(q, sp):
+        return pltpu.make_async_copy(
+            stage_h.at[q], outh_ref.at[q * planes + sp], out_h.at[q]
+        )
+
+    row = lax.broadcasted_iota(jnp.int32, (length, length), 0)
+    earlier = (lax.broadcasted_iota(jnp.int32, (length, length), 1) < row).astype(LOW)
+    lane = lax.broadcasted_iota(jnp.int32, (2 * length, TAIL), 1).astype(FULL)
+    slot = lax.broadcasted_iota(jnp.int32, (slots, 2 * length), 0).astype(FULL)
+
+    def one_hot(q, sp):
+        routes = load_d[q, :, MODEL_WIDTH:].astype(FULL)
+        named = (routes[:, 0:1] == lane).astype(FULL)
+        for k in range(1, TOPK):
+            named = named + (routes[:, k : k + 1] == lane).astype(FULL)
+        for k in range(2):
+            here = slice(k * length, (k + 1) * length)
+            rank = jnp.dot(earlier, named[here].astype(LOW), preferred_element_type=FULL)
+            rank = jnp.where(named[here] > 0, rank + k * (slots // 2), -1.0)
+            place[:, here] = rank.T
+        rows = place[pl.ds(pl.multiple_of(e * EXP_DEV, EXP_DEV), EXP_DEV), :]
+        for j in range(EXP_DEV):
+            hot[q, sp, pl.ds(j * slots, slots), :] = (slot == rows[j : j + 1, :]).astype(LOW)
+
+    def dispatch_d(sp, i):
+        def one(q, carry):
+            @pl.when(i > 0)
+            def _():
+                copy_out(stage_d, outd_ref, out_d, q, sp).wait()
+                copy_hot(q, sp).wait()
+
+            for k in range(2):
+                load(q, sp, k).wait()
+            one_hot(q, sp)
+            stage_h[q] = hot[q, sp].T
+            copy_hot(q, sp).start()
+
+            def tile(t, inner):
+                at = pl.ds(pl.multiple_of(t * TILE, TILE), TILE)
+                got = jnp.dot(
+                    hot[q, sp], load_d[q, :, at], preferred_element_type=FULL
+                ).astype(LOW)
+                stage_d[q, :, :, at] = got.reshape(EXP_DEV, slots, TILE)
+                return inner
+
+            lax.fori_loop(0, MODEL_WIDTH // TILE, tile, 0)
+            copy_out(stage_d, outd_ref, out_d, q, sp).start()
+            return carry
+
+        lax.fori_loop(0, 4, one, 0)
+
     def dispatch(sp, i):
         for k, other in enumerate((core, core + flip_x - e, core + flip_y - e, core + diagonal - e)):
             arrived(buf.at[other, sp], c_recv.at[k, sp])
 
         def one(q, carry):
-            one_hot_pair(place_ref, q * planes + sp, hot, slots)
-            d_wide = load_d.shape[2]
-
             @pl.when(i > 0)
             def _():
                 copy_out(stage_x, outx_ref, out_x, q, sp).wait()
-                copy_out(stage_d, outd_ref, out_d, q, sp).wait()
-
-            for k in range(2):
-                load(q, sp, k).wait()
-
-            def columns_of(at, wide, with_d):
+
+            def columns_of(at, wide):
                 rows = jnp.concatenate(
                     [buf[2 * q, sp, :, at], buf[2 * q + 1, sp, :, at]], axis=0
                 )
-                got = jnp.dot(hot[...], rows, preferred_element_type=FULL).astype(LOW)
+                got = jnp.dot(hot[q, sp], rows, preferred_element_type=FULL).astype(LOW)
                 stage_x[q, :, :, at] = got.reshape(EXP_DEV, slots, wide)
-                if with_d:
-                    got = jnp.dot(
-                        hot[...], load_d[q, :, at], preferred_element_type=FULL
-                    ).astype(LOW)
-                    stage_d[q, :, :, at] = got.reshape(EXP_DEV, slots, wide)
 
             def tile(t, inner):
-                columns_of(pl.ds(pl.multiple_of(t * TILE, TILE), TILE), TILE, True)
+                columns_of(pl.ds(pl.multiple_of(t * TILE, TILE), TILE), TILE)
                 return inner
 
             lax.fori_loop(0, MODEL_WIDTH // TILE, tile, 0)
             if width > MODEL_WIDTH:
-                columns_of(pl.ds(MODEL_WIDTH, width - MODEL_WIDTH), width - MODEL_WIDTH, False)
+                columns_of(pl.ds(MODEL_WIDTH, width - MODEL_WIDTH), width - MODEL_WIDTH)
             copy_out(stage_x, outx_ref, out_x, q, sp).start()
-            copy_out(stage_d, outd_ref, out_d, q, sp).start()
             return carry
 
         lax.fori_loop(0, 4, one, 0)
 
     def step(i, carry):
-        for lag, work in ((0, step_first), (1, step_second), (2, step_third), (3, dispatch)):
+        for lag, work in ((0, step_first), (1, step_second), (2, step_third), (0, dispatch_d), (3, dispatch)):
             sp, there = plane_at(i - lag)
 
             @pl.when(there)
             def _(sp=sp, lag=lag, work=work):
-                if lag in (0, 3):
+                if work in (step_second, step_third):
+                    work(sp)
+                else:
                     work(sp, i - lag)
-                else:
-                    work(sp)
-
-        sp, there = plane_at(i - 2)
+
+        sp, there = plane_at(i + 1)
 
         @pl.when(there)
         def _():
@@ -284,6 +315,7 @@
 
         return carry
 
+    start_loads(s)
     lax.fori_loop(0, 2 * planes + 2, step, 0)
 
     def drain(sp, carry):
@@ -304,27 +336,32 @@
     for q in range(4):
         copy_out(stage_x, outx_ref, out_x, q, 0).wait()
         copy_out(stage_d, outd_ref, out_d, q, 0).wait()
-
-
-def gather_dispatch(rows, d_all, place, planes, slots, identity):
+        copy_hot(q, 0).wait()
+
+
+def gather_dispatch(rows, d_all, planes, slots, identity):
     owners = lax.axis_size("expert")
     length, width = rows.shape
-    total = place.shape[0] * slots
+    pairs = owners * planes // 2
+    total = pairs * slots
     kernel = functools.partial(gather_dispatch_kernel, planes, slots)
     return pl.pallas_call(
         kernel,
         out_shape=[
             jax.ShapeDtypeStruct((EXP_DEV, total, width), LOW),
             jax.ShapeDtypeStruct((EXP_DEV, total, MODEL_WIDTH), LOW),
+            jax.ShapeDtypeStruct((pairs, 2 * length, EXP_DEV * slots), LOW),
         ],
-        in_specs=[VM, ANY, VM],
-        out_specs=[ANY, ANY],
+        in_specs=[VM, ANY],
+        out_specs=[ANY, ANY, ANY],
         scratch_shapes=[
             pltpu.VMEM((owners, planes, length, width), LOW),
-            pltpu.VMEM((EXP_DEV * slots, 2 * length), LOW),
+            pltpu.VMEM((4, planes, EXP_DEV * slots, 2 * length), LOW),
+            pltpu.VMEM((TAIL, 2 * length), FULL),
             pltpu.VMEM((4, EXP_DEV, slots, width), LOW),
             pltpu.VMEM((4, EXP_DEV, slots, MODEL_WIDTH), LOW),
-            pltpu.VMEM((4, 2 * length, MODEL_WIDTH), LOW),
+            pltpu.VMEM((4, 2 * length, EXP_DEV * slots), LOW),
+            pltpu.VMEM((4, 2 * length, MODEL_WIDTH + TAIL), LOW),
             DMA((2, planes)),
             DMA((planes,)),
             DMA((2, planes)),
@@ -335,12 +372,13 @@
             DMA((4, planes)),
             DMA((4,)),
             DMA((4,)),
+            DMA((4,)),
             DMA((4, 2)),
         ],
         compiler_params=pltpu.CompilerParams(
             collective_id=identity, has_side_effects=True, vmem_limit_bytes=VMEM_LIMIT
         ),
-    )(rows, d_all, place)
+    )(rows, d_all)
 
 
 def expert_kernel(
@@ -553,9 +591,6 @@
         if kind == 1:
             settled(0, sp)
             pl.semaphore_wait(free.at[sp], 1)
-        for k in range(2):
-            fetch_hot(k, sp).start()
-            fetch(kind, k, sp).start()
         for k, q in enumerate(order):
             fetch_hot(k, sp).wait()
             fetch(kind, k, sp).wait()
@@ -586,6 +621,11 @@
             if k < 2:
                 fetch_hot(k + 2, sp).start()
                 fetch(kind, k + 2, sp).start()
+
+    def fetch_first(kind, sp):
+        for k in range(2):
+            fetch_hot(k, sp).start()
+            fetch(kind, k, sp).start()
 
     def pairs(kind, sp):
         for k, q in enumerate(order):
@@ -643,7 +683,7 @@
     span = 2 * planes - 1
 
     def step(t, carry):
-        for lag, job in ((0, work), (1, pairs), (2, sides), (3, line)):
+        for lag, job in ((0, fetch_first), (1, pairs), (2, sides), (0, work), (3, line)):
             for kind in range(2):
                 sp, there = plane_at(t - lag - kind * span)
 
@@ -800,8 +840,16 @@
     return pltpu.roll(v, HEAD_SIZE // 2, 1)
 
 
+def head_gains(rows, planes):
+    total = rows[0, :, :HEAD_SIZE].astype(FULL)
+    for sp in range(1, planes):
+        part = rows[sp, :, :HEAD_SIZE].astype(FULL)
+        total = total + pltpu.roll(part, sp * (HEAD_SIZE // planes), 1)
+    return total[2:3], total[3:4]
+
+
 def front_kernel(
-    planes, owners, w_ref, router_ref, gain_ref, tok_ref, d_ref, freq_ref, out_ref,
+    planes, owners, qkv_ref, router_ref, gain_ref, tok_ref, d_ref, freq_ref, out_ref,
     d_all, w_out_all, w_all_out, r_all, gains, tail_ref, h1_ref, proj_ref, probs_ref, mixed_ref, branch_ref,
     w_all, tok_all, w_mine, q_rows, mine, away, c_in, x_in, y_in, x_half, y_half,
     keep_sem, w_send, w_recv, v_send, v_recv, k_send, k_recv, r_send, r_recv, g_send, g_recv,
@@ -820,7 +868,7 @@
     heads = count // HEAD_SIZE
     pieces = 8
     out_part = count // pieces
-    deep = w_ref.shape[0]
+    deep = qkv_ref.shape[0]
     query_cols = count
     kv_at = pl.ds(pl.multiple_of(count + HEAD_SIZE * (e % 2), HEAD_SIZE), HEAD_SIZE)
 
@@ -898,14 +946,21 @@
     load_o = pltpu.make_async_copy(out_ref.at[rows], w_mine, keep_sem.at[1])
     keep_w = pltpu.make_async_copy(w_all, w_all_out, keep_sem.at[2])
     keep_o = pltpu.make_async_copy(w_mine, w_out_all, keep_sem.at[3])
+    at = pl.ds(pl.multiple_of(e * count, count), count)
+    load_w = pltpu.make_async_copy(
+        qkv_ref.at[:, at], w_all.at[s, :, pl.ds(0, query_cols)], keep_sem.at[4]
+    )
+    kv_from = (QUERY_HEADS + e % 2 * KEY_VALUE_HEADS + e * KEY_VALUE_HEADS // owners) * HEAD_SIZE
+    at = pl.ds(pl.multiple_of(kv_from, HEAD_SIZE), HEAD_SIZE)
+    load_v = pltpu.make_async_copy(qkv_ref.at[:, at], w_all.at[s, :, kv_at], keep_sem.at[5])
     keep_d.start()
 
     @pl.when(s == home)
     def _():
         load_o.start()
 
-    w_all[s, :, :query_cols] = w_ref[:, :query_cols]
-    w_all[s, :, kv_at] = w_ref[:, query_cols:]
+    load_w.start()
+    load_v.start()
     r_all[e, s] = router_ref[...]
     gains[s] = gain_ref[...]
     tok_all[e] = tok_ref[...]
@@ -941,7 +996,9 @@
     both_ways(g_copy, s)
     keep_d.wait()
     both_ways(d_copy, s)
+    load_w.wait()
     both_ways(w_copy, s)
+    load_v.wait()
     both_ways(v_copy, s)
     both_ways(r_copy, s)
     k_copy(s).start()
@@ -992,11 +1049,7 @@
     def distant(n):
         return (s - home == n) | (home - s == n)
 
-    gain_query = gains[0, 2:3, :HEAD_SIZE].astype(FULL)
-    gain_key = gains[0, 3:4, :HEAD_SIZE].astype(FULL)
-    for sp in range(1, planes):
-        gain_query = gain_query + gains[sp, 2:3, :HEAD_SIZE].astype(FULL)
-        gain_key = gain_key + gains[sp, 3:4, :HEAD_SIZE].astype(FULL)
+    gain_query, gain_key = head_gains(gains, planes)
     row = lax.broadcasted_iota(jnp.int32, (length, length), 0).astype(FULL)
     column = lax.broadcasted_iota(jnp.int32, (length, length), 1).astype(FULL)
 
@@ -1153,7 +1206,7 @@
             out(owners, length, count),
             out(length, MODEL_WIDTH, dtype=FULL),
         ],
-        in_specs=[VM, VM, VM, VM, VM, VM, ANY],
+        in_specs=[ANY, VM, VM, VM, VM, VM, ANY],
         out_specs=[ANY, ANY, ANY, VM, VM, VM, VM, VM, VM, VM, VM],
         scratch_shapes=[
             pltpu.VMEM((planes, w.shape[0], qkv_cols), LOW),
@@ -1167,7 +1220,7 @@
             pltpu.VMEM(block, LOW),
             pltpu.VMEM(part, LOW),
             pltpu.VMEM(part, LOW),
-            DMA((4,)),
+            DMA((6,)),
             DMA((2, planes)),
             DMA((planes,)),
             DMA((2, planes)),
@@ -1320,7 +1373,7 @@
 
 def back_kernel(
     planes, owners, dm_ref, w_out_ref, mixed_ref, proj_ref, probs_ref, places_ref, gain_ref,
-    freq_ref, h1_ref, w_ref, unit_ref, tail_ref,
+    freq_ref, h1_ref, w_ref, tok_ref, h2_ref, dl_ref, gain_two_ref,
     out_rows, out_head, out_rest, dh1_ref,
     dm_all, mixed_t, rows, q_rows, dm_rows, dproj, column,
     acc_rows, acc_head, acc_rest, sibling, u_rows, u_head, u_rest, d_rows, d_head, d_rest, pair_in,
@@ -1364,9 +1417,10 @@
     dm_all[e] = dm_ref[...]
     for b in range(owners):
         mixed_t[:, b * length : (b + 1) * length] = mixed_ref[b].T
-    second()
-    third()
-    last()
+
+    def lane_at(j):
+        flipped = [(e // bit + j // bit) % 2 * bit for bit in (1, 2, 4)]
+        return flipped[0] + flipped[1] + flipped[2]
 
     def spread(other):
         return send(
@@ -1374,31 +1428,21 @@
             a_send.at[other], a_recv.at[e], (other, s),
         )
 
-    for other in range(owners):
-        at = pl.ds(other * share_cols, share_cols)
-        got = jnp.dot(
-            mixed_t[...],
-            dm_all[:, :, at].reshape(owners * length, share_cols),
-            preferred_element_type=FULL,
-        ).astype(LOW)
-        rows[:, at] = got
-
-        @pl.when(other != e)
-        def _(other=other):
-            spread(other).start()
-
-        @pl.when(other == e)
-        def _(got=got):
-            acc_rows[e] = got
-
     column[...] = jnp.zeros_like(column)
-    gain_query = gain_ref[0, 2:3, :HEAD_SIZE].astype(FULL)
-    gain_key = gain_ref[0, 3:4, :HEAD_SIZE].astype(FULL)
-    for sp in range(1, planes):
-        gain_query = gain_query + gain_ref[sp, 2:3, :HEAD_SIZE].astype(FULL)
-        gain_key = gain_key + gain_ref[sp, 3:4, :HEAD_SIZE].astype(FULL)
-
-    def attend(b, carry):
+    gain_query, gain_key = head_gains(gain_ref, planes)
+
+    def attend(j, carry):
+        b = lane_at(j)
+        for at, step in ((2, second), (6, third)):
+
+            @pl.when(j == at)
+            def _(step=step):
+                step()
+
+        @pl.when(j % 2 == 1)
+        def _():
+            arrived(dm_all.at[b], gcr.at[j // 2])
+
         places = places_ref[b].astype(FULL)[:, 1:2]
         cosine, sine = rope_tables(places, freq_ref[0:1, :])
 
@@ -1448,6 +1492,26 @@
         return carry
 
     lax.fori_loop(0, owners, attend, 0)
+    for other in range(owners):
+        at = pl.ds(other * share_cols, share_cols)
+        got = jnp.dot(
+            mixed_t[...],
+            dm_all[:, :, at].reshape(owners * length, share_cols),
+            preferred_element_type=FULL,
+        ).astype(LOW)
+        rows[:, at] = got
+
+        @pl.when(other != e)
+        def _(other=other):
+            spread(other).start()
+
+        @pl.when(other == e)
+        def _(got=got):
+            acc_rows[e] = got
+
+
+    resident = tok_ref[...].astype(FULL)
+    inverse_one = lax.rsqrt(jnp.mean(resident * resident, axis=1, keepdims=True) + EPS)
 
     def left_of(sp):
         at = pl.ds(pl.multiple_of(sp * deep, deep), deep)
@@ -1467,9 +1531,11 @@
         key, value = got[:, :HEAD_SIZE], got[:, HEAD_SIZE:]
         at = pl.ds(pl.multiple_of(sp * deep, deep), deep)
         column[GAIN_ONE : GAIN_ONE + 1, :] = jnp.sum(
-            dh1_ref[:, at] * unit_ref[:, at], axis=0, keepdims=True
+            dh1_ref[:, at] * (tok_ref[:, at].astype(FULL) * inverse_one), axis=0, keepdims=True
         )
-        extra = (tail_ref[sp].astype(FULL) + column[...].T).astype(LOW)
+        column[GAIN_TWO : GAIN_TWO + 1, :] = gain_two_ref[:, at]
+        extra = lax.dot_general(h2_ref[:, at], dl_ref[...], tn, preferred_element_type=FULL)
+        extra = (extra + column[...].T).astype(LOW)
         top, low = extra[: deep // 2], extra[deep // 2 :]
 
         def put(into, kv, part):
@@ -1625,7 +1691,10 @@
     lax.fori_loop(0, planes, drain, 0)
 
 
-def back(dm, w_out, mixed, proj, probs, places, gains, frequency, h1, w, units, tail, planes, owners, identity):
+def back(
+    dm, w_out, mixed, proj, probs, places, gains, frequency, h1, w, tokens, h2, d_logits, gain_two,
+    planes, owners, identity,
+):
     length = dm.shape[0]
     count = w_out.shape[0]
     share_cols = MODEL_WIDTH // owners
@@ -1647,7 +1716,7 @@
         functools.partial(back_kernel, planes, owners),
         out_shape=[jax.ShapeDtypeStruct((owners,) + shape, LOW) for shape in shapes]
         + [jax.ShapeDtypeStruct(block, FULL)],
-        in_specs=[VM] * 12,
+        in_specs=[VM] * 14,
         out_specs=[ANY, ANY, ANY, VM],
         scratch_shapes=[
             vmem(owners, *block),
@@ -1702,10 +1771,16 @@
         compiler_params=pltpu.CompilerParams(
             collective_id=identity, has_side_effects=True, vmem_limit_bytes=VMEM_LIMIT
         ),
-    )(dm, w_out, mixed, proj, probs, places, gains, frequency, h1, w, units, tail)
-
-
-def finish_kernel(owners, rows_ref, head_ref, rest_ref, out_rows, out_qkv, out_tail):
+    )(
+        dm, w_out, mixed, proj, probs, places, gains, frequency, h1, w, tokens, h2, d_logits,
+        gain_two,
+    )
+
+
+def finish_kernel(
+    owners, rows_ref, head_ref, rest_ref, tok_ref, middle_ref, mix_ref, dm_ref, dh1_ref, gain_ref,
+    out_rows, out_qkv, out_router, out_gains, result_ref, dtok_ref,
+):
     i = pl.program_id(0)
 
     @pl.when(i < owners)
@@ -1723,40 +1798,67 @@
 
     @pl.when(i == 0)
     def _():
-        height = out_tail.shape[0] // 2
+        height = out_router.shape[0] // 2
+        experts = out_router.shape[1]
         for at in range(2):
             total = jnp.zeros((height, TAIL), FULL)
             for lane in range(at, owners, 2):
                 total = total + rest_ref[lane, 4:].reshape(-1, TAIL).astype(FULL)
-            out_tail[at * height : (at + 1) * height, :] = total
-
-
-def finish_grads(rows, head, rest, owners):
+            here = slice(at * height, (at + 1) * height)
+            out_router[here, :] = total[:, :experts]
+            out_gains[:, here] = total.T[experts : experts + 8]
+
+    @pl.when(i == 1)
+    def _():
+        result_ref[...] = (middle_ref[...] + mix_ref[...]).astype(LOW)
+
+    @pl.when(i == 2)
+    def _():
+        resident = tok_ref[...].astype(FULL)
+        units, inverse = unit_norm(resident)
+        back = norm_back(dh1_ref[...], units, inverse, gain_ref[...])
+        dtok_ref[...] = (dm_ref[...] + back).astype(LOW)
+
+
+def finish_grads(rows, head, rest, tokens, middle, mix, d_middle, d_h1, gain, owners):
     rows = rows.reshape(owners, -1, rows.shape[-1])
     head = head.reshape(owners, -1, head.shape[-1])
     count, share = rows.shape[1:]
     height, wide = head.shape[1:]
     last = owners - 1
+
+    def whole(shape):
+        return pl.BlockSpec(shape, lambda i: (0,) * len(shape))
+
+    block = tokens.shape
     return pl.pallas_call(
         functools.partial(finish_kernel, owners),
         grid=(owners + 2,),
         in_specs=[
             pl.BlockSpec((1, count, share), lambda i: (jnp.minimum(i, last), 0, 0)),
             pl.BlockSpec((1, height, wide), lambda i: (jnp.minimum(i, last), 0, 0)),
-            pl.BlockSpec(rest.shape, lambda i: (0, 0, 0, 0)),
-        ],
+            whole(rest.shape),
+        ]
+        + [whole(block)] * 5
+        + [whole(gain.shape)],
         out_specs=[
             pl.BlockSpec((count, share), lambda i: (0, jnp.minimum(i, last))),
             pl.BlockSpec((height, wide), lambda i: (0, i)),
-            pl.BlockSpec((height, TAIL), lambda i: (0, 0)),
+            whole((height, TAIL // 2)),
+            whole((8, height)),
+            whole(block),
+            whole(block),
         ],
         out_shape=[
             jax.ShapeDtypeStruct((count, owners * share), FULL),
             jax.ShapeDtypeStruct((height, (owners + 2) * wide), FULL),
-            jax.ShapeDtypeStruct((height, TAIL), FULL),
+            jax.ShapeDtypeStruct((height, TAIL // 2), FULL),
+            jax.ShapeDtypeStruct((8, height), FULL),
+            jax.ShapeDtypeStruct(block, LOW),
+            jax.ShapeDtypeStruct(block, LOW),
         ],
         compiler_params=pltpu.CompilerParams(vmem_limit_bytes=VMEM_LIMIT),
-    )(rows, head, rest)
+    )(rows, head, rest, tokens, middle, mix, d_middle, d_h1, gain)
 
 
 def gathered_layer(
@@ -2099,22 +2201,12 @@
     rows_in = qkv_weight.shape[0]
     per = query_gain.shape[0]
 
-    kv_head = me * KEY_VALUE_HEADS // owners
-    k_at = QUERY_HEADS * HEAD_SIZE + kv_head * HEAD_SIZE
-    v_at = k_at + KEY_VALUE_HEADS * HEAD_SIZE
-    mine = jnp.concatenate(
-        [
-            lax.dynamic_slice_in_dim(qkv_weight, me * query_cols, query_cols, 1),
-            lax.dynamic_slice_in_dim(qkv_weight, jnp.where(me % 2 == 0, k_at, v_at), HEAD_SIZE, 1),
-        ],
-        axis=1,
-    )
     router_rows = rows_in // owners
     router_part = lax.dynamic_slice_in_dim(router, me * router_rows, router_rows, 0)
     router_part = columns([router_part], router_rows)
-    gain_rows = jnp.zeros((16, rows_in), LOW).at[0].set(attn_gain).at[1].set(ffn_gain)
-    gain_rows = lax.dynamic_update_slice(gain_rows, query_gain[None], (2, plane * per))
-    gain_rows = lax.dynamic_update_slice(gain_rows, k_gain[None], (3, plane * per))
+    gain_rows = [attn_gain, ffn_gain]
+    gain_rows += [jnp.pad(gain, (0, rows_in - per)) for gain in (query_gain, k_gain)]
+    gain_rows = jnp.pad(jnp.stack(gain_rows), ((0, 12), (0, 0)))
     segment_row = segments[0]
     token_tail = columns([segment_row[:, None], positions_of(segment_row)[:, None]], length)
     token_rows = jnp.concatenate([tokens, token_tail], axis=1)
@@ -2123,27 +2215,12 @@
     frequency = THETA ** (-2.0 * jnp.arange(half, dtype=FULL) / HEAD_SIZE)
     frequency = jnp.broadcast_to(jnp.tile(frequency, 2)[None, :], (8, HEAD_SIZE))
     d_all, w_mine, w_all, router_all, gain_all, tail, h1, projected, probs_low, mixed, branch = front(
-        mine, router_part, gain_rows, token_rows, w_out, d_rows, frequency, planes, owners, 5
+        qkv_weight, router_part, gain_rows, token_rows, w_out, d_rows, frequency, planes, owners, 5
     )
     gains = gain_all.astype(FULL)
     gain_one, gain_two = gains[:, 0].reshape(-1), gains[:, 1].reshape(-1)
     router_full = router_all.transpose(1, 0, 2, 3).reshape(MODEL_WIDTH, -1)[:, :experts_all]
 
-    places = jnp.arange(length, dtype=jnp.int32)
-    route_all = d_all[..., MODEL_WIDTH : MODEL_WIDTH + TOPK].reshape(blocks, length, TOPK)
-    own_experts = (me * EXP_DEV + jnp.arange(EXP_DEV, dtype=jnp.int32)).astype(FULL)
-    match = jnp.sum((route_all.astype(FULL)[:, :, :, None] == own_experts).astype(FULL), axis=2)
-    earlier = (places[None, :] < places[:, None]).astype(LOW)
-    rank = dot("ts,bsj->btj", earlier, match.astype(LOW))
-    offset = (capacity * jnp.arange(2, dtype=jnp.int32)).astype(FULL)
-    place = jnp.where(match > 0, rank, -1.0).reshape(owners // 2, 2, planes, length, EXP_DEV)
-    place = jnp.where(place >= 0, place + offset[:, None, None, None], -1.0)
-    by_token = place.transpose(0, 2, 1, 3, 4).reshape(blocks // 2, 2 * length, EXP_DEV)
-    place = by_token.transpose(0, 2, 1)
-    slot_ids = jnp.arange(EXP_DEV * slots, dtype=jnp.int32)
-    widen = (slot_ids // slots == jnp.arange(EXP_DEV, dtype=jnp.int32)[:, None]).astype(LOW)
-    hot = dot("ptj,js->pts", by_token.astype(LOW), widen)
-    hot = (hot == (slot_ids % slots).astype(FULL)).astype(LOW)
     lanes = jnp.arange(2 * experts_all, dtype=jnp.int32) % experts_all
     own = (me * EXP_DEV + jnp.arange(EXP_DEV, dtype=jnp.int32))[:, None] == lanes
     sel = jnp.broadcast_to(own.astype(FULL)[:, None, :], (EXP_DEV, 8, 2 * experts_all))
@@ -2162,7 +2239,7 @@
     gates_rest = (gates - gates_high.astype(FULL)).astype(LOW)
     h_rows = jnp.concatenate([h2, gates_high, gates_rest], axis=1)
 
-    x, dy = gather_dispatch(h_rows, d_all, place, planes, slots, 1)
+    x, dy, hot = gather_dispatch(h_rows, d_all, planes, slots, 1)
     y, dx, d_gate, d_up, d_down = expert_pass(sel, x, dy, w_gate, w_up, w_down.swapaxes(1, 2))
     d_down = d_down.swapaxes(1, 2)
     d_home, mixture = combine_home(hot, dx, y, length, planes, slots, 2)
@@ -2174,30 +2251,26 @@
     d_logits = chance * (d_chance - jnp.sum(d_chance * chance, axis=1, keepdims=True))
     d_logits = d_logits.astype(LOW)
     d_h2 = d_home[:, :MODEL_WIDTH] + dot("ne,de->nd", d_logits, router_full)
-    d_gain_two = jnp.sum(d_h2 * unit_two, axis=0)
+    d_gain_two = jnp.sum(d_h2 * unit_two, axis=0, keepdims=True)
     d_middle = upstream + norm_back(d_h2, unit_two, inverse_two, gain_two)
-    d_router = dot("nd,ne->de", h2, d_logits)
-
-    resident = tokens.astype(FULL)
-    unit_one, inverse_one = unit_norm(resident)
-    d_tail = columns([d_router, d_gain_two[:, None]], MODEL_WIDTH)
+
     *parts, d_h1 = back(
         d_middle.astype(LOW), w_mine, mixed, projected, probs_low, tail, gain_all, frequency, h1,
-        w_all, unit_one, d_tail.reshape(planes, rows_in, -1), planes, owners, 4,
-    )
-    d_w_out, d_qkv_weight, d_rest = finish_grads(*parts, owners)
-    result = (middle + mixture).astype(LOW)
-    d_tokens = (d_middle + norm_back(d_h1, unit_one, inverse_one, gain_one)).astype(LOW)
+        w_all, tokens, h2, columns([d_logits], length), d_gain_two, planes, owners, 4,
+    )
+    d_w_out, d_qkv_weight, d_router, d_gains, result, d_tokens = finish_grads(
+        *parts, tokens, middle, mixture, d_middle, d_h1, gain_one[None], owners
+    )
     return (
         result,
         d_tokens,
-        d_rest[:, GAIN_ONE],
+        d_gains[GAIN_ONE - experts_all],
         d_qkv_weight,
-        lax.dynamic_slice_in_dim(d_rest[:, GAIN_QUERY], plane * per, per, 0),
-        lax.dynamic_slice_in_dim(d_rest[:, GAIN_KEY], plane * per, per, 0),
+        lax.dynamic_slice_in_dim(d_gains[GAIN_QUERY - experts_all], plane * per, per, 0),
+        lax.dynamic_slice_in_dim(d_gains[GAIN_KEY - experts_all], plane * per, per, 0),
         d_w_out,
-        d_rest[:, experts_all],
-        d_rest[:, :experts_all],
+        d_gains[0],
+        d_router,
         d_gate,
         d_up,
         d_down,

time: 744 us -> 690 us (0.927)
  Pallas kernels: 686 us -> 648 us
  local copies, waits for them, and re-layouts: 21.5 us -> 13.7 us
    pallas_call x1, Pallas kernels: 179 us -> 159 us  [back(): pl.pallas_call(functools.partial(back_kernel, planes, owners), out_shape=...]
    pallas_call x1, Pallas kernels: 173 us -> 158 us  [combine_home(): pl.pallas_call(functools.partial(combine_home_kernel, planes, slots), out...]
where the time goes in v6:
time: 690 us; the launch traced here: 678 us
  Pallas kernels  648 us (94%)
  local copies, waits for them, and re-layouts  13.7 us (2%)
  other arithmetic  12 us (2%)
    pallas_call x1, Pallas kernels, front(): pl.pallas_call(functools.partial(front_kernel, planes, owners), out_shape...  161 us
    pallas_call x1, Pallas kernels, back(): pl.pallas_call(functools.partial(back_kernel, planes, owners), out_shape=...  159 us
    pallas_call x1, Pallas kernels, combine_home(): pl.pallas_call(functools.partial(combine_home_kernel, planes, slots), out...  158 us
    pallas_call x1, Pallas kernels, gather_dispatch(): pl.pallas_call(kernel, out_shape=[jax.ShapeDtypeStruct((EXP_DEV, total, w...  84.5 us
    pallas_call x1, Pallas kernels, expert_pass(): pl.pallas_call(expert_kernel, grid=(EXP_DEV,), in_specs=[spec(*sel.shape[...  71.6 us
    pallas_call x1, Pallas kernels, finish_grads(): pl.pallas_call(functools.partial(finish_kernel, owners), grid=(owners + 2...  14.4 us

profile of v6, /device:TPU:0, one launch (start us, length us, event | category | flops | bytes accessed | tf_op | source)
XLA Modules:
  0.0 677.9 jit_solution(11830806964401802174)
XLA Ops:
  0.6 0.0 copy-start
  0.7 0.9 convert_reduce_fusion.1
  1.6 0.7 convert_bitcast_fusion.1
  2.3 0.1 broadcast_in_dim.12
  2.4 0.7 pad.28
  3.0 0.7 pad.29
  3.7 0.7 stack.15
  4.4 0.7 stack.16
  5.1 0.7 convert_element_type.91
  5.8 0.1 compare_convert_fusion
  5.8 0.6 broadcast_in_dim.13.freq_ref
  6.4 0.6 fusion.16.gain_ref
  7.1 0.1 constant_dynamic-slice_fusion.2
  7.1 0.1 copy.64
  7.2 0.6 pad.27.router_ref
  7.9 0.6 broadcast_in_dim.14.sel_ref
  8.5 0.1 copy.58
  8.6 0.1 copy.57
  8.7 0.7 convert_reduce_fusion
  9.5 0.1 copy.61
  9.6 2.3 fusion.2
  11.8 161.0 %shard_map.229 = (bf16[8,4,128,2176]{3,2,1,0:T(8,128)(2,1)}, bf16[512,2048]{1,0:T(8,128)(2,1)}, bf16[4,512,768]{2,1,0:T(8,128)(2,1)}, bf16[8,4,64,128]{3,2,1,0:T...) custom-call(bf16[512,5120]{1,0:T(8,128)(2,1)} %qkv_ref.1, ...), custom_call_target="tpu_custom_call" | custom-call | tf_op jit(solution)/shard_map/pallas_call | solution.py:1194
  172.9 1.1 copy.59
  174.0 1.4 multiply_reduce_fusion.2
  175.4 1.4 fusion.24
  176.9 0.2 multiply_convert_fusion.h2_ref
  177.0 0.0 copy-start.4
  177.1 0.4 fusion.26
  177.4 0.1 copy.60
  177.5 0.2 fusion.9
  177.7 0.2 fusion.22
  177.9 0.1 subtract_convert_fusion
  178.0 0.9 concatenate.15.x_ref
  179.0 84.5 %shard_map.230 = (bf16[8,768,2176]{2,1,0:T(8,128)(2,1)}, bf16[8,768,2048]{2,1,0:T(8,128)(2,1)}, bf16[16,256,384]{2,1,0:T(8,128)(2,1)}) custom-call(bf16[128,2176]{1,0:T(8,128)(2,1)} %concatenate.15.x_ref, bf16[8,4,128,2176]{3,2,1,0:T(8,128)(2,1)} %get-tuple-element.46.d_ref), custom_call_target="tpu_custom_call" | custom-call | tf_op jit(solution)/shard_map/pallas_call | solution.py:348
  263.5 71.6 %shard_map.231 = (bf16[8,768,2048]{2,1,0:T(8,128)(2,1)}, bf16[8,768,2176]{2,1,0:T(8,128)(2,1)}, f32[8,192,2048]{2,1,0:T(8,128)}, f32[8,192,2048]{2,1,0:T(8,128)}, f32[8,192,2048]{2,1,0:T(8,128)}) custom-call(f32[8,8,128]{2,1,0:T(8,128)} %broadcast_in_dim.14.sel_ref, bf16[8,768,2176]{2,1,0:T(8,128)(2,1)} %get-tuple-element.48.x_ref, ...), custom_call_target="tpu_custom_call" | custom-call | flops 43486543872 | bytes 167772160 | tf_op jit(solution)/shard_map/pallas_call | solution.py:453
  335.1 158.2 %shard_map.232 = (f32[128,2176]{1,0:T(8,128)}, f32[128,2048]{1,0:T(8,128)}) custom-call(bf16[16,256,384]{2,1,0:T(8,128)(2,1)} %get-tuple-element.47.hot_ref, bf16[8,768,2176]{2,1,0:T(8,128)(2,1)} %get-tuple-element.50.v_ref, bf16[8,768,2048]{2,1,0:T(8,128)(2,1)} %get-tuple-element.51.m_ref), custom_call_target="tpu_custom_call" | custom-call | tf_op jit(solution)/shard_map/pallas_call | solution.py:709
  493.3 1.1 multiply_reduce_fusion.4
  494.4 1.2 multiply_reduce_fusion.3
  495.6 0.1 multiply_convert_fusion.1
  495.7 2.3 multiply_reduce_fusion
  498.1 0.6 pad.33.dl_ref
  498.7 1.5 fusion.21
  500.2 158.5 %shard_map.233 = (bf16[8,2,512,256]{3,2,1,0:T(8,128)(2,1)}, bf16[8,2,256,512]{3,2,1,0:T(8,128)(2,1)}, bf16[8,6,128,128]{3,2,1,0:T(8,128)(2,1)}, f32[128,2048]{1,0:T(8,128)}) custom-call(bf16[128,2048]{1,0:T(8,128)(2,1)} %get-tuple-element.136.dm_ref, bf16[512,2048]{1,0:T(8,128)(2,1)} %get-tuple-element.53.w_out_ref, ...), custom_call_target="tpu_custom_call" | custom-call | tf_op jit(solution)/shard_map/pallas_call | solution.py:1715
  658.7 14.4 %shard_map.234 = (f32[1024,2048]{1,0:T(8,128)}, f32[512,5120]{1,0:T(8,128)}, f32[512,64]{1,0:T(8,128)}, f32[8,512]{1,0:T(8,128)}, bf16[128,2048]{1,0:T(8,128)(2,1)}, /*index=5*/bf16[128,2048]{1,0:T(8,128)(2,1)}) custom-call(bf16[8,1024,256]{2,1,0:T(8,128)(2,1)} %bitcast.24, bf16[8,512,512]{2,1,0:T(8,128)(2,1)} %bitcast.25, ...), custom_call_target="tpu_custom_call" | custom-call | tf_op jit(solution)/shard_map/pallas_call | solution.py:1834
  673.2 1.5 fusion.25
  674.6 0.6 fusion.18
  675.2 0.6 fusion.17
  675.8 1.7 copy.63
  (20 shorter events, 0.1 us)
Async XLA Ops:
  0.6 6.4 copy-start
  11.8 162.1 %copy-start.3 = (bf16[128,2048]{1,0:T(8,128)(2,1)S(1)}, bf16[128,2048]{1,0:T(8,128)(2,1)}, u32[]{:S(2)}) copy-start(bf16[128,2048]{1,0:T(8,128)(2,1)} %tok_ref.3) | copy-start | bytes 1572868
  175.4 323.3 %copy-start.2 = (f32[128,2048]{1,0:T(8,128)}, f32[128,2048]{1,0:T(8,128)S(1)}, u32[]{:S(2)}) copy-start(f32[128,2048]{1,0:T(8,128)S(1)} %get-tuple-element.143.middle_ref) | copy-start | bytes 3145732
  177.0 86.4 %copy-start.4 = (bf16[128,2048]{1,0:T(8,128)(2,1)}, bf16[128,2048]{1,0:T(8,128)(2,1)S(1)}, u32[]{:S(2)}) copy-start(bf16[128,2048]{1,0:T(8,128)(2,1)S(1)} %multiply_convert_fusion.h2_ref) | copy-start | bytes 1572868
  493.3 5.4 copy-start.5
  658.7 18.8 %copy-start.1 = (bf16[512,64]{0,1:T(8,128)(2,1)S(1)}, bf16[512,64]{0,1:T(8,128)(2,1)}, u32[]{:S(2)}) copy-start(bf16[512,64]{0,1:T(8,128)(2,1)} %param.23) | copy-start | bytes 196612

commit v7 on v6

--- a/solution.py
+++ b/solution.py
@@ -297,7 +297,7 @@
         lax.fori_loop(0, 4, one, 0)
 
     def step(i, carry):
-        for lag, work in ((0, step_first), (1, step_second), (2, step_third), (0, dispatch_d), (3, dispatch)):
+        for lag, work in ((0, step_first), (2, step_second), (4, step_third), (0, dispatch_d), (5, dispatch)):
             sp, there = plane_at(i - lag)
 
             @pl.when(there)
@@ -316,7 +316,7 @@
         return carry
 
     start_loads(s)
-    lax.fori_loop(0, 2 * planes + 2, step, 0)
+    lax.fori_loop(0, 2 * planes + 4, step, 0)
 
     def drain(sp, carry):
         for copy in first(sp) + from_x(sp) + from_y(sp) + [from_diagonal(sp)]:
@@ -683,7 +683,7 @@
     span = 2 * planes - 1
 
     def step(t, carry):
-        for lag, job in ((0, fetch_first), (1, pairs), (2, sides), (0, work), (3, line)):
+        for lag, job in ((0, fetch_first), (1, pairs), (3, sides), (0, work), (5, line)):
             for kind in range(2):
                 sp, there = plane_at(t - lag - kind * span)
 
@@ -693,7 +693,7 @@
 
         return carry
 
-    lax.fori_loop(0, 2 * span + 3, step, 0)
+    lax.fori_loop(0, 2 * span + 5, step, 0)
 
     def drain(sp, carry):
         settled(1, sp)
@@ -1492,24 +1492,6 @@
         return carry
 
     lax.fori_loop(0, owners, attend, 0)
-    for other in range(owners):
-        at = pl.ds(other * share_cols, share_cols)
-        got = jnp.dot(
-            mixed_t[...],
-            dm_all[:, :, at].reshape(owners * length, share_cols),
-            preferred_element_type=FULL,
-        ).astype(LOW)
-        rows[:, at] = got
-
-        @pl.when(other != e)
-        def _(other=other):
-            spread(other).start()
-
-        @pl.when(other == e)
-        def _(got=got):
-            acc_rows[e] = got
-
-
     resident = tok_ref[...].astype(FULL)
     inverse_one = lax.rsqrt(jnp.mean(resident * resident, axis=1, keepdims=True) + EPS)
 
@@ -1640,27 +1622,45 @@
         pc_send, pc_recv, px_send, px_recv, py_send, py_recv,
     )
     pair(1, planes - 1)
-    p_begin()
+    for other in range(owners):
+        at = pl.ds(other * share_cols, share_cols)
+        got = jnp.dot(
+            mixed_t[...],
+            dm_all[:, :, at].reshape(owners * length, share_cols),
+            preferred_element_type=FULL,
+        ).astype(LOW)
+        rows[:, at] = got
+
+        @pl.when(other != e)
+        def _(other=other):
+            spread(other).start()
+
+        @pl.when(other == e)
+        def _(got=got):
+            acc_rows[e] = got
     for n in range(planes - 2, 0, -1):
         pair(1, n)
+        if n == planes - 2:
+            p_begin()
+    pair(0, planes - 1)
     p_middle()
-    pair(0, planes - 1)
+    own(1)
+    for n in range(planes - 2, 1, -1):
+        pair(0, n)
     p_finish()
     for sp in range(planes):
         make_rest(sp)
-    for n in range(planes - 2, 0, -1):
-        pair(0, n)
-    own(1)
+    pair(0, 1)
+    steps(1)[1]()
     pair(2, planes - 1)
-    steps(1)[1]()
+    own(0)
+    steps(1)[2]()
     for n in range(planes - 2, 0, -1):
         pair(2, n)
-    own(0)
-    steps(1)[2]()
+    steps(0)[1]()
     own(2)
-    steps(0)[1]()
+    steps(0)[2]()
     steps(2)[1]()
-    steps(0)[2]()
     steps(2)[2]()
     for k in range(3):
         keep(k).wait()

time: 690 us -> 665 us (0.964)
  Pallas kernels: 648 us -> 630 us
    pallas_call x1, Pallas kernels: 159 us -> 138 us  [back(): pl.pallas_call(functools.partial(back_kernel, planes, owners), out_shape=...]
where the time goes in v7:
time: 665 us; the launch traced here: 659 us
  Pallas kernels  630 us (95%)
  local copies, waits for them, and re-layouts  13.7 us (2%)
  other arithmetic  12 us (2%)
    pallas_call x1, Pallas kernels, front(): pl.pallas_call(functools.partial(front_kernel, planes, owners), out_shape...  161 us
    pallas_call x1, Pallas kernels, combine_home(): pl.pallas_call(functools.partial(combine_home_kernel, planes, slots), out...  156 us
    pallas_call x1, Pallas kernels, back(): pl.pallas_call(functools.partial(back_kernel, planes, owners), out_shape=...  138 us
    pallas_call x1, Pallas kernels, gather_dispatch(): pl.pallas_call(kernel, out_shape=[jax.ShapeDtypeStruct((EXP_DEV, total, w...  87.9 us
    pallas_call x1, Pallas kernels, expert_pass(): pl.pallas_call(expert_kernel, grid=(EXP_DEV,), in_specs=[spec(*sel.shape[...  71.6 us
    pallas_call x1, Pallas kernels, finish_grads(): pl.pallas_call(functools.partial(finish_kernel, owners), grid=(owners + 2...  14.4 us

profile of v7, /device:TPU:0, one launch (start us, length us, event | category | flops | bytes accessed | tf_op | source)
XLA Modules:
  0.0 659.2 jit_solution(13216177834750521099)
XLA Ops:
  0.6 0.0 copy-start
  0.7 0.9 convert_reduce_fusion.1
  1.6 0.7 convert_bitcast_fusion.1
  2.3 0.1 broadcast_in_dim.12
  2.4 0.7 pad.28
  3.0 0.7 pad.29
  3.7 0.7 stack.15
  4.4 0.7 stack.16
  5.1 0.7 convert_element_type.91
  5.8 0.1 compare_convert_fusion
  5.8 0.6 broadcast_in_dim.13.freq_ref
  6.4 0.6 fusion.16.gain_ref
  7.1 0.1 constant_dynamic-slice_fusion.2
  7.1 0.1 copy.64
  7.2 0.6 pad.27.router_ref
  7.9 0.6 broadcast_in_dim.14.sel_ref
  8.5 0.1 copy.58
  8.6 0.1 copy.57
  8.7 0.7 convert_reduce_fusion
  9.5 0.1 copy.61
  9.6 2.3 fusion.2
  11.8 161.0 %shard_map.229 = (bf16[8,4,128,2176]{3,2,1,0:T(8,128)(2,1)}, bf16[512,2048]{1,0:T(8,128)(2,1)}, bf16[4,512,768]{2,1,0:T(8,128)(2,1)}, bf16[8,4,64,128]{3,2,1,0:T...) custom-call(bf16[512,5120]{1,0:T(8,128)(2,1)} %qkv_ref.1, ...), custom_call_target="tpu_custom_call" | custom-call | tf_op jit(solution)/shard_map/pallas_call | solution.py:1194
  172.9 1.1 copy.59
  174.0 1.4 multiply_reduce_fusion.2
  175.4 1.4 fusion.24
  176.9 0.2 multiply_convert_fusion.h2_ref
  177.0 0.0 copy-start.4
  177.1 0.4 fusion.26
  177.4 0.1 copy.60
  177.5 0.2 fusion.9
  177.7 0.2 fusion.22
  177.9 0.1 subtract_convert_fusion
  178.0 0.9 concatenate.15.x_ref
  179.0 87.9 %shard_map.230 = (bf16[8,768,2176]{2,1,0:T(8,128)(2,1)}, bf16[8,768,2048]{2,1,0:T(8,128)(2,1)}, bf16[16,256,384]{2,1,0:T(8,128)(2,1)}) custom-call(bf16[128,2176]{1,0:T(8,128)(2,1)} %concatenate.15.x_ref, bf16[8,4,128,2176]{3,2,1,0:T(8,128)(2,1)} %get-tuple-element.46.d_ref), custom_call_target="tpu_custom_call" | custom-call | tf_op jit(solution)/shard_map/pallas_call | solution.py:348
  266.9 71.6 %shard_map.231 = (bf16[8,768,2048]{2,1,0:T(8,128)(2,1)}, bf16[8,768,2176]{2,1,0:T(8,128)(2,1)}, f32[8,192,2048]{2,1,0:T(8,128)}, f32[8,192,2048]{2,1,0:T(8,128)}, f32[8,192,2048]{2,1,0:T(8,128)}) custom-call(f32[8,8,128]{2,1,0:T(8,128)} %broadcast_in_dim.14.sel_ref, bf16[8,768,2176]{2,1,0:T(8,128)(2,1)} %get-tuple-element.48.x_ref, ...), custom_call_target="tpu_custom_call" | custom-call | flops 43486543872 | bytes 167772160 | tf_op jit(solution)/shard_map/pallas_call | solution.py:453
  338.5 156.3 %shard_map.232 = (f32[128,2176]{1,0:T(8,128)}, f32[128,2048]{1,0:T(8,128)}) custom-call(bf16[16,256,384]{2,1,0:T(8,128)(2,1)} %get-tuple-element.47.hot_ref, bf16[8,768,2176]{2,1,0:T(8,128)(2,1)} %get-tuple-element.50.v_ref, bf16[8,768,2048]{2,1,0:T(8,128)(2,1)} %get-tuple-element.51.m_ref), custom_call_target="tpu_custom_call" | custom-call | tf_op jit(solution)/shard_map/pallas_call | solution.py:709
  494.8 1.1 multiply_reduce_fusion.4
  495.9 1.2 multiply_reduce_fusion.3
  497.0 0.1 multiply_convert_fusion.1
  497.2 2.3 multiply_reduce_fusion
  499.5 0.6 pad.33.dl_ref
  500.1 1.5 fusion.21
  501.6 138.4 %shard_map.233 = (bf16[8,2,512,256]{3,2,1,0:T(8,128)(2,1)}, bf16[8,2,256,512]{3,2,1,0:T(8,128)(2,1)}, bf16[8,6,128,128]{3,2,1,0:T(8,128)(2,1)}, f32[128,2048]{1,0:T(8,128)}) custom-call(bf16[128,2048]{1,0:T(8,128)(2,1)} %get-tuple-element.136.dm_ref, bf16[512,2048]{1,0:T(8,128)(2,1)} %get-tuple-element.53.w_out_ref, ...), custom_call_target="tpu_custom_call" | custom-call | tf_op jit(solution)/shard_map/pallas_call | solution.py:1715
  640.0 14.4 %shard_map.234 = (f32[1024,2048]{1,0:T(8,128)}, f32[512,5120]{1,0:T(8,128)}, f32[512,64]{1,0:T(8,128)}, f32[8,512]{1,0:T(8,128)}, bf16[128,2048]{1,0:T(8,128)(2,1)}, /*index=5*/bf16[128,2048]{1,0:T(8,128)(2,1)}) custom-call(bf16[8,1024,256]{2,1,0:T(8,128)(2,1)} %bitcast.24, bf16[8,512,512]{2,1,0:T(8,128)(2,1)} %bitcast.25, ...), custom_call_target="tpu_custom_call" | custom-call | tf_op jit(solution)/shard_map/pallas_call | solution.py:1834
  654.4 1.5 fusion.25
  655.9 0.6 fusion.18
  656.5 0.6 fusion.17
  657.1 1.7 copy.63
  (20 shorter events, 0.1 us)
Async XLA Ops:
  0.6 6.4 copy-start
  11.8 162.1 %copy-start.3 = (bf16[128,2048]{1,0:T(8,128)(2,1)S(1)}, bf16[128,2048]{1,0:T(8,128)(2,1)}, u32[]{:S(2)}) copy-start(bf16[128,2048]{1,0:T(8,128)(2,1)} %tok_ref.3) | copy-start | bytes 1572868
  175.4 324.7 %copy-start.2 = (f32[128,2048]{1,0:T(8,128)}, f32[128,2048]{1,0:T(8,128)S(1)}, u32[]{:S(2)}) copy-start(f32[128,2048]{1,0:T(8,128)S(1)} %get-tuple-element.143.middle_ref) | copy-start | bytes 3145732
  177.0 89.8 %copy-start.4 = (bf16[128,2048]{1,0:T(8,128)(2,1)}, bf16[128,2048]{1,0:T(8,128)(2,1)S(1)}, u32[]{:S(2)}) copy-start(bf16[128,2048]{1,0:T(8,128)(2,1)S(1)} %multiply_convert_fusion.h2_ref) | copy-start | bytes 1572868
  494.8 5.4 copy-start.5
  640.0 18.8 %copy-start.1 = (bf16[512,64]{0,1:T(8,128)(2,1)S(1)}, bf16[512,64]{0,1:T(8,128)(2,1)}, u32[]{:S(2)}) copy-start(bf16[512,64]{0,1:T(8,128)(2,1)} %param.23) | copy-start | bytes 196612

commit v8 on v7

--- a/solution.py
+++ b/solution.py
@@ -2,6 +2,7 @@
 
 import jax
 import jax.numpy as jnp
+import numpy as np
 from jax import lax
 from jax.experimental import pallas as pl
 from jax.experimental.pallas import tpu as pltpu
@@ -2204,16 +2205,17 @@
     router_rows = rows_in // owners
     router_part = lax.dynamic_slice_in_dim(router, me * router_rows, router_rows, 0)
     router_part = columns([router_part], router_rows)
-    gain_rows = [attn_gain, ffn_gain]
-    gain_rows += [jnp.pad(gain, (0, rows_in - per)) for gain in (query_gain, k_gain)]
-    gain_rows = jnp.pad(jnp.stack(gain_rows), ((0, 12), (0, 0)))
+    row = lax.broadcasted_iota(jnp.int32, (16, rows_in), 0)
+    gain_rows = jnp.zeros((16, rows_in), LOW)
+    for at, gain in enumerate((attn_gain, ffn_gain, query_gain, k_gain)):
+        gain = jnp.pad(gain, (0, rows_in - gain.shape[0]))
+        gain_rows = jnp.where(row == at, gain[None, :], gain_rows)
     segment_row = segments[0]
     token_tail = columns([segment_row[:, None], positions_of(segment_row)[:, None]], length)
     token_rows = jnp.concatenate([tokens, token_tail], axis=1)
     d_rows = jnp.concatenate([d_out, columns([routes], length)], axis=1)
-    half = HEAD_SIZE // 2
-    frequency = THETA ** (-2.0 * jnp.arange(half, dtype=FULL) / HEAD_SIZE)
-    frequency = jnp.broadcast_to(jnp.tile(frequency, 2)[None, :], (8, HEAD_SIZE))
+    frequency = THETA ** (-2.0 * np.arange(HEAD_SIZE // 2) / HEAD_SIZE)
+    frequency = jnp.asarray(np.tile(frequency, (8, 2)).astype(np.float32))
     d_all, w_mine, w_all, router_all, gain_all, tail, h1, projected, probs_low, mixed, branch = front(
         qkv_weight, router_part, gain_rows, token_rows, w_out, d_rows, frequency, planes, owners, 5
     )

time: 665 us -> 664 us (level)
  no operation moved by 1% of the time
where the time goes in v8:
time: 664 us; the launch traced here: 658 us
  Pallas kernels  630 us (95%)
  other arithmetic  12.7 us (2%)
  local copies, waits for them, and re-layouts  11.6 us (2%)
    pallas_call x1, Pallas kernels, front(): pl.pallas_call(functools.partial(front_kernel, planes, owners), out_shape...  161 us
    pallas_call x1, Pallas kernels, combine_home(): pl.pallas_call(functools.partial(combine_home_kernel, planes, slots), out...  156 us
    pallas_call x1, Pallas kernels, back(): pl.pallas_call(functools.partial(back_kernel, planes, owners), out_shape=...  138 us
    pallas_call x1, Pallas kernels, gather_dispatch(): pl.pallas_call(kernel, out_shape=[jax.ShapeDtypeStruct((EXP_DEV, total, w...  87.9 us
    pallas_call x1, Pallas kernels, expert_pass(): pl.pallas_call(expert_kernel, grid=(EXP_DEV,), in_specs=[spec(*sel.shape[...  71.6 us
    pallas_call x1, Pallas kernels, finish_grads(): pl.pallas_call(functools.partial(finish_kernel, owners), grid=(owners + 2...  14.4 us

profile of v8, /device:TPU:0, one launch (start us, length us, event | category | flops | bytes accessed | tf_op | source)
XLA Modules:
  0.0 658.0 jit_solution(6120234819815304698)
XLA Ops:
  0.6 0.0 copy-start
  0.7 0.9 convert_reduce_fusion.1
  1.6 0.7 convert_bitcast_fusion.1
  2.3 0.7 pad.25
  2.9 0.7 pad.24
  3.6 0.7 convert_element_type.89
  4.3 0.1 compare_convert_fusion
  4.4 1.4 select_select_fusion.gain_ref
  5.8 0.0 copy-done
  5.8 0.1 constant_dynamic-slice_fusion.2
  5.8 0.1 copy.65
  5.9 0.6 pad.23.router_ref
  6.6 0.6 broadcast_in_dim.58.sel_ref
  7.2 0.1 copy.59
  7.3 0.1 copy.58
  7.4 0.7 convert_reduce_fusion
  8.2 0.1 copy.62
  8.3 2.3 fusion.2
  10.5 161.0 %shard_map.238 = (bf16[8,4,128,2176]{3,2,1,0:T(8,128)(2,1)}, bf16[512,2048]{1,0:T(8,128)(2,1)}, bf16[4,512,768]{2,1,0:T(8,128)(2,1)}, bf16[8,4,64,128]{3,2,1,0:T...) custom-call(bf16[512,5120]{1,0:T(8,128)(2,1)} %qkv_ref.1, ...), custom_call_target="tpu_custom_call" | custom-call | tf_op jit(solution)/shard_map/pallas_call | solution.py:1195
  171.6 1.1 copy.60
  172.7 1.4 multiply_reduce_fusion.2
  174.1 1.4 fusion.17
  175.6 0.2 multiply_convert_fusion.h2_ref
  175.7 0.0 copy-start.4
  175.8 0.4 fusion.19
  176.1 0.1 copy.61
  176.2 0.2 fusion.9
  176.4 0.2 fusion.15
  176.6 0.1 subtract_convert_fusion
  176.7 0.9 concatenate.15.x_ref
  177.7 87.9 %shard_map.239 = (bf16[8,768,2176]{2,1,0:T(8,128)(2,1)}, bf16[8,768,2048]{2,1,0:T(8,128)(2,1)}, bf16[16,256,384]{2,1,0:T(8,128)(2,1)}) custom-call(bf16[128,2176]{1,0:T(8,128)(2,1)} %concatenate.15.x_ref, bf16[8,4,128,2176]{3,2,1,0:T(8,128)(2,1)} %get-tuple-element.46.d_ref), custom_call_target="tpu_custom_call" | custom-call | tf_op jit(solution)/shard_map/pallas_call | solution.py:349
  265.6 71.6 %shard_map.240 = (bf16[8,768,2048]{2,1,0:T(8,128)(2,1)}, bf16[8,768,2176]{2,1,0:T(8,128)(2,1)}, f32[8,192,2048]{2,1,0:T(8,128)}, f32[8,192,2048]{2,1,0:T(8,128)}, f32[8,192,2048]{2,1,0:T(8,128)}) custom-call(f32[8,8,128]{2,1,0:T(8,128)} %broadcast_in_dim.58.sel_ref, bf16[8,768,2176]{2,1,0:T(8,128)(2,1)} %get-tuple-element.48.x_ref, ...), custom_call_target="tpu_custom_call" | custom-call | flops 43486543872 | bytes 167772160 | tf_op jit(solution)/shard_map/pallas_call | solution.py:454
  337.2 156.3 %shard_map.241 = (f32[128,2176]{1,0:T(8,128)}, f32[128,2048]{1,0:T(8,128)}) custom-call(bf16[16,256,384]{2,1,0:T(8,128)(2,1)} %get-tuple-element.47.hot_ref, bf16[8,768,2176]{2,1,0:T(8,128)(2,1)} %get-tuple-element.50.v_ref, bf16[8,768,2048]{2,1,0:T(8,128)(2,1)} %get-tuple-element.51.m_ref), custom_call_target="tpu_custom_call" | custom-call | tf_op jit(solution)/shard_map/pallas_call | solution.py:710
  493.5 0.0 copy-start.5
  493.5 1.1 multiply_reduce_fusion.4
  494.6 1.2 multiply_reduce_fusion.3
  495.7 0.1 multiply_convert_fusion.1
  495.9 2.3 multiply_reduce_fusion
  498.2 0.6 pad.28.dl_ref
  498.8 1.5 fusion.14
  500.3 138.4 %shard_map.242 = (bf16[8,2,512,256]{3,2,1,0:T(8,128)(2,1)}, bf16[8,2,256,512]{3,2,1,0:T(8,128)(2,1)}, bf16[8,6,128,128]{3,2,1,0:T(8,128)(2,1)}, f32[128,2048]{1,0:T(8,128)}) custom-call(bf16[128,2048]{1,0:T(8,128)(2,1)} %get-tuple-element.136.dm_ref, bf16[512,2048]{1,0:T(8,128)(2,1)} %get-tuple-element.53.w_out_ref, ...), custom_call_target="tpu_custom_call" | custom-call | tf_op jit(solution)/shard_map/pallas_call | solution.py:1716
  638.8 0.0 copy-start.1
  638.8 14.4 %shard_map.243 = (f32[1024,2048]{1,0:T(8,128)}, f32[512,5120]{1,0:T(8,128)}, f32[512,64]{1,0:T(8,128)}, f32[8,512]{1,0:T(8,128)}, bf16[128,2048]{1,0:T(8,128)(2,1)}, /*index=5*/bf16[128,2048]{1,0:T(8,128)(2,1)}) custom-call(bf16[8,1024,256]{2,1,0:T(8,128)(2,1)} %bitcast.24, bf16[8,512,512]{2,1,0:T(8,128)(2,1)} %bitcast.25, ...), custom_call_target="tpu_custom_call" | custom-call | tf_op jit(solution)/shard_map/pallas_call | solution.py:1835
  653.2 1.5 fusion.18
  654.6 0.6 fusion.11
  655.2 0.6 fusion.10
  655.8 1.7 copy.64
  657.5 0.0 copy-done.1
  (14 shorter events, 0.1 us)
Async XLA Ops:
  0.6 5.1 copy-start
  10.5 162.1 %copy-start.3 = (bf16[128,2048]{1,0:T(8,128)(2,1)S(1)}, bf16[128,2048]{1,0:T(8,128)(2,1)}, u32[]{:S(2)}) copy-start(bf16[128,2048]{1,0:T(8,128)(2,1)} %tok_ref.3) | copy-start | bytes 1572868
  174.1 324.7 %copy-start.2 = (f32[128,2048]{1,0:T(8,128)}, f32[128,2048]{1,0:T(8,128)S(1)}, u32[]{:S(2)}) copy-start(f32[128,2048]{1,0:T(8,128)S(1)} %get-tuple-element.143.middle_ref) | copy-start | bytes 3145732
  175.7 89.8 %copy-start.4 = (bf16[128,2048]{1,0:T(8,128)(2,1)}, bf16[128,2048]{1,0:T(8,128)(2,1)S(1)}, u32[]{:S(2)}) copy-start(bf16[128,2048]{1,0:T(8,128)(2,1)S(1)} %multiply_convert_fusion.h2_ref) | copy-start | bytes 1572868
  493.5 5.4 copy-start.5
  638.8 18.8 %copy-start.1 = (bf16[512,64]{0,1:T(8,128)(2,1)S(1)}, bf16[512,64]{0,1:T(8,128)(2,1)}, u32[]{:S(2)}) copy-start(bf16[512,64]{0,1:T(8,128)(2,1)} %param.24) | copy-start | bytes 196612
